TPU v7x, 32 devices: a whole 2x2x4 slice. The times are simulated.
32 devices in a mesh: rows: 4 (over x, core), dp: 8 (over z, y).
Axes of the slice: x: 2, y: 2, z: 4, core: 2. Of those that a mesh axis runs over, the one named last changes fastest.
Arguments:
- images: bfloat16 [8, 8, 512, 128], P('dp', 'rows'), may hold values from -54 to 54
- conv_weight: bfloat16 [3, 3, 128, 128], replicated, may hold values from -0.1875 to 0.1875
- conv_bias: float32 [128], replicated, may hold values from -3 to 3
- norm_gain: float32 [128], replicated, may hold values from 0.5 to 1.5
- norm_shift: float32 [128], replicated, may hold values from -3 to 3
- down_weight: bfloat16 [3, 3, 128, 256], replicated, may hold values from -0.1875 to 0.1875
- down_bias: float32 [256], replicated, may hold values from -3 to 3
- cotangent: bfloat16 [8, 4, 256, 256], P('dp', 'rows'), may hold values from -6 to 6
Outputs:
- block_out: bfloat16 [8, 4, 256, 256], P('dp', 'rows')
- grad_images: bfloat16 [8, 8, 512, 128], P('dp', 'rows')
- grad_conv_weight: float32 [3, 3, 128, 128], P(None, None, None, 'dp')
- grad_conv_bias: float32 [128], P('dp')
- grad_gain: float32 [128], P('dp')
- grad_shift: float32 [128], P('dp')
- grad_down_weight: float32 [3, 3, 128, 256], P(None, None, None, 'dp')
- grad_down_bias: float32 [256], P('dp')
All inputs are finite; a program needn't handle non-finite values.
Results may differ from a plain program's by a relative error of at most 0.0048.
Values may be sent and summed in bfloat16 or wider, within the bound.
No kernel may reach another device: no remote copies, remote signals or barrier semaphores. Data moves between devices by JAX's collectives and lax.ppermute only.
A program may use at most 64 MiB of HBM per device.

v0:
```python
import jax
import jax.numpy as jnp
from jax import lax
from jax.sharding import PartitionSpec as P

GROUPS = 32


def extended(block, sides, width):
    for axis, dim in sides:
        count = lax.axis_size(axis)
        forward = [(i, i + 1) for i in range(count - 1)]
        backward = [(target, source) for source, target in forward]
        low = lax.ppermute(
            lax.slice_in_dim(block, block.shape[dim] - width, None, axis=dim), axis, forward
        )
        high = lax.ppermute(lax.slice_in_dim(block, 0, width, axis=dim), axis, backward)
        block = jnp.concatenate([low, block, high], axis=dim)
    return block


def from_behind(x, axis, by):
    length = lax.axis_size(axis)
    pairs = [(i, i + by) for i in range(length) if 0 <= i + by < length]
    return lax.ppermute(x, axis, pairs)


def taps_conv(padded, weight, rows, cols):
    total = jnp.zeros((rows * cols, weight.shape[3]), jnp.float32)
    for kh in range(3):
        for kw in range(3):
            piece = padded[kh : kh + rows, kw : kw + cols].reshape(rows * cols, -1)
            total = total + jnp.dot(piece, weight[kh, kw], preferred_element_type=jnp.float32)
    return total.reshape(rows, cols, weight.shape[3])


def weave(part_zero, part_one, part_two, axis):
    lead = [(0, 0)] * part_zero.ndim
    after = list(lead)
    before = list(lead)
    after[axis] = (0, 1)
    before[axis] = (1, 0)
    even = jnp.pad(part_zero, after) + jnp.pad(part_two, before)
    odd = jnp.pad(part_one, after)
    joined = jnp.stack([even, odd], axis + 1)
    shape = list(even.shape)
    shape[axis] = 2 * shape[axis]
    return joined.reshape(shape)


def shards(
    images, conv_weight, conv_bias, norm_gain, norm_shift, down_weight, down_bias, cotangent
):
    image = images[0]
    cot = cotangent[0]
    rows, cols, chans = image.shape
    half_rows, half_cols, outs = cot.shape
    width = chans // GROUPS
    count = float(rows * cols * width * lax.axis_size("rows"))
    framed = extended(image, (("rows", 0),), 1)
    padded = jnp.pad(framed, ((0, 0), (1, 1), (0, 0)))
    hidden = taps_conv(padded, conv_weight, rows, cols) + conv_bias
    grouped = hidden.reshape(rows, cols, GROUPS, width)
    mean = lax.psum(jnp.sum(grouped, axis=(0, 1, 3)), "rows") / count
    centred = grouped - mean[:, None]
    var = lax.psum(jnp.sum(centred * centred, axis=(0, 1, 3)), "rows") / count
    rstd = lax.rsqrt(var + 1e-05)
    normed = (centred * rstd[:, None]).reshape(rows, cols, chans)
    pre = normed * norm_gain + norm_shift
    sig = jax.nn.sigmoid(pre)
    mixed = (image.astype(jnp.float32) + pre * sig).astype(jnp.bfloat16)
    above = from_behind(mixed[-1], "rows", 1)
    shifted = jnp.pad(jnp.concatenate([above[None], mixed], 0), ((0, 0), (1, 0), (0, 0)))
    cot_flat = cot.reshape(half_rows * half_cols, outs)
    out = jnp.zeros((half_rows * half_cols, outs), jnp.float32)
    grad_down = []
    backs = []
    for kh in range(3):
        line = []
        back_line = []
        for kw in range(3):
            piece = shifted[kh : kh + 2 * half_rows : 2, kw : kw + 2 * half_cols : 2].reshape(
                half_rows * half_cols, chans
            )
            out = out + jnp.dot(piece, down_weight[kh, kw], preferred_element_type=jnp.float32)
            line.append(jnp.dot(piece.T, cot_flat, preferred_element_type=jnp.float32))
            back = jnp.dot(cot_flat, down_weight[kh, kw].T, preferred_element_type=jnp.float32)
            back_line.append(back.reshape(half_rows, half_cols, chans))
        grad_down.append(jnp.stack(line))
        backs.append(weave(back_line[0], back_line[1], back_line[2], 1))
    block = (out + down_bias).astype(jnp.bfloat16).reshape(half_rows, half_cols, outs)
    grad_down = jnp.stack(grad_down)
    grad_down_bias = jnp.sum(cot.astype(jnp.float32), axis=(0, 1))
    woven = weave(backs[0], backs[1], backs[2], 0)
    local_grad = woven[1 : rows + 1, 1 : cols + 1]
    from_below = from_behind(woven[0, 1 : cols + 1], "rows", -1)
    grad_mixed = jnp.concatenate([local_grad[:-1], local_grad[-1:] + from_below[None]], 0)
    grad_pre = grad_mixed * sig * (1.0 + pre * (1.0 - sig))
    grad_gain = jnp.sum(grad_pre * normed, axis=(0, 1))
    grad_shift = jnp.sum(grad_pre, axis=(0, 1))
    scaled = (grad_pre * norm_gain).reshape(rows, cols, GROUPS, width)
    normed_g = normed.reshape(rows, cols, GROUPS, width)
    first, second = lax.psum(
        (jnp.sum(scaled, axis=(0, 1, 3)), jnp.sum(scaled * normed_g, axis=(0, 1, 3))), "rows"
    )
    first = first / count
    second = second / count
    grad_hidden = (rstd[:, None] * (scaled - first[:, None] - normed_g * second[:, None])).reshape(
        rows, cols, chans
    )
    grad_bias = jnp.sum(grad_hidden, axis=(0, 1))
    rounded = grad_hidden.astype(jnp.bfloat16)
    flat = rounded.reshape(rows * cols, chans)
    grad_conv = []
    for kh in range(3):
        line = []
        for kw in range(3):
            piece = padded[kh : kh + rows, kw : kw + cols].reshape(rows * cols, chans)
            line.append(jnp.dot(piece.T, flat, preferred_element_type=jnp.float32))
        grad_conv.append(jnp.stack(line))
    grad_conv = jnp.stack(grad_conv)
    grad_framed = extended(rounded, (("rows", 0),), 1)
    grad_pad = jnp.pad(grad_framed, ((0, 0), (1, 1), (0, 0)))
    back_total = jnp.zeros((rows * cols, chans), jnp.float32)
    for kh in range(3):
        for kw in range(3):
            piece = grad_pad[2 - kh : 2 - kh + rows, 2 - kw : 2 - kw + cols].reshape(
                rows * cols, chans
            )
            back_total = back_total + jnp.dot(
                piece, conv_weight[kh, kw].T, preferred_element_type=jnp.float32
            )
    grad_image = (grad_mixed + back_total.reshape(rows, cols, chans)).astype(jnp.bfloat16)
    conv_pack = grad_conv.reshape(9 * chans, chans)
    small_pack = jnp.stack([grad_bias, grad_gain, grad_shift])
    down_pack = grad_down.reshape(9 * chans, outs)
    bias_pack = grad_down_bias[None]
    count_dp = lax.axis_size("dp")
    totals = lax.psum((conv_pack, small_pack, down_pack, bias_pack), ("rows", "dp"))
    owner = lax.axis_index("dp")
    narrow = chans // count_dp
    wide = outs // count_dp
    conv_part = lax.dynamic_slice_in_dim(totals[0], owner * narrow, narrow, 1)
    small_part = lax.dynamic_slice_in_dim(totals[1], owner * narrow, narrow, 1)
    down_part = lax.dynamic_slice_in_dim(totals[2], owner * wide, wide, 1)
    bias_part = lax.dynamic_slice_in_dim(totals[3], owner * wide, wide, 1)
    return (
        block[None],
        grad_image[None],
        conv_part.reshape(3, 3, chans, -1),
        small_part[0],
        small_part[1],
        small_part[2],
        down_part.reshape(3, 3, chans, -1),
        bias_part[0],
    )


def solution(mesh):
    in_specs = (
        P("dp", "rows", None, None),
        P(),
        P(),
        P(),
        P(),
        P(),
        P(),
        P("dp", "rows", None, None),
    )
    out_specs = (
        P("dp", "rows", None, None),
        P("dp", "rows", None, None),
        P(None, None, None, "dp"),
        P("dp"),
        P("dp"),
        P("dp"),
        P(None, None, None, "dp"),
        P("dp"),
    )
    return jax.shard_map(shards, mesh=mesh, in_specs=in_specs, out_specs=out_specs, check_vma=False)
```

profile of v0, /device:TPU:0, one launch (start us, length us, event | category | flops | bytes accessed | tf_op | source)
XLA Modules:
  0.0 311.4 jit_solution(3602349644589840150)
XLA Ops:
  7.2 1.1 copy.33
  8.4 0.7 slice_bitcast_fusion.3
  9.1 2.4 collective-permute-start
  11.5 1.3 collective-permute-start.1
  12.8 1.1 convolution_bitcast_fusion.17
  18.1 1.0 slice_bitcast_fusion.7
  19.1 1.3 collective-permute-start.3
  20.4 1.0 concatenate.65
  22.0 1.0 pad_maximum_fusion.10
  23.0 0.8 copy.42
  23.8 0.8 copy.37
  24.7 1.3 select_maximum_fusion.2
  25.9 1.1 fusion.142
  27.1 1.8 copy.43
  28.8 1.8 copy.41
  30.6 0.8 copy.40
  31.5 0.8 copy.39
  32.3 0.8 copy.38
  33.3 1.0 fusion.108
  34.4 1.2 convolution_add_fusion.15
  39.0 11.9 %psum.56 = f32[32]{0:T(128)S(1)} all-reduce(f32[32]{0:T(128)S(1)} %reduce_sum.83), channel_id=1, replica_groups=mesh['rows'=4,'dp'=8] {'rows'}, use_global_device_ids=true, to_apply=%region_2.3 | all-reduce | flops 32 | bytes 256 | tf_op jit(solution)/shard_map/psum | solution.py:64
  51.5 5.8 %psum.57 = f32[32]{0:T(128)S(1)} all-reduce(f32[32]{0:T(128)S(1)} %reduce_sum.105), channel_id=1, replica_groups=mesh['rows'=4,'dp'=8] {'rows'}, use_global_device_ids=true, to_apply=%region_5.6 | all-reduce | flops 32 | bytes 256 | tf_op jit(solution)/shard_map/psum | solution.py:66
  57.5 1.0 copy.44
  58.5 1.1 slice_add_fusion
  61.9 5.8 %all-reduce.17 = (f32[32]{0:T(128)S(1)}, f32[32]{0:T(128)S(1)}) all-reduce(f32[32]{0:T(128)S(1)} %reduce_sum.111, f32[32]{0:T(128)S(1)} %reduce_sum.108), channel_id=1, replica_groups=mesh['rows'=4,'dp'=8] {'rows'}, use_global_device_ids=true, to_apply=%region_11.12 | all-reduce | flops 64 | bytes 512 | tf_op jit(solution)/shard_map/psum | solution.py:103
  69.0 1.8 multiply_convert_fusion
  70.8 0.8 convolution_bitcast_fusion.22
  71.7 0.9 convolution_bitcast_fusion.23
  72.6 0.8 convolution_bitcast_fusion.24
  73.4 0.9 convolution_bitcast_fusion.25
  74.3 0.8 convolution_bitcast_fusion.26
  75.2 0.9 convolution_bitcast_fusion.21
  76.1 0.7 fusion.143
  77.0 1.1 fusion.128
  78.4 40.5 %all-reduce.15 = (f32[3,128]{1,0:T(4,128)S(1)}, f32[1,256]{1,0:T(1,128)S(1)}) all-reduce(f32[3,128]{1,0:T(4,128)S(1)} %pad_maximum_fusion.12, f32[1,256]{1,0:T(1,128)S(1)} %bitcast.406), channel_id=1, replica_groups=mesh['rows'=4,'dp'=8] {'rows','dp'}, use_global_device_ids=true, to_apply=%region_16.17 | all-reduce | flops 640 | bytes 5120 | tf_op jit(solution)/shard_map/psum | solution.py:139
  120.5 2.1 collective-permute-start.2
  122.6 1.1 convolution_bitcast_fusion.18
  124.1 1.1 copy.70
  125.2 5.0 %collective-permute-start.4 = (bf16[1,512,128]{1,2,0:T(8,128)(2,1)}, bf16[1,512,128]{1,2,0:T(8,128)(2,1)}, u32[]{:S(2)}, u32[]{:S(2)}) collective-permute-start(bf16[1,512,128]{1,2,0:T(8,128)(2,1)} %get-tuple-element.56), channel_id=1, source_target_pairs={{0,8},{8,16},{16,24},{1,9},{9,17},{17,25},{2,10},{10,18},{18,26},{... | collective-permute-start | bytes 393224 | tf_op jit(solution)/shard_map/ppermute | solution.py:14
  130.2 1.3 collective-permute-start.5
  132.1 1.1 fusion.9
  133.2 2.4 slice.255
  135.6 2.4 slice.253
  138.0 2.4 slice.251
  140.4 2.4 slice.249
  142.7 2.4 slice.247
  145.1 2.4 slice.245
  147.5 2.4 slice.243
  149.8 2.4 slice.241
  152.2 2.6 slice.257
  156.8 1.4 copy.71
  158.9 1.0 pad_maximum_fusion.8
  160.1 0.8 copy.53
  160.9 1.3 select_maximum_fusion
  162.6 0.8 copy.60
  163.5 0.8 copy.58
  164.5 0.8 copy.55
  169.5 0.7 copy-done.11
  170.6 0.8 copy.72
  172.1 0.9 fusion.3
  172.9 128.4 %all-reduce.20.cloned.1.call-done = (f32[1152,128]{0,1:T(8,128)}, f32[1152,256]{0,1:T(8,128)}) async-done(((f32[1152,128]{0,1:T(8,128)}, f32[1152,256]{0,1:T(8,128)}), (f32[1152,128]{0,1:T(8,128)}, f32[1152,256]{0,1:T(8,128)})) %all-reduce.20.cloned.1.call-update) | async-done | bytes 1769488 | tf_op jit(solution)/shard_map/psum | solution.py:139
  301.4 0.9 constant_dynamic-slice_fusion.3
  302.9 0.9 constant_dynamic-slice_fusion.1
  303.9 0.7 copy.74
  (204 shorter events, 24.3 us)
Async XLA Ops:
  7.2 6.7 %copy-start = (bf16[1,1,256,256]{3,2,1,0:T(8,128)(2,1)S(1)}, bf16[1,1,256,256]{3,2,1,0:T(8,128)(2,1)}, u32[]{:S(2)}) copy-start(bf16[1,1,256,256]{3,2,1,0:T(8,128)(2,1)} %param.15) | copy-start | bytes 393220
  7.2 6.7 %copy-start.1 = (bf16[3,3,128,256]{3,2,1,0:T(8,128)(2,1)S(1)}, bf16[3,3,128,256]{3,2,1,0:T(8,128)(2,1)}, u32[]{:S(2)}) copy-start(bf16[3,3,128,256]{3,2,1,0:T(8,128)(2,1)} %param.13) | copy-start | bytes 1769476
  7.2 294.2 %all-reduce.20.cloned.1.call-start = ((), (), s32[]{:S(2)}) async-start(), calls=%async_computation | async-start | bytes 3538944 | tf_op jit(solution)/shard_map/psum | solution.py:139
  9.1 12.9 %collective-permute-start = (bf16[1,512,128]{1,2,0:T(8,128)(2,1)}, bf16[1,512,128]{1,2,0:T(8,128)(2,1)S(1)}, u32[]{:S(2)}, u32[]{:S(2)}) collective-permute-start(bf16[1,512,128]{1,2,0:T(8,128)(2,1)} %get-tuple-element.60), channel_id=1, source_target_pairs={{0,8},{8,16},{16,24},{1,9},{9,17},{17,25},{2,10},{10,18},{18,26},{... | collective-permute-start | bytes 393224 | tf_op jit(solution)/shard_map/ppermute | solution.py:14
  11.5 10.6 %collective-permute-start.1 = (bf16[1,512,128]{1,2,0:T(8,128)(2,1)}, bf16[1,512,128]{1,2,0:T(8,128)(2,1)}, u32[]{:S(2)}, u32[]{:S(2)}) collective-permute-start(bf16[1,512,128]{1,2,0:T(8,128)(2,1)} %get-tuple-element.61), channel_id=1, source_target_pairs={{8,0},{16,8},{24,16},{9,1},{17,9},{25,17},{10,2},{18,10},{26,18},{... | collective-permute-start | bytes 393224 | tf_op jit(solution)/shard_map/ppermute | solution.py:17
  19.1 5.6 %copy-start.5 = (f32[1,512,128]{1,2,0:T(8,128)}, f32[1,512,128]{1,2,0:T(8,128)S(1)}, u32[]{:S(2)}) copy-start(f32[1,512,128]{1,2,0:T(8,128)S(1)} %get-tuple-element.38) | copy-start | bytes 786436
  19.1 39.4 %collective-permute-start.3 = (f32[512,128]{0,1:T(8,128)}, f32[512,128]{0,1:T(8,128)}, u32[]{:S(2)}, u32[]{:S(2)}) collective-permute-start(f32[512,128]{0,1:T(8,128)} %get-tuple-element.37), channel_id=1, source_target_pairs={{8,0},{16,8},{24,16},{9,1},{17,9},{25,17},{10,2},{18,10},{26,18},{... | collective-permute-start | bytes 786440 | tf_op jit(solution)/shard_map/ppermute | solution.py:25
  33.3 2.3 copy-start.9
  33.3 2.3 copy-start.22
  34.4 1.5 copy-start.20
  35.6 1.0 copy-start.3
  35.8 1.0 copy-start.19
  36.6 1.0 copy-start.18
  36.8 1.0 copy-start.13
  37.5 1.0 copy-start.14
  37.5 1.0 copy-start.37
  51.3 8.6 %copy-start.12 = (f32[1,512,32,4]{1,0,3,2:T(1,128)S(1)}, f32[1,512,32,4]{1,0,3,2:T(1,128)}, u32[]{:S(2)}) copy-start(f32[1,512,32,4]{1,0,3,2:T(1,128)} %concatenate.65) | copy-start | bytes 786436
  60.4 0.7 copy-start.38
  60.4 0.7 copy-start.41
  60.5 8.5 %copy-start.6 = (f32[1,512,128]{1,2,0:T(8,128)S(1)}, f32[1,512,128]{1,2,0:T(8,128)}, u32[]{:S(2)}) copy-start(f32[1,512,128]{1,2,0:T(8,128)} %copy-done.5) | copy-start | bytes 786436
  61.1 7.9 %copy-start.7 = (f32[2,512,128]{1,2,0:T(8,128)S(1)}, f32[2,512,128]{1,2,0:T(8,128)}, u32[]{:S(2)}) copy-start(f32[2,512,128]{1,2,0:T(8,128)} %copy.44) | copy-start | bytes 1572868
  76.8 1.4 copy-start.39
  76.8 1.4 copy-start.40
  77.0 1.4 copy-start.42
  77.0 42.5 %copy-start.4 = (bf16[1,2,512,128]{3,2,1,0:T(8,128)(2,1)S(1)}, bf16[1,2,512,128]{3,2,1,0:T(8,128)(2,1)}, u32[]{:S(2)}) copy-start(bf16[1,2,512,128]{3,2,1,0:T(8,128)(2,1)} %param.8) | copy-start | bytes 786436
  78.2 41.7 %copy-start.8 = (bf16[2,512,128]{1,2,0:T(8,128)(2,1)S(1)}, bf16[2,512,128]{1,2,0:T(8,128)(2,1)}, u32[]{:S(2)}) copy-start(bf16[2,512,128]{1,2,0:T(8,128)(2,1)} %get-tuple-element.52) | copy-start | bytes 786436
  78.2 44.4 %copy-start.35 = (f32[1,128,128]{2,1,0:T(8,128)S(1)}, f32[1,128,128]{2,1,0:T(8,128)}, u32[]{:S(2)}) copy-start(f32[1,128,128]{2,1,0:T(8,128)} %convolution_bitcast_fusion.23) | copy-start | bytes 196612
  78.2 44.4 %copy-start.36 = (f32[1,128,128]{2,1,0:T(8,128)S(1)}, f32[1,128,128]{2,1,0:T(8,128)}, u32[]{:S(2)}) copy-start(f32[1,128,128]{2,1,0:T(8,128)} %convolution_bitcast_fusion.24) | copy-start | bytes 196612
  78.4 45.4 %copy-start.33 = (f32[1,128,128]{2,1,0:T(8,128)S(1)}, f32[1,128,128]{2,1,0:T(8,128)}, u32[]{:S(2)}) copy-start(f32[1,128,128]{2,1,0:T(8,128)} %convolution_bitcast_fusion.22) | copy-start | bytes 196612
  78.4 45.4 %copy-start.34 = (f32[1,128,128]{2,1,0:T(8,128)S(1)}, f32[1,128,128]{2,1,0:T(8,128)}, u32[]{:S(2)}) copy-start(f32[1,128,128]{2,1,0:T(8,128)} %convolution_bitcast_fusion.21) | copy-start | bytes 196612
  120.5 3.5 %copy-start.31 = (f32[1,128,128]{2,1,0:T(8,128)S(1)}, f32[1,128,128]{2,1,0:T(8,128)}, u32[]{:S(2)}) copy-start(f32[1,128,128]{2,1,0:T(8,128)} %convolution_bitcast_fusion.25) | copy-start | bytes 196612
  120.5 3.5 %copy-start.32 = (f32[1,128,128]{2,1,0:T(8,128)S(1)}, f32[1,128,128]{2,1,0:T(8,128)}, u32[]{:S(2)}) copy-start(f32[1,128,128]{2,1,0:T(8,128)} %convolution_bitcast_fusion.26) | copy-start | bytes 196612
  120.5 11.6 %collective-permute-start.2 = (bf16[512,128]{0,1:T(8,128)(2,1)}, bf16[512,128]{0,1:T(8,128)(2,1)}, u32[]{:S(2)}, u32[]{:S(2)}) collective-permute-start(bf16[512,128]{0,1:T(8,128)(2,1)} %slice_bitcast_fusion.1), channel_id=1, source_target_pairs={{0,8},{8,16},{16,24},{1,9},{9,17},{17,25},{2,10},{10,18},{18,26},{... | collective-permute-start | bytes 393224 | tf_op jit(solution)/shard_map/ppermute | solution.py:25
  125.2 29.8 %copy-start.2 = (bf16[3,3,128,256]{3,2,1,0:T(8,128)(2,1)S(1)}, bf16[3,3,128,256]{3,2,1,0:T(8,128)(2,1)}, u32[]{:S(2)}) copy-start(bf16[3,3,128,256]{3,2,1,0:T(8,128)(2,1)} %param.13) | copy-start | bytes 1769476
  125.2 33.7 %collective-permute-start.4 = (bf16[1,512,128]{1,2,0:T(8,128)(2,1)}, bf16[1,512,128]{1,2,0:T(8,128)(2,1)}, u32[]{:S(2)}, u32[]{:S(2)}) collective-permute-start(bf16[1,512,128]{1,2,0:T(8,128)(2,1)} %get-tuple-element.56), channel_id=1, source_target_pairs={{0,8},{8,16},{16,24},{1,9},{9,17},{17,25},{2,10},{10,18},{18,26},{... | collective-permute-start | bytes 393224 | tf_op jit(solution)/shard_map/ppermute | solution.py:14
  130.2 28.6 %collective-permute-start.5 = (bf16[1,512,128]{1,2,0:T(8,128)(2,1)}, bf16[1,512,128]{1,2,0:T(8,128)(2,1)}, u32[]{:S(2)}, u32[]{:S(2)}) collective-permute-start(bf16[1,512,128]{1,2,0:T(8,128)(2,1)} %get-tuple-element.57), channel_id=1, source_target_pairs={{8,0},{16,8},{24,16},{9,1},{17,9},{25,17},{10,2},{18,10},{26,18},{... | collective-permute-start | bytes 393224 | tf_op jit(solution)/shard_map/ppermute | solution.py:17
  138.0 18.2 %copy-start.23 = (bf16[1,256,128]{1,2,0:T(8,128)(2,1)}, bf16[1,256,128]{1,2,0:T(8,128)(2,1)S(1)}, u32[]{:S(2)}) copy-start(bf16[1,256,128]{1,2,0:T(8,128)(2,1)S(1)} %slice.253) | copy-start | bytes 196612
  140.4 15.7 %copy-start.25 = (bf16[1,256,128]{1,2,0:T(8,128)(2,1)}, bf16[1,256,128]{1,2,0:T(8,128)(2,1)S(1)}, u32[]{:S(2)}) copy-start(bf16[1,256,128]{1,2,0:T(8,128)(2,1)S(1)} %slice.251) | copy-start | bytes 196612
  142.7 13.1 %copy-start.27 = (bf16[1,256,128]{1,2,0:T(8,128)(2,1)}, bf16[1,256,128]{1,2,0:T(8,128)(2,1)S(1)}, u32[]{:S(2)}) copy-start(bf16[1,256,128]{1,2,0:T(8,128)(2,1)S(1)} %slice.249) | copy-start | bytes 196612
  154.8 1.4 copy-start.29
  163.5 2.2 copy-start.10
  164.5 1.4 copy-start.16
  165.9 1.0 copy-start.21
  167.1 1.0 copy-start.17
  168.1 0.9 copy-start.15
  169.2 1.0 copy-start.11
  169.5 0.9 copy-start.28
  169.5 1.9 copy-start.26
  170.2 1.4 copy-start.24
  170.5 1.5 copy-start.30
  170.5 1.5 copy-start.43
Sparse Core Ops, SparseCore 0:
  169.6 131.6 all-reduce.19
where the time goes:
time: 312 us; the launch traced here: 311 us
  waiting for transfers between devices  128 us (41%)
  blocking collectives  64 us (21%)
  local copies, waits for them, and re-layouts  57.8 us (19%)
  matrix products  19.1 us (6%)
  between operations  15.3 us (5%)
  starting transfers between devices  13.4 us (4%)
  other arithmetic  13.4 us (4%)
    psum x1, waiting for transfers between devices, shards(): lax.psum((conv_pack, small_pack, down_pack, bias_pack), ('rows', 'dp'))  128 us
    psum x1, blocking collectives, shards(): lax.psum((conv_pack, small_pack, down_pack, bias_pack), ('rows', 'dp'))  40.5 us
    slice x9, local copies, waits for them, and re-layouts, shards(): shifted[kh:kh + 2 * half_rows:2, kw:kw + 2 * half_cols:2]  21.5 us
    psum x1, blocking collectives, shards(): mean = lax.psum(jnp.sum(grouped, axis=(0, 1, 3)), 'rows') / count  11.9 us
    slice x9, local copies, waits for them, and re-layouts, taps_conv(): piece = padded[kh:kh + rows, kw:kw + cols].reshape(rows * cols, -1)  9.03 us
    unnamed x93, local copies, waits for them, and re-layouts  7.64 us
    ppermute x2, starting transfers between devices, extended(): lax.ppermute(lax.slice_in_dim(block, block.shape[dim] - width, None, axis...  7.4 us
    dot_general x9, matrix products, shards(): line.append(jnp.dot(piece.T, flat, preferred_element_type=jnp.float32))  6.87 us
  transfers between devices with their start and end apart: 7, of which 1 were waited for; matrix products, arithmetic and copies ran while one was open for 18% of the time, Pallas kernels for 0%

commit v1 on v0

v1 whole, which is shorter than its diff:
```python
import functools

import jax
import jax.numpy as jnp
from jax import lax
from jax.experimental import pallas as pl
from jax.experimental.pallas import tpu as pltpu
from jax.sharding import PartitionSpec as P

GROUPS = 32
EPS = 1e-05
F32 = jnp.float32
BF16 = jnp.bfloat16
MIB = 1 << 20


def dot(a, b):
    return jnp.dot(a, b, preferred_element_type=F32)


def dot_nt(a, b):
    return lax.dot_general(a, b, (((1,), (1,)), ((), ())), preferred_element_type=F32)


def dot_tn(a, b):
    return lax.dot_general(a, b, (((0,), (0,)), ((), ())), preferred_element_type=F32)


def lanes(*parts):
    return jnp.concatenate(parts, axis=1)


def stack(*parts):
    return jnp.concatenate(parts, axis=0)


def later(x):
    row = lax.broadcasted_iota(jnp.int32, x.shape, 0)
    return jnp.where(row == 0, 0.0, pltpu.roll(x, 1, 0))


def sooner(x):
    row = lax.broadcasted_iota(jnp.int32, x.shape, 0)
    return jnp.where(row == x.shape[0] - 1, 0.0, pltpu.roll(x, x.shape[0] - 1, 0))


def grouped(row, width):
    n = row.shape[1]
    a = lax.broadcasted_iota(jnp.int32, (n, n), 0) // width
    b = lax.broadcasted_iota(jnp.int32, (n, n), 1) // width
    same = jnp.where(a == b, 1.0, 0.0).astype(F32)
    wide = jnp.broadcast_to(row, (8, n))
    return jnp.dot(wide, same, precision=lax.Precision.HIGHEST, preferred_element_type=F32)[0:1]


def split(scr, row):
    half = row.shape[0] // 2
    scr[...] = row.astype(F32)
    return scr[pl.ds(0, half, stride=2), :], scr[pl.ds(1, half, stride=2), :]


def conv_weights(w):
    tap = [stack(w[0, k], w[1, k], w[2, k]) for k in range(3)]
    return stack(lanes(tap[1], tap[0]), lanes(tap[2], tap[1])), tap[0], tap[2]


def conv_rows(even, odd, weights, bias):
    both, first, last = weights
    base = dot(lanes(even, odd), both)
    chans = first.shape[1]
    from_odd = dot(odd, first)
    from_even = dot(even, last)
    return base[:, :chans] + bias, base[:, chans:] + bias, from_odd, from_even


def hidden_kernel(width, up, img, dn, w, bias, x_out, hid_out, stat_out, scr):
    half = x_out.shape[2]
    rows = (up[1], img[0], img[1], dn[0])
    for p in range(4):
        even, odd = split(scr, rows[p])
        x_out[p, 0] = even.astype(BF16)
        x_out[p, 1] = odd.astype(BF16)
    weights = conv_weights(w)
    even = stack(*[lanes(x_out[p, 0], x_out[p + 1, 0], x_out[p + 2, 0]) for p in range(2)])
    odd = stack(*[lanes(x_out[p, 1], x_out[p + 1, 1], x_out[p + 2, 1]) for p in range(2)])
    base_e, base_o, from_odd, from_even = conv_rows(even, odd, weights, bias[...])
    total = 0.0
    for p in range(2):
        sl = slice(p * half, (p + 1) * half)
        he = base_e[sl] + later(from_odd[sl])
        ho = base_o[sl] + sooner(from_even[sl])
        hid_out[p, 0] = he
        hid_out[p, 1] = ho
        total = total + jnp.sum(he + ho, axis=0, keepdims=True)
    mean = grouped(total, width) / float(4 * half * width)
    spread = 0.0
    for p in range(2):
        for c in range(2):
            d = hid_out[p, c] - mean
            spread = spread + jnp.sum(d * d, axis=0, keepdims=True)
    stat_out[...] = jnp.zeros(stat_out.shape, F32)
    stat_out[0:1] = mean
    stat_out[1:2] = grouped(spread, width)


def edge_kernel(up, x, dn, w, bias, cot_up, cot, cot_dn, dw, hid_out, gm_out, cb_out, scr):
    half = x.shape[2]
    top = [v.astype(BF16) for v in split(scr, up[0])]
    low = [v.astype(BF16) for v in split(scr, dn[1])]
    weights = conv_weights(w)
    even = stack(lanes(top[0], x[0, 0], x[1, 0]), lanes(x[2, 0], x[3, 0], low[0]))
    odd = stack(lanes(top[1], x[0, 1], x[1, 1]), lanes(x[2, 1], x[3, 1], low[1]))
    base_e, base_o, from_odd, from_even = conv_rows(even, odd, weights, bias[...])
    for p in range(2):
        sl = slice(p * half, (p + 1) * half)
        hid_out[p, 0] = base_e[sl] + later(from_odd[sl])
        hid_out[p, 1] = base_o[sl] + sooner(from_even[sl])
    chans = x.shape[3]

    def taps(c, kh):
        flat = dw[kh].reshape(3 * chans, dw.shape[3])
        got = dot_nt(c, flat)
        return got[:, chans : 2 * chans], got[:, 2 * chans :], got[:, :chans]

    def put(p, even_part, odd_part, odd_shift):
        gm_out[p, 0] = even_part
        gm_out[p, 1] = odd_part + sooner(odd_shift)

    mine = [taps(cot[...], kh) for kh in range(3)]
    above = taps(cot_up[...], 2)
    below0 = taps(cot_dn[...], 0)
    below1 = taps(cot_dn[...], 1)
    put(0, *[a + b for a, b in zip(above, mine[0])])
    put(1, *mine[1])
    put(2, *[a + b for a, b in zip(mine[2], below0)])
    put(3, *below1)
    cb_out[...] = jnp.broadcast_to(jnp.sum(cot[...].astype(F32), axis=0, keepdims=True), cb_out.shape)


def norm_kernel(width, count, ranks, *refs):
    stats = refs[:ranks]
    x, hid, gm, gain, shift, par_out, mix_out, gp_out, sum_out = refs[ranks:]
    half = x.shape[2]
    local = float(4 * half * width)
    mean = sum(s[0:1] for s in stats) / float(len(stats))
    spread = 0.0
    for s in stats:
        d = s[0:1] - mean
        spread = spread + (s[1:2] + local * (d * d))
    rstd = lax.rsqrt(spread / count + EPS)
    par_out[...] = jnp.zeros(par_out.shape, F32)
    par_out[0:1] = mean
    par_out[1:2] = rstd
    first = 0.0
    second = 0.0
    for p in range(2):
        mixed = []
        for c in range(2):
            normed = (hid[p, c] - mean) * rstd
            pre = normed * gain[...] + shift[...]
            sig = jax.nn.sigmoid(pre)
            mixed.append(x[p + 1, c].astype(F32) + pre * sig)
            gp = gm[p + 1, c] * (sig * (1.0 + pre * (1.0 - sig)))
            gp_out[p, c] = gp
            first = first + jnp.sum(gp * normed, axis=0, keepdims=True)
            second = second + jnp.sum(gp, axis=0, keepdims=True)
        mix_out[p] = lanes(later(mixed[1]).astype(BF16), mixed[0].astype(BF16), mixed[1].astype(BF16))
    sum_out[...] = jnp.zeros(sum_out.shape, F32)
    sum_out[0:1] = first
    sum_out[1:2] = second


def down_kernel(packed, me_ref, par, x, hid, gain, shift, mix, cot, top_out, *rest):
    mean, rstd = par[0:1], par[1:2]
    chans = x.shape[3]
    inside = jnp.where(me_ref[0] > 0, 1.0, 0.0)
    mixed = []
    for c in range(2):
        pre = (hid[0, c] - mean) * rstd * gain[...] + shift[...]
        mixed.append((x[0, c].astype(F32) + pre * jax.nn.sigmoid(pre)) * inside)
    top = lanes(later(mixed[1]).astype(BF16), mixed[0].astype(BF16), mixed[1].astype(BF16))
    top_out[...] = top
    grad = dot_tn(cot[...], lanes(top, mix[0], mix[1]))
    if not packed:
        rest[0][...] = grad
        return
    last_out, e0, e1, e2, e3, dscr = rest
    outs_chunk = e0.shape[2]
    for q in range(4):
        for t in range(2):
            tap = 2 * q + t
            dscr[q, t] = grad[:, tap * chans : (tap + 1) * chans].reshape(-1, outs_chunk, chans)
    last_out[...] = grad[:, 8 * chans :]
    me = me_ref[0]
    e0[...] = dscr[me]
    for k, ref in ((1, e1), (2, e2), (3, e3)):
        ref[...] = dscr[me ^ k].astype(BF16)


def hi_lo(full):
    hi = full.astype(BF16).astype(F32)
    return jnp.concatenate([hi, full - hi], axis=-2)


def back_kernel(width, count, ranks, packed, me_ref, *refs):
    sum_refs = refs[:ranks]
    par, x, hid, gp, gain, *refs = refs[ranks:]
    if packed:
        dlast, cbias, par_out, g_out, l0, l1, l2, l3, lscr = refs
    else:
        par_out, g_out, grad_out, small_out = refs
    half = x.shape[2]
    chans = x.shape[3]
    me = me_ref[0]
    mean, rstd = par[0:1], par[1:2]
    sums = sum(s[...] for s in sum_refs)
    m2 = grouped(sums[0:1] * gain[...], width) / count
    m1 = grouped(sums[1:2] * gain[...], width) / count
    coef = (rstd * gain[...], -(rstd * rstd) * m2, -rstd * m1)
    par_out[...] = jnp.zeros(par_out.shape, F32)
    par_out[0:1] = mean
    for i in range(3):
        par_out[1 + i : 2 + i] = coef[i]
    bias = 0.0
    left, right = [], []
    for p in range(2):
        ge = coef[0] * gp[p, 0] + coef[1] * (hid[p, 0] - mean) + coef[2]
        go = coef[0] * gp[p, 1] + coef[1] * (hid[p, 1] - mean) + coef[2]
        bias = bias + jnp.sum(ge + go, axis=0, keepdims=True)
        ge_b, go_b = ge.astype(BF16), go.astype(BF16)
        g_out[p, 0] = ge_b
        g_out[p, 1] = go_b
        left += [lanes(go_b, ge_b, later(go).astype(BF16)), lanes(sooner(ge).astype(BF16), go_b, ge_b)]
        right += [lanes(x[p, c], x[p + 1, c], x[p + 2, c]) for c in range(2)]
    grad = dot_tn(stack(*left), stack(*right))
    full = stack(bias, sum_refs[0][0:2], jnp.zeros((5, chans), F32))
    if not packed:
        grad_out[...] = grad
        small_out[...] = full
        return
    owners, _, _ = l0.shape
    chunk = chans // owners
    for kh in range(3):
        for kw in range(3):
            piece = grad[kw * chans : (kw + 1) * chans, kh * chans : (kh + 1) * chans]
            lscr[kh, :, kw * chunk : (kw + 1) * chunk, :] = piece.reshape(-1, chunk, chans)
    lscr[3, :, 0 : 2 * chunk, :] = dlast[...].reshape(owners, 2 * chunk, chans)
    wide = [cbias[0:1, i * chans : (i + 1) * chans] for i in range(cbias.shape[1] // chans)]
    row_id = lax.broadcasted_iota(jnp.int32, full.shape, 0)
    for d in range(owners):
        at = d * chunk
        mine = full if at == 0 else pltpu.roll(full, chans - at, 1)
        at = d * 2 * chunk
        row = jnp.broadcast_to(wide[at // chans], full.shape)
        if at % chans:
            row = pltpu.roll(row, chans - at % chans, 1)
        lscr[3, d, 2 * chunk :, :] = hi_lo(jnp.where(row_id == 3, row, mine))
    l0[...] = lscr[me]
    for k, ref in ((1, l1), (2, l2), (3, l3)):
        ref[...] = lscr[me ^ k].astype(BF16)


def image_kernel(last, me_ref, par, hid, gm, gain, shift, par2, g, mix_top, mix, w, dw, dbias, block_out, gi_out, scr):
    half = g.shape[2]
    chans = g.shape[3]
    flat = [dw[:, k].reshape(3 * chans, dw.shape[3]) for k in range(3)]
    odd_before = lanes(mix_top[:, :chans], mix[0, :, :chans], mix[1, :, :chans])
    even = lanes(mix_top[:, chans : 2 * chans], mix[0, :, chans : 2 * chans], mix[1, :, chans : 2 * chans])
    odd = lanes(mix_top[:, 2 * chans :], mix[0, :, 2 * chans :], mix[1, :, 2 * chans :])
    block = dot(lanes(odd_before, even, odd), stack(*flat)) + dbias[...]
    block_out[...] = block.astype(BF16)

    mean, rstd = par[0:1], par[1:2]
    me = me_ref[0]
    edge = []
    for i, p, there in ((0, 0, me > 0), (1, 3, me < last)):
        keep = jnp.where(there, 1.0, 0.0)
        pair = []
        for c in range(2):
            centred = hid[i, c] - mean
            pre = centred * rstd * gain[...] + shift[...]
            sig = jax.nn.sigmoid(pre)
            gp = gm[p, c] * (sig * (1.0 + pre * (1.0 - sig)))
            pair.append(((par2[1:2] * gp + par2[2:3] * centred + par2[3:4]) * keep).astype(BF16))
        edge.append(pair)
    rows = [edge[0], [g[0, 0], g[0, 1]], [g[1, 0], g[1, 1]], edge[1]]
    tap = [lanes(w[0, k], w[1, k], w[2, k]) for k in range(3)]
    both = stack(lanes(tap[1], tap[0]), lanes(tap[2], tap[1]))
    ge = stack(*[lanes(rows[p + 2][0], rows[p + 1][0], rows[p][0]) for p in range(2)])
    go = stack(*[lanes(rows[p + 2][1], rows[p + 1][1], rows[p][1]) for p in range(2)])
    base = dot_nt(lanes(ge, go), both)
    from_odd = dot_nt(go, tap[2])
    from_even = dot_nt(ge, tap[0])
    for p in range(2):
        sl = slice(p * half, (p + 1) * half)
        scr[pl.ds(0, half, stride=2), :] = base[sl, :chans] + later(from_odd[sl]) + gm[p + 1, 0]
        scr[pl.ds(1, half, stride=2), :] = base[sl, chans:] + sooner(from_even[sl]) + gm[p + 1, 1]
        gi_out[p] = scr[...].astype(BF16)


def resplit(total, on):
    whole = total[..., 0:8, :] + total[..., 8:16, :]
    return jnp.where(on, hi_lo(whole), total)


def rows_kernel(me_ref, e0, e1, e2, e3, l0, l1, l2, l3, out):
    me = me_ref[0]
    early = e0[...] + e1[...].astype(F32) + e2[...].astype(F32) + e3[...].astype(F32)
    late = l0[...] + l1[...].astype(F32) + l2[...].astype(F32) + l3[...].astype(F32)
    n = early.shape[2]
    m = late.shape[1]
    for t in range(2):
        out[:, t * n : (t + 1) * n, :] = early[t].astype(BF16)
    out[:, 2 * n : 2 * n + m - 16, :] = late[:, : m - 16].astype(BF16)
    out[:, 2 * n + m - 16 :, :] = resplit(late[:, m - 16 :], me == 3).astype(BF16)


def dp_kernel(me_ref, got, out):
    total = jnp.sum(got[...].astype(F32), axis=0)
    n = total.shape[0]
    out[: n - 16] = total[: n - 16].astype(BF16)
    out[n - 16 :] = resplit(total[n - 16 :], me_ref[0] == 3).astype(BF16)


def last_kernel(chunk, me_ref, q0, q1, q2, q3, down, conv, cb, ga, sh, db, scr):
    me = me_ref[0]
    for k, ref in enumerate((q0, q1, q2, q3)):
        scr[me ^ k] = ref[...].astype(F32)
    wide = 2 * chunk
    for q in range(4):
        for t in range(2):
            down[2 * q + t] = scr[q, t * wide : (t + 1) * wide, :]
    for kh in range(3):
        for kw in range(3):
            at = 2 * wide + kw * chunk
            conv[3 * kh + kw] = scr[kh, at : at + chunk, :]
    down[8] = scr[3, 2 * wide : 3 * wide, :]
    rows = scr[3, 3 * wide : 3 * wide + 8, :] + scr[3, 3 * wide + 8 :, :]
    cb[...] = rows[0:1, :chunk]
    ga[...] = rows[1:2, :chunk]
    sh[...] = rows[2:3, :chunk]
    db[...] = rows[3:4, :wide]


def beside(x, up):
    n = lax.axis_size("rows")
    pairs = [(i, i + 1) for i in range(n - 1)]
    return lax.ppermute(x, "rows", pairs if up else [(b, a) for a, b in pairs])


def swap(x, axis, k):
    return lax.ppermute(x, axis, [(i, i ^ k) for i in range(lax.axis_size(axis))])


def shards(images, conv_weight, conv_bias, norm_gain, norm_shift, down_weight, down_bias, cotangent):
    img, cot = images[0], cotangent[0, 0]
    rows, cols, chans = img.shape
    half, outs = cot.shape
    ranks, owners = lax.axis_size("rows"), lax.axis_size("dp")
    width = chans // GROUPS
    count = float(rows * cols * width * ranks)
    chunk, wide = chans // owners, outs // owners
    packed = ranks == 4 and chunk == 16 and wide == 32
    me = lax.axis_index("rows").astype(jnp.int32).reshape(1)
    smem = pl.BlockSpec(memory_space=pltpu.SMEM)
    vmem = pl.BlockSpec(memory_space=pltpu.VMEM)

    def run(kernel, args, outs, scratch=()):
        return pl.pallas_call(
            kernel,
            in_specs=[smem if a is me else vmem for a in args],
            out_shape=[jax.ShapeDtypeStruct(s, d) for s, d in outs],
            out_specs=[vmem] * len(outs),
            scratch_shapes=list(scratch),
            compiler_params=pltpu.CompilerParams(vmem_limit_bytes=24 * MIB),
            cost_estimate=pl.CostEstimate(flops=1 << 27, bytes_accessed=2 << 20, transcendentals=0),
        )(*args)

    def with_swaps(mine, others):
        return [mine] + [swap(other, "rows", k + 1) for k, other in enumerate(others)]

    bias = conv_bias.reshape(1, chans)
    gain = norm_gain.reshape(1, chans)
    shift = norm_shift.reshape(1, chans)
    dbias = down_bias.reshape(1, outs)
    up, dn = beside(img, True), beside(img, False)
    cot_up, cot_dn = beside(cot, True), beside(cot, False)
    row_scr = pltpu.VMEM((cols, chans), F32)
    block_of = (2, 2, half, chans)
    tile = ((8, chans), F32)
    x, hid, stat = run(
        functools.partial(hidden_kernel, width),
        (up, img, dn, conv_weight, bias),
        [((4, 2, half, chans), BF16), (block_of, F32), tile],
        [row_scr],
    )
    stats = with_swaps(stat, [stat] * (ranks - 1))
    hid_edge, gm, cbias = run(
        edge_kernel,
        (up, x, dn, conv_weight, bias, cot_up, cot, cot_dn, down_weight),
        [(block_of, F32), ((4, 2, half, chans), F32), ((8, outs), F32)],
        [row_scr],
    )
    par, mix, gp, sums = run(
        functools.partial(norm_kernel, width, count, ranks),
        (*stats, x, hid, gm, gain, shift),
        [tile, ((2, half, 3 * chans), BF16), (block_of, F32), tile],
    )
    all_sums = with_swaps(sums, [sums] * (ranks - 1))
    early_shape = (2, owners, wide, chans)
    late_shape = (owners, 3 * chunk, chans)
    deep = 2 * wide + 3 * chunk

    def by_rank(shape):
        return [(shape, F32)] + [(shape, BF16)] * (ranks - 1)

    mix_top, *down_grad = run(
        functools.partial(down_kernel, packed),
        (me, par, x, hid_edge, gain, shift, mix, cot),
        [((half, 3 * chans), BF16)]
        + ([((outs, chans), F32)] + by_rank(early_shape) if packed else [((outs, 9 * chans), F32)]),
        [pltpu.VMEM((4,) + early_shape, F32)] if packed else [],
    )
    if packed:
        dlast, *early = down_grad
        early = with_swaps(early[0], early[1:])
    par2, g, *conv_grad = run(
        functools.partial(back_kernel, width, count, ranks, packed),
        (me, *all_sums, par, x, hid, gp, gain) + ((dlast, cbias) if packed else ()),
        [tile, (block_of, BF16)] + (by_rank(late_shape) if packed else [((3 * chans, 3 * chans), F32), tile]),
        [pltpu.VMEM((4,) + late_shape, F32)] if packed else [],
    )
    if packed:
        late = with_swaps(conv_grad[0], conv_grad[1:])
    block, gi = run(
        functools.partial(image_kernel, ranks - 1),
        (me, par, hid_edge, gm, gain, shift, par2, g, mix_top, mix, conv_weight, down_weight, dbias),
        [((half, outs), BF16), ((rows, cols, chans), BF16)],
        [row_scr],
    )
    if packed:
        (mine,) = run(rows_kernel, (me, *early, *late), [((owners, deep, chans), BF16)])
        got = lax.all_to_all(mine, "dp", 0, 0)
        (part,) = run(dp_kernel, (me, got), [((deep, chans), BF16)])
        down, conv, cb, ga, sh, db = run(
            functools.partial(last_kernel, chunk),
            (me, *with_swaps(part, [part] * (ranks - 1))),
            [((9, wide, chans), F32), ((9, chunk, chans), F32)] + [((1, chunk), F32)] * 3 + [((1, wide), F32)],
            [pltpu.VMEM((4, deep, chans), F32)],
        )
    else:
        totals = lax.psum((down_grad[0], conv_grad[0], conv_grad[1], cbias[:1]), ("rows", "dp"))
        owner = lax.axis_index("dp")
        down = totals[0].reshape(outs, 9, chans).transpose(1, 0, 2)
        down = lax.dynamic_slice_in_dim(down, owner * wide, wide, 1)
        conv = totals[1].reshape(3, chans, 3, chans).transpose(2, 0, 1, 3).reshape(9, chans, chans)
        conv = lax.dynamic_slice_in_dim(conv, owner * chunk, chunk, 1)
        cb, ga, sh = lax.dynamic_slice_in_dim(totals[2], owner * chunk, chunk, 1)[:3]
        db = lax.dynamic_slice_in_dim(totals[3], owner * wide, wide, 1)
    return (
        block[None, None],
        gi[None],
        conv.reshape(3, 3, chunk, chans).transpose(0, 1, 3, 2),
        cb.reshape(-1),
        ga.reshape(-1),
        sh.reshape(-1),
        down.reshape(3, 3, wide, chans).transpose(0, 1, 3, 2),
        db.reshape(-1),
    )


def solution(mesh):
    spec = P("dp", "rows", None, None)
    in_specs = (spec, P(), P(), P(), P(), P(), P(), spec)
    last = P(None, None, None, "dp")
    out_specs = (spec, spec, last, P("dp"), P("dp"), P("dp"), last, P("dp"))
    return jax.shard_map(shards, mesh=mesh, in_specs=in_specs, out_specs=out_specs, check_vma=False)
```

time: 312 us -> 59.2 us (0.19)
  waiting for transfers between devices: 128 us -> 10.6 us
  local copies, waits for them, and re-layouts: 57.8 us -> 3.9 us
  blocking collectives: 64 us -> 14.5 us
  matrix products: 19.1 us -> 0 us
  between operations: 15.3 us -> 0.81 us
  other arithmetic: 13.4 us -> 0 us
  starting transfers between devices: 13.4 us -> 22.7 us
  Pallas kernels: 0 us -> 6.36 us
    psum x1 -> x0, waiting for transfers between devices: 128 us -> none  [shards(): lax.psum((conv_pack, small_pack, down_pack, bias_pack), ('rows', 'dp'))]
    psum x4 -> x0, blocking collectives: 64 us -> none  [the longest x1 40.5 us: shards(): lax.psum((conv_pack, small_pack, down_pack, bias_pack), ('rows', 'dp'))]
    slice x29 -> x0, local copies, waits for them, and re-layouts: 36.3 us -> none  [the longest x9 21.5 us: shards(): shifted[kh:kh + 2 * half_rows:2, kw:kw + 2 * half_cols:2]]
    dot_general x54 -> x0, matrix products: 19.1 us -> none  [the longest x9 6.87 us: shards(): line.append(jnp.dot(piece.T, flat, preferred_element_type=jnp.float32))]
    all_to_all x0 -> x1, blocking collectives: none -> 14.5 us  [shards(): got = lax.all_to_all(mine, 'dp', 0, 0)]
    ppermute x6 -> x19, waiting for transfers between devices: 0.02 us -> 10.6 us  [the longest x15 10.6 us: swap(): lax.ppermute(x, axis, [(i, i ^ k) for i in range(lax.axis_size(axis))])]
    ppermute x6 -> x19, starting transfers between devices: 13.3 us -> 22.7 us  [the longest x15 12 us: swap(): lax.ppermute(x, axis, [(i, i ^ k) for i in range(lax.axis_size(axis))])]
    pallas_call x0 -> x9, Pallas kernels: none -> 6.36 us  [run(): pl.pallas_call(kernel, in_specs=[smem if a is me else vmem for a in args]...]
  transfers between devices with their start and end apart: 7 -> 19, of which waited for: 1 -> 5; matrix products, arithmetic and copies ran while one was open for 18% -> 0% of each run, Pallas kernels for 0% -> 7%
where the time goes in v1:
time: 59.2 us; the launch traced here: 58.8 us
  starting transfers between devices  22.7 us (38%)
  blocking collectives  14.5 us (24%)
  waiting for transfers between devices  10.6 us (18%)
  Pallas kernels  6.36 us (11%)
  local copies, waits for them, and re-layouts  3.9 us (7%)
  between operations  0.81 us (1%)
    all_to_all x1, blocking collectives, shards(): got = lax.all_to_all(mine, 'dp', 0, 0)  14.5 us
    ppermute x15, starting transfers between devices, swap(): lax.ppermute(x, axis, [(i, i ^ k) for i in range(lax.axis_size(axis))])  12 us
    ppermute x4, starting transfers between devices, beside(): return lax.ppermute(x, 'rows', pairs if up else [(b, a) for a, b in pairs])  10.7 us
    ppermute x15, waiting for transfers between devices, swap(): lax.ppermute(x, axis, [(i, i ^ k) for i in range(lax.axis_size(axis))])  10.6 us
    pallas_call x9, Pallas kernels, run(): pl.pallas_call(kernel, in_specs=[smem if a is me else vmem for a in args]...  6.36 us
    unnamed x18, local copies, waits for them, and re-layouts  3.9 us
  transfers between devices with their start and end apart: 19, of which 5 were waited for; matrix products, arithmetic and copies ran while one was open for 0% of the time, Pallas kernels for 7%

profile of v1, /device:TPU:0, one launch (start us, length us, event | category | flops | bytes accessed | tf_op | source)
XLA Modules:
  0.0 58.8 jit_solution(6260747539944723892)
XLA Ops:
  0.6 1.3 %collective-permute-start.1 = (bf16[2,512,128]{2,1,0:T(8,128)(2,1)}, bf16[2,512,128]{2,1,0:T(8,128)(2,1)S(1)}, u32[]{:S(2)}, u32[]{:S(2)}) collective-permute-start(bf16[2,512,128]{2,1,0:T(8,128)(2,1)} %bitcast.23), channel_id=1, source_target_pairs={{8,0},{16,8},{24,16},{9,1},{17,9},{25,17},{10,2},{18,10},{26,18},{... | collective-permute-start | bytes 786440 | tf_op jit(solution)/shard_map/ppermute | solution.py:348
  1.9 3.0 %collective-permute-start = (bf16[2,512,128]{2,1,0:T(8,128)(2,1)}, bf16[2,512,128]{2,1,0:T(8,128)(2,1)S(1)}, u32[]{:S(2)}, u32[]{:S(2)}) collective-permute-start(bf16[2,512,128]{2,1,0:T(8,128)(2,1)} %bitcast.24), channel_id=1, source_target_pairs={{0,8},{8,16},{16,24},{1,9},{9,17},{17,25},{2,10},{10,18},{18,26},{... | collective-permute-start | bytes 786440 | tf_op jit(solution)/shard_map/ppermute | solution.py:348
  5.0 1.3 %collective-permute-start.6 = (bf16[256,256]{1,0:T(8,128)(2,1)}, bf16[256,256]{1,0:T(8,128)(2,1)S(1)}, u32[]{:S(2)}, u32[]{:S(2)}) collective-permute-start(bf16[256,256]{1,0:T(8,128)(2,1)} %bitcast.19), channel_id=1, source_target_pairs={{8,0},{16,8},{24,16},{9,1},{17,9},{25,17},{10,2},{18,10},{26,18},{... | collective-permute-start | bytes 393224 | tf_op jit(solution)/shard_map/ppermute | solution.py:348
  6.3 5.1 %collective-permute-start.5 = (bf16[256,256]{1,0:T(8,128)(2,1)}, bf16[256,256]{1,0:T(8,128)(2,1)S(1)}, u32[]{:S(2)}, u32[]{:S(2)}) collective-permute-start(bf16[256,256]{1,0:T(8,128)(2,1)} %bitcast.20), channel_id=1, source_target_pairs={{0,8},{8,16},{16,24},{1,9},{9,17},{17,25},{2,10},{10,18},{18,26},{... | collective-permute-start | bytes 393224 | tf_op jit(solution)/shard_map/ppermute | solution.py:348
  11.4 0.0 copy-start.7
  11.4 0.0 collective-permute-done.1.dn
  11.4 0.0 collective-permute-done.up
  11.4 0.6 %copy-done.7 = f32[128]{0:T(128)S(1)} copy-done((f32[128]{0:T(128)S(1)}, f32[128]{0:T(128)}, u32[]{:S(2)}) %copy-start.7) | copy-done | bytes 536
  12.0 0.0 copy-start
  12.0 1.0 %copy-done = bf16[3,3,128,128]{3,2,1,0:T(8,128)(2,1)S(1)} copy-done((bf16[3,3,128,128]{3,2,1,0:T(8,128)(2,1)S(1)}, bf16[3,3,128,128]{3,2,1,0:T(8,128)(2,1)}, u32[]{:S(2)}) %copy-start) | copy-done | bytes 294936
  13.0 0.0 copy-start.4
  13.0 0.9 %copy-done.4 = bf16[1,2,512,128]{3,2,1,0:T(8,128)(2,1)S(1)} copy-done((bf16[1,2,512,128]{3,2,1,0:T(8,128)(2,1)S(1)}, bf16[1,2,512,128]{3,2,1,0:T(8,128)(2,1)}, u32[]{:S(2)}) %copy-start.4) | copy-done | bytes 262168
  14.0 0.0 copy-start.1
  14.0 0.0 copy-start.2
  14.0 0.0 copy-start.3
  14.0 1.1 %shard_map.143 = (bf16[4,2,256,128]{3,2,1,0:T(8,128)(2,1)S(1)}, f32[2,2,256,128]{3,2,1,0:T(8,128)S(1)}, f32[8,128]{1,0:T(8,128)S(1)}) custom-call(bf16[2,512,128]{2,1,0:T(8,128)(2,1)S(1)} %collective-permute-done.up, bf16[2,512,128]{2,1,0:T(8,128)(2,1)S(1)} %bitcast.25, bf16[2,512,128]{2,1,0:T(8,128)(2,1)S(1)} %collective-permute-done.1.dn, ...), custom_call_target="tpu_custom_call" | custom-call | flops 134217728 | bytes 2097152 | tf_op jit(solution)/shard_map/pallas_call | solution.py:369
  15.1 0.0 collective-permute-start.4
  15.1 3.4 %collective-permute-start.3 = (f32[8,128]{1,0:T(8,128)S(1)}, f32[8,128]{1,0:T(8,128)S(1)}, u32[]{:S(2)}, u32[]{:S(2)}) collective-permute-start(f32[8,128]{1,0:T(8,128)S(1)} %get-tuple-element.38.refs_0_), channel_id=1, source_target_pairs={{0,16},{8,24},{16,0},{24,8},{1,17},{9,25},{17,1},{25,9},{2,18},{10... | collective-permute-start | bytes 12296 | tf_op jit(solution)/shard_map/ppermute | solution.py:352
  18.4 0.0 collective-permute-start.2
  18.4 0.0 collective-permute-done.6.cot_dn
  18.5 0.0 collective-permute-done.5.cot_up
  18.5 0.0 copy-done.1
  18.5 0.0 copy-done.2
  18.5 0.0 copy-done.3
  18.5 1.0 %shard_map.144 = (f32[2,2,256,128]{3,2,1,0:T(8,128)S(1)}, f32[4,2,256,128]{3,2,1,0:T(8,128)S(1)}, f32[8,256]{1,0:T(8,128)S(1)}) custom-call(bf16[2,512,128]{2,1,0:T(8,128)(2,1)S(1)} %collective-permute-done.up, bf16[4,2,256,128]{3,2,1,0:T(8,128)(2,1)S(1)} %get-tuple-element.39.x.refs_4_.refs_5_, bf16[2,512,128]{2,1,0:T(8,128)(2,1)S(1)} %collective-permute-done.1.dn, ...), custom_call_target="tpu_custom_call" | custom-call | flops 134217728 | bytes 2097152 | tf_op jit(solution)/shard_map/pallas_call | solution.py:369
  19.5 0.0 collective-permute-done.4.refs_3_
  19.5 0.6 collective-permute-done.3.refs_2_
  20.1 0.0 collective-permute-done.2.refs_1_
  20.1 0.0 copy-start.5
  20.1 0.0 copy-start.6
  20.1 0.7 %copy-done.5 = f32[128]{0:T(128)S(1)} copy-done((f32[128]{0:T(128)S(1)}, f32[128]{0:T(128)}, u32[]{:S(2)}) %copy-start.5) | copy-done | bytes 536
  20.7 0.0 copy-done.6
  20.7 0.4 shard_map.145
  21.1 0.1 collective-permute-start.9
  21.2 2.0 %collective-permute-start.8 = (f32[8,128]{1,0:T(8,128)S(1)}, f32[8,128]{1,0:T(8,128)S(1)}, u32[]{:S(2)}, u32[]{:S(2)}) collective-permute-start(f32[8,128]{1,0:T(8,128)S(1)} %get-tuple-element.44.refs_0_), channel_id=1, source_target_pairs={{0,16},{8,24},{16,0},{24,8},{1,17},{9,25},{17,1},{25,9},{2,18},{10... | collective-permute-start | bytes 12296 | tf_op jit(solution)/shard_map/ppermute | solution.py:352
  23.3 0.0 collective-permute-start.7
  23.3 0.5 shard_map.146
  23.8 0.4 collective-permute-done.9.refs_3_
  24.2 0.7 %collective-permute-done.8.refs_2_ = f32[8,128]{1,0:T(8,128)S(1)} collective-permute-done((f32[8,128]{1,0:T(8,128)S(1)}, f32[8,128]{1,0:T(8,128)S(1)}, u32[]{:S(2)}, u32[]{:S(2)}) %collective-permute-start.8) | collective-permute-done | bytes 4128 | tf_op jit(solution)/shard_map/ppermute | solution.py:352
  24.9 0.0 collective-permute-done.7.refs_1_
  24.9 0.9 %shard_map.147 = (f32[8,128]{1,0:T(8,128)S(1)}, bf16[2,2,256,128]{3,2,1,0:T(8,128)(2,1)S(1)}, f32[8,48,128]{2,1,0:T(8,128)S(1)}, bf16[8,48,128]{2,1,0:T(8,128)(2...) custom-call(s32[1]{0:T(128)} %bitcast.me_ref, f32[8,128]{1,0:T(8,128)S(1)} %get-tuple-element.44.refs_0_, ...), custom_call_target="tpu_custom_call" | custom-call | flops 134217728 | bytes 2097152 | tf_op jit(solution)/shard_map/pallas_call | solution.py:369
  25.8 0.9 %collective-permute-start.13 = (bf16[8,48,128]{2,1,0:T(8,128)(2,1)S(1)}, bf16[8,48,128]{2,1,0:T(8,128)(2,1)S(1)}, u32[]{:S(2)}, u32[]{:S(2)}) collective-permute-start(bf16[8,48,128]{2,1,0:T(8,128)(2,1)S(1)} %get-tuple-element.59), channel_id=1, source_target_pairs={{0,8},{8,0},{16,24},{24,16},{1,9},{9,1},{17,25},{25,17},{2,10},{10... | collective-permute-start | bytes 294920 | tf_op jit(solution)/shard_map/ppermute | solution.py:352
  26.7 0.1 collective-permute-start.10
  26.8 1.5 %collective-permute-start.11 = (bf16[2,8,32,128]{3,2,1,0:T(8,128)(2,1)S(1)}, bf16[2,8,32,128]{3,2,1,0:T(8,128)(2,1)S(1)}, u32[]{:S(2)}, u32[]{:S(2)}) collective-permute-start(bf16[2,8,32,128]{3,2,1,0:T(8,128)(2,1)S(1)} %get-tuple-element.56), channel_id=1, source_target_pairs={{0,16},{8,24},{16,0},{24,8},{1,17},{9,25},{17,1},{25,9},{2,18},{10... | collective-permute-start | bytes 393224 | tf_op jit(solution)/shard_map/ppermute | solution.py:352
  28.4 0.3 collective-permute-start.12
  28.6 1.2 %collective-permute-start.14 = (bf16[8,48,128]{2,1,0:T(8,128)(2,1)S(1)}, bf16[8,48,128]{2,1,0:T(8,128)(2,1)S(1)}, u32[]{:S(2)}, u32[]{:S(2)}) collective-permute-start(bf16[8,48,128]{2,1,0:T(8,128)(2,1)S(1)} %get-tuple-element.60), channel_id=1, source_target_pairs={{0,16},{8,24},{16,0},{24,8},{1,17},{9,25},{17,1},{25,9},{2,18},{10... | collective-permute-start | bytes 294920 | tf_op jit(solution)/shard_map/ppermute | solution.py:352
  29.8 0.0 collective-permute-done.13.l1
  29.8 0.5 collective-permute-start.15
  30.3 7.7 %collective-permute-done.14.l2 = bf16[8,48,128]{2,1,0:T(8,128)(2,1)S(1)} collective-permute-done((bf16[8,48,128]{2,1,0:T(8,128)(2,1)S(1)}, bf16[8,48,128]{2,1,0:T(8,128)(2,1)S(1)}, u32[]{:S(2)}, u32[]{:S(2)}) %collective-permute-start.14) | collective-permute-done | bytes 98336 | tf_op jit(solution)/shard_map/ppermute | solution.py:352
  38.0 1.2 %collective-permute-done.15.l3 = bf16[8,48,128]{2,1,0:T(8,128)(2,1)S(1)} collective-permute-done((bf16[8,48,128]{2,1,0:T(8,128)(2,1)S(1)}, bf16[8,48,128]{2,1,0:T(8,128)(2,1)S(1)}, u32[]{:S(2)}, u32[]{:S(2)}) %collective-permute-start.15) | collective-permute-done | bytes 98336 | tf_op jit(solution)/shard_map/ppermute | solution.py:352
  39.2 0.0 collective-permute-done.10.e1
  39.2 0.0 collective-permute-done.11.e2
  39.2 0.0 collective-permute-done.12.e3
  39.3 0.1 shard_map.149
  39.4 14.5 %all_to_all.5.got = bf16[8,112,128]{2,1,0:T(8,128)(2,1)S(1)} all-to-all(bf16[8,112,128]{2,1,0:T(8,128)(2,1)S(1)} %shard_map.149), channel_id=1, replica_groups=mesh['rows'=4,'dp'=8] {'dp'}, dimensions={0} | all-to-all | bytes 458752 | tf_op jit(solution)/shard_map/all_to_all | solution.py:443
  53.9 0.1 collective-permute-start.18
  54.0 1.3 %collective-permute-start.17 = (bf16[112,128]{1,0:T(8,128)(2,1)S(1)}, bf16[112,128]{1,0:T(8,128)(2,1)S(1)}, u32[]{:S(2)}, u32[]{:S(2)}) collective-permute-start(bf16[112,128]{1,0:T(8,128)(2,1)S(1)} %shard_map.150.q0), channel_id=1, source_target_pairs={{0,16},{8,24},{16,0},{24,8},{1,17},{9,25},{17,1},{25,9},{2,18},{10... | collective-permute-start | bytes 86024 | tf_op jit(solution)/shard_map/ppermute | solution.py:352
  55.3 0.6 %collective-permute-start.16 = (bf16[112,128]{1,0:T(8,128)(2,1)S(1)}, bf16[112,128]{1,0:T(8,128)(2,1)S(1)}, u32[]{:S(2)}, u32[]{:S(2)}) collective-permute-start(bf16[112,128]{1,0:T(8,128)(2,1)S(1)} %shard_map.150.q0), channel_id=1, source_target_pairs={{0,8},{8,0},{16,24},{24,16},{1,9},{9,1},{17,25},{25,17},{2,10},{10... | collective-permute-start | bytes 86024 | tf_op jit(solution)/shard_map/ppermute | solution.py:352
  55.9 0.7 %copy-done.8 = f32[256]{0:T(256)S(1)} copy-done((f32[256]{0:T(256)S(1)}, f32[256]{0:T(256)}, u32[]{:S(2)}) %copy-start.8) | copy-done | bytes 1048
  56.5 1.6 %shard_map.148 = (bf16[256,256]{1,0:T(8,128)(2,1)}, bf16[2,512,128]{2,1,0:T(8,128)(2,1)}) custom-call(s32[1]{0:T(128)} %bitcast.me_ref, f32[8,128]{1,0:T(8,128)S(1)} %get-tuple-element.42.par.refs_4_, f32[2,2,256,128]{3,2,1,0:T(8,128)S(1)} %get-tuple-element.43.hid, f32[4,2,256,128]{3,2,1,0:T(8,128)S(1)} %get-tuple-element.41.refs_6_.gm, ...), custom_call_target="tpu_custom_call" | custom-call | flops 134217728 | bytes 2097152 | tf_op jit(solution)/shard_map/pallas_call | solution.py:369
  58.1 0.0 collective-permute-done.18.q3
  58.1 0.0 collective-permute-done.17.q2
  58.1 0.0 collective-permute-done.16.q1
  58.1 0.7 %shard_map.151 = (f32[9,32,128]{2,1,0:T(8,128)}, f32[9,16,128]{2,1,0:T(8,128)}, f32[1,16]{1,0:T(1,128)}, f32[1,16]{1,0:T(1,128)}, f32[1,16]{1,0:T(1,128)}, /*index=5*/f32[1,32]{1,0:T(1,128)}) custom-call(s32[1]{0:T(128)} %bitcast.me_ref, bf16[112,128]{1,0:T(8,128)(2,1)S(1)} %shard_map.150.q0, bf16[112,128]{1,0:T(8,128)(2,1)S(1)} %collective-permute-done.16.q1, ...), custom_call_target="tpu_custom_call" | custom-call | flops 134217728 | bytes 2097152 | tf_op jit(solution)/shard_map/pallas_call | solution.py:369
  (2 shorter events, 0.0 us)
Async XLA Ops:
  0.6 10.8 %collective-permute-start.1 = (bf16[2,512,128]{2,1,0:T(8,128)(2,1)}, bf16[2,512,128]{2,1,0:T(8,128)(2,1)S(1)}, u32[]{:S(2)}, u32[]{:S(2)}) collective-permute-start(bf16[2,512,128]{2,1,0:T(8,128)(2,1)} %bitcast.23), channel_id=1, source_target_pairs={{8,0},{16,8},{24,16},{9,1},{17,9},{25,17},{10,2},{18,10},{26,18},{... | collective-permute-start | bytes 786440 | tf_op jit(solution)/shard_map/ppermute | solution.py:348
  1.9 9.5 %collective-permute-start = (bf16[2,512,128]{2,1,0:T(8,128)(2,1)}, bf16[2,512,128]{2,1,0:T(8,128)(2,1)S(1)}, u32[]{:S(2)}, u32[]{:S(2)}) collective-permute-start(bf16[2,512,128]{2,1,0:T(8,128)(2,1)} %bitcast.24), channel_id=1, source_target_pairs={{0,8},{8,16},{16,24},{1,9},{9,17},{17,25},{2,10},{10,18},{18,26},{... | collective-permute-start | bytes 786440 | tf_op jit(solution)/shard_map/ppermute | solution.py:348
  5.0 13.5 %collective-permute-start.6 = (bf16[256,256]{1,0:T(8,128)(2,1)}, bf16[256,256]{1,0:T(8,128)(2,1)S(1)}, u32[]{:S(2)}, u32[]{:S(2)}) collective-permute-start(bf16[256,256]{1,0:T(8,128)(2,1)} %bitcast.19), channel_id=1, source_target_pairs={{8,0},{16,8},{24,16},{9,1},{17,9},{25,17},{10,2},{18,10},{26,18},{... | collective-permute-start | bytes 393224 | tf_op jit(solution)/shard_map/ppermute | solution.py:348
  6.3 12.2 %collective-permute-start.5 = (bf16[256,256]{1,0:T(8,128)(2,1)}, bf16[256,256]{1,0:T(8,128)(2,1)S(1)}, u32[]{:S(2)}, u32[]{:S(2)}) collective-permute-start(bf16[256,256]{1,0:T(8,128)(2,1)} %bitcast.20), channel_id=1, source_target_pairs={{0,8},{8,16},{16,24},{1,9},{9,17},{17,25},{2,10},{10,18},{18,26},{... | collective-permute-start | bytes 393224 | tf_op jit(solution)/shard_map/ppermute | solution.py:348
  11.4 0.7 %copy-start.7 = (f32[128]{0:T(128)S(1)}, f32[128]{0:T(128)}, u32[]{:S(2)}) copy-start(f32[128]{0:T(128)} %param.10) | copy-start | bytes 1540
  12.0 1.0 %copy-start = (bf16[3,3,128,128]{3,2,1,0:T(8,128)(2,1)S(1)}, bf16[3,3,128,128]{3,2,1,0:T(8,128)(2,1)}, u32[]{:S(2)}) copy-start(bf16[3,3,128,128]{3,2,1,0:T(8,128)(2,1)} %w.5) | copy-start | bytes 884740
  13.0 0.9 %copy-start.4 = (bf16[1,2,512,128]{3,2,1,0:T(8,128)(2,1)S(1)}, bf16[1,2,512,128]{3,2,1,0:T(8,128)(2,1)}, u32[]{:S(2)}) copy-start(bf16[1,2,512,128]{3,2,1,0:T(8,128)(2,1)} %param.8) | copy-start | bytes 786436
  14.0 4.5 %copy-start.1 = (bf16[3,3,128,128]{3,2,1,0:T(8,128)(2,1)S(1)}, bf16[3,3,128,128]{3,2,1,0:T(8,128)(2,1)}, u32[]{:S(2)}) copy-start(bf16[3,3,128,128]{3,2,1,0:T(8,128)(2,1)} %w.5) | copy-start | bytes 884740
  14.0 4.5 %copy-start.2 = (bf16[3,3,128,256]{3,2,1,0:T(8,128)(2,1)S(1)}, bf16[3,3,128,256]{3,2,1,0:T(8,128)(2,1)}, u32[]{:S(2)}) copy-start(bf16[3,3,128,256]{3,2,1,0:T(8,128)(2,1)} %dw.3) | copy-start | bytes 1769476
  14.0 4.5 %copy-start.3 = (bf16[1,1,256,256]{3,2,1,0:T(8,128)(2,1)S(1)}, bf16[1,1,256,256]{3,2,1,0:T(8,128)(2,1)}, u32[]{:S(2)}) copy-start(bf16[1,1,256,256]{3,2,1,0:T(8,128)(2,1)} %param.15) | copy-start | bytes 393220
  15.1 4.4 %collective-permute-start.4 = (f32[8,128]{1,0:T(8,128)S(1)}, f32[8,128]{1,0:T(8,128)S(1)}, u32[]{:S(2)}, u32[]{:S(2)}) collective-permute-start(f32[8,128]{1,0:T(8,128)S(1)} %get-tuple-element.38.refs_0_), channel_id=1, source_target_pairs={{0,24},{8,16},{16,8},{24,0},{1,25},{9,17},{17,9},{25,1},{2,26},{10... | collective-permute-start | bytes 12296 | tf_op jit(solution)/shard_map/ppermute | solution.py:352
  15.1 5.0 %collective-permute-start.3 = (f32[8,128]{1,0:T(8,128)S(1)}, f32[8,128]{1,0:T(8,128)S(1)}, u32[]{:S(2)}, u32[]{:S(2)}) collective-permute-start(f32[8,128]{1,0:T(8,128)S(1)} %get-tuple-element.38.refs_0_), channel_id=1, source_target_pairs={{0,16},{8,24},{16,0},{24,8},{1,17},{9,25},{17,1},{25,9},{2,18},{10... | collective-permute-start | bytes 12296 | tf_op jit(solution)/shard_map/ppermute | solution.py:352
  18.4 1.6 %collective-permute-start.2 = (f32[8,128]{1,0:T(8,128)S(1)}, f32[8,128]{1,0:T(8,128)S(1)}, u32[]{:S(2)}, u32[]{:S(2)}) collective-permute-start(f32[8,128]{1,0:T(8,128)S(1)} %get-tuple-element.38.refs_0_), channel_id=1, source_target_pairs={{0,8},{8,0},{16,24},{24,16},{1,9},{9,1},{17,25},{25,17},{2,10},{10... | collective-permute-start | bytes 12296 | tf_op jit(solution)/shard_map/ppermute | solution.py:352
  20.1 0.7 %copy-start.5 = (f32[128]{0:T(128)S(1)}, f32[128]{0:T(128)}, u32[]{:S(2)}) copy-start(f32[128]{0:T(128)} %param.11) | copy-start | bytes 1540
  20.1 0.7 %copy-start.6 = (f32[128]{0:T(128)S(1)}, f32[128]{0:T(128)}, u32[]{:S(2)}) copy-start(f32[128]{0:T(128)} %param.12) | copy-start | bytes 1540
  21.1 3.1 %collective-permute-start.9 = (f32[8,128]{1,0:T(8,128)S(1)}, f32[8,128]{1,0:T(8,128)S(1)}, u32[]{:S(2)}, u32[]{:S(2)}) collective-permute-start(f32[8,128]{1,0:T(8,128)S(1)} %get-tuple-element.44.refs_0_), channel_id=1, source_target_pairs={{0,24},{8,16},{16,8},{24,0},{1,25},{9,17},{17,9},{25,1},{2,26},{10... | collective-permute-start | bytes 12296 | tf_op jit(solution)/shard_map/ppermute | solution.py:352
  21.2 3.7 %collective-permute-start.8 = (f32[8,128]{1,0:T(8,128)S(1)}, f32[8,128]{1,0:T(8,128)S(1)}, u32[]{:S(2)}, u32[]{:S(2)}) collective-permute-start(f32[8,128]{1,0:T(8,128)S(1)} %get-tuple-element.44.refs_0_), channel_id=1, source_target_pairs={{0,16},{8,24},{16,0},{24,8},{1,17},{9,25},{17,1},{25,9},{2,18},{10... | collective-permute-start | bytes 12296 | tf_op jit(solution)/shard_map/ppermute | solution.py:352
  23.3 1.6 %collective-permute-start.7 = (f32[8,128]{1,0:T(8,128)S(1)}, f32[8,128]{1,0:T(8,128)S(1)}, u32[]{:S(2)}, u32[]{:S(2)}) collective-permute-start(f32[8,128]{1,0:T(8,128)S(1)} %get-tuple-element.44.refs_0_), channel_id=1, source_target_pairs={{0,8},{8,0},{16,24},{24,16},{1,9},{9,1},{17,25},{25,17},{2,10},{10... | collective-permute-start | bytes 12296 | tf_op jit(solution)/shard_map/ppermute | solution.py:352
  25.8 4.0 %collective-permute-start.13 = (bf16[8,48,128]{2,1,0:T(8,128)(2,1)S(1)}, bf16[8,48,128]{2,1,0:T(8,128)(2,1)S(1)}, u32[]{:S(2)}, u32[]{:S(2)}) collective-permute-start(bf16[8,48,128]{2,1,0:T(8,128)(2,1)S(1)} %get-tuple-element.59), channel_id=1, source_target_pairs={{0,8},{8,0},{16,24},{24,16},{1,9},{9,1},{17,25},{25,17},{2,10},{10... | collective-permute-start | bytes 294920 | tf_op jit(solution)/shard_map/ppermute | solution.py:352
  26.7 12.5 %collective-permute-start.10 = (bf16[2,8,32,128]{3,2,1,0:T(8,128)(2,1)S(1)}, bf16[2,8,32,128]{3,2,1,0:T(8,128)(2,1)S(1)}, u32[]{:S(2)}, u32[]{:S(2)}) collective-permute-start(bf16[2,8,32,128]{3,2,1,0:T(8,128)(2,1)S(1)} %get-tuple-element.55), channel_id=1, source_target_pairs={{0,8},{8,0},{16,24},{24,16},{1,9},{9,1},{17,25},{25,17},{2,10},{10... | collective-permute-start | bytes 393224 | tf_op jit(solution)/shard_map/ppermute | solution.py:352
  26.8 12.4 %collective-permute-start.11 = (bf16[2,8,32,128]{3,2,1,0:T(8,128)(2,1)S(1)}, bf16[2,8,32,128]{3,2,1,0:T(8,128)(2,1)S(1)}, u32[]{:S(2)}, u32[]{:S(2)}) collective-permute-start(bf16[2,8,32,128]{3,2,1,0:T(8,128)(2,1)S(1)} %get-tuple-element.56), channel_id=1, source_target_pairs={{0,16},{8,24},{16,0},{24,8},{1,17},{9,25},{17,1},{25,9},{2,18},{10... | collective-permute-start | bytes 393224 | tf_op jit(solution)/shard_map/ppermute | solution.py:352
  28.4 10.9 %collective-permute-start.12 = (bf16[2,8,32,128]{3,2,1,0:T(8,128)(2,1)S(1)}, bf16[2,8,32,128]{3,2,1,0:T(8,128)(2,1)S(1)}, u32[]{:S(2)}, u32[]{:S(2)}) collective-permute-start(bf16[2,8,32,128]{3,2,1,0:T(8,128)(2,1)S(1)} %get-tuple-element.57), channel_id=1, source_target_pairs={{0,24},{8,16},{16,8},{24,0},{1,25},{9,17},{17,9},{25,1},{2,26},{10... | collective-permute-start | bytes 393224 | tf_op jit(solution)/shard_map/ppermute | solution.py:352
  28.6 9.4 %collective-permute-start.14 = (bf16[8,48,128]{2,1,0:T(8,128)(2,1)S(1)}, bf16[8,48,128]{2,1,0:T(8,128)(2,1)S(1)}, u32[]{:S(2)}, u32[]{:S(2)}) collective-permute-start(bf16[8,48,128]{2,1,0:T(8,128)(2,1)S(1)} %get-tuple-element.60), channel_id=1, source_target_pairs={{0,16},{8,24},{16,0},{24,8},{1,17},{9,25},{17,1},{25,9},{2,18},{10... | collective-permute-start | bytes 294920 | tf_op jit(solution)/shard_map/ppermute | solution.py:352
  29.8 9.4 %collective-permute-start.15 = (bf16[8,48,128]{2,1,0:T(8,128)(2,1)S(1)}, bf16[8,48,128]{2,1,0:T(8,128)(2,1)S(1)}, u32[]{:S(2)}, u32[]{:S(2)}) collective-permute-start(bf16[8,48,128]{2,1,0:T(8,128)(2,1)S(1)} %get-tuple-element.61), channel_id=1, source_target_pairs={{0,24},{8,16},{16,8},{24,0},{1,25},{9,17},{17,9},{25,1},{2,26},{10... | collective-permute-start | bytes 294920 | tf_op jit(solution)/shard_map/ppermute | solution.py:352
  53.9 4.2 %collective-permute-start.18 = (bf16[112,128]{1,0:T(8,128)(2,1)S(1)}, bf16[112,128]{1,0:T(8,128)(2,1)S(1)}, u32[]{:S(2)}, u32[]{:S(2)}) collective-permute-start(bf16[112,128]{1,0:T(8,128)(2,1)S(1)} %shard_map.150.q0), channel_id=1, source_target_pairs={{0,24},{8,16},{16,8},{24,0},{1,25},{9,17},{17,9},{25,1},{2,26},{10... | collective-permute-start | bytes 86024 | tf_op jit(solution)/shard_map/ppermute | solution.py:352
  54.0 4.1 %collective-permute-start.17 = (bf16[112,128]{1,0:T(8,128)(2,1)S(1)}, bf16[112,128]{1,0:T(8,128)(2,1)S(1)}, u32[]{:S(2)}, u32[]{:S(2)}) collective-permute-start(bf16[112,128]{1,0:T(8,128)(2,1)S(1)} %shard_map.150.q0), channel_id=1, source_target_pairs={{0,16},{8,24},{16,0},{24,8},{1,17},{9,25},{17,1},{25,9},{2,18},{10... | collective-permute-start | bytes 86024 | tf_op jit(solution)/shard_map/ppermute | solution.py:352
  55.3 2.8 %collective-permute-start.16 = (bf16[112,128]{1,0:T(8,128)(2,1)S(1)}, bf16[112,128]{1,0:T(8,128)(2,1)S(1)}, u32[]{:S(2)}, u32[]{:S(2)}) collective-permute-start(bf16[112,128]{1,0:T(8,128)(2,1)S(1)} %shard_map.150.q0), channel_id=1, source_target_pairs={{0,8},{8,0},{16,24},{24,16},{1,9},{9,1},{17,25},{25,17},{2,10},{10... | collective-permute-start | bytes 86024 | tf_op jit(solution)/shard_map/ppermute | solution.py:352
  55.9 0.7 %copy-start.8 = (f32[256]{0:T(256)S(1)}, f32[256]{0:T(256)}, u32[]{:S(2)}) copy-start(f32[256]{0:T(256)} %param.14) | copy-start | bytes 3076

commit v2 on v1

--- a/solution.py
+++ b/solution.py
@@ -73,13 +73,50 @@
     return base[:, :chans] + bias, base[:, chans:] + bias, from_odd, from_even
 
 
-def hidden_kernel(width, up, img, dn, w, bias, x_out, hid_out, stat_out, scr):
-    half = x_out.shape[2]
-    rows = (up[1], img[0], img[1], dn[0])
-    for p in range(4):
-        even, odd = split(scr, rows[p])
+def first_kernel(me_ref, out):
+    out[...] = jnp.zeros(out.shape, F32)
+
+
+def prep_kernel(ahead, img, w, dw, cot, bias, gain, shift, dbias, *refs):
+    outs, (x_out, gm_out, cb_out, img_v, scr, sems) = refs[:7], refs[7:]
+    pairs = list(zip((img, w, dw, cot, bias, gain, shift, dbias), (img_v,) + outs))
+    copies = [pltpu.make_async_copy(src, dst, sems.at[i]) for i, (src, dst) in enumerate(pairs)]
+    for copy in copies:
+        copy.start()
+    copies[0].wait()
+    for p in range(2):
+        even, odd = split(scr, img_v[p])
         x_out[p, 0] = even.astype(BF16)
         x_out[p, 1] = odd.astype(BF16)
+    for copy in copies[1:]:
+        copy.wait()
+    dw_v, cot_v = outs[1], outs[2]
+    for p, kh in enumerate(range(3)):
+        even, odd, late = back_taps(cot_v[...], dw_v, kh)
+        gm_out[p, 0] = even
+        gm_out[p, 1] = odd + sooner(late)
+    cb_out[...] = jnp.broadcast_to(jnp.sum(cot_v[...].astype(F32), axis=0, keepdims=True), cb_out.shape)
+
+
+def back_taps(c, dw, kh):
+    chans, outs = dw.shape[2:]
+    got = dot_nt(c, dw[kh].reshape(3 * chans, outs))
+    return got[:, chans : 2 * chans], got[:, 2 * chans :], got[:, :chans]
+
+
+def either(flag, a, b):
+    return jnp.where(flag, a.astype(F32), b.astype(F32))
+
+
+def hidden_kernel(width, me_ref, core, chip, own, w, bias, x_out, hid_out, stat_out, scr):
+    half = x_out.shape[2]
+    odd_rank = (me_ref[0] & 1) == 1
+    for p, row in ((0, either(odd_rank, core[1], chip[1])), (3, either(odd_rank, chip[0], core[0]))):
+        even, odd = split(scr, row)
+        x_out[p, 0] = even.astype(BF16)
+        x_out[p, 1] = odd.astype(BF16)
+    for p in range(2):
+        x_out[p + 1] = own[p]
     weights = conv_weights(w)
     even = stack(*[lanes(x_out[p, 0], x_out[p + 1, 0], x_out[p + 2, 0]) for p in range(2)])
     odd = stack(*[lanes(x_out[p, 1], x_out[p + 1, 1], x_out[p + 2, 1]) for p in range(2)])
@@ -103,10 +140,11 @@
     stat_out[1:2] = grouped(spread, width)
 
 
-def edge_kernel(up, x, dn, w, bias, cot_up, cot, cot_dn, dw, hid_out, gm_out, cb_out, scr):
+def edge_kernel(me_ref, core, chip, x, w, bias, cot_core, cot_chip, dw, own_gm, hid_out, gm_out, scr):
     half = x.shape[2]
-    top = [v.astype(BF16) for v in split(scr, up[0])]
-    low = [v.astype(BF16) for v in split(scr, dn[1])]
+    odd_rank = (me_ref[0] & 1) == 1
+    top = [v.astype(BF16) for v in split(scr, either(odd_rank, core[0], chip[0]))]
+    low = [v.astype(BF16) for v in split(scr, either(odd_rank, chip[1], core[1]))]
     weights = conv_weights(w)
     even = stack(lanes(top[0], x[0, 0], x[1, 0]), lanes(x[2, 0], x[3, 0], low[0]))
     odd = stack(lanes(top[1], x[0, 1], x[1, 1]), lanes(x[2, 1], x[3, 1], low[1]))
@@ -115,26 +153,14 @@
         sl = slice(p * half, (p + 1) * half)
         hid_out[p, 0] = base_e[sl] + later(from_odd[sl])
         hid_out[p, 1] = base_o[sl] + sooner(from_even[sl])
-    chans = x.shape[3]
-
-    def taps(c, kh):
-        flat = dw[kh].reshape(3 * chans, dw.shape[3])
-        got = dot_nt(c, flat)
-        return got[:, chans : 2 * chans], got[:, 2 * chans :], got[:, :chans]
-
-    def put(p, even_part, odd_part, odd_shift):
-        gm_out[p, 0] = even_part
-        gm_out[p, 1] = odd_part + sooner(odd_shift)
-
-    mine = [taps(cot[...], kh) for kh in range(3)]
-    above = taps(cot_up[...], 2)
-    below0 = taps(cot_dn[...], 0)
-    below1 = taps(cot_dn[...], 1)
-    put(0, *[a + b for a, b in zip(above, mine[0])])
-    put(1, *mine[1])
-    put(2, *[a + b for a, b in zip(mine[2], below0)])
-    put(3, *below1)
-    cb_out[...] = jnp.broadcast_to(jnp.sum(cot[...].astype(F32), axis=0, keepdims=True), cb_out.shape)
+    above = either(odd_rank, cot_core[...], cot_chip[...]).astype(BF16)
+    below = either(odd_rank, cot_chip[...], cot_core[...]).astype(BF16)
+    zero = jnp.zeros((half, x.shape[3]), F32)
+    for p, c, kh in ((0, above, 2), (1, None, 0), (2, below, 0), (3, below, 1)):
+        even, odd, late = back_taps(c, dw, kh) if c is not None else (zero, zero, zero)
+        own = own_gm[p] if p < 3 else (zero, zero)
+        gm_out[p, 0] = own[0] + even
+        gm_out[p, 1] = own[1] + (odd + sooner(late) if c is not None else odd)
 
 
 def norm_kernel(width, count, ranks, *refs):
@@ -184,17 +210,20 @@
     if not packed:
         rest[0][...] = grad
         return
-    last_out, e0, e1, e2, e3, dscr = rest
-    outs_chunk = e0.shape[2]
+    last_out, keep_out, send_out, dscr = rest
+    outs_chunk = keep_out.shape[3]
     for q in range(4):
         for t in range(2):
             tap = 2 * q + t
             dscr[q, t] = grad[:, tap * chans : (tap + 1) * chans].reshape(-1, outs_chunk, chans)
     last_out[...] = grad[:, 8 * chans :]
-    me = me_ref[0]
-    e0[...] = dscr[me]
-    for k, ref in ((1, e1), (2, e2), (3, e3)):
-        ref[...] = dscr[me ^ k].astype(BF16)
+    halve(me_ref[0] & 1, dscr, keep_out, send_out)
+
+
+def halve(core, quarters, keep_out, send_out):
+    for i in range(2):
+        keep_out[i] = quarters[2 * i + core]
+        send_out[i] = quarters[2 * i + 1 - core].astype(BF16)
 
 
 def hi_lo(full):
@@ -206,7 +235,7 @@
     sum_refs = refs[:ranks]
     par, x, hid, gp, gain, *refs = refs[ranks:]
     if packed:
-        dlast, cbias, par_out, g_out, l0, l1, l2, l3, lscr = refs
+        dlast, cbias, keep, got, par_out, g_out, early_own, early_send, keep_out, send_out, lscr = refs
     else:
         par_out, g_out, grad_out, small_out = refs
     half = x.shape[2]
@@ -238,7 +267,7 @@
         grad_out[...] = grad
         small_out[...] = full
         return
-    owners, _, _ = l0.shape
+    owners = lscr.shape[1]
     chunk = chans // owners
     for kh in range(3):
         for kw in range(3):
@@ -255,12 +284,13 @@
         if at % chans:
             row = pltpu.roll(row, chans - at % chans, 1)
         lscr[3, d, 2 * chunk :, :] = hi_lo(jnp.where(row_id == 3, row, mine))
-    l0[...] = lscr[me]
-    for k, ref in ((1, l1), (2, l2), (3, l3)):
-        ref[...] = lscr[me ^ k].astype(BF16)
-
-
-def image_kernel(last, me_ref, par, hid, gm, gain, shift, par2, g, mix_top, mix, w, dw, dbias, block_out, gi_out, scr):
+    halve(me & 1, lscr, keep_out, send_out)
+    chip = me >> 1
+    early_own[...] = keep[chip] + got[chip].astype(F32)
+    early_send[...] = (keep[1 - chip] + got[1 - chip].astype(F32)).astype(BF16)
+
+
+def image_kernel(last, me_ref, par, hid, gm, gain, shift, par2, g, mix_top, mix, w, dw, dbias, block_out, gi_out, done_out, scr):
     half = g.shape[2]
     chans = g.shape[3]
     flat = [dw[:, k].reshape(3 * chans, dw.shape[3]) for k in range(3)]
@@ -296,6 +326,7 @@
         scr[pl.ds(0, half, stride=2), :] = base[sl, :chans] + later(from_odd[sl]) + gm[p + 1, 0]
         scr[pl.ds(1, half, stride=2), :] = base[sl, chans:] + sooner(from_even[sl]) + gm[p + 1, 1]
         gi_out[p] = scr[...].astype(BF16)
+    done_out[...] = jnp.zeros(done_out.shape, F32)
 
 
 def resplit(total, on):
@@ -303,16 +334,25 @@
     return jnp.where(on, hi_lo(whole), total)
 
 
-def rows_kernel(me_ref, e0, e1, e2, e3, l0, l1, l2, l3, out):
+def core_kernel(me_ref, keep, got, own, send):
     me = me_ref[0]
-    early = e0[...] + e1[...].astype(F32) + e2[...].astype(F32) + e3[...].astype(F32)
-    late = l0[...] + l1[...].astype(F32) + l2[...].astype(F32) + l3[...].astype(F32)
+    core, chip = me & 1, me >> 1
+    own[...] = keep[chip] + got[chip].astype(F32)
+    other = keep[1 - chip] + got[1 - chip].astype(F32)
+    m = other.shape[1] - 16
+    send[:, :m] = other[:, :m].astype(BF16)
+    send[:, m:] = resplit(other[:, m:], 2 * (1 - chip) + core == 3).astype(BF16)
+
+
+def rows_kernel(me_ref, early_own, early_got, late_own, late_got, after, out):
+    early = early_own[...] + early_got[...].astype(F32)
+    late = late_own[...] + late_got[...].astype(F32)
     n = early.shape[2]
     m = late.shape[1]
     for t in range(2):
         out[:, t * n : (t + 1) * n, :] = early[t].astype(BF16)
     out[:, 2 * n : 2 * n + m - 16, :] = late[:, : m - 16].astype(BF16)
-    out[:, 2 * n + m - 16 :, :] = resplit(late[:, m - 16 :], me == 3).astype(BF16)
+    out[:, 2 * n + m - 16 :, :] = resplit(late[:, m - 16 :], me_ref[0] == 3).astype(BF16)
 
 
 def dp_kernel(me_ref, got, out):
@@ -342,10 +382,9 @@
     db[...] = rows[3:4, :wide]
 
 
-def beside(x, up):
+def across(x):
     n = lax.axis_size("rows")
-    pairs = [(i, i + 1) for i in range(n - 1)]
-    return lax.ppermute(x, "rows", pairs if up else [(b, a) for a, b in pairs])
+    return lax.ppermute(x, "rows", [p for i in range(1, n - 1, 2) for p in ((i, i + 1), (i + 1, i))])
 
 
 def swap(x, axis, k):
@@ -364,41 +403,56 @@
     me = lax.axis_index("rows").astype(jnp.int32).reshape(1)
     smem = pl.BlockSpec(memory_space=pltpu.SMEM)
     vmem = pl.BlockSpec(memory_space=pltpu.VMEM)
-
-    def run(kernel, args, outs, scratch=()):
+    hbm = pl.BlockSpec(memory_space=pltpu.HBM)
+
+    def run(kernel, args, outs, scratch=(), specs=None, cost=1 << 27):
         return pl.pallas_call(
             kernel,
-            in_specs=[smem if a is me else vmem for a in args],
+            in_specs=specs or [smem if a is me else vmem for a in args],
             out_shape=[jax.ShapeDtypeStruct(s, d) for s, d in outs],
             out_specs=[vmem] * len(outs),
             scratch_shapes=list(scratch),
             compiler_params=pltpu.CompilerParams(vmem_limit_bytes=24 * MIB),
-            cost_estimate=pl.CostEstimate(flops=1 << 27, bytes_accessed=2 << 20, transcendentals=0),
+            cost_estimate=pl.CostEstimate(flops=cost, bytes_accessed=1 << 10, transcendentals=0),
         )(*args)
 
     def with_swaps(mine, others):
         return [mine] + [swap(other, "rows", k + 1) for k, other in enumerate(others)]
 
-    bias = conv_bias.reshape(1, chans)
-    gain = norm_gain.reshape(1, chans)
-    shift = norm_shift.reshape(1, chans)
-    dbias = down_bias.reshape(1, outs)
-    up, dn = beside(img, True), beside(img, False)
-    cot_up, cot_dn = beside(cot, True), beside(cot, False)
+    chip_img, core_img = across(img), swap(img, "rows", 1)
     row_scr = pltpu.VMEM((cols, chans), F32)
     block_of = (2, 2, half, chans)
     tile = ((8, chans), F32)
+    (ahead,) = run(first_kernel, (me,), [tile], cost=1 << 34)
+    raw = (
+        img,
+        conv_weight,
+        down_weight,
+        cot,
+        conv_bias.reshape(1, chans),
+        norm_gain.reshape(1, chans),
+        norm_shift.reshape(1, chans),
+        down_bias.reshape(1, outs),
+    )
+    w, dw, cot, bias, gain, shift, dbias, own_x, own_gm, cbias = run(
+        prep_kernel,
+        (ahead, *raw),
+        [(v.shape, v.dtype) for v in raw[1:]] + [(block_of, BF16), ((3, 2, half, chans), F32), ((8, outs), F32)],
+        [pltpu.VMEM(img.shape, BF16), row_scr, pltpu.SemaphoreType.DMA((len(raw),))],
+        [vmem] + [hbm] * len(raw),
+    )
+    chip_cot, core_cot = across(cot), swap(cot, "rows", 1)
     x, hid, stat = run(
         functools.partial(hidden_kernel, width),
-        (up, img, dn, conv_weight, bias),
+        (me, core_img, chip_img, own_x, w, bias),
         [((4, 2, half, chans), BF16), (block_of, F32), tile],
         [row_scr],
     )
     stats = with_swaps(stat, [stat] * (ranks - 1))
-    hid_edge, gm, cbias = run(
+    hid_edge, gm = run(
         edge_kernel,
-        (up, x, dn, conv_weight, bias, cot_up, cot, cot_dn, down_weight),
-        [(block_of, F32), ((4, 2, half, chans), F32), ((8, outs), F32)],
+        (me, core_img, chip_img, x, w, bias, core_cot, chip_cot, dw, own_gm),
+        [(block_of, F32), ((4, 2, half, chans), F32)],
         [row_scr],
     )
     par, mix, gp, sums = run(
@@ -411,35 +465,47 @@
     late_shape = (owners, 3 * chunk, chans)
     deep = 2 * wide + 3 * chunk
 
-    def by_rank(shape):
-        return [(shape, F32)] + [(shape, BF16)] * (ranks - 1)
-
     mix_top, *down_grad = run(
         functools.partial(down_kernel, packed),
         (me, par, x, hid_edge, gain, shift, mix, cot),
         [((half, 3 * chans), BF16)]
-        + ([((outs, chans), F32)] + by_rank(early_shape) if packed else [((outs, 9 * chans), F32)]),
+        + (
+            [((outs, chans), F32), ((2,) + early_shape, F32), ((2,) + early_shape, BF16)]
+            if packed
+            else [((outs, 9 * chans), F32)]
+        ),
         [pltpu.VMEM((4,) + early_shape, F32)] if packed else [],
     )
     if packed:
-        dlast, *early = down_grad
-        early = with_swaps(early[0], early[1:])
+        dlast, keep, send = down_grad
+        got = swap(send, "rows", 1)
     par2, g, *conv_grad = run(
         functools.partial(back_kernel, width, count, ranks, packed),
-        (me, *all_sums, par, x, hid, gp, gain) + ((dlast, cbias) if packed else ()),
-        [tile, (block_of, BF16)] + (by_rank(late_shape) if packed else [((3 * chans, 3 * chans), F32), tile]),
+        (me, *all_sums, par, x, hid, gp, gain) + ((dlast, cbias, keep, got) if packed else ()),
+        [tile, (block_of, BF16)]
+        + (
+            [(early_shape, F32), (early_shape, BF16), ((2,) + late_shape, F32), ((2,) + late_shape, BF16)]
+            if packed
+            else [((3 * chans, 3 * chans), F32), tile]
+        ),
         [pltpu.VMEM((4,) + late_shape, F32)] if packed else [],
     )
+    block, gi, done = run(
+        functools.partial(image_kernel, ranks - 1),
+        (me, par, hid_edge, gm, gain, shift, par2, g, mix_top, mix, w, dw, dbias),
+        [((half, outs), BF16), ((rows, cols, chans), BF16), tile],
+        [row_scr],
+    )
     if packed:
-        late = with_swaps(conv_grad[0], conv_grad[1:])
-    block, gi = run(
-        functools.partial(image_kernel, ranks - 1),
-        (me, par, hid_edge, gm, gain, shift, par2, g, mix_top, mix, conv_weight, down_weight, dbias),
-        [((half, outs), BF16), ((rows, cols, chans), BF16)],
-        [row_scr],
-    )
-    if packed:
-        (mine,) = run(rows_kernel, (me, *early, *late), [((owners, deep, chans), BF16)])
+        early_own, early_send, keep, send = conv_grad
+        late_own, late_send = run(
+            core_kernel, (me, keep, swap(send, "rows", 1)), [(late_shape, F32), (late_shape, BF16)]
+        )
+        (mine,) = run(
+            rows_kernel,
+            (me, early_own, swap(early_send, "rows", 2), late_own, swap(late_send, "rows", 2), done),
+            [((owners, deep, chans), BF16)],
+        )
         got = lax.all_to_all(mine, "dp", 0, 0)
         (part,) = run(dp_kernel, (me, got), [((deep, chans), BF16)])
         down, conv, cb, ga, sh, db = run(

time: 59.2 us -> 49.6 us (0.84)
  starting transfers between devices: 22.7 us -> 16.6 us
  local copies, waits for them, and re-layouts: 3.9 us -> 1.21 us
  waiting for transfers between devices: 10.6 us -> 9.5 us
  Pallas kernels: 6.36 us -> 7.28 us
    ppermute x4 -> x2, starting transfers between devices: 10.7 us -> 1.35 us  [across(): lax.ppermute(x, 'rows', [p for i in range(1, n - 1, 2) for p in ((i, i +...]
    ppermute x15, starting transfers between devices: 12 us -> 15.3 us  [swap(): lax.ppermute(x, axis, [(i, i ^ k) for i in range(lax.axis_size(axis))])]
    unnamed x18 -> x16, local copies, waits for them, and re-layouts: 3.9 us -> 1.21 us
    ppermute x15, waiting for transfers between devices: 10.6 us -> 9.49 us  [swap(): lax.ppermute(x, axis, [(i, i ^ k) for i in range(lax.axis_size(axis))])]
    pallas_call x9 -> x12, Pallas kernels: 6.36 us -> 7.28 us  [run(): pl.pallas_call(kernel, in_specs=specs or [smem if a is me else vmem for a...]
  transfers between devices with their start and end apart: 19 -> 17, of which waited for: 5 -> 8; matrix products, arithmetic and copies ran while one was open for 0% -> 0% of each run, Pallas kernels for 7% -> 9%
where the time goes in v2:
time: 49.6 us; the launch traced here: 49.4 us
  starting transfers between devices  16.6 us (33%)
  blocking collectives  14 us (28%)
  waiting for transfers between devices  9.5 us (19%)
  Pallas kernels  7.28 us (15%)
  local copies, waits for them, and re-layouts  1.21 us (2%)
  between operations  0.78 us (2%)
    ppermute x15, starting transfers between devices, swap(): lax.ppermute(x, axis, [(i, i ^ k) for i in range(lax.axis_size(axis))])  15.3 us
    all_to_all x1, blocking collectives, shards(): got = lax.all_to_all(mine, 'dp', 0, 0)  14 us
    ppermute x15, waiting for transfers between devices, swap(): lax.ppermute(x, axis, [(i, i ^ k) for i in range(lax.axis_size(axis))])  9.49 us
    pallas_call x12, Pallas kernels, run(): pl.pallas_call(kernel, in_specs=specs or [smem if a is me else vmem for a...  7.28 us
    ppermute x2, starting transfers between devices, across(): lax.ppermute(x, 'rows', [p for i in range(1, n - 1, 2) for p in ((i, i +...  1.35 us
    unnamed x16, local copies, waits for them, and re-layouts  1.21 us
  transfers between devices with their start and end apart: 17, of which 8 were waited for; matrix products, arithmetic and copies ran while one was open for 0% of the time, Pallas kernels for 9%

profile of v2, /device:TPU:0, one launch (start us, length us, event | category | flops | bytes accessed | tf_op | source)
XLA Modules:
  0.0 49.4 jit_solution(1050107038679861490)
XLA Ops:
  0.6 0.7 %collective-permute-start.1 = (bf16[2,512,128]{2,1,0:T(8,128)(2,1)}, bf16[2,512,128]{2,1,0:T(8,128)(2,1)S(1)}, u32[]{:S(2)}, u32[]{:S(2)}) collective-permute-start(bf16[2,512,128]{2,1,0:T(8,128)(2,1)} %bitcast.19), channel_id=1, source_target_pairs={{8,16},{16,8},{9,17},{17,9},{10,18},{18,10},{11,19},{19,11},{12,20... | collective-permute-start | bytes 786440 | tf_op jit(solution)/shard_map/ppermute | solution.py:387
  1.3 4.3 %collective-permute-start = (bf16[2,512,128]{2,1,0:T(8,128)(2,1)}, bf16[2,512,128]{2,1,0:T(8,128)(2,1)S(1)}, u32[]{:S(2)}, u32[]{:S(2)}) collective-permute-start(bf16[2,512,128]{2,1,0:T(8,128)(2,1)} %bitcast.20), channel_id=1, source_target_pairs={{0,8},{8,0},{16,24},{24,16},{1,9},{9,1},{17,25},{25,17},{2,10},{10... | collective-permute-start | bytes 786440 | tf_op jit(solution)/shard_map/ppermute | solution.py:391
  5.7 0.0 copy-start
  5.7 0.0 copy-start.1
  5.7 0.0 copy-start.2
  5.7 0.0 copy-start.3
  5.7 0.0 copy-start.6
  5.7 0.0 copy-start.7
  5.7 0.0 copy-start.4
  5.7 0.0 copy-start.5
  5.7 1.0 %copy-done = bf16[3,3,128,256]{3,2,1,0:T(8,128)(2,1)S(1)} copy-done((bf16[3,3,128,256]{3,2,1,0:T(8,128)(2,1)S(1)}, bf16[3,3,128,256]{3,2,1,0:T(8,128)(2,1)}, u32[]{:S(2)}) %copy-start) | copy-done | bytes 589848
  6.7 0.1 copy-done.1
  6.8 0.1 copy-done.2
  6.9 0.0 copy-done.3
  6.9 0.0 copy-done.6
  6.9 0.0 copy-done.7
  6.9 0.0 copy-done.4
  6.9 0.0 copy-done.5
  6.9 0.9 %shard_map.144 = (bf16[3,3,128,128]{3,2,1,0:T(8,128)(2,1)S(1)}, bf16[3,3,128,256]{3,2,1,0:T(8,128)(2,1)S(1)}, bf16[256,256]{1,0:T(8,128)(2,1)S(1)}, f32[1,128]{1...) custom-call(f32[8,128]{1,0:T(8,128)S(1)} %shard_map.143.ahead, ...), custom_call_target="tpu_custom_call" | custom-call | flops 134217728 | bytes 1024 | tf_op jit(solution)/shard_map/pallas_call | solution.py:409
  7.9 0.7 %collective-permute-start.6 = (bf16[256,256]{1,0:T(8,128)(2,1)S(1)}, bf16[256,256]{1,0:T(8,128)(2,1)S(1)}, u32[]{:S(2)}, u32[]{:S(2)}) collective-permute-start(bf16[256,256]{1,0:T(8,128)(2,1)S(1)} %get-tuple-element.54.cot), channel_id=1, source_target_pairs={{8,16},{16,8},{9,17},{17,9},{10,18},{18,10},{11,19},{19,11},{12,20... | collective-permute-start | bytes 393224 | tf_op jit(solution)/shard_map/ppermute | solution.py:387
  8.5 1.3 %collective-permute-start.5 = (bf16[256,256]{1,0:T(8,128)(2,1)S(1)}, bf16[256,256]{1,0:T(8,128)(2,1)S(1)}, u32[]{:S(2)}, u32[]{:S(2)}) collective-permute-start(bf16[256,256]{1,0:T(8,128)(2,1)S(1)} %get-tuple-element.54.cot), channel_id=1, source_target_pairs={{0,8},{8,0},{16,24},{24,16},{1,9},{9,1},{17,25},{25,17},{2,10},{10... | collective-permute-start | bytes 393224 | tf_op jit(solution)/shard_map/ppermute | solution.py:391
  9.9 0.0 collective-permute-done.1.chip
  9.9 0.0 collective-permute-done.core
  9.9 1.1 %shard_map.145 = (bf16[4,2,256,128]{3,2,1,0:T(8,128)(2,1)S(1)}, f32[2,2,256,128]{3,2,1,0:T(8,128)S(1)}, f32[8,128]{1,0:T(8,128)S(1)}) custom-call(s32[1]{0:T(128)} %bitcast.me_ref, bf16[2,512,128]{2,1,0:T(8,128)(2,1)S(1)} %collective-permute-done.core, bf16[2,512,128]{2,1,0:T(8,128)(2,1)S(1)} %collective-permute-done.1.chip, ...), custom_call_target="tpu_custom_call" | custom-call | flops 134217728 | bytes 1024 | tf_op jit(solution)/shard_map/pallas_call | solution.py:409
  11.0 1.7 %collective-permute-start.4 = (f32[8,128]{1,0:T(8,128)S(1)}, f32[8,128]{1,0:T(8,128)S(1)}, u32[]{:S(2)}, u32[]{:S(2)}) collective-permute-start(f32[8,128]{1,0:T(8,128)S(1)} %get-tuple-element.51.refs_0_), channel_id=1, source_target_pairs={{0,24},{8,16},{16,8},{24,0},{1,25},{9,17},{17,9},{25,1},{2,26},{10... | collective-permute-start | bytes 12296 | tf_op jit(solution)/shard_map/ppermute | solution.py:391
  12.7 0.0 collective-permute-start.3
  12.7 0.2 collective-permute-start.2
  12.9 0.0 collective-permute-done.6.cot_chip
  12.9 0.0 collective-permute-done.5.cot_core
  12.9 0.8 %shard_map.146 = (f32[2,2,256,128]{3,2,1,0:T(8,128)S(1)}, f32[4,2,256,128]{3,2,1,0:T(8,128)S(1)}) custom-call(s32[1]{0:T(128)} %bitcast.me_ref, bf16[2,512,128]{2,1,0:T(8,128)(2,1)S(1)} %collective-permute-done.core, bf16[2,512,128]{2,1,0:T(8,128)(2,1)S(1)} %collective-permute-done.1.chip, bf16[4,2,256,128]{3,2,1,0:T(8,128)(2,1)S(1)} %get-tuple-element.52.x.refs_4_.refs_5_, ...), custom_call_target="tpu_custom_call" | custom-call | flops 134217728 | bytes 1024 | tf_op jit(solution)/shard_map/pallas_call | solution.py:409
  13.7 0.3 collective-permute-done.4.refs_3_
  14.1 2.3 %collective-permute-done.3.refs_2_ = f32[8,128]{1,0:T(8,128)S(1)} collective-permute-done((f32[8,128]{1,0:T(8,128)S(1)}, f32[8,128]{1,0:T(8,128)S(1)}, u32[]{:S(2)}, u32[]{:S(2)}) %collective-permute-start.3) | collective-permute-done | bytes 4128 | tf_op jit(solution)/shard_map/ppermute | solution.py:391
  16.3 0.0 collective-permute-done.2.refs_1_
  16.3 0.4 shard_map.147
  16.7 0.6 %shard_map.148 = (bf16[256,384]{1,0:T(8,128)(2,1)S(1)}, f32[256,128]{1,0:T(8,128)S(1)}, f32[2,2,8,32,128]{4,3,2,1,0:T(8,128)S(1)}, bf16[2,2,8,32,128]{4,3,2,1,0:T(8,128)(2,1)S(1)}) custom-call(s32[1]{0:T(128)} %bitcast.me_ref, f32[8,128]{1,0:T(8,128)S(1)} %get-tuple-element.60.par.refs_4_, bf16[4,2,256,128]{3,2,1,0:T(8,128)(2,1)S(1)} %get-tuple-element.52.x.refs_4_.refs_5_, ...), custom_call_target="tpu_custom_call" | custom-call | flops 134217728 | bytes 1024 | tf_op jit(solution)/shard_map/pallas_call | solution.py:409
  17.3 0.1 collective-permute-start.10
  17.4 0.2 collective-permute-start.9
  17.6 2.0 %collective-permute-start.8 = (f32[8,128]{1,0:T(8,128)S(1)}, f32[8,128]{1,0:T(8,128)S(1)}, u32[]{:S(2)}, u32[]{:S(2)}) collective-permute-start(f32[8,128]{1,0:T(8,128)S(1)} %get-tuple-element.62.refs_0_), channel_id=1, source_target_pairs={{0,16},{8,24},{16,0},{24,8},{1,17},{9,25},{17,1},{25,9},{2,18},{10... | collective-permute-start | bytes 12296 | tf_op jit(solution)/shard_map/ppermute | solution.py:391
  19.6 0.0 collective-permute-start.7
  19.6 1.0 %collective-permute-done.9.refs_3_ = f32[8,128]{1,0:T(8,128)S(1)} collective-permute-done((f32[8,128]{1,0:T(8,128)S(1)}, f32[8,128]{1,0:T(8,128)S(1)}, u32[]{:S(2)}, u32[]{:S(2)}) %collective-permute-start.9) | collective-permute-done | bytes 4128 | tf_op jit(solution)/shard_map/ppermute | solution.py:391
  20.5 0.7 %collective-permute-done.8.refs_2_ = f32[8,128]{1,0:T(8,128)S(1)} collective-permute-done((f32[8,128]{1,0:T(8,128)S(1)}, f32[8,128]{1,0:T(8,128)S(1)}, u32[]{:S(2)}, u32[]{:S(2)}) %collective-permute-start.8) | collective-permute-done | bytes 4128 | tf_op jit(solution)/shard_map/ppermute | solution.py:391
  21.2 0.0 collective-permute-done.7.refs_1_
  21.2 0.0 collective-permute-done.10.refs_12_
  21.2 1.0 %shard_map.149 = (f32[8,128]{1,0:T(8,128)S(1)}, bf16[2,2,256,128]{3,2,1,0:T(8,128)(2,1)S(1)}, f32[2,8,32,128]{3,2,1,0:T(8,128)S(1)}, bf16[2,8,32,128]{3,2,1,0:T(...) custom-call(s32[1]{0:T(128)} %bitcast.me_ref, ...), custom_call_target="tpu_custom_call" | custom-call | flops 134217728 | bytes 1024 | tf_op jit(solution)/shard_map/pallas_call | solution.py:409
  22.2 0.1 collective-permute-start.12
  22.3 2.0 %collective-permute-start.11 = (bf16[2,8,32,128]{3,2,1,0:T(8,128)(2,1)S(1)}, bf16[2,8,32,128]{3,2,1,0:T(8,128)(2,1)S(1)}, u32[]{:S(2)}, u32[]{:S(2)}) collective-permute-start(bf16[2,8,32,128]{3,2,1,0:T(8,128)(2,1)S(1)} %get-tuple-element.76), channel_id=1, source_target_pairs={{0,16},{8,24},{16,0},{24,8},{1,17},{9,25},{17,1},{25,9},{2,18},{10... | collective-permute-start | bytes 393224 | tf_op jit(solution)/shard_map/ppermute | solution.py:391
  24.3 0.0 collective-permute-done.12.got
  24.3 0.1 shard_map.151
  24.4 1.4 %collective-permute-start.13 = (bf16[8,48,128]{2,1,0:T(8,128)(2,1)S(1)}, bf16[8,48,128]{2,1,0:T(8,128)(2,1)S(1)}, u32[]{:S(2)}, u32[]{:S(2)}) collective-permute-start(bf16[8,48,128]{2,1,0:T(8,128)(2,1)S(1)} %get-tuple-element.80), channel_id=1, source_target_pairs={{0,16},{8,24},{16,0},{24,8},{1,17},{9,25},{17,1},{25,9},{2,18},{10... | collective-permute-start | bytes 294920 | tf_op jit(solution)/shard_map/ppermute | solution.py:391
  25.8 1.5 %shard_map.150 = (bf16[256,256]{1,0:T(8,128)(2,1)}, bf16[2,512,128]{2,1,0:T(8,128)(2,1)}, f32[8,128]{1,0:T(8,128)S(1)}) custom-call(s32[1]{0:T(128)} %bitcast.me_ref, f32[8,128]{1,0:T(8,128)S(1)} %get-tuple-element.60.par.refs_4_, f32[2,2,256,128]{3,2,1,0:T(8,128)S(1)} %get-tuple-element.61.hid, f32[4,2,256,128]{3,2,1,0:T(8,128)S(1)} %get-tuple-element.57.refs_6_.gm, ...), custom_call_target="tpu_custom_call" | custom-call | flops 134217728 | bytes 1024 | tf_op jit(solution)/shard_map/pallas_call | solution.py:409
  27.3 1.4 %collective-permute-done.11.early_got = bf16[2,8,32,128]{3,2,1,0:T(8,128)(2,1)S(1)} collective-permute-done((bf16[2,8,32,128]{3,2,1,0:T(8,128)(2,1)S(1)}, bf16[2,8,32,128]{3,2,1,0:T(8,128)(2,1)S(1)}, u32[]{:S(2)}, u32[]{:S(2)}) %collective-permute-start.11) | collective-permute-done | bytes 131104 | tf_op jit(solution)/shard_map/ppermute | solution.py:391
  28.7 1.8 %collective-permute-done.13.late_got = bf16[8,48,128]{2,1,0:T(8,128)(2,1)S(1)} collective-permute-done((bf16[8,48,128]{2,1,0:T(8,128)(2,1)S(1)}, bf16[8,48,128]{2,1,0:T(8,128)(2,1)S(1)}, u32[]{:S(2)}, u32[]{:S(2)}) %collective-permute-start.13) | collective-permute-done | bytes 98336 | tf_op jit(solution)/shard_map/ppermute | solution.py:391
  30.5 0.1 shard_map.152
  30.6 14.0 %all_to_all.5.got = bf16[8,112,128]{2,1,0:T(8,128)(2,1)S(1)} all-to-all(bf16[8,112,128]{2,1,0:T(8,128)(2,1)S(1)} %shard_map.152), channel_id=1, replica_groups=mesh['rows'=4,'dp'=8] {'dp'}, dimensions={0} | all-to-all | bytes 458752 | tf_op jit(solution)/shard_map/all_to_all | solution.py:509
  44.7 0.1 collective-permute-start.16
  44.7 1.7 %collective-permute-start.15 = (bf16[112,128]{1,0:T(8,128)(2,1)S(1)}, bf16[112,128]{1,0:T(8,128)(2,1)S(1)}, u32[]{:S(2)}, u32[]{:S(2)}) collective-permute-start(bf16[112,128]{1,0:T(8,128)(2,1)S(1)} %shard_map.153.q0), channel_id=1, source_target_pairs={{0,16},{8,24},{16,0},{24,8},{1,17},{9,25},{17,1},{25,9},{2,18},{10... | collective-permute-start | bytes 86024 | tf_op jit(solution)/shard_map/ppermute | solution.py:391
  46.4 0.2 collective-permute-start.14
  46.6 1.6 %collective-permute-done.16.q3 = bf16[112,128]{1,0:T(8,128)(2,1)S(1)} collective-permute-done((bf16[112,128]{1,0:T(8,128)(2,1)S(1)}, bf16[112,128]{1,0:T(8,128)(2,1)S(1)}, u32[]{:S(2)}, u32[]{:S(2)}) %collective-permute-start.16) | collective-permute-done | bytes 28704 | tf_op jit(solution)/shard_map/ppermute | solution.py:391
  48.2 0.5 %collective-permute-done.15.q2 = bf16[112,128]{1,0:T(8,128)(2,1)S(1)} collective-permute-done((bf16[112,128]{1,0:T(8,128)(2,1)S(1)}, bf16[112,128]{1,0:T(8,128)(2,1)S(1)}, u32[]{:S(2)}, u32[]{:S(2)}) %collective-permute-start.15) | collective-permute-done | bytes 28704 | tf_op jit(solution)/shard_map/ppermute | solution.py:391
  48.7 0.0 collective-permute-done.14.q1
  48.7 0.7 %shard_map.154 = (f32[9,32,128]{2,1,0:T(8,128)}, f32[9,16,128]{2,1,0:T(8,128)}, f32[1,16]{1,0:T(1,128)}, f32[1,16]{1,0:T(1,128)}, f32[1,16]{1,0:T(1,128)}, /*index=5*/f32[1,32]{1,0:T(1,128)}) custom-call(s32[1]{0:T(128)} %bitcast.me_ref, bf16[112,128]{1,0:T(8,128)(2,1)S(1)} %shard_map.153.q0, bf16[112,128]{1,0:T(8,128)(2,1)S(1)} %collective-permute-done.14.q1, ...), custom_call_target="tpu_custom_call" | custom-call | flops 134217728 | bytes 1024 | tf_op jit(solution)/shard_map/pallas_call | solution.py:409
  (2 shorter events, 0.0 us)
Async XLA Ops:
  0.6 9.2 %collective-permute-start.1 = (bf16[2,512,128]{2,1,0:T(8,128)(2,1)}, bf16[2,512,128]{2,1,0:T(8,128)(2,1)S(1)}, u32[]{:S(2)}, u32[]{:S(2)}) collective-permute-start(bf16[2,512,128]{2,1,0:T(8,128)(2,1)} %bitcast.19), channel_id=1, source_target_pairs={{8,16},{16,8},{9,17},{17,9},{10,18},{18,10},{11,19},{19,11},{12,20... | collective-permute-start | bytes 786440 | tf_op jit(solution)/shard_map/ppermute | solution.py:387
  1.3 8.6 %collective-permute-start = (bf16[2,512,128]{2,1,0:T(8,128)(2,1)}, bf16[2,512,128]{2,1,0:T(8,128)(2,1)S(1)}, u32[]{:S(2)}, u32[]{:S(2)}) collective-permute-start(bf16[2,512,128]{2,1,0:T(8,128)(2,1)} %bitcast.20), channel_id=1, source_target_pairs={{0,8},{8,0},{16,24},{24,16},{1,9},{9,1},{17,25},{25,17},{2,10},{10... | collective-permute-start | bytes 786440 | tf_op jit(solution)/shard_map/ppermute | solution.py:391
  5.7 1.1 %copy-start = (bf16[3,3,128,256]{3,2,1,0:T(8,128)(2,1)S(1)}, bf16[3,3,128,256]{3,2,1,0:T(8,128)(2,1)}, u32[]{:S(2)}) copy-start(bf16[3,3,128,256]{3,2,1,0:T(8,128)(2,1)} %dw.1) | copy-start | bytes 1769476
  5.7 1.1 %copy-start.1 = (bf16[3,3,128,128]{3,2,1,0:T(8,128)(2,1)S(1)}, bf16[3,3,128,128]{3,2,1,0:T(8,128)(2,1)}, u32[]{:S(2)}) copy-start(bf16[3,3,128,128]{3,2,1,0:T(8,128)(2,1)} %w.1) | copy-start | bytes 884740
  5.7 1.2 %copy-start.2 = (bf16[1,2,512,128]{3,2,1,0:T(8,128)(2,1)S(1)}, bf16[1,2,512,128]{3,2,1,0:T(8,128)(2,1)}, u32[]{:S(2)}) copy-start(bf16[1,2,512,128]{3,2,1,0:T(8,128)(2,1)} %param.8) | copy-start | bytes 786436
  5.7 1.2 %copy-start.3 = (bf16[1,1,256,256]{3,2,1,0:T(8,128)(2,1)S(1)}, bf16[1,1,256,256]{3,2,1,0:T(8,128)(2,1)}, u32[]{:S(2)}) copy-start(bf16[1,1,256,256]{3,2,1,0:T(8,128)(2,1)} %param.15) | copy-start | bytes 393220
  5.7 1.2 %copy-start.6 = (f32[128]{0:T(128)S(1)}, f32[128]{0:T(128)}, u32[]{:S(2)}) copy-start(f32[128]{0:T(128)} %param.11) | copy-start | bytes 1540
  5.7 1.2 %copy-start.7 = (f32[128]{0:T(128)S(1)}, f32[128]{0:T(128)}, u32[]{:S(2)}) copy-start(f32[128]{0:T(128)} %param.12) | copy-start | bytes 1540
  5.7 1.2 %copy-start.4 = (f32[256]{0:T(256)S(1)}, f32[256]{0:T(256)}, u32[]{:S(2)}) copy-start(f32[256]{0:T(256)} %param.14) | copy-start | bytes 3076
  5.7 1.2 %copy-start.5 = (f32[128]{0:T(128)S(1)}, f32[128]{0:T(128)}, u32[]{:S(2)}) copy-start(f32[128]{0:T(128)} %param.10) | copy-start | bytes 1540
  7.9 5.0 %collective-permute-start.6 = (bf16[256,256]{1,0:T(8,128)(2,1)S(1)}, bf16[256,256]{1,0:T(8,128)(2,1)S(1)}, u32[]{:S(2)}, u32[]{:S(2)}) collective-permute-start(bf16[256,256]{1,0:T(8,128)(2,1)S(1)} %get-tuple-element.54.cot), channel_id=1, source_target_pairs={{8,16},{16,8},{9,17},{17,9},{10,18},{18,10},{11,19},{19,11},{12,20... | collective-permute-start | bytes 393224 | tf_op jit(solution)/shard_map/ppermute | solution.py:387
  8.5 4.4 %collective-permute-start.5 = (bf16[256,256]{1,0:T(8,128)(2,1)S(1)}, bf16[256,256]{1,0:T(8,128)(2,1)S(1)}, u32[]{:S(2)}, u32[]{:S(2)}) collective-permute-start(bf16[256,256]{1,0:T(8,128)(2,1)S(1)} %get-tuple-element.54.cot), channel_id=1, source_target_pairs={{0,8},{8,0},{16,24},{24,16},{1,9},{9,1},{17,25},{25,17},{2,10},{10... | collective-permute-start | bytes 393224 | tf_op jit(solution)/shard_map/ppermute | solution.py:391
  11.0 3.1 %collective-permute-start.4 = (f32[8,128]{1,0:T(8,128)S(1)}, f32[8,128]{1,0:T(8,128)S(1)}, u32[]{:S(2)}, u32[]{:S(2)}) collective-permute-start(f32[8,128]{1,0:T(8,128)S(1)} %get-tuple-element.51.refs_0_), channel_id=1, source_target_pairs={{0,24},{8,16},{16,8},{24,0},{1,25},{9,17},{17,9},{25,1},{2,26},{10... | collective-permute-start | bytes 12296 | tf_op jit(solution)/shard_map/ppermute | solution.py:391
  12.7 3.6 %collective-permute-start.3 = (f32[8,128]{1,0:T(8,128)S(1)}, f32[8,128]{1,0:T(8,128)S(1)}, u32[]{:S(2)}, u32[]{:S(2)}) collective-permute-start(f32[8,128]{1,0:T(8,128)S(1)} %get-tuple-element.51.refs_0_), channel_id=1, source_target_pairs={{0,16},{8,24},{16,0},{24,8},{1,17},{9,25},{17,1},{25,9},{2,18},{10... | collective-permute-start | bytes 12296 | tf_op jit(solution)/shard_map/ppermute | solution.py:391
  12.7 3.6 %collective-permute-start.2 = (f32[8,128]{1,0:T(8,128)S(1)}, f32[8,128]{1,0:T(8,128)S(1)}, u32[]{:S(2)}, u32[]{:S(2)}) collective-permute-start(f32[8,128]{1,0:T(8,128)S(1)} %get-tuple-element.51.refs_0_), channel_id=1, source_target_pairs={{0,8},{8,0},{16,24},{24,16},{1,9},{9,1},{17,25},{25,17},{2,10},{10... | collective-permute-start | bytes 12296 | tf_op jit(solution)/shard_map/ppermute | solution.py:391
  17.3 3.9 %collective-permute-start.10 = (bf16[2,2,8,32,128]{4,3,2,1,0:T(8,128)(2,1)S(1)}, bf16[2,2,8,32,128]{4,3,2,1,0:T(8,128)(2,1)S(1)}, u32[]{:S(2)}, u32[]{:S(2)}) collective-permute-start(bf16[2,2,8,32,128]{4,3,2,1,0:T(8,128)(2,1)S(1)} %get-tuple-element.68), channel_id=1, source_target_pairs={{0,8},{8,0},{16,24},{24,16},{1,9},{9,1},{17,25},{25,17},{2,10},{10... | collective-permute-start | bytes 786440 | tf_op jit(solution)/shard_map/ppermute | solution.py:391
  17.4 3.1 %collective-permute-start.9 = (f32[8,128]{1,0:T(8,128)S(1)}, f32[8,128]{1,0:T(8,128)S(1)}, u32[]{:S(2)}, u32[]{:S(2)}) collective-permute-start(f32[8,128]{1,0:T(8,128)S(1)} %get-tuple-element.62.refs_0_), channel_id=1, source_target_pairs={{0,24},{8,16},{16,8},{24,0},{1,25},{9,17},{17,9},{25,1},{2,26},{10... | collective-permute-start | bytes 12296 | tf_op jit(solution)/shard_map/ppermute | solution.py:391
  17.6 3.6 %collective-permute-start.8 = (f32[8,128]{1,0:T(8,128)S(1)}, f32[8,128]{1,0:T(8,128)S(1)}, u32[]{:S(2)}, u32[]{:S(2)}) collective-permute-start(f32[8,128]{1,0:T(8,128)S(1)} %get-tuple-element.62.refs_0_), channel_id=1, source_target_pairs={{0,16},{8,24},{16,0},{24,8},{1,17},{9,25},{17,1},{25,9},{2,18},{10... | collective-permute-start | bytes 12296 | tf_op jit(solution)/shard_map/ppermute | solution.py:391
  19.6 1.6 %collective-permute-start.7 = (f32[8,128]{1,0:T(8,128)S(1)}, f32[8,128]{1,0:T(8,128)S(1)}, u32[]{:S(2)}, u32[]{:S(2)}) collective-permute-start(f32[8,128]{1,0:T(8,128)S(1)} %get-tuple-element.62.refs_0_), channel_id=1, source_target_pairs={{0,8},{8,0},{16,24},{24,16},{1,9},{9,1},{17,25},{25,17},{2,10},{10... | collective-permute-start | bytes 12296 | tf_op jit(solution)/shard_map/ppermute | solution.py:391
  22.2 2.1 %collective-permute-start.12 = (bf16[2,8,48,128]{3,2,1,0:T(8,128)(2,1)S(1)}, bf16[2,8,48,128]{3,2,1,0:T(8,128)(2,1)S(1)}, u32[]{:S(2)}, u32[]{:S(2)}) collective-permute-start(bf16[2,8,48,128]{3,2,1,0:T(8,128)(2,1)S(1)} %get-tuple-element.78), channel_id=1, source_target_pairs={{0,8},{8,0},{16,24},{24,16},{1,9},{9,1},{17,25},{25,17},{2,10},{10... | collective-permute-start | bytes 589832 | tf_op jit(solution)/shard_map/ppermute | solution.py:391
  22.3 6.4 %collective-permute-start.11 = (bf16[2,8,32,128]{3,2,1,0:T(8,128)(2,1)S(1)}, bf16[2,8,32,128]{3,2,1,0:T(8,128)(2,1)S(1)}, u32[]{:S(2)}, u32[]{:S(2)}) collective-permute-start(bf16[2,8,32,128]{3,2,1,0:T(8,128)(2,1)S(1)} %get-tuple-element.76), channel_id=1, source_target_pairs={{0,16},{8,24},{16,0},{24,8},{1,17},{9,25},{17,1},{25,9},{2,18},{10... | collective-permute-start | bytes 393224 | tf_op jit(solution)/shard_map/ppermute | solution.py:391
  24.4 6.1 %collective-permute-start.13 = (bf16[8,48,128]{2,1,0:T(8,128)(2,1)S(1)}, bf16[8,48,128]{2,1,0:T(8,128)(2,1)S(1)}, u32[]{:S(2)}, u32[]{:S(2)}) collective-permute-start(bf16[8,48,128]{2,1,0:T(8,128)(2,1)S(1)} %get-tuple-element.80), channel_id=1, source_target_pairs={{0,16},{8,24},{16,0},{24,8},{1,17},{9,25},{17,1},{25,9},{2,18},{10... | collective-permute-start | bytes 294920 | tf_op jit(solution)/shard_map/ppermute | solution.py:391
  44.7 3.5 %collective-permute-start.16 = (bf16[112,128]{1,0:T(8,128)(2,1)S(1)}, bf16[112,128]{1,0:T(8,128)(2,1)S(1)}, u32[]{:S(2)}, u32[]{:S(2)}) collective-permute-start(bf16[112,128]{1,0:T(8,128)(2,1)S(1)} %shard_map.153.q0), channel_id=1, source_target_pairs={{0,24},{8,16},{16,8},{24,0},{1,25},{9,17},{17,9},{25,1},{2,26},{10... | collective-permute-start | bytes 86024 | tf_op jit(solution)/shard_map/ppermute | solution.py:391
  44.7 3.9 %collective-permute-start.15 = (bf16[112,128]{1,0:T(8,128)(2,1)S(1)}, bf16[112,128]{1,0:T(8,128)(2,1)S(1)}, u32[]{:S(2)}, u32[]{:S(2)}) collective-permute-start(bf16[112,128]{1,0:T(8,128)(2,1)S(1)} %shard_map.153.q0), channel_id=1, source_target_pairs={{0,16},{8,24},{16,0},{24,8},{1,17},{9,25},{17,1},{25,9},{2,18},{10... | collective-permute-start | bytes 86024 | tf_op jit(solution)/shard_map/ppermute | solution.py:391
  46.4 2.3 %collective-permute-start.14 = (bf16[112,128]{1,0:T(8,128)(2,1)S(1)}, bf16[112,128]{1,0:T(8,128)(2,1)S(1)}, u32[]{:S(2)}, u32[]{:S(2)}) collective-permute-start(bf16[112,128]{1,0:T(8,128)(2,1)S(1)} %shard_map.153.q0), channel_id=1, source_target_pairs={{0,8},{8,0},{16,24},{24,16},{1,9},{9,1},{17,25},{25,17},{2,10},{10... | collective-permute-start | bytes 86024 | tf_op jit(solution)/shard_map/ppermute | solution.py:391

commit v3 on v2

--- a/solution.py
+++ b/solution.py
@@ -12,6 +12,7 @@
 F32 = jnp.float32
 BF16 = jnp.bfloat16
 MIB = 1 << 20
+BACK = 1 << 32
 
 
 def dot(a, b):
@@ -220,10 +221,14 @@
     halve(me_ref[0] & 1, dscr, keep_out, send_out)
 
 
-def halve(core, quarters, keep_out, send_out):
+def halve(core, quarters, keep_out, *send_outs):
+    n = len(send_outs)
     for i in range(2):
         keep_out[i] = quarters[2 * i + core]
-        send_out[i] = quarters[2 * i + 1 - core].astype(BF16)
+        other = quarters[2 * i + 1 - core].astype(BF16)
+        size = other.shape[-2] // n
+        for j, ref in enumerate(send_outs):
+            ref[i] = other[..., j * size : (j + 1) * size, :]
 
 
 def hi_lo(full):
@@ -233,9 +238,9 @@
 
 def back_kernel(width, count, ranks, packed, me_ref, *refs):
     sum_refs = refs[:ranks]
-    par, x, hid, gp, gain, *refs = refs[ranks:]
+    par, x, hid, gp, gain, _, *refs = refs[ranks:]
     if packed:
-        dlast, cbias, keep, got, par_out, g_out, early_own, early_send, keep_out, send_out, lscr = refs
+        dlast, cbias, par_out, g_out, keep_out, *send_outs, lscr = refs
     else:
         par_out, g_out, grad_out, small_out = refs
     half = x.shape[2]
@@ -284,22 +289,23 @@
         if at % chans:
             row = pltpu.roll(row, chans - at % chans, 1)
         lscr[3, d, 2 * chunk :, :] = hi_lo(jnp.where(row_id == 3, row, mine))
-    halve(me & 1, lscr, keep_out, send_out)
-    chip = me >> 1
-    early_own[...] = keep[chip] + got[chip].astype(F32)
-    early_send[...] = (keep[1 - chip] + got[1 - chip].astype(F32)).astype(BF16)
-
-
-def image_kernel(last, me_ref, par, hid, gm, gain, shift, par2, g, mix_top, mix, w, dw, dbias, block_out, gi_out, done_out, scr):
-    half = g.shape[2]
-    chans = g.shape[3]
-    flat = [dw[:, k].reshape(3 * chans, dw.shape[3]) for k in range(3)]
+    halve(me & 1, lscr, keep_out, *send_outs)
+
+
+def block_kernel(ahead, mix_top, mix, dw, dbias, block_out, done_out):
+    chans, outs = dw.shape[2:]
+    flat = [dw[:, k].reshape(3 * chans, outs) for k in range(3)]
     odd_before = lanes(mix_top[:, :chans], mix[0, :, :chans], mix[1, :, :chans])
     even = lanes(mix_top[:, chans : 2 * chans], mix[0, :, chans : 2 * chans], mix[1, :, chans : 2 * chans])
     odd = lanes(mix_top[:, 2 * chans :], mix[0, :, 2 * chans :], mix[1, :, 2 * chans :])
     block = dot(lanes(odd_before, even, odd), stack(*flat)) + dbias[...]
     block_out[...] = block.astype(BF16)
-
+    done_out[...] = jnp.zeros(done_out.shape, F32)
+
+
+def image_kernel(last, me_ref, par, hid, gm, gain, shift, par2, g, w, gi_out, done_out, scr):
+    half = g.shape[2]
+    chans = g.shape[3]
     mean, rstd = par[0:1], par[1:2]
     me = me_ref[0]
     edge = []
@@ -329,37 +335,57 @@
     done_out[...] = jnp.zeros(done_out.shape, F32)
 
 
-def resplit(total, on):
-    whole = total[..., 0:8, :] + total[..., 8:16, :]
-    return jnp.where(on, hi_lo(whole), total)
-
-
-def core_kernel(me_ref, keep, got, own, send):
-    me = me_ref[0]
+def rounded(total, on):
+    n = total.shape[0] - 16
+    last = total[n:]
+    whole = last[0:8] + last[8:16]
+    last = jnp.where(on, hi_lo(whole), last)
+    return stack(total[:n], last).astype(BF16)
+
+
+def early_kernel(me_ref, keep, got, own, send, done_out):
+    done_out[...] = jnp.zeros(done_out.shape, F32)
+    chip = me_ref[0] >> 1
+    own[...] = keep[chip] + got[chip].astype(F32)
+    send[...] = (keep[1 - chip] + got[1 - chip].astype(F32)).astype(BF16)
+
+
+def late_kernel(me_ref, owner_ref, keep, got0, got1, got2, e_own, e_got, own, sx, sy, sxy, ey_own, ey_send):
+    me, side = me_ref[0], owner_ref[0] & 1
     core, chip = me & 1, me >> 1
-    own[...] = keep[chip] + got[chip].astype(F32)
-    other = keep[1 - chip] + got[1 - chip].astype(F32)
-    m = other.shape[1] - 16
-    send[:, :m] = other[:, :m].astype(BF16)
-    send[:, m:] = resplit(other[:, m:], 2 * (1 - chip) + core == 3).astype(BF16)
-
-
-def rows_kernel(me_ref, early_own, early_got, late_own, late_got, after, out):
-    early = early_own[...] + early_got[...].astype(F32)
-    late = late_own[...] + late_got[...].astype(F32)
+    mine, other = me == 3, 2 * (1 - chip) + core == 3
+
+    def total(x, d):
+        parts = [got[x, d].astype(F32) for got in (got0, got1, got2)]
+        return keep[x, d] + jnp.concatenate(parts, axis=0)
+
+    for z in range(own.shape[0]):
+        here, there = 2 * z + side, 2 * z + 1 - side
+        own[z] = total(chip, here)
+        sx[z] = rounded(total(1 - chip, here), other)
+        sy[z] = rounded(total(chip, there), mine)
+        sxy[z] = rounded(total(1 - chip, there), other)
+        for t in range(2):
+            ey_own[t, z] = e_own[t, here] + e_got[t, here].astype(F32)
+            ey_send[t, z] = (e_own[t, there] + e_got[t, there].astype(F32)).astype(BF16)
+
+
+def pack_kernel(me_ref, owner_ref, own, gx, gy, gxy, ey_own, ey_got, after, out, s1, s2, s3, scr):
+    z = owner_ref[0] >> 1
+    early = ey_own[...] + ey_got[...].astype(F32)
     n = early.shape[2]
-    m = late.shape[1]
     for t in range(2):
-        out[:, t * n : (t + 1) * n, :] = early[t].astype(BF16)
-    out[:, 2 * n : 2 * n + m - 16, :] = late[:, : m - 16].astype(BF16)
-    out[:, 2 * n + m - 16 :, :] = resplit(late[:, m - 16 :], me_ref[0] == 3).astype(BF16)
-
-
-def dp_kernel(me_ref, got, out):
-    total = jnp.sum(got[...].astype(F32), axis=0)
-    n = total.shape[0]
-    out[: n - 16] = total[: n - 16].astype(BF16)
-    out[n - 16 :] = resplit(total[n - 16 :], me_ref[0] == 3).astype(BF16)
+        scr[:, t * n : (t + 1) * n, :] = early[t]
+    scr[:, 2 * n :, :] = own[...] + gx[...].astype(F32) + gy[...].astype(F32) + gxy[...].astype(F32)
+    out[...] = scr[z]
+    for k, ref in ((1, s1), (2, s2), (3, s3)):
+        ref[...] = rounded(scr[z ^ k], me_ref[0] == 3)
+
+
+def sum_kernel(me_ref, own, g1, g2, g3, out, send):
+    total = own[...] + g1[...].astype(F32) + g2[...].astype(F32) + g3[...].astype(F32)
+    out[...] = total
+    send[...] = rounded(total, me_ref[0] == 3)
 
 
 def last_kernel(chunk, me_ref, q0, q1, q2, q3, down, conv, cb, ga, sh, db, scr):
@@ -391,6 +417,12 @@
     return lax.ppermute(x, axis, [(i, i ^ k) for i in range(lax.axis_size(axis))])
 
 
+def swap_both(x, k_rows, k_dp):
+    both = ("rows", "dp")
+    k = k_rows * lax.axis_size("dp") + k_dp
+    return lax.ppermute(x, both, [(i, i ^ k) for i in range(lax.axis_size(both))])
+
+
 def shards(images, conv_weight, conv_bias, norm_gain, norm_shift, down_weight, down_bias, cotangent):
     img, cot = images[0], cotangent[0, 0]
     rows, cols, chans = img.shape
@@ -399,8 +431,9 @@
     width = chans // GROUPS
     count = float(rows * cols * width * ranks)
     chunk, wide = chans // owners, outs // owners
-    packed = ranks == 4 and chunk == 16 and wide == 32
+    packed = ranks == 4 and owners == 8 and chunk == 16 and wide == 32
     me = lax.axis_index("rows").astype(jnp.int32).reshape(1)
+    owner = lax.axis_index("dp").astype(jnp.int32).reshape(1)
     smem = pl.BlockSpec(memory_space=pltpu.SMEM)
     vmem = pl.BlockSpec(memory_space=pltpu.VMEM)
     hbm = pl.BlockSpec(memory_space=pltpu.HBM)
@@ -408,7 +441,7 @@
     def run(kernel, args, outs, scratch=(), specs=None, cost=1 << 27):
         return pl.pallas_call(
             kernel,
-            in_specs=specs or [smem if a is me else vmem for a in args],
+            in_specs=specs or [smem if a is me or a is owner else vmem for a in args],
             out_shape=[jax.ShapeDtypeStruct(s, d) for s, d in outs],
             out_specs=[vmem] * len(outs),
             scratch_shapes=list(scratch),
@@ -416,8 +449,8 @@
             cost_estimate=pl.CostEstimate(flops=cost, bytes_accessed=1 << 10, transcendentals=0),
         )(*args)
 
-    def with_swaps(mine, others):
-        return [mine] + [swap(other, "rows", k + 1) for k, other in enumerate(others)]
+    def with_swaps(mine, other):
+        return [mine] + [swap(other, "rows", k) for k in range(1, ranks)]
 
     chip_img, core_img = across(img), swap(img, "rows", 1)
     row_scr = pltpu.VMEM((cols, chans), F32)
@@ -448,7 +481,7 @@
         [((4, 2, half, chans), BF16), (block_of, F32), tile],
         [row_scr],
     )
-    stats = with_swaps(stat, [stat] * (ranks - 1))
+    stats = with_swaps(stat, stat)
     hid_edge, gm = run(
         edge_kernel,
         (me, core_img, chip_img, x, w, bias, core_cot, chip_cot, dw, own_gm),
@@ -460,7 +493,7 @@
         (*stats, x, hid, gm, gain, shift),
         [tile, ((2, half, 3 * chans), BF16), (block_of, F32), tile],
     )
-    all_sums = with_swaps(sums, [sums] * (ranks - 1))
+    all_sums = with_swaps(sums, sums)
     early_shape = (2, owners, wide, chans)
     late_shape = (owners, 3 * chunk, chans)
     deep = 2 * wide + 3 * chunk
@@ -478,45 +511,60 @@
     )
     if packed:
         dlast, keep, send = down_grad
-        got = swap(send, "rows", 1)
+        early_own, early_send, ahead = run(
+            early_kernel, (me, keep, swap(send, "rows", 1)), [(early_shape, F32), (early_shape, BF16), tile]
+        )
+        early_got = swap(early_send, "rows", 2)
+    block, block_done = run(block_kernel, (ahead, mix_top, mix, dw, dbias), [((half, outs), BF16), tile])
     par2, g, *conv_grad = run(
         functools.partial(back_kernel, width, count, ranks, packed),
-        (me, *all_sums, par, x, hid, gp, gain) + ((dlast, cbias, keep, got) if packed else ()),
+        (me, *all_sums, par, x, hid, gp, gain, block_done) + ((dlast, cbias) if packed else ()),
         [tile, (block_of, BF16)]
         + (
-            [(early_shape, F32), (early_shape, BF16), ((2,) + late_shape, F32), ((2,) + late_shape, BF16)]
+            [((2,) + late_shape, F32)] + [((2, owners, chunk, chans), BF16)] * 3
             if packed
             else [((3 * chans, 3 * chans), F32), tile]
         ),
         [pltpu.VMEM((4,) + late_shape, F32)] if packed else [],
-    )
-    block, gi, done = run(
+        cost=BACK,
+    )
+    gi, done = run(
         functools.partial(image_kernel, ranks - 1),
-        (me, par, hid_edge, gm, gain, shift, par2, g, mix_top, mix, w, dw, dbias),
-        [((half, outs), BF16), ((rows, cols, chans), BF16), tile],
+        (me, par, hid_edge, gm, gain, shift, par2, g, w),
+        [((rows, cols, chans), BF16), tile],
         [row_scr],
     )
     if packed:
-        early_own, early_send, keep, send = conv_grad
-        late_own, late_send = run(
-            core_kernel, (me, keep, swap(send, "rows", 1)), [(late_shape, F32), (late_shape, BF16)]
+        keep, *sends = conv_grad
+        zs = owners // 2
+        late_cut, early_cut = (zs, 3 * chunk, chans), (2, zs, wide, chans)
+        late_own, sx, sy, sxy, early_own, early_send = run(
+            late_kernel,
+            (me, owner, keep, *[swap(send, "rows", 1) for send in sends], early_own, early_got),
+            [(late_cut, F32)] + [(late_cut, BF16)] * 3 + [(early_cut, F32), (early_cut, BF16)],
         )
-        (mine,) = run(
-            rows_kernel,
-            (me, early_own, swap(early_send, "rows", 2), late_own, swap(late_send, "rows", 2), done),
-            [((owners, deep, chans), BF16)],
+        gxy = swap_both(sxy, 2, 1)
+        late_got = swap(sx, "rows", 2), swap(sy, "dp", 1), gxy
+        part, *sends = run(
+            pack_kernel,
+            (me, owner, late_own, *late_got, early_own, swap(early_send, "dp", 1), done),
+            [((deep, chans), F32)] + [((deep, chans), BF16)] * 3,
+            [pltpu.VMEM((zs, deep, chans), F32)],
         )
-        got = lax.all_to_all(mine, "dp", 0, 0)
-        (part,) = run(dp_kernel, (me, got), [((deep, chans), BF16)])
+        part, send = run(
+            sum_kernel,
+            (me, part, *[swap(sends[k], "dp", 2 * k + 2) for k in (1, 2, 0)]),
+            [((deep, chans), F32), ((deep, chans), BF16)],
+        )
         down, conv, cb, ga, sh, db = run(
             functools.partial(last_kernel, chunk),
-            (me, *with_swaps(part, [part] * (ranks - 1))),
+            (me, *with_swaps(part, send)),
             [((9, wide, chans), F32), ((9, chunk, chans), F32)] + [((1, chunk), F32)] * 3 + [((1, wide), F32)],
             [pltpu.VMEM((4, deep, chans), F32)],
         )
     else:
         totals = lax.psum((down_grad[0], conv_grad[0], conv_grad[1], cbias[:1]), ("rows", "dp"))
-        owner = lax.axis_index("dp")
+        owner = owner[0]
         down = totals[0].reshape(outs, 9, chans).transpose(1, 0, 2)
         down = lax.dynamic_slice_in_dim(down, owner * wide, wide, 1)
         conv = totals[1].reshape(3, chans, 3, chans).transpose(2, 0, 1, 3).reshape(9, chans, chans)

time: 49.6 us -> 46.6 us (0.940)
  blocking collectives: 14 us -> 0 us
  starting transfers between devices: 16.6 us -> 23.8 us
  waiting for transfers between devices: 9.5 us -> 12.4 us
  Pallas kernels: 7.28 us -> 8.24 us
    all_to_all x1 -> x0, blocking collectives: 14 us -> none  [shards(): got = lax.all_to_all(mine, 'dp', 0, 0)]
    ppermute x15 -> x22, starting transfers between devices: 15.3 us -> 20.4 us  [swap(): lax.ppermute(x, axis, [(i, i ^ k) for i in range(lax.axis_size(axis))])]
    ppermute x0 -> x1, starting transfers between devices: none -> 2.06 us  [swap_both(): lax.ppermute(x, both, [(i, i ^ k) for i in range(lax.axis_size(both))])]
    ppermute x15 -> x22, waiting for transfers between devices: 9.49 us -> 11.2 us  [swap(): lax.ppermute(x, axis, [(i, i ^ k) for i in range(lax.axis_size(axis))])]
    ppermute x0 -> x1, waiting for transfers between devices: none -> 1.13 us  [swap_both(): lax.ppermute(x, both, [(i, i ^ k) for i in range(lax.axis_size(both))])]
    pallas_call x12 -> x14, Pallas kernels: 7.28 us -> 8.24 us  [run(): pl.pallas_call(kernel, in_specs=specs or [smem if a is me or a is owner e...]
  transfers between devices with their start and end apart: 17 -> 25, of which waited for: 8 -> 13; matrix products, arithmetic and copies ran while one was open for 0% -> 0% of each run, Pallas kernels for 9% -> 14%
where the time goes in v3:
time: 46.6 us; the launch traced here: 46.5 us
  starting transfers between devices  23.8 us (51%)
  waiting for transfers between devices  12.4 us (27%)
  Pallas kernels  8.24 us (18%)
  local copies, waits for them, and re-layouts  1.19 us (3%)
  between operations  0.84 us (2%)
    ppermute x22, starting transfers between devices, swap(): lax.ppermute(x, axis, [(i, i ^ k) for i in range(lax.axis_size(axis))])  20.4 us
    ppermute x22, waiting for transfers between devices, swap(): lax.ppermute(x, axis, [(i, i ^ k) for i in range(lax.axis_size(axis))])  11.2 us
    pallas_call x14, Pallas kernels, run(): pl.pallas_call(kernel, in_specs=specs or [smem if a is me or a is owner e...  8.24 us
    ppermute x1, starting transfers between devices, swap_both(): lax.ppermute(x, both, [(i, i ^ k) for i in range(lax.axis_size(both))])  2.06 us
    ppermute x2, starting transfers between devices, across(): lax.ppermute(x, 'rows', [p for i in range(1, n - 1, 2) for p in ((i, i +...  1.32 us
    unnamed x16, local copies, waits for them, and re-layouts  1.19 us
    ppermute x1, waiting for transfers between devices, swap_both(): lax.ppermute(x, both, [(i, i ^ k) for i in range(lax.axis_size(both))])  1.13 us
  transfers between devices with their start and end apart: 25, of which 13 were waited for; matrix products, arithmetic and copies ran while one was open for 0% of the time, Pallas kernels for 14%

profile of v3, /device:TPU:0, one launch (start us, length us, event | category | flops | bytes accessed | tf_op | source)
XLA Modules:
  0.0 46.5 jit_solution(4704459999320525585)
XLA Ops:
  0.6 0.5 %collective-permute-start = (bf16[2,512,128]{2,1,0:T(8,128)(2,1)}, bf16[2,512,128]{2,1,0:T(8,128)(2,1)S(1)}, u32[]{:S(2)}, u32[]{:S(2)}) collective-permute-start(bf16[2,512,128]{2,1,0:T(8,128)(2,1)} %bitcast.20), channel_id=1, source_target_pairs={{0,8},{8,0},{16,24},{24,16},{1,9},{9,1},{17,25},{25,17},{2,10},{10... | collective-permute-start | bytes 786440 | tf_op jit(solution)/shard_map/ppermute | solution.py:417
  1.2 0.7 %collective-permute-start.1 = (bf16[2,512,128]{2,1,0:T(8,128)(2,1)}, bf16[2,512,128]{2,1,0:T(8,128)(2,1)S(1)}, u32[]{:S(2)}, u32[]{:S(2)}) collective-permute-start(bf16[2,512,128]{2,1,0:T(8,128)(2,1)} %bitcast.21), channel_id=1, source_target_pairs={{8,16},{16,8},{9,17},{17,9},{10,18},{18,10},{11,19},{19,11},{12,20... | collective-permute-start | bytes 786440 | tf_op jit(solution)/shard_map/ppermute | solution.py:413
  1.9 0.0 copy-start.4
  1.9 0.0 copy-start.5
  1.9 1.0 %copy-done = bf16[3,3,128,256]{3,2,1,0:T(8,128)(2,1)S(1)} copy-done((bf16[3,3,128,256]{3,2,1,0:T(8,128)(2,1)S(1)}, bf16[3,3,128,256]{3,2,1,0:T(8,128)(2,1)}, u32[]{:S(2)}) %copy-start) | copy-done | bytes 589848
  2.9 0.1 copy-done.1
  3.0 0.1 copy-done.2
  3.0 0.0 copy-done.3
  3.1 0.9 %shard_map.144 = (bf16[3,3,128,128]{3,2,1,0:T(8,128)(2,1)S(1)}, bf16[3,3,128,256]{3,2,1,0:T(8,128)(2,1)S(1)}, bf16[256,256]{1,0:T(8,128)(2,1)S(1)}, f32[1,128]{1...) custom-call(f32[8,128]{1,0:T(8,128)S(1)} %shard_map.143.ahead, ...), custom_call_target="tpu_custom_call" | custom-call | flops 134217728 | bytes 1024 | tf_op jit(solution)/shard_map/pallas_call | solution.py:442
  4.0 3.9 %collective-permute-start.5 = (bf16[256,256]{1,0:T(8,128)(2,1)S(1)}, bf16[256,256]{1,0:T(8,128)(2,1)S(1)}, u32[]{:S(2)}, u32[]{:S(2)}) collective-permute-start(bf16[256,256]{1,0:T(8,128)(2,1)S(1)} %get-tuple-element.68.cot), channel_id=1, source_target_pairs={{0,8},{8,0},{16,24},{24,16},{1,9},{9,1},{17,25},{25,17},{2,10},{10... | collective-permute-start | bytes 393224 | tf_op jit(solution)/shard_map/ppermute | solution.py:417
  7.9 0.7 %collective-permute-start.6 = (bf16[256,256]{1,0:T(8,128)(2,1)S(1)}, bf16[256,256]{1,0:T(8,128)(2,1)S(1)}, u32[]{:S(2)}, u32[]{:S(2)}) collective-permute-start(bf16[256,256]{1,0:T(8,128)(2,1)S(1)} %get-tuple-element.68.cot), channel_id=1, source_target_pairs={{8,16},{16,8},{9,17},{17,9},{10,18},{18,10},{11,19},{19,11},{12,20... | collective-permute-start | bytes 393224 | tf_op jit(solution)/shard_map/ppermute | solution.py:413
  8.6 0.0 collective-permute-done.core
  8.6 0.0 collective-permute-done.1.chip
  8.6 1.1 %shard_map.145 = (bf16[4,2,256,128]{3,2,1,0:T(8,128)(2,1)S(1)}, f32[2,2,256,128]{3,2,1,0:T(8,128)S(1)}, f32[8,128]{1,0:T(8,128)S(1)}) custom-call(s32[1]{0:T(128)} %bitcast.me_ref, bf16[2,512,128]{2,1,0:T(8,128)(2,1)S(1)} %collective-permute-done.core, bf16[2,512,128]{2,1,0:T(8,128)(2,1)S(1)} %collective-permute-done.1.chip, ...), custom_call_target="tpu_custom_call" | custom-call | flops 134217728 | bytes 1024 | tf_op jit(solution)/shard_map/pallas_call | solution.py:442
  9.7 1.3 %collective-permute-start.2 = (f32[8,128]{1,0:T(8,128)S(1)}, f32[8,128]{1,0:T(8,128)S(1)}, u32[]{:S(2)}, u32[]{:S(2)}) collective-permute-start(f32[8,128]{1,0:T(8,128)S(1)} %get-tuple-element.65.refs_0_), channel_id=1, source_target_pairs={{0,8},{8,0},{16,24},{24,16},{1,9},{9,1},{17,25},{25,17},{2,10},{10... | collective-permute-start | bytes 12296 | tf_op jit(solution)/shard_map/ppermute | solution.py:417
  11.0 1.6 %collective-permute-start.3 = (f32[8,128]{1,0:T(8,128)S(1)}, f32[8,128]{1,0:T(8,128)S(1)}, u32[]{:S(2)}, u32[]{:S(2)}) collective-permute-start(f32[8,128]{1,0:T(8,128)S(1)} %get-tuple-element.65.refs_0_), channel_id=1, source_target_pairs={{0,16},{8,24},{16,0},{24,8},{1,17},{9,25},{17,1},{25,9},{2,18},{10... | collective-permute-start | bytes 12296 | tf_op jit(solution)/shard_map/ppermute | solution.py:417
  12.7 0.1 collective-permute-start.4
  12.8 0.0 collective-permute-done.5.cot_core
  12.8 0.0 collective-permute-done.6.cot_chip
  12.8 0.9 %shard_map.146 = (f32[2,2,256,128]{3,2,1,0:T(8,128)S(1)}, f32[4,2,256,128]{3,2,1,0:T(8,128)S(1)}) custom-call(s32[1]{0:T(128)} %bitcast.me_ref, bf16[2,512,128]{2,1,0:T(8,128)(2,1)S(1)} %collective-permute-done.core, bf16[2,512,128]{2,1,0:T(8,128)(2,1)S(1)} %collective-permute-done.1.chip, bf16[4,2,256,128]{3,2,1,0:T(8,128)(2,1)S(1)} %get-tuple-element.66.x.refs_4_.refs_5_, ...), custom_call_target="tpu_custom_call" | custom-call | flops 134217728 | bytes 1024 | tf_op jit(solution)/shard_map/pallas_call | solution.py:442
  13.7 1.0 %collective-permute-done.3.refs_2_ = f32[8,128]{1,0:T(8,128)S(1)} collective-permute-done((f32[8,128]{1,0:T(8,128)S(1)}, f32[8,128]{1,0:T(8,128)S(1)}, u32[]{:S(2)}, u32[]{:S(2)}) %collective-permute-start.3) | collective-permute-done | bytes 4128 | tf_op jit(solution)/shard_map/ppermute | solution.py:417
  14.7 1.1 %collective-permute-done.4.refs_3_ = f32[8,128]{1,0:T(8,128)S(1)} collective-permute-done((f32[8,128]{1,0:T(8,128)S(1)}, f32[8,128]{1,0:T(8,128)S(1)}, u32[]{:S(2)}, u32[]{:S(2)}) %collective-permute-start.4) | collective-permute-done | bytes 4128 | tf_op jit(solution)/shard_map/ppermute | solution.py:417
  15.7 0.4 shard_map.147
  16.1 0.6 %shard_map.148 = (bf16[256,384]{1,0:T(8,128)(2,1)S(1)}, f32[256,128]{1,0:T(8,128)S(1)}, f32[2,2,8,32,128]{4,3,2,1,0:T(8,128)S(1)}, bf16[2,2,8,32,128]{4,3,2,1,0:T(8,128)(2,1)S(1)}) custom-call(s32[1]{0:T(128)} %bitcast.me_ref, f32[8,128]{1,0:T(8,128)S(1)} %get-tuple-element.74.par.refs_4_, bf16[4,2,256,128]{3,2,1,0:T(8,128)(2,1)S(1)} %get-tuple-element.66.x.refs_4_.refs_5_, ...), custom_call_target="tpu_custom_call" | custom-call | flops 134217728 | bytes 1024 | tf_op jit(solution)/shard_map/pallas_call | solution.py:442
  16.7 0.3 collective-permute-start.7
  17.0 0.5 %collective-permute-start.10 = (f32[8,128]{1,0:T(8,128)S(1)}, f32[8,128]{1,0:T(8,128)S(1)}, u32[]{:S(2)}, u32[]{:S(2)}) collective-permute-start(f32[8,128]{1,0:T(8,128)S(1)} %get-tuple-element.83.refs_0_), channel_id=1, source_target_pairs={{0,24},{8,16},{16,8},{24,0},{1,25},{9,17},{17,9},{25,1},{2,26},{10... | collective-permute-start | bytes 12296 | tf_op jit(solution)/shard_map/ppermute | solution.py:417
  17.5 0.1 collective-permute-start.8
  17.6 1.5 %collective-permute-start.9 = (f32[8,128]{1,0:T(8,128)S(1)}, f32[8,128]{1,0:T(8,128)S(1)}, u32[]{:S(2)}, u32[]{:S(2)}) collective-permute-start(f32[8,128]{1,0:T(8,128)S(1)} %get-tuple-element.83.refs_0_), channel_id=1, source_target_pairs={{0,16},{8,24},{16,0},{24,8},{1,17},{9,25},{17,1},{25,9},{2,18},{10... | collective-permute-start | bytes 12296 | tf_op jit(solution)/shard_map/ppermute | solution.py:417
  19.1 0.0 collective-permute-done.7.got
  19.1 0.1 shard_map.149
  19.2 0.6 %collective-permute-start.14 = (bf16[2,8,32,128]{3,2,1,0:T(8,128)(2,1)S(1)}, bf16[2,8,32,128]{3,2,1,0:T(8,128)(2,1)S(1)}, u32[]{:S(2)}, u32[]{:S(2)}) collective-permute-start(bf16[2,8,32,128]{3,2,1,0:T(8,128)(2,1)S(1)} %get-tuple-element.96), channel_id=1, source_target_pairs={{0,16},{8,24},{16,0},{24,8},{1,17},{9,25},{17,1},{25,9},{2,18},{10... | collective-permute-start | bytes 393224 | tf_op jit(solution)/shard_map/ppermute | solution.py:417
  19.8 1.0 %shard_map.150 = (bf16[256,256]{1,0:T(8,128)(2,1)}, f32[8,128]{1,0:T(8,128)S(1)}) custom-call(f32[8,128]{1,0:T(8,128)S(1)} %get-tuple-element.79.ahead, bf16[256,384]{1,0:T(8,128)(2,1)S(1)} %get-tuple-element.80.mix_top, bf16[2,256,384]{2,1,0:T(8,128)(2,1)S(1)} %get-tuple-element.76.mix, bf16[3,3,128,256]{3,2,1,0:T(8,128)(2,1)S(1)} %get-tuple-element.69.dw, ...), custom_call_target="tpu_custom_call" | custom-call | flops 134217728 | bytes 1024 | tf_op jit(solution)/shard_map/pallas_call | solution.py:442
  20.8 0.0 collective-permute-done.10.refs_3_
  20.8 0.4 collective-permute-done.9.refs_2_
  21.2 1.0 %shard_map.151 = (f32[8,128]{1,0:T(8,128)S(1)}, bf16[2,2,256,128]{3,2,1,0:T(8,128)(2,1)S(1)}, f32[2,8,48,128]{3,2,1,0:T(8,128)S(1)}, bf16[2,8,16,128]{3,2,1,0:T(...) custom-call(s32[1]{0:T(128)} %bitcast.me_ref, ...), custom_call_target="tpu_custom_call" | custom-call | flops 4294967296 | bytes 1024 | tf_op jit(solution)/shard_map/pallas_call | solution.py:442
  22.2 0.1 collective-permute-start.11
  22.3 0.5 %collective-permute-start.12 = (bf16[2,8,16,128]{3,2,1,0:T(8,128)(2,1)S(1)}, bf16[2,8,16,128]{3,2,1,0:T(8,128)(2,1)S(1)}, u32[]{:S(2)}, u32[]{:S(2)}) collective-permute-start(bf16[2,8,16,128]{3,2,1,0:T(8,128)(2,1)S(1)} %get-tuple-element.93), channel_id=1, source_target_pairs={{0,8},{8,0},{16,24},{24,16},{1,9},{9,1},{17,25},{25,17},{2,10},{10... | collective-permute-start | bytes 196616 | tf_op jit(solution)/shard_map/ppermute | solution.py:417
  22.8 0.1 collective-permute-start.13
  22.9 0.7 %collective-permute-done.11.got0 = bf16[2,8,16,128]{3,2,1,0:T(8,128)(2,1)S(1)} collective-permute-done((bf16[2,8,16,128]{3,2,1,0:T(8,128)(2,1)S(1)}, bf16[2,8,16,128]{3,2,1,0:T(8,128)(2,1)S(1)}, u32[]{:S(2)}, u32[]{:S(2)}) %collective-permute-start.11) | collective-permute-done | bytes 65568 | tf_op jit(solution)/shard_map/ppermute | solution.py:417
  23.6 0.2 collective-permute-done.12.got1
  23.7 0.4 collective-permute-done.13.got2
  24.1 0.6 %collective-permute-done.14.e_got = bf16[2,8,32,128]{3,2,1,0:T(8,128)(2,1)S(1)} collective-permute-done((bf16[2,8,32,128]{3,2,1,0:T(8,128)(2,1)S(1)}, bf16[2,8,32,128]{3,2,1,0:T(8,128)(2,1)S(1)}, u32[]{:S(2)}, u32[]{:S(2)}) %collective-permute-start.14) | collective-permute-done | bytes 131104 | tf_op jit(solution)/shard_map/ppermute | solution.py:417
  24.7 0.1 shard_map.153
  24.8 1.6 %collective-permute-start.18 = (bf16[2,4,32,128]{3,2,1,0:T(8,128)(2,1)S(1)}, bf16[2,4,32,128]{3,2,1,0:T(8,128)(2,1)S(1)}, u32[]{:S(2)}, u32[]{:S(2)}) collective-permute-start(bf16[2,4,32,128]{3,2,1,0:T(8,128)(2,1)S(1)} %get-tuple-element.102), channel_id=1, source_target_pairs={{0,1},{1,0},{2,3},{3,2},{4,5},{5,4},{6,7},{7,6},{8,9},{9,8},{10,11... | collective-permute-start | bytes 196616 | tf_op jit(solution)/shard_map/ppermute | solution.py:417
  26.4 1.0 %collective-permute-start.15 = (bf16[4,48,128]{2,1,0:T(8,128)(2,1)S(1)}, bf16[4,48,128]{2,1,0:T(8,128)(2,1)S(1)}, u32[]{:S(2)}, u32[]{:S(2)}) collective-permute-start(bf16[4,48,128]{2,1,0:T(8,128)(2,1)S(1)} %get-tuple-element.98), channel_id=1, source_target_pairs={{0,16},{8,24},{16,0},{24,8},{1,17},{9,25},{17,1},{25,9},{2,18},{10... | collective-permute-start | bytes 147464 | tf_op jit(solution)/shard_map/ppermute | solution.py:417
  27.4 0.4 collective-permute-start.16
  27.8 2.1 %collective-permute-start.17 = (bf16[4,48,128]{2,1,0:T(8,128)(2,1)S(1)}, bf16[4,48,128]{2,1,0:T(8,128)(2,1)S(1)}, u32[]{:S(2)}, u32[]{:S(2)}) collective-permute-start(bf16[4,48,128]{2,1,0:T(8,128)(2,1)S(1)} %get-tuple-element.100), channel_id=1, source_target_pairs={{0,17},{1,16},{2,19},{3,18},{4,21},{5,20},{6,23},{7,22},{8,25},{9,... | collective-permute-start | bytes 147464 | tf_op jit(solution)/shard_map/ppermute | solution.py:423
  29.8 1.5 %shard_map.152 = (bf16[2,512,128]{2,1,0:T(8,128)(2,1)}, f32[8,128]{1,0:T(8,128)S(1)}) custom-call(s32[1]{0:T(128)} %bitcast.me_ref, f32[8,128]{1,0:T(8,128)S(1)} %get-tuple-element.74.par.refs_4_, f32[2,2,256,128]{3,2,1,0:T(8,128)S(1)} %get-tuple-element.75.hid, f32[4,2,256,128]{3,2,1,0:T(8,128)S(1)} %get-tuple-element.71.refs_6_.gm, ...), custom_call_target="tpu_custom_call" | custom-call | flops 134217728 | bytes 1024 | tf_op jit(solution)/shard_map/pallas_call | solution.py:442
  31.3 0.0 collective-permute-done.15.gx
  31.3 0.3 collective-permute-done.16.gy
  31.6 1.1 %collective-permute-done.17.gxy = bf16[4,48,128]{2,1,0:T(8,128)(2,1)S(1)} collective-permute-done((bf16[4,48,128]{2,1,0:T(8,128)(2,1)S(1)}, bf16[4,48,128]{2,1,0:T(8,128)(2,1)S(1)}, u32[]{:S(2)}, u32[]{:S(2)}) %collective-permute-start.17) | collective-permute-done | bytes 49184 | tf_op jit(solution)/shard_map/ppermute | solution.py:423
  32.8 0.1 shard_map.154
  32.8 2.7 %collective-permute-start.19 = (bf16[112,128]{1,0:T(8,128)(2,1)S(1)}, bf16[112,128]{1,0:T(8,128)(2,1)S(1)}, u32[]{:S(2)}, u32[]{:S(2)}) collective-permute-start(bf16[112,128]{1,0:T(8,128)(2,1)S(1)} %get-tuple-element.105), channel_id=1, source_target_pairs={{0,4},{1,5},{2,6},{3,7},{4,0},{5,1},{6,2},{7,3},{8,12},{9,13},{10,... | collective-permute-start | bytes 86024 | tf_op jit(solution)/shard_map/ppermute | solution.py:417
  35.6 1.4 %collective-permute-start.20 = (bf16[112,128]{1,0:T(8,128)(2,1)S(1)}, bf16[112,128]{1,0:T(8,128)(2,1)S(1)}, u32[]{:S(2)}, u32[]{:S(2)}) collective-permute-start(bf16[112,128]{1,0:T(8,128)(2,1)S(1)} %get-tuple-element.106), channel_id=1, source_target_pairs={{0,6},{1,7},{2,4},{3,5},{4,2},{5,3},{6,0},{7,1},{8,14},{9,15},{10,... | collective-permute-start | bytes 86024 | tf_op jit(solution)/shard_map/ppermute | solution.py:417
  36.9 0.2 collective-permute-start.21
  37.2 0.5 %collective-permute-done.19.g1 = bf16[112,128]{1,0:T(8,128)(2,1)S(1)} collective-permute-done((bf16[112,128]{1,0:T(8,128)(2,1)S(1)}, bf16[112,128]{1,0:T(8,128)(2,1)S(1)}, u32[]{:S(2)}, u32[]{:S(2)}) %collective-permute-start.19) | collective-permute-done | bytes 28704 | tf_op jit(solution)/shard_map/ppermute | solution.py:417
  37.7 3.6 %collective-permute-done.20.g2 = bf16[112,128]{1,0:T(8,128)(2,1)S(1)} collective-permute-done((bf16[112,128]{1,0:T(8,128)(2,1)S(1)}, bf16[112,128]{1,0:T(8,128)(2,1)S(1)}, u32[]{:S(2)}, u32[]{:S(2)}) %collective-permute-start.20) | collective-permute-done | bytes 28704 | tf_op jit(solution)/shard_map/ppermute | solution.py:417
  41.2 0.0 collective-permute-done.21.g3
  41.3 0.1 collective-permute-start.22
  41.3 1.1 %collective-permute-start.23 = (bf16[112,128]{1,0:T(8,128)(2,1)S(1)}, bf16[112,128]{1,0:T(8,128)(2,1)S(1)}, u32[]{:S(2)}, u32[]{:S(2)}) collective-permute-start(bf16[112,128]{1,0:T(8,128)(2,1)S(1)} %get-tuple-element.109), channel_id=1, source_target_pairs={{0,16},{8,24},{16,0},{24,8},{1,17},{9,25},{17,1},{25,9},{2,18},{10... | collective-permute-start | bytes 86024 | tf_op jit(solution)/shard_map/ppermute | solution.py:417
  42.4 0.8 %collective-permute-start.24 = (bf16[112,128]{1,0:T(8,128)(2,1)S(1)}, bf16[112,128]{1,0:T(8,128)(2,1)S(1)}, u32[]{:S(2)}, u32[]{:S(2)}) collective-permute-start(bf16[112,128]{1,0:T(8,128)(2,1)S(1)} %get-tuple-element.109), channel_id=1, source_target_pairs={{0,24},{8,16},{16,8},{24,0},{1,25},{9,17},{17,9},{25,1},{2,26},{10... | collective-permute-start | bytes 86024 | tf_op jit(solution)/shard_map/ppermute | solution.py:417
  43.2 2.1 %collective-permute-done.23.q2 = bf16[112,128]{1,0:T(8,128)(2,1)S(1)} collective-permute-done((bf16[112,128]{1,0:T(8,128)(2,1)S(1)}, bf16[112,128]{1,0:T(8,128)(2,1)S(1)}, u32[]{:S(2)}, u32[]{:S(2)}) %collective-permute-start.23) | collective-permute-done | bytes 28704 | tf_op jit(solution)/shard_map/ppermute | solution.py:417
  45.3 0.4 collective-permute-done.24.q3
  45.7 0.7 %shard_map.156 = (f32[9,32,128]{2,1,0:T(8,128)}, f32[9,16,128]{2,1,0:T(8,128)}, f32[1,16]{1,0:T(1,128)}, f32[1,16]{1,0:T(1,128)}, f32[1,16]{1,0:T(1,128)}, /*index=5*/f32[1,32]{1,0:T(1,128)}) custom-call(s32[1]{0:T(128)} %bitcast.me_ref, f32[112,128]{1,0:T(8,128)S(1)} %get-tuple-element.108.q0, bf16[112,128]{1,0:T(8,128)(2,1)S(1)} %collective-permute-done.22.q1, ...), custom_call_target="tpu_custom_call" | custom-call | flops 134217728 | bytes 1024 | tf_op jit(solution)/shard_map/pallas_call | solution.py:442
  (16 shorter events, 0.1 us)
Async XLA Ops:
  0.6 8.0 %collective-permute-start = (bf16[2,512,128]{2,1,0:T(8,128)(2,1)}, bf16[2,512,128]{2,1,0:T(8,128)(2,1)S(1)}, u32[]{:S(2)}, u32[]{:S(2)}) collective-permute-start(bf16[2,512,128]{2,1,0:T(8,128)(2,1)} %bitcast.20), channel_id=1, source_target_pairs={{0,8},{8,0},{16,24},{24,16},{1,9},{9,1},{17,25},{25,17},{2,10},{10... | collective-permute-start | bytes 786440 | tf_op jit(solution)/shard_map/ppermute | solution.py:417
  1.2 7.5 %collective-permute-start.1 = (bf16[2,512,128]{2,1,0:T(8,128)(2,1)}, bf16[2,512,128]{2,1,0:T(8,128)(2,1)S(1)}, u32[]{:S(2)}, u32[]{:S(2)}) collective-permute-start(bf16[2,512,128]{2,1,0:T(8,128)(2,1)} %bitcast.21), channel_id=1, source_target_pairs={{8,16},{16,8},{9,17},{17,9},{10,18},{18,10},{11,19},{19,11},{12,20... | collective-permute-start | bytes 786440 | tf_op jit(solution)/shard_map/ppermute | solution.py:413
  1.8 1.1 %copy-start = (bf16[3,3,128,256]{3,2,1,0:T(8,128)(2,1)S(1)}, bf16[3,3,128,256]{3,2,1,0:T(8,128)(2,1)}, u32[]{:S(2)}) copy-start(bf16[3,3,128,256]{3,2,1,0:T(8,128)(2,1)} %dw.1) | copy-start | bytes 1769476
  1.8 1.1 %copy-start.1 = (bf16[3,3,128,128]{3,2,1,0:T(8,128)(2,1)S(1)}, bf16[3,3,128,128]{3,2,1,0:T(8,128)(2,1)}, u32[]{:S(2)}) copy-start(bf16[3,3,128,128]{3,2,1,0:T(8,128)(2,1)} %w.1) | copy-start | bytes 884740
  1.9 1.2 %copy-start.2 = (bf16[1,2,512,128]{3,2,1,0:T(8,128)(2,1)S(1)}, bf16[1,2,512,128]{3,2,1,0:T(8,128)(2,1)}, u32[]{:S(2)}) copy-start(bf16[1,2,512,128]{3,2,1,0:T(8,128)(2,1)} %param.8) | copy-start | bytes 786436
  1.9 1.2 %copy-start.3 = (bf16[1,1,256,256]{3,2,1,0:T(8,128)(2,1)S(1)}, bf16[1,1,256,256]{3,2,1,0:T(8,128)(2,1)}, u32[]{:S(2)}) copy-start(bf16[1,1,256,256]{3,2,1,0:T(8,128)(2,1)} %param.15) | copy-start | bytes 393220
  1.9 1.2 %copy-start.6 = (f32[128]{0:T(128)S(1)}, f32[128]{0:T(128)}, u32[]{:S(2)}) copy-start(f32[128]{0:T(128)} %param.11) | copy-start | bytes 1540
  1.9 1.2 %copy-start.7 = (f32[128]{0:T(128)S(1)}, f32[128]{0:T(128)}, u32[]{:S(2)}) copy-start(f32[128]{0:T(128)} %param.12) | copy-start | bytes 1540
  1.9 1.2 %copy-start.4 = (f32[256]{0:T(256)S(1)}, f32[256]{0:T(256)}, u32[]{:S(2)}) copy-start(f32[256]{0:T(256)} %param.14) | copy-start | bytes 3076
  1.9 1.2 %copy-start.5 = (f32[128]{0:T(128)S(1)}, f32[128]{0:T(128)}, u32[]{:S(2)}) copy-start(f32[128]{0:T(128)} %param.10) | copy-start | bytes 1540
  4.0 8.8 %collective-permute-start.5 = (bf16[256,256]{1,0:T(8,128)(2,1)S(1)}, bf16[256,256]{1,0:T(8,128)(2,1)S(1)}, u32[]{:S(2)}, u32[]{:S(2)}) collective-permute-start(bf16[256,256]{1,0:T(8,128)(2,1)S(1)} %get-tuple-element.68.cot), channel_id=1, source_target_pairs={{0,8},{8,0},{16,24},{24,16},{1,9},{9,1},{17,25},{25,17},{2,10},{10... | collective-permute-start | bytes 393224 | tf_op jit(solution)/shard_map/ppermute | solution.py:417
  7.9 4.9 %collective-permute-start.6 = (bf16[256,256]{1,0:T(8,128)(2,1)S(1)}, bf16[256,256]{1,0:T(8,128)(2,1)S(1)}, u32[]{:S(2)}, u32[]{:S(2)}) collective-permute-start(bf16[256,256]{1,0:T(8,128)(2,1)S(1)} %get-tuple-element.68.cot), channel_id=1, source_target_pairs={{8,16},{16,8},{9,17},{17,9},{10,18},{18,10},{11,19},{19,11},{12,20... | collective-permute-start | bytes 393224 | tf_op jit(solution)/shard_map/ppermute | solution.py:413
  9.7 4.0 %collective-permute-start.2 = (f32[8,128]{1,0:T(8,128)S(1)}, f32[8,128]{1,0:T(8,128)S(1)}, u32[]{:S(2)}, u32[]{:S(2)}) collective-permute-start(f32[8,128]{1,0:T(8,128)S(1)} %get-tuple-element.65.refs_0_), channel_id=1, source_target_pairs={{0,8},{8,0},{16,24},{24,16},{1,9},{9,1},{17,25},{25,17},{2,10},{10... | collective-permute-start | bytes 12296 | tf_op jit(solution)/shard_map/ppermute | solution.py:417
  11.0 3.6 %collective-permute-start.3 = (f32[8,128]{1,0:T(8,128)S(1)}, f32[8,128]{1,0:T(8,128)S(1)}, u32[]{:S(2)}, u32[]{:S(2)}) collective-permute-start(f32[8,128]{1,0:T(8,128)S(1)} %get-tuple-element.65.refs_0_), channel_id=1, source_target_pairs={{0,16},{8,24},{16,0},{24,8},{1,17},{9,25},{17,1},{25,9},{2,18},{10... | collective-permute-start | bytes 12296 | tf_op jit(solution)/shard_map/ppermute | solution.py:417
  12.7 3.0 %collective-permute-start.4 = (f32[8,128]{1,0:T(8,128)S(1)}, f32[8,128]{1,0:T(8,128)S(1)}, u32[]{:S(2)}, u32[]{:S(2)}) collective-permute-start(f32[8,128]{1,0:T(8,128)S(1)} %get-tuple-element.65.refs_0_), channel_id=1, source_target_pairs={{0,24},{8,16},{16,8},{24,0},{1,25},{9,17},{17,9},{25,1},{2,26},{10... | collective-permute-start | bytes 12296 | tf_op jit(solution)/shard_map/ppermute | solution.py:417
  16.7 2.4 %collective-permute-start.7 = (bf16[2,2,8,32,128]{4,3,2,1,0:T(8,128)(2,1)S(1)}, bf16[2,2,8,32,128]{4,3,2,1,0:T(8,128)(2,1)S(1)}, u32[]{:S(2)}, u32[]{:S(2)}) collective-permute-start(bf16[2,2,8,32,128]{4,3,2,1,0:T(8,128)(2,1)S(1)} %get-tuple-element.78), channel_id=1, source_target_pairs={{0,8},{8,0},{16,24},{24,16},{1,9},{9,1},{17,25},{25,17},{2,10},{10... | collective-permute-start | bytes 786440 | tf_op jit(solution)/shard_map/ppermute | solution.py:417
  17.0 3.8 %collective-permute-start.10 = (f32[8,128]{1,0:T(8,128)S(1)}, f32[8,128]{1,0:T(8,128)S(1)}, u32[]{:S(2)}, u32[]{:S(2)}) collective-permute-start(f32[8,128]{1,0:T(8,128)S(1)} %get-tuple-element.83.refs_0_), channel_id=1, source_target_pairs={{0,24},{8,16},{16,8},{24,0},{1,25},{9,17},{17,9},{25,1},{2,26},{10... | collective-permute-start | bytes 12296 | tf_op jit(solution)/shard_map/ppermute | solution.py:417
  17.5 3.3 %collective-permute-start.8 = (f32[8,128]{1,0:T(8,128)S(1)}, f32[8,128]{1,0:T(8,128)S(1)}, u32[]{:S(2)}, u32[]{:S(2)}) collective-permute-start(f32[8,128]{1,0:T(8,128)S(1)} %get-tuple-element.83.refs_0_), channel_id=1, source_target_pairs={{0,8},{8,0},{16,24},{24,16},{1,9},{9,1},{17,25},{25,17},{2,10},{10... | collective-permute-start | bytes 12296 | tf_op jit(solution)/shard_map/ppermute | solution.py:417
  17.6 3.6 %collective-permute-start.9 = (f32[8,128]{1,0:T(8,128)S(1)}, f32[8,128]{1,0:T(8,128)S(1)}, u32[]{:S(2)}, u32[]{:S(2)}) collective-permute-start(f32[8,128]{1,0:T(8,128)S(1)} %get-tuple-element.83.refs_0_), channel_id=1, source_target_pairs={{0,16},{8,24},{16,0},{24,8},{1,17},{9,25},{17,1},{25,9},{2,18},{10... | collective-permute-start | bytes 12296 | tf_op jit(solution)/shard_map/ppermute | solution.py:417
  19.2 5.5 %collective-permute-start.14 = (bf16[2,8,32,128]{3,2,1,0:T(8,128)(2,1)S(1)}, bf16[2,8,32,128]{3,2,1,0:T(8,128)(2,1)S(1)}, u32[]{:S(2)}, u32[]{:S(2)}) collective-permute-start(bf16[2,8,32,128]{3,2,1,0:T(8,128)(2,1)S(1)} %get-tuple-element.96), channel_id=1, source_target_pairs={{0,16},{8,24},{16,0},{24,8},{1,17},{9,25},{17,1},{25,9},{2,18},{10... | collective-permute-start | bytes 393224 | tf_op jit(solution)/shard_map/ppermute | solution.py:417
  22.2 1.3 %collective-permute-start.11 = (bf16[2,8,16,128]{3,2,1,0:T(8,128)(2,1)S(1)}, bf16[2,8,16,128]{3,2,1,0:T(8,128)(2,1)S(1)}, u32[]{:S(2)}, u32[]{:S(2)}) collective-permute-start(bf16[2,8,16,128]{3,2,1,0:T(8,128)(2,1)S(1)} %get-tuple-element.92), channel_id=1, source_target_pairs={{0,8},{8,0},{16,24},{24,16},{1,9},{9,1},{17,25},{25,17},{2,10},{10... | collective-permute-start | bytes 196616 | tf_op jit(solution)/shard_map/ppermute | solution.py:417
  22.3 1.4 %collective-permute-start.12 = (bf16[2,8,16,128]{3,2,1,0:T(8,128)(2,1)S(1)}, bf16[2,8,16,128]{3,2,1,0:T(8,128)(2,1)S(1)}, u32[]{:S(2)}, u32[]{:S(2)}) collective-permute-start(bf16[2,8,16,128]{3,2,1,0:T(8,128)(2,1)S(1)} %get-tuple-element.93), channel_id=1, source_target_pairs={{0,8},{8,0},{16,24},{24,16},{1,9},{9,1},{17,25},{25,17},{2,10},{10... | collective-permute-start | bytes 196616 | tf_op jit(solution)/shard_map/ppermute | solution.py:417
  22.8 1.3 %collective-permute-start.13 = (bf16[2,8,16,128]{3,2,1,0:T(8,128)(2,1)S(1)}, bf16[2,8,16,128]{3,2,1,0:T(8,128)(2,1)S(1)}, u32[]{:S(2)}, u32[]{:S(2)}) collective-permute-start(bf16[2,8,16,128]{3,2,1,0:T(8,128)(2,1)S(1)} %get-tuple-element.94), channel_id=1, source_target_pairs={{0,8},{8,0},{16,24},{24,16},{1,9},{9,1},{17,25},{25,17},{2,10},{10... | collective-permute-start | bytes 196616 | tf_op jit(solution)/shard_map/ppermute | solution.py:417
  24.8 8.0 %collective-permute-start.18 = (bf16[2,4,32,128]{3,2,1,0:T(8,128)(2,1)S(1)}, bf16[2,4,32,128]{3,2,1,0:T(8,128)(2,1)S(1)}, u32[]{:S(2)}, u32[]{:S(2)}) collective-permute-start(bf16[2,4,32,128]{3,2,1,0:T(8,128)(2,1)S(1)} %get-tuple-element.102), channel_id=1, source_target_pairs={{0,1},{1,0},{2,3},{3,2},{4,5},{5,4},{6,7},{7,6},{8,9},{9,8},{10,11... | collective-permute-start | bytes 196616 | tf_op jit(solution)/shard_map/ppermute | solution.py:417
  26.4 4.9 %collective-permute-start.15 = (bf16[4,48,128]{2,1,0:T(8,128)(2,1)S(1)}, bf16[4,48,128]{2,1,0:T(8,128)(2,1)S(1)}, u32[]{:S(2)}, u32[]{:S(2)}) collective-permute-start(bf16[4,48,128]{2,1,0:T(8,128)(2,1)S(1)} %get-tuple-element.98), channel_id=1, source_target_pairs={{0,16},{8,24},{16,0},{24,8},{1,17},{9,25},{17,1},{25,9},{2,18},{10... | collective-permute-start | bytes 147464 | tf_op jit(solution)/shard_map/ppermute | solution.py:417
  27.4 4.3 %collective-permute-start.16 = (bf16[4,48,128]{2,1,0:T(8,128)(2,1)S(1)}, bf16[4,48,128]{2,1,0:T(8,128)(2,1)S(1)}, u32[]{:S(2)}, u32[]{:S(2)}) collective-permute-start(bf16[4,48,128]{2,1,0:T(8,128)(2,1)S(1)} %get-tuple-element.99), channel_id=1, source_target_pairs={{0,1},{1,0},{2,3},{3,2},{4,5},{5,4},{6,7},{7,6},{8,9},{9,8},{10,11... | collective-permute-start | bytes 147464 | tf_op jit(solution)/shard_map/ppermute | solution.py:417
  27.8 5.0 %collective-permute-start.17 = (bf16[4,48,128]{2,1,0:T(8,128)(2,1)S(1)}, bf16[4,48,128]{2,1,0:T(8,128)(2,1)S(1)}, u32[]{:S(2)}, u32[]{:S(2)}) collective-permute-start(bf16[4,48,128]{2,1,0:T(8,128)(2,1)S(1)} %get-tuple-element.100), channel_id=1, source_target_pairs={{0,17},{1,16},{2,19},{3,18},{4,21},{5,20},{6,23},{7,22},{8,25},{9,... | collective-permute-start | bytes 147464 | tf_op jit(solution)/shard_map/ppermute | solution.py:423
  32.8 4.8 %collective-permute-start.19 = (bf16[112,128]{1,0:T(8,128)(2,1)S(1)}, bf16[112,128]{1,0:T(8,128)(2,1)S(1)}, u32[]{:S(2)}, u32[]{:S(2)}) collective-permute-start(bf16[112,128]{1,0:T(8,128)(2,1)S(1)} %get-tuple-element.105), channel_id=1, source_target_pairs={{0,4},{1,5},{2,6},{3,7},{4,0},{5,1},{6,2},{7,3},{8,12},{9,13},{10,... | collective-permute-start | bytes 86024 | tf_op jit(solution)/shard_map/ppermute | solution.py:417
  35.6 5.7 %collective-permute-start.20 = (bf16[112,128]{1,0:T(8,128)(2,1)S(1)}, bf16[112,128]{1,0:T(8,128)(2,1)S(1)}, u32[]{:S(2)}, u32[]{:S(2)}) collective-permute-start(bf16[112,128]{1,0:T(8,128)(2,1)S(1)} %get-tuple-element.106), channel_id=1, source_target_pairs={{0,6},{1,7},{2,4},{3,5},{4,2},{5,3},{6,0},{7,1},{8,14},{9,15},{10,... | collective-permute-start | bytes 86024 | tf_op jit(solution)/shard_map/ppermute | solution.py:417
  36.9 4.3 %collective-permute-start.21 = (bf16[112,128]{1,0:T(8,128)(2,1)S(1)}, bf16[112,128]{1,0:T(8,128)(2,1)S(1)}, u32[]{:S(2)}, u32[]{:S(2)}) collective-permute-start(bf16[112,128]{1,0:T(8,128)(2,1)S(1)} %get-tuple-element.107), channel_id=1, source_target_pairs={{0,2},{1,3},{2,0},{3,1},{4,6},{5,7},{6,4},{7,5},{8,10},{9,11},{10,... | collective-permute-start | bytes 86024 | tf_op jit(solution)/shard_map/ppermute | solution.py:417
  41.3 1.9 %collective-permute-start.22 = (bf16[112,128]{1,0:T(8,128)(2,1)S(1)}, bf16[112,128]{1,0:T(8,128)(2,1)S(1)}, u32[]{:S(2)}, u32[]{:S(2)}) collective-permute-start(bf16[112,128]{1,0:T(8,128)(2,1)S(1)} %get-tuple-element.109), channel_id=1, source_target_pairs={{0,8},{8,0},{16,24},{24,16},{1,9},{9,1},{17,25},{25,17},{2,10},{10... | collective-permute-start | bytes 86024 | tf_op jit(solution)/shard_map/ppermute | solution.py:417
  41.3 3.9 %collective-permute-start.23 = (bf16[112,128]{1,0:T(8,128)(2,1)S(1)}, bf16[112,128]{1,0:T(8,128)(2,1)S(1)}, u32[]{:S(2)}, u32[]{:S(2)}) collective-permute-start(bf16[112,128]{1,0:T(8,128)(2,1)S(1)} %get-tuple-element.109), channel_id=1, source_target_pairs={{0,16},{8,24},{16,0},{24,8},{1,17},{9,25},{17,1},{25,9},{2,18},{10... | collective-permute-start | bytes 86024 | tf_op jit(solution)/shard_map/ppermute | solution.py:417
  42.4 3.3 %collective-permute-start.24 = (bf16[112,128]{1,0:T(8,128)(2,1)S(1)}, bf16[112,128]{1,0:T(8,128)(2,1)S(1)}, u32[]{:S(2)}, u32[]{:S(2)}) collective-permute-start(bf16[112,128]{1,0:T(8,128)(2,1)S(1)} %get-tuple-element.109), channel_id=1, source_target_pairs={{0,24},{8,16},{16,8},{24,0},{1,25},{9,17},{17,9},{25,1},{2,26},{10... | collective-permute-start | bytes 86024 | tf_op jit(solution)/shard_map/ppermute | solution.py:417

commit v4 on v3

--- a/solution.py
+++ b/solution.py
@@ -211,24 +211,24 @@
     if not packed:
         rest[0][...] = grad
         return
-    last_out, keep_out, send_out, dscr = rest
+    last_out, keep_out, send_out = rest
     outs_chunk = keep_out.shape[3]
-    for q in range(4):
-        for t in range(2):
-            tap = 2 * q + t
-            dscr[q, t] = grad[:, tap * chans : (tap + 1) * chans].reshape(-1, outs_chunk, chans)
-    last_out[...] = grad[:, 8 * chans :]
-    halve(me_ref[0] & 1, dscr, keep_out, send_out)
-
-
-def halve(core, quarters, keep_out, *send_outs):
-    n = len(send_outs)
+    taps = [grad[:, t * chans : (t + 1) * chans] for t in range(9)]
+    last_out[...] = taps[8]
+    for t in range(2):
+        quarters = [taps[2 * q + t].reshape(-1, outs_chunk, chans) for q in range(4)]
+        halve(me_ref[0] & 1, quarters, keep_out, [send_out], (t,))
+
+
+def halve(core, quarters, keep_out, send_outs, at=()):
+    first = core == 0
     for i in range(2):
-        keep_out[i] = quarters[2 * i + core]
-        other = quarters[2 * i + 1 - core].astype(BF16)
-        size = other.shape[-2] // n
+        one, two = quarters[2 * i], quarters[2 * i + 1]
+        keep_out[(i, *at)] = jnp.where(first, one, two)
+        other = jnp.where(first, two, one).astype(BF16)
+        size = other.shape[0] // len(send_outs)
         for j, ref in enumerate(send_outs):
-            ref[i] = other[..., j * size : (j + 1) * size, :]
+            ref[(i, *at)] = other[j * size : (j + 1) * size]
 
 
 def hi_lo(full):
@@ -240,7 +240,7 @@
     sum_refs = refs[:ranks]
     par, x, hid, gp, gain, _, *refs = refs[ranks:]
     if packed:
-        dlast, cbias, par_out, g_out, keep_out, *send_outs, lscr = refs
+        dlast, cbias, par_out, g_out, keep_out, *send_outs = refs
     else:
         par_out, g_out, grad_out, small_out = refs
     half = x.shape[2]
@@ -272,15 +272,11 @@
         grad_out[...] = grad
         small_out[...] = full
         return
-    owners = lscr.shape[1]
+    owners = keep_out.shape[1]
     chunk = chans // owners
-    for kh in range(3):
-        for kw in range(3):
-            piece = grad[kw * chans : (kw + 1) * chans, kh * chans : (kh + 1) * chans]
-            lscr[kh, :, kw * chunk : (kw + 1) * chunk, :] = piece.reshape(-1, chunk, chans)
-    lscr[3, :, 0 : 2 * chunk, :] = dlast[...].reshape(owners, 2 * chunk, chans)
     wide = [cbias[0:1, i * chans : (i + 1) * chans] for i in range(cbias.shape[1] // chans)]
     row_id = lax.broadcasted_iota(jnp.int32, full.shape, 0)
+    small = []
     for d in range(owners):
         at = d * chunk
         mine = full if at == 0 else pltpu.roll(full, chans - at, 1)
@@ -288,8 +284,19 @@
         row = jnp.broadcast_to(wide[at // chans], full.shape)
         if at % chans:
             row = pltpu.roll(row, chans - at % chans, 1)
-        lscr[3, d, 2 * chunk :, :] = hi_lo(jnp.where(row_id == 3, row, mine))
-    halve(me & 1, lscr, keep_out, *send_outs)
+        small.append(hi_lo(jnp.where(row_id == 3, row, mine))[None])
+    quarters = [
+        jnp.concatenate(
+            [
+                grad[kw * chans : (kw + 1) * chans, kh * chans : (kh + 1) * chans].reshape(owners, chunk, chans)
+                for kw in range(3)
+            ],
+            axis=1,
+        )
+        for kh in range(3)
+    ]
+    quarters.append(jnp.concatenate([dlast[...].reshape(owners, 2 * chunk, chans), stack(*small)], axis=1))
+    halve(me & 1, quarters, keep_out, send_outs)
 
 
 def block_kernel(ahead, mix_top, mix, dw, dbias, block_out, done_out):
@@ -350,33 +357,33 @@
     send[...] = (keep[1 - chip] + got[1 - chip].astype(F32)).astype(BF16)
 
 
-def late_kernel(me_ref, owner_ref, keep, got0, got1, got2, e_own, e_got, own, sx, sy, sxy, ey_own, ey_send):
+def late_kernel(me_ref, owner_ref, keep, got0, got1, e_own, e_got, own, sx, sy, sxy):
     me, side = me_ref[0], owner_ref[0] & 1
     core, chip = me & 1, me >> 1
     mine, other = me == 3, 2 * (1 - chip) + core == 3
-
-    def total(x, d):
-        parts = [got[x, d].astype(F32) for got in (got0, got1, got2)]
-        return keep[x, d] + jnp.concatenate(parts, axis=0)
+    n = e_own.shape[2]
+
+    def total(x, z, y):
+        got = (got0, got1)[z // 2]
+        return keep[x, 2 * z + y] + got[x, 2 * (z % 2) + y].astype(F32)
 
     for z in range(own.shape[0]):
         here, there = 2 * z + side, 2 * z + 1 - side
-        own[z] = total(chip, here)
-        sx[z] = rounded(total(1 - chip, here), other)
-        sy[z] = rounded(total(chip, there), mine)
-        sxy[z] = rounded(total(1 - chip, there), other)
         for t in range(2):
-            ey_own[t, z] = e_own[t, here] + e_got[t, here].astype(F32)
-            ey_send[t, z] = (e_own[t, there] + e_got[t, there].astype(F32)).astype(BF16)
-
-
-def pack_kernel(me_ref, owner_ref, own, gx, gy, gxy, ey_own, ey_got, after, out, s1, s2, s3, scr):
+            own[z, t * n : (t + 1) * n] = e_own[t, here] + e_got[t, here].astype(F32)
+            sy[z, t * n : (t + 1) * n] = (e_own[t, there] + e_got[t, there].astype(F32)).astype(BF16)
+        own[z, 2 * n :] = total(chip, z, side)
+        sy[z, 2 * n :] = rounded(total(chip, z, 1 - side), mine)
+        sx[z] = rounded(total(1 - chip, z, side), other)
+        sxy[z] = rounded(total(1 - chip, z, 1 - side), other)
+
+
+def pack_kernel(me_ref, owner_ref, own, gx, gy, gxy, after, out, s1, s2, s3, scr):
     z = owner_ref[0] >> 1
-    early = ey_own[...] + ey_got[...].astype(F32)
-    n = early.shape[2]
-    for t in range(2):
-        scr[:, t * n : (t + 1) * n, :] = early[t]
-    scr[:, 2 * n :, :] = own[...] + gx[...].astype(F32) + gy[...].astype(F32) + gxy[...].astype(F32)
+    n = own.shape[1] - gx.shape[1]
+    scr[:, :n, :] = own[:, :n, :] + gy[:, :n, :].astype(F32)
+    late = gx[...].astype(F32) + gy[:, n:, :].astype(F32) + gxy[...].astype(F32)
+    scr[:, n:, :] = own[:, n:, :] + late
     out[...] = scr[z]
     for k, ref in ((1, s1), (2, s2), (3, s3)):
         ref[...] = rounded(scr[z ^ k], me_ref[0] == 3)
@@ -507,7 +514,6 @@
             if packed
             else [((outs, 9 * chans), F32)]
         ),
-        [pltpu.VMEM((4,) + early_shape, F32)] if packed else [],
     )
     if packed:
         dlast, keep, send = down_grad
@@ -521,11 +527,10 @@
         (me, *all_sums, par, x, hid, gp, gain, block_done) + ((dlast, cbias) if packed else ()),
         [tile, (block_of, BF16)]
         + (
-            [((2,) + late_shape, F32)] + [((2, owners, chunk, chans), BF16)] * 3
+            [((2,) + late_shape, F32)] + [((2, owners // 2, 3 * chunk, chans), BF16)] * 2
             if packed
             else [((3 * chans, 3 * chans), F32), tile]
         ),
-        [pltpu.VMEM((4,) + late_shape, F32)] if packed else [],
         cost=BACK,
     )
     gi, done = run(
@@ -537,19 +542,19 @@
     if packed:
         keep, *sends = conv_grad
         zs = owners // 2
-        late_cut, early_cut = (zs, 3 * chunk, chans), (2, zs, wide, chans)
-        late_own, sx, sy, sxy, early_own, early_send = run(
+        late_cut, both_cut = (zs, 3 * chunk, chans), (zs, deep, chans)
+        own, sx, sy, sxy = run(
             late_kernel,
             (me, owner, keep, *[swap(send, "rows", 1) for send in sends], early_own, early_got),
-            [(late_cut, F32)] + [(late_cut, BF16)] * 3 + [(early_cut, F32), (early_cut, BF16)],
+            [(both_cut, F32), (late_cut, BF16), (both_cut, BF16), (late_cut, BF16)],
         )
         gxy = swap_both(sxy, 2, 1)
-        late_got = swap(sx, "rows", 2), swap(sy, "dp", 1), gxy
+        gx, gy = swap(sx, "rows", 2), swap(sy, "dp", 1)
         part, *sends = run(
             pack_kernel,
-            (me, owner, late_own, *late_got, early_own, swap(early_send, "dp", 1), done),
+            (me, owner, own, gx, gy, gxy, done),
             [((deep, chans), F32)] + [((deep, chans), BF16)] * 3,
-            [pltpu.VMEM((zs, deep, chans), F32)],
+            [pltpu.VMEM(both_cut, F32)],
         )
         part, send = run(
             sum_kernel,

time: 46.6 us -> 46 us (0.987)
  starting transfers between devices: 23.8 us -> 22.1 us
  waiting for transfers between devices: 12.4 us -> 13.7 us
    ppermute x1, starting transfers between devices: 2.06 us -> 0.96 us  [swap_both(): lax.ppermute(x, both, [(i, i ^ k) for i in range(lax.axis_size(both))])]
    ppermute x1, waiting for transfers between devices: 1.13 us -> 1.9 us  [swap_both(): lax.ppermute(x, both, [(i, i ^ k) for i in range(lax.axis_size(both))])]
    ppermute x22 -> x20, starting transfers between devices: 20.4 us -> 19.8 us  [swap(): lax.ppermute(x, axis, [(i, i ^ k) for i in range(lax.axis_size(axis))])]
    ppermute x22 -> x20, waiting for transfers between devices: 11.2 us -> 11.8 us  [swap(): lax.ppermute(x, axis, [(i, i ^ k) for i in range(lax.axis_size(axis))])]
  transfers between devices with their start and end apart: 25 -> 23, of which waited for: 13 -> 12; matrix products, arithmetic and copies ran while one was open for 0% -> 0% of each run, Pallas kernels for 14% -> 14%
where the time goes in v4:
time: 46 us; the launch traced here: 45.8 us
  starting transfers between devices  22.1 us (48%)
  waiting for transfers between devices  13.7 us (30%)
  Pallas kernels  7.97 us (17%)
  local copies, waits for them, and re-layouts  1.19 us (3%)
  between operations  0.85 us (2%)
    ppermute x20, starting transfers between devices, swap(): lax.ppermute(x, axis, [(i, i ^ k) for i in range(lax.axis_size(axis))])  19.8 us
    ppermute x20, waiting for transfers between devices, swap(): lax.ppermute(x, axis, [(i, i ^ k) for i in range(lax.axis_size(axis))])  11.8 us
    pallas_call x14, Pallas kernels, run(): pl.pallas_call(kernel, in_specs=specs or [smem if a is me or a is owner e...  7.97 us
    ppermute x1, waiting for transfers between devices, swap_both(): lax.ppermute(x, both, [(i, i ^ k) for i in range(lax.axis_size(both))])  1.9 us
    ppermute x2, starting transfers between devices, across(): lax.ppermute(x, 'rows', [p for i in range(1, n - 1, 2) for p in ((i, i +...  1.32 us
    unnamed x16, local copies, waits for them, and re-layouts  1.19 us
    ppermute x1, starting transfers between devices, swap_both(): lax.ppermute(x, both, [(i, i ^ k) for i in range(lax.axis_size(both))])  0.96 us
  transfers between devices with their start and end apart: 23, of which 12 were waited for; matrix products, arithmetic and copies ran while one was open for 0% of the time, Pallas kernels for 14%

profile of v4, /device:TPU:0, one launch (start us, length us, event | category | flops | bytes accessed | tf_op | source)
XLA Modules:
  0.0 45.8 jit_solution(18398062521138315396)
XLA Ops:
  0.6 0.5 %collective-permute-start = (bf16[2,512,128]{2,1,0:T(8,128)(2,1)}, bf16[2,512,128]{2,1,0:T(8,128)(2,1)S(1)}, u32[]{:S(2)}, u32[]{:S(2)}) collective-permute-start(bf16[2,512,128]{2,1,0:T(8,128)(2,1)} %bitcast.20), channel_id=1, source_target_pairs={{0,8},{8,0},{16,24},{24,16},{1,9},{9,1},{17,25},{25,17},{2,10},{10... | collective-permute-start | bytes 786440 | tf_op jit(solution)/shard_map/ppermute | solution.py:424
  1.2 0.7 %collective-permute-start.1 = (bf16[2,512,128]{2,1,0:T(8,128)(2,1)}, bf16[2,512,128]{2,1,0:T(8,128)(2,1)S(1)}, u32[]{:S(2)}, u32[]{:S(2)}) collective-permute-start(bf16[2,512,128]{2,1,0:T(8,128)(2,1)} %bitcast.21), channel_id=1, source_target_pairs={{8,16},{16,8},{9,17},{17,9},{10,18},{18,10},{11,19},{19,11},{12,20... | collective-permute-start | bytes 786440 | tf_op jit(solution)/shard_map/ppermute | solution.py:420
  1.9 0.0 copy-start.4
  1.9 0.0 copy-start.5
  1.9 1.0 %copy-done = bf16[3,3,128,256]{3,2,1,0:T(8,128)(2,1)S(1)} copy-done((bf16[3,3,128,256]{3,2,1,0:T(8,128)(2,1)S(1)}, bf16[3,3,128,256]{3,2,1,0:T(8,128)(2,1)}, u32[]{:S(2)}) %copy-start) | copy-done | bytes 589848
  2.9 0.1 copy-done.1
  3.0 0.1 copy-done.2
  3.0 0.0 copy-done.3
  3.1 0.9 %shard_map.144 = (bf16[3,3,128,128]{3,2,1,0:T(8,128)(2,1)S(1)}, bf16[3,3,128,256]{3,2,1,0:T(8,128)(2,1)S(1)}, bf16[256,256]{1,0:T(8,128)(2,1)S(1)}, f32[1,128]{1...) custom-call(f32[8,128]{1,0:T(8,128)S(1)} %shard_map.143.ahead, ...), custom_call_target="tpu_custom_call" | custom-call | flops 134217728 | bytes 1024 | tf_op jit(solution)/shard_map/pallas_call | solution.py:449
  4.0 3.9 %collective-permute-start.5 = (bf16[256,256]{1,0:T(8,128)(2,1)S(1)}, bf16[256,256]{1,0:T(8,128)(2,1)S(1)}, u32[]{:S(2)}, u32[]{:S(2)}) collective-permute-start(bf16[256,256]{1,0:T(8,128)(2,1)S(1)} %get-tuple-element.65.cot), channel_id=1, source_target_pairs={{0,8},{8,0},{16,24},{24,16},{1,9},{9,1},{17,25},{25,17},{2,10},{10... | collective-permute-start | bytes 393224 | tf_op jit(solution)/shard_map/ppermute | solution.py:424
  7.9 0.7 %collective-permute-start.6 = (bf16[256,256]{1,0:T(8,128)(2,1)S(1)}, bf16[256,256]{1,0:T(8,128)(2,1)S(1)}, u32[]{:S(2)}, u32[]{:S(2)}) collective-permute-start(bf16[256,256]{1,0:T(8,128)(2,1)S(1)} %get-tuple-element.65.cot), channel_id=1, source_target_pairs={{8,16},{16,8},{9,17},{17,9},{10,18},{18,10},{11,19},{19,11},{12,20... | collective-permute-start | bytes 393224 | tf_op jit(solution)/shard_map/ppermute | solution.py:420
  8.6 0.0 collective-permute-done.core
  8.6 0.0 collective-permute-done.1.chip
  8.6 1.1 %shard_map.145 = (bf16[4,2,256,128]{3,2,1,0:T(8,128)(2,1)S(1)}, f32[2,2,256,128]{3,2,1,0:T(8,128)S(1)}, f32[8,128]{1,0:T(8,128)S(1)}) custom-call(s32[1]{0:T(128)} %bitcast.me_ref, bf16[2,512,128]{2,1,0:T(8,128)(2,1)S(1)} %collective-permute-done.core, bf16[2,512,128]{2,1,0:T(8,128)(2,1)S(1)} %collective-permute-done.1.chip, ...), custom_call_target="tpu_custom_call" | custom-call | flops 134217728 | bytes 1024 | tf_op jit(solution)/shard_map/pallas_call | solution.py:449
  9.7 1.3 %collective-permute-start.2 = (f32[8,128]{1,0:T(8,128)S(1)}, f32[8,128]{1,0:T(8,128)S(1)}, u32[]{:S(2)}, u32[]{:S(2)}) collective-permute-start(f32[8,128]{1,0:T(8,128)S(1)} %get-tuple-element.62.refs_0_), channel_id=1, source_target_pairs={{0,8},{8,0},{16,24},{24,16},{1,9},{9,1},{17,25},{25,17},{2,10},{10... | collective-permute-start | bytes 12296 | tf_op jit(solution)/shard_map/ppermute | solution.py:424
  11.0 1.6 %collective-permute-start.3 = (f32[8,128]{1,0:T(8,128)S(1)}, f32[8,128]{1,0:T(8,128)S(1)}, u32[]{:S(2)}, u32[]{:S(2)}) collective-permute-start(f32[8,128]{1,0:T(8,128)S(1)} %get-tuple-element.62.refs_0_), channel_id=1, source_target_pairs={{0,16},{8,24},{16,0},{24,8},{1,17},{9,25},{17,1},{25,9},{2,18},{10... | collective-permute-start | bytes 12296 | tf_op jit(solution)/shard_map/ppermute | solution.py:424
  12.7 0.1 collective-permute-start.4
  12.8 0.0 collective-permute-done.5.cot_core
  12.8 0.0 collective-permute-done.6.cot_chip
  12.8 0.9 %shard_map.146 = (f32[2,2,256,128]{3,2,1,0:T(8,128)S(1)}, f32[4,2,256,128]{3,2,1,0:T(8,128)S(1)}) custom-call(s32[1]{0:T(128)} %bitcast.me_ref, bf16[2,512,128]{2,1,0:T(8,128)(2,1)S(1)} %collective-permute-done.core, bf16[2,512,128]{2,1,0:T(8,128)(2,1)S(1)} %collective-permute-done.1.chip, bf16[4,2,256,128]{3,2,1,0:T(8,128)(2,1)S(1)} %get-tuple-element.63.x.refs_4_.refs_5_, ...), custom_call_target="tpu_custom_call" | custom-call | flops 134217728 | bytes 1024 | tf_op jit(solution)/shard_map/pallas_call | solution.py:449
  13.7 0.0 collective-permute-done.2.refs_1_
  13.7 1.0 %collective-permute-done.3.refs_2_ = f32[8,128]{1,0:T(8,128)S(1)} collective-permute-done((f32[8,128]{1,0:T(8,128)S(1)}, f32[8,128]{1,0:T(8,128)S(1)}, u32[]{:S(2)}, u32[]{:S(2)}) %collective-permute-start.3) | collective-permute-done | bytes 4128 | tf_op jit(solution)/shard_map/ppermute | solution.py:424
  14.7 1.1 %collective-permute-done.4.refs_3_ = f32[8,128]{1,0:T(8,128)S(1)} collective-permute-done((f32[8,128]{1,0:T(8,128)S(1)}, f32[8,128]{1,0:T(8,128)S(1)}, u32[]{:S(2)}, u32[]{:S(2)}) %collective-permute-start.4) | collective-permute-done | bytes 4128 | tf_op jit(solution)/shard_map/ppermute | solution.py:424
  15.7 0.4 shard_map.147
  16.1 0.4 shard_map.148
  16.6 0.3 collective-permute-start.7
  16.8 0.5 %collective-permute-start.10 = (f32[8,128]{1,0:T(8,128)S(1)}, f32[8,128]{1,0:T(8,128)S(1)}, u32[]{:S(2)}, u32[]{:S(2)}) collective-permute-start(f32[8,128]{1,0:T(8,128)S(1)} %get-tuple-element.80.refs_0_), channel_id=1, source_target_pairs={{0,24},{8,16},{16,8},{24,0},{1,25},{9,17},{17,9},{25,1},{2,26},{10... | collective-permute-start | bytes 12296 | tf_op jit(solution)/shard_map/ppermute | solution.py:424
  17.4 0.1 collective-permute-start.8
  17.4 1.5 %collective-permute-start.9 = (f32[8,128]{1,0:T(8,128)S(1)}, f32[8,128]{1,0:T(8,128)S(1)}, u32[]{:S(2)}, u32[]{:S(2)}) collective-permute-start(f32[8,128]{1,0:T(8,128)S(1)} %get-tuple-element.80.refs_0_), channel_id=1, source_target_pairs={{0,16},{8,24},{16,0},{24,8},{1,17},{9,25},{17,1},{25,9},{2,18},{10... | collective-permute-start | bytes 12296 | tf_op jit(solution)/shard_map/ppermute | solution.py:424
  19.0 0.0 collective-permute-done.7.got
  19.0 0.1 shard_map.149
  19.0 0.6 %collective-permute-start.13 = (bf16[2,8,32,128]{3,2,1,0:T(8,128)(2,1)S(1)}, bf16[2,8,32,128]{3,2,1,0:T(8,128)(2,1)S(1)}, u32[]{:S(2)}, u32[]{:S(2)}) collective-permute-start(bf16[2,8,32,128]{3,2,1,0:T(8,128)(2,1)S(1)} %get-tuple-element.92), channel_id=1, source_target_pairs={{0,16},{8,24},{16,0},{24,8},{1,17},{9,25},{17,1},{25,9},{2,18},{10... | collective-permute-start | bytes 393224 | tf_op jit(solution)/shard_map/ppermute | solution.py:424
  19.6 1.0 %shard_map.150 = (bf16[256,256]{1,0:T(8,128)(2,1)}, f32[8,128]{1,0:T(8,128)S(1)}) custom-call(f32[8,128]{1,0:T(8,128)S(1)} %get-tuple-element.76.ahead, bf16[256,384]{1,0:T(8,128)(2,1)S(1)} %get-tuple-element.77.mix_top, bf16[2,256,384]{2,1,0:T(8,128)(2,1)S(1)} %get-tuple-element.73.mix, bf16[3,3,128,256]{3,2,1,0:T(8,128)(2,1)S(1)} %get-tuple-element.66.dw, ...), custom_call_target="tpu_custom_call" | custom-call | flops 134217728 | bytes 1024 | tf_op jit(solution)/shard_map/pallas_call | solution.py:449
  20.6 0.0 collective-permute-done.10.refs_3_
  20.6 0.0 collective-permute-done.8.refs_1_
  20.6 0.4 collective-permute-done.9.refs_2_
  21.1 0.9 %shard_map.151 = (f32[8,128]{1,0:T(8,128)S(1)}, bf16[2,2,256,128]{3,2,1,0:T(8,128)(2,1)S(1)}, f32[2,8,48,128]{3,2,1,0:T(8,128)S(1)}, bf16[2,4,48,128]{3,2,1,0:T(8,128)(2,1)S(1)}, bf16[2,4,48,128]{3,2,1,0:T(8,128)(2,1)S(1)}) custom-call(s32[1]{0:T(128)} %bitcast.me_ref, f32[8,128]{1,0:T(8,128)S(1)} %get-tuple-element.80.refs_0_, ...), custom_call_target="tpu_custom_call" | custom-call | flops 4294967296 | bytes 1024 | tf_op jit(solution)/shard_map/pallas_call | solution.py:449
  21.9 0.1 collective-permute-start.11
  22.0 0.5 %collective-permute-start.12 = (bf16[2,4,48,128]{3,2,1,0:T(8,128)(2,1)S(1)}, bf16[2,4,48,128]{3,2,1,0:T(8,128)(2,1)S(1)}, u32[]{:S(2)}, u32[]{:S(2)}) collective-permute-start(bf16[2,4,48,128]{3,2,1,0:T(8,128)(2,1)S(1)} %get-tuple-element.90), channel_id=1, source_target_pairs={{0,8},{8,0},{16,24},{24,16},{1,9},{9,1},{17,25},{25,17},{2,10},{10... | collective-permute-start | bytes 294920 | tf_op jit(solution)/shard_map/ppermute | solution.py:424
  22.5 0.8 %collective-permute-done.11.got0 = bf16[2,4,48,128]{3,2,1,0:T(8,128)(2,1)S(1)} collective-permute-done((bf16[2,4,48,128]{3,2,1,0:T(8,128)(2,1)S(1)}, bf16[2,4,48,128]{3,2,1,0:T(8,128)(2,1)S(1)}, u32[]{:S(2)}, u32[]{:S(2)}) %collective-permute-start.11) | collective-permute-done | bytes 98336 | tf_op jit(solution)/shard_map/ppermute | solution.py:424
  23.3 0.2 collective-permute-done.12.got1
  23.4 1.1 %collective-permute-done.13.e_got = bf16[2,8,32,128]{3,2,1,0:T(8,128)(2,1)S(1)} collective-permute-done((bf16[2,8,32,128]{3,2,1,0:T(8,128)(2,1)S(1)}, bf16[2,8,32,128]{3,2,1,0:T(8,128)(2,1)S(1)}, u32[]{:S(2)}, u32[]{:S(2)}) %collective-permute-start.13) | collective-permute-done | bytes 131104 | tf_op jit(solution)/shard_map/ppermute | solution.py:424
  24.5 0.1 shard_map.153
  24.6 1.6 %collective-permute-start.15 = (bf16[4,112,128]{2,1,0:T(8,128)(2,1)S(1)}, bf16[4,112,128]{2,1,0:T(8,128)(2,1)S(1)}, u32[]{:S(2)}, u32[]{:S(2)}) collective-permute-start(bf16[4,112,128]{2,1,0:T(8,128)(2,1)S(1)} %get-tuple-element.95), channel_id=1, source_target_pairs={{0,1},{1,0},{2,3},{3,2},{4,5},{5,4},{6,7},{7,6},{8,9},{9,8},{10,11... | collective-permute-start | bytes 344072 | tf_op jit(solution)/shard_map/ppermute | solution.py:424
  26.2 1.0 %collective-permute-start.14 = (bf16[4,48,128]{2,1,0:T(8,128)(2,1)S(1)}, bf16[4,48,128]{2,1,0:T(8,128)(2,1)S(1)}, u32[]{:S(2)}, u32[]{:S(2)}) collective-permute-start(bf16[4,48,128]{2,1,0:T(8,128)(2,1)S(1)} %get-tuple-element.94), channel_id=1, source_target_pairs={{0,16},{8,24},{16,0},{24,8},{1,17},{9,25},{17,1},{25,9},{2,18},{10... | collective-permute-start | bytes 147464 | tf_op jit(solution)/shard_map/ppermute | solution.py:424
  27.2 1.0 %collective-permute-start.16 = (bf16[4,48,128]{2,1,0:T(8,128)(2,1)S(1)}, bf16[4,48,128]{2,1,0:T(8,128)(2,1)S(1)}, u32[]{:S(2)}, u32[]{:S(2)}) collective-permute-start(bf16[4,48,128]{2,1,0:T(8,128)(2,1)S(1)} %get-tuple-element.96), channel_id=1, source_target_pairs={{0,17},{1,16},{2,19},{3,18},{4,21},{5,20},{6,23},{7,22},{8,25},{9,... | collective-permute-start | bytes 147464 | tf_op jit(solution)/shard_map/ppermute | solution.py:430
  28.2 1.5 %shard_map.152 = (bf16[2,512,128]{2,1,0:T(8,128)(2,1)}, f32[8,128]{1,0:T(8,128)S(1)}) custom-call(s32[1]{0:T(128)} %bitcast.me_ref, f32[8,128]{1,0:T(8,128)S(1)} %get-tuple-element.71.par.refs_4_, f32[2,2,256,128]{3,2,1,0:T(8,128)S(1)} %get-tuple-element.72.hid, f32[4,2,256,128]{3,2,1,0:T(8,128)S(1)} %get-tuple-element.68.refs_6_.gm, ...), custom_call_target="tpu_custom_call" | custom-call | flops 134217728 | bytes 1024 | tf_op jit(solution)/shard_map/pallas_call | solution.py:449
  29.6 0.7 %collective-permute-done.14.gx = bf16[4,48,128]{2,1,0:T(8,128)(2,1)S(1)} collective-permute-done((bf16[4,48,128]{2,1,0:T(8,128)(2,1)S(1)}, bf16[4,48,128]{2,1,0:T(8,128)(2,1)S(1)}, u32[]{:S(2)}, u32[]{:S(2)}) %collective-permute-start.14) | collective-permute-done | bytes 49184 | tf_op jit(solution)/shard_map/ppermute | solution.py:424
  30.3 1.9 %collective-permute-done.16.gxy = bf16[4,48,128]{2,1,0:T(8,128)(2,1)S(1)} collective-permute-done((bf16[4,48,128]{2,1,0:T(8,128)(2,1)S(1)}, bf16[4,48,128]{2,1,0:T(8,128)(2,1)S(1)}, u32[]{:S(2)}, u32[]{:S(2)}) %collective-permute-start.16) | collective-permute-done | bytes 49184 | tf_op jit(solution)/shard_map/ppermute | solution.py:430
  32.2 0.0 collective-permute-done.15.gy
  32.2 0.1 shard_map.154
  32.3 2.7 %collective-permute-start.17 = (bf16[112,128]{1,0:T(8,128)(2,1)S(1)}, bf16[112,128]{1,0:T(8,128)(2,1)S(1)}, u32[]{:S(2)}, u32[]{:S(2)}) collective-permute-start(bf16[112,128]{1,0:T(8,128)(2,1)S(1)} %get-tuple-element.99), channel_id=1, source_target_pairs={{0,4},{1,5},{2,6},{3,7},{4,0},{5,1},{6,2},{7,3},{8,12},{9,13},{10,... | collective-permute-start | bytes 86024 | tf_op jit(solution)/shard_map/ppermute | solution.py:424
  34.9 1.3 %collective-permute-start.18 = (bf16[112,128]{1,0:T(8,128)(2,1)S(1)}, bf16[112,128]{1,0:T(8,128)(2,1)S(1)}, u32[]{:S(2)}, u32[]{:S(2)}) collective-permute-start(bf16[112,128]{1,0:T(8,128)(2,1)S(1)} %get-tuple-element.100), channel_id=1, source_target_pairs={{0,6},{1,7},{2,4},{3,5},{4,2},{5,3},{6,0},{7,1},{8,14},{9,15},{10,... | collective-permute-start | bytes 86024 | tf_op jit(solution)/shard_map/ppermute | solution.py:424
  36.3 0.2 collective-permute-start.19
  36.5 0.8 %collective-permute-done.17.g1 = bf16[112,128]{1,0:T(8,128)(2,1)S(1)} collective-permute-done((bf16[112,128]{1,0:T(8,128)(2,1)S(1)}, bf16[112,128]{1,0:T(8,128)(2,1)S(1)}, u32[]{:S(2)}, u32[]{:S(2)}) %collective-permute-start.17) | collective-permute-done | bytes 28704 | tf_op jit(solution)/shard_map/ppermute | solution.py:424
  37.3 3.3 %collective-permute-done.18.g2 = bf16[112,128]{1,0:T(8,128)(2,1)S(1)} collective-permute-done((bf16[112,128]{1,0:T(8,128)(2,1)S(1)}, bf16[112,128]{1,0:T(8,128)(2,1)S(1)}, u32[]{:S(2)}, u32[]{:S(2)}) %collective-permute-start.18) | collective-permute-done | bytes 28704 | tf_op jit(solution)/shard_map/ppermute | solution.py:424
  40.6 0.0 collective-permute-done.19.g3
  40.6 0.1 collective-permute-start.20
  40.7 1.1 %collective-permute-start.21 = (bf16[112,128]{1,0:T(8,128)(2,1)S(1)}, bf16[112,128]{1,0:T(8,128)(2,1)S(1)}, u32[]{:S(2)}, u32[]{:S(2)}) collective-permute-start(bf16[112,128]{1,0:T(8,128)(2,1)S(1)} %get-tuple-element.103), channel_id=1, source_target_pairs={{0,16},{8,24},{16,0},{24,8},{1,17},{9,25},{17,1},{25,9},{2,18},{10... | collective-permute-start | bytes 86024 | tf_op jit(solution)/shard_map/ppermute | solution.py:424
  41.8 0.8 %collective-permute-start.22 = (bf16[112,128]{1,0:T(8,128)(2,1)S(1)}, bf16[112,128]{1,0:T(8,128)(2,1)S(1)}, u32[]{:S(2)}, u32[]{:S(2)}) collective-permute-start(bf16[112,128]{1,0:T(8,128)(2,1)S(1)} %get-tuple-element.103), channel_id=1, source_target_pairs={{0,24},{8,16},{16,8},{24,0},{1,25},{9,17},{17,9},{25,1},{2,26},{10... | collective-permute-start | bytes 86024 | tf_op jit(solution)/shard_map/ppermute | solution.py:424
  42.6 0.0 collective-permute-done.20.q1
  42.6 2.1 %collective-permute-done.21.q2 = bf16[112,128]{1,0:T(8,128)(2,1)S(1)} collective-permute-done((bf16[112,128]{1,0:T(8,128)(2,1)S(1)}, bf16[112,128]{1,0:T(8,128)(2,1)S(1)}, u32[]{:S(2)}, u32[]{:S(2)}) %collective-permute-start.21) | collective-permute-done | bytes 28704 | tf_op jit(solution)/shard_map/ppermute | solution.py:424
  44.6 0.4 collective-permute-done.22.q3
  45.1 0.7 %shard_map.156 = (f32[9,32,128]{2,1,0:T(8,128)}, f32[9,16,128]{2,1,0:T(8,128)}, f32[1,16]{1,0:T(1,128)}, f32[1,16]{1,0:T(1,128)}, f32[1,16]{1,0:T(1,128)}, /*index=5*/f32[1,32]{1,0:T(1,128)}) custom-call(s32[1]{0:T(128)} %bitcast.me_ref, f32[112,128]{1,0:T(8,128)S(1)} %get-tuple-element.102.q0, bf16[112,128]{1,0:T(8,128)(2,1)S(1)} %collective-permute-done.20.q1, ...), custom_call_target="tpu_custom_call" | custom-call | flops 134217728 | bytes 1024 | tf_op jit(solution)/shard_map/pallas_call | solution.py:449
  (12 shorter events, 0.0 us)
Async XLA Ops:
  0.6 8.0 %collective-permute-start = (bf16[2,512,128]{2,1,0:T(8,128)(2,1)}, bf16[2,512,128]{2,1,0:T(8,128)(2,1)S(1)}, u32[]{:S(2)}, u32[]{:S(2)}) collective-permute-start(bf16[2,512,128]{2,1,0:T(8,128)(2,1)} %bitcast.20), channel_id=1, source_target_pairs={{0,8},{8,0},{16,24},{24,16},{1,9},{9,1},{17,25},{25,17},{2,10},{10... | collective-permute-start | bytes 786440 | tf_op jit(solution)/shard_map/ppermute | solution.py:424
  1.2 7.5 %collective-permute-start.1 = (bf16[2,512,128]{2,1,0:T(8,128)(2,1)}, bf16[2,512,128]{2,1,0:T(8,128)(2,1)S(1)}, u32[]{:S(2)}, u32[]{:S(2)}) collective-permute-start(bf16[2,512,128]{2,1,0:T(8,128)(2,1)} %bitcast.21), channel_id=1, source_target_pairs={{8,16},{16,8},{9,17},{17,9},{10,18},{18,10},{11,19},{19,11},{12,20... | collective-permute-start | bytes 786440 | tf_op jit(solution)/shard_map/ppermute | solution.py:420
  1.8 1.1 %copy-start = (bf16[3,3,128,256]{3,2,1,0:T(8,128)(2,1)S(1)}, bf16[3,3,128,256]{3,2,1,0:T(8,128)(2,1)}, u32[]{:S(2)}) copy-start(bf16[3,3,128,256]{3,2,1,0:T(8,128)(2,1)} %dw.1) | copy-start | bytes 1769476
  1.8 1.1 %copy-start.1 = (bf16[3,3,128,128]{3,2,1,0:T(8,128)(2,1)S(1)}, bf16[3,3,128,128]{3,2,1,0:T(8,128)(2,1)}, u32[]{:S(2)}) copy-start(bf16[3,3,128,128]{3,2,1,0:T(8,128)(2,1)} %w.1) | copy-start | bytes 884740
  1.9 1.2 %copy-start.2 = (bf16[1,2,512,128]{3,2,1,0:T(8,128)(2,1)S(1)}, bf16[1,2,512,128]{3,2,1,0:T(8,128)(2,1)}, u32[]{:S(2)}) copy-start(bf16[1,2,512,128]{3,2,1,0:T(8,128)(2,1)} %param.8) | copy-start | bytes 786436
  1.9 1.2 %copy-start.3 = (bf16[1,1,256,256]{3,2,1,0:T(8,128)(2,1)S(1)}, bf16[1,1,256,256]{3,2,1,0:T(8,128)(2,1)}, u32[]{:S(2)}) copy-start(bf16[1,1,256,256]{3,2,1,0:T(8,128)(2,1)} %param.15) | copy-start | bytes 393220
  1.9 1.2 %copy-start.6 = (f32[128]{0:T(128)S(1)}, f32[128]{0:T(128)}, u32[]{:S(2)}) copy-start(f32[128]{0:T(128)} %param.11) | copy-start | bytes 1540
  1.9 1.2 %copy-start.7 = (f32[128]{0:T(128)S(1)}, f32[128]{0:T(128)}, u32[]{:S(2)}) copy-start(f32[128]{0:T(128)} %param.12) | copy-start | bytes 1540
  1.9 1.2 %copy-start.4 = (f32[256]{0:T(256)S(1)}, f32[256]{0:T(256)}, u32[]{:S(2)}) copy-start(f32[256]{0:T(256)} %param.14) | copy-start | bytes 3076
  1.9 1.2 %copy-start.5 = (f32[128]{0:T(128)S(1)}, f32[128]{0:T(128)}, u32[]{:S(2)}) copy-start(f32[128]{0:T(128)} %param.10) | copy-start | bytes 1540
  4.0 8.8 %collective-permute-start.5 = (bf16[256,256]{1,0:T(8,128)(2,1)S(1)}, bf16[256,256]{1,0:T(8,128)(2,1)S(1)}, u32[]{:S(2)}, u32[]{:S(2)}) collective-permute-start(bf16[256,256]{1,0:T(8,128)(2,1)S(1)} %get-tuple-element.65.cot), channel_id=1, source_target_pairs={{0,8},{8,0},{16,24},{24,16},{1,9},{9,1},{17,25},{25,17},{2,10},{10... | collective-permute-start | bytes 393224 | tf_op jit(solution)/shard_map/ppermute | solution.py:424
  7.9 4.9 %collective-permute-start.6 = (bf16[256,256]{1,0:T(8,128)(2,1)S(1)}, bf16[256,256]{1,0:T(8,128)(2,1)S(1)}, u32[]{:S(2)}, u32[]{:S(2)}) collective-permute-start(bf16[256,256]{1,0:T(8,128)(2,1)S(1)} %get-tuple-element.65.cot), channel_id=1, source_target_pairs={{8,16},{16,8},{9,17},{17,9},{10,18},{18,10},{11,19},{19,11},{12,20... | collective-permute-start | bytes 393224 | tf_op jit(solution)/shard_map/ppermute | solution.py:420
  9.7 4.0 %collective-permute-start.2 = (f32[8,128]{1,0:T(8,128)S(1)}, f32[8,128]{1,0:T(8,128)S(1)}, u32[]{:S(2)}, u32[]{:S(2)}) collective-permute-start(f32[8,128]{1,0:T(8,128)S(1)} %get-tuple-element.62.refs_0_), channel_id=1, source_target_pairs={{0,8},{8,0},{16,24},{24,16},{1,9},{9,1},{17,25},{25,17},{2,10},{10... | collective-permute-start | bytes 12296 | tf_op jit(solution)/shard_map/ppermute | solution.py:424
  11.0 3.6 %collective-permute-start.3 = (f32[8,128]{1,0:T(8,128)S(1)}, f32[8,128]{1,0:T(8,128)S(1)}, u32[]{:S(2)}, u32[]{:S(2)}) collective-permute-start(f32[8,128]{1,0:T(8,128)S(1)} %get-tuple-element.62.refs_0_), channel_id=1, source_target_pairs={{0,16},{8,24},{16,0},{24,8},{1,17},{9,25},{17,1},{25,9},{2,18},{10... | collective-permute-start | bytes 12296 | tf_op jit(solution)/shard_map/ppermute | solution.py:424
  12.7 3.0 %collective-permute-start.4 = (f32[8,128]{1,0:T(8,128)S(1)}, f32[8,128]{1,0:T(8,128)S(1)}, u32[]{:S(2)}, u32[]{:S(2)}) collective-permute-start(f32[8,128]{1,0:T(8,128)S(1)} %get-tuple-element.62.refs_0_), channel_id=1, source_target_pairs={{0,24},{8,16},{16,8},{24,0},{1,25},{9,17},{17,9},{25,1},{2,26},{10... | collective-permute-start | bytes 12296 | tf_op jit(solution)/shard_map/ppermute | solution.py:424
  16.6 2.4 %collective-permute-start.7 = (bf16[2,2,8,32,128]{4,3,2,1,0:T(8,128)(2,1)S(1)}, bf16[2,2,8,32,128]{4,3,2,1,0:T(8,128)(2,1)S(1)}, u32[]{:S(2)}, u32[]{:S(2)}) collective-permute-start(bf16[2,2,8,32,128]{4,3,2,1,0:T(8,128)(2,1)S(1)} %get-tuple-element.75), channel_id=1, source_target_pairs={{0,8},{8,0},{16,24},{24,16},{1,9},{9,1},{17,25},{25,17},{2,10},{10... | collective-permute-start | bytes 786440 | tf_op jit(solution)/shard_map/ppermute | solution.py:424
  16.8 3.8 %collective-permute-start.10 = (f32[8,128]{1,0:T(8,128)S(1)}, f32[8,128]{1,0:T(8,128)S(1)}, u32[]{:S(2)}, u32[]{:S(2)}) collective-permute-start(f32[8,128]{1,0:T(8,128)S(1)} %get-tuple-element.80.refs_0_), channel_id=1, source_target_pairs={{0,24},{8,16},{16,8},{24,0},{1,25},{9,17},{17,9},{25,1},{2,26},{10... | collective-permute-start | bytes 12296 | tf_op jit(solution)/shard_map/ppermute | solution.py:424
  17.4 3.3 %collective-permute-start.8 = (f32[8,128]{1,0:T(8,128)S(1)}, f32[8,128]{1,0:T(8,128)S(1)}, u32[]{:S(2)}, u32[]{:S(2)}) collective-permute-start(f32[8,128]{1,0:T(8,128)S(1)} %get-tuple-element.80.refs_0_), channel_id=1, source_target_pairs={{0,8},{8,0},{16,24},{24,16},{1,9},{9,1},{17,25},{25,17},{2,10},{10... | collective-permute-start | bytes 12296 | tf_op jit(solution)/shard_map/ppermute | solution.py:424
  17.4 3.6 %collective-permute-start.9 = (f32[8,128]{1,0:T(8,128)S(1)}, f32[8,128]{1,0:T(8,128)S(1)}, u32[]{:S(2)}, u32[]{:S(2)}) collective-permute-start(f32[8,128]{1,0:T(8,128)S(1)} %get-tuple-element.80.refs_0_), channel_id=1, source_target_pairs={{0,16},{8,24},{16,0},{24,8},{1,17},{9,25},{17,1},{25,9},{2,18},{10... | collective-permute-start | bytes 12296 | tf_op jit(solution)/shard_map/ppermute | solution.py:424
  19.0 5.5 %collective-permute-start.13 = (bf16[2,8,32,128]{3,2,1,0:T(8,128)(2,1)S(1)}, bf16[2,8,32,128]{3,2,1,0:T(8,128)(2,1)S(1)}, u32[]{:S(2)}, u32[]{:S(2)}) collective-permute-start(bf16[2,8,32,128]{3,2,1,0:T(8,128)(2,1)S(1)} %get-tuple-element.92), channel_id=1, source_target_pairs={{0,16},{8,24},{16,0},{24,8},{1,17},{9,25},{17,1},{25,9},{2,18},{10... | collective-permute-start | bytes 393224 | tf_op jit(solution)/shard_map/ppermute | solution.py:424
  21.9 1.4 %collective-permute-start.11 = (bf16[2,4,48,128]{3,2,1,0:T(8,128)(2,1)S(1)}, bf16[2,4,48,128]{3,2,1,0:T(8,128)(2,1)S(1)}, u32[]{:S(2)}, u32[]{:S(2)}) collective-permute-start(bf16[2,4,48,128]{3,2,1,0:T(8,128)(2,1)S(1)} %get-tuple-element.89), channel_id=1, source_target_pairs={{0,8},{8,0},{16,24},{24,16},{1,9},{9,1},{17,25},{25,17},{2,10},{10... | collective-permute-start | bytes 294920 | tf_op jit(solution)/shard_map/ppermute | solution.py:424
  22.0 1.4 %collective-permute-start.12 = (bf16[2,4,48,128]{3,2,1,0:T(8,128)(2,1)S(1)}, bf16[2,4,48,128]{3,2,1,0:T(8,128)(2,1)S(1)}, u32[]{:S(2)}, u32[]{:S(2)}) collective-permute-start(bf16[2,4,48,128]{3,2,1,0:T(8,128)(2,1)S(1)} %get-tuple-element.90), channel_id=1, source_target_pairs={{0,8},{8,0},{16,24},{24,16},{1,9},{9,1},{17,25},{25,17},{2,10},{10... | collective-permute-start | bytes 294920 | tf_op jit(solution)/shard_map/ppermute | solution.py:424
  24.6 7.6 %collective-permute-start.15 = (bf16[4,112,128]{2,1,0:T(8,128)(2,1)S(1)}, bf16[4,112,128]{2,1,0:T(8,128)(2,1)S(1)}, u32[]{:S(2)}, u32[]{:S(2)}) collective-permute-start(bf16[4,112,128]{2,1,0:T(8,128)(2,1)S(1)} %get-tuple-element.95), channel_id=1, source_target_pairs={{0,1},{1,0},{2,3},{3,2},{4,5},{5,4},{6,7},{7,6},{8,9},{9,8},{10,11... | collective-permute-start | bytes 344072 | tf_op jit(solution)/shard_map/ppermute | solution.py:424
  26.2 4.1 %collective-permute-start.14 = (bf16[4,48,128]{2,1,0:T(8,128)(2,1)S(1)}, bf16[4,48,128]{2,1,0:T(8,128)(2,1)S(1)}, u32[]{:S(2)}, u32[]{:S(2)}) collective-permute-start(bf16[4,48,128]{2,1,0:T(8,128)(2,1)S(1)} %get-tuple-element.94), channel_id=1, source_target_pairs={{0,16},{8,24},{16,0},{24,8},{1,17},{9,25},{17,1},{25,9},{2,18},{10... | collective-permute-start | bytes 147464 | tf_op jit(solution)/shard_map/ppermute | solution.py:424
  27.2 5.0 %collective-permute-start.16 = (bf16[4,48,128]{2,1,0:T(8,128)(2,1)S(1)}, bf16[4,48,128]{2,1,0:T(8,128)(2,1)S(1)}, u32[]{:S(2)}, u32[]{:S(2)}) collective-permute-start(bf16[4,48,128]{2,1,0:T(8,128)(2,1)S(1)} %get-tuple-element.96), channel_id=1, source_target_pairs={{0,17},{1,16},{2,19},{3,18},{4,21},{5,20},{6,23},{7,22},{8,25},{9,... | collective-permute-start | bytes 147464 | tf_op jit(solution)/shard_map/ppermute | solution.py:430
  32.3 5.1 %collective-permute-start.17 = (bf16[112,128]{1,0:T(8,128)(2,1)S(1)}, bf16[112,128]{1,0:T(8,128)(2,1)S(1)}, u32[]{:S(2)}, u32[]{:S(2)}) collective-permute-start(bf16[112,128]{1,0:T(8,128)(2,1)S(1)} %get-tuple-element.99), channel_id=1, source_target_pairs={{0,4},{1,5},{2,6},{3,7},{4,0},{5,1},{6,2},{7,3},{8,12},{9,13},{10,... | collective-permute-start | bytes 86024 | tf_op jit(solution)/shard_map/ppermute | solution.py:424
  34.9 5.7 %collective-permute-start.18 = (bf16[112,128]{1,0:T(8,128)(2,1)S(1)}, bf16[112,128]{1,0:T(8,128)(2,1)S(1)}, u32[]{:S(2)}, u32[]{:S(2)}) collective-permute-start(bf16[112,128]{1,0:T(8,128)(2,1)S(1)} %get-tuple-element.100), channel_id=1, source_target_pairs={{0,6},{1,7},{2,4},{3,5},{4,2},{5,3},{6,0},{7,1},{8,14},{9,15},{10,... | collective-permute-start | bytes 86024 | tf_op jit(solution)/shard_map/ppermute | solution.py:424
  36.3 4.3 %collective-permute-start.19 = (bf16[112,128]{1,0:T(8,128)(2,1)S(1)}, bf16[112,128]{1,0:T(8,128)(2,1)S(1)}, u32[]{:S(2)}, u32[]{:S(2)}) collective-permute-start(bf16[112,128]{1,0:T(8,128)(2,1)S(1)} %get-tuple-element.101), channel_id=1, source_target_pairs={{0,2},{1,3},{2,0},{3,1},{4,6},{5,7},{6,4},{7,5},{8,10},{9,11},{10,... | collective-permute-start | bytes 86024 | tf_op jit(solution)/shard_map/ppermute | solution.py:424
  40.6 1.9 %collective-permute-start.20 = (bf16[112,128]{1,0:T(8,128)(2,1)S(1)}, bf16[112,128]{1,0:T(8,128)(2,1)S(1)}, u32[]{:S(2)}, u32[]{:S(2)}) collective-permute-start(bf16[112,128]{1,0:T(8,128)(2,1)S(1)} %get-tuple-element.103), channel_id=1, source_target_pairs={{0,8},{8,0},{16,24},{24,16},{1,9},{9,1},{17,25},{25,17},{2,10},{10... | collective-permute-start | bytes 86024 | tf_op jit(solution)/shard_map/ppermute | solution.py:424
  40.7 3.9 %collective-permute-start.21 = (bf16[112,128]{1,0:T(8,128)(2,1)S(1)}, bf16[112,128]{1,0:T(8,128)(2,1)S(1)}, u32[]{:S(2)}, u32[]{:S(2)}) collective-permute-start(bf16[112,128]{1,0:T(8,128)(2,1)S(1)} %get-tuple-element.103), channel_id=1, source_target_pairs={{0,16},{8,24},{16,0},{24,8},{1,17},{9,25},{17,1},{25,9},{2,18},{10... | collective-permute-start | bytes 86024 | tf_op jit(solution)/shard_map/ppermute | solution.py:424
  41.8 3.3 %collective-permute-start.22 = (bf16[112,128]{1,0:T(8,128)(2,1)S(1)}, bf16[112,128]{1,0:T(8,128)(2,1)S(1)}, u32[]{:S(2)}, u32[]{:S(2)}) collective-permute-start(bf16[112,128]{1,0:T(8,128)(2,1)S(1)} %get-tuple-element.103), channel_id=1, source_target_pairs={{0,24},{8,16},{16,8},{24,0},{1,25},{9,17},{17,9},{25,1},{2,26},{10... | collective-permute-start | bytes 86024 | tf_op jit(solution)/shard_map/ppermute | solution.py:424

commit v5 on v4

--- a/solution.py
+++ b/solution.py
@@ -74,7 +74,7 @@
     return base[:, :chans] + bias, base[:, chans:] + bias, from_odd, from_even
 
 
-def first_kernel(me_ref, out):
+def first_kernel(out):
     out[...] = jnp.zeros(out.shape, F32)
 
 
@@ -109,9 +109,9 @@
     return jnp.where(flag, a.astype(F32), b.astype(F32))
 
 
-def hidden_kernel(width, me_ref, core, chip, own, w, bias, x_out, hid_out, stat_out, scr):
+def hidden_kernel(width, core, chip, own, w, bias, x_out, hid_out, stat_out, scr):
     half = x_out.shape[2]
-    odd_rank = (me_ref[0] & 1) == 1
+    odd_rank = (lax.axis_index("rows") & 1) == 1
     for p, row in ((0, either(odd_rank, core[1], chip[1])), (3, either(odd_rank, chip[0], core[0]))):
         even, odd = split(scr, row)
         x_out[p, 0] = even.astype(BF16)
@@ -141,9 +141,9 @@
     stat_out[1:2] = grouped(spread, width)
 
 
-def edge_kernel(me_ref, core, chip, x, w, bias, cot_core, cot_chip, dw, own_gm, hid_out, gm_out, scr):
+def edge_kernel(core, chip, x, w, bias, cot_core, cot_chip, dw, own_gm, hid_out, gm_out, scr):
     half = x.shape[2]
-    odd_rank = (me_ref[0] & 1) == 1
+    odd_rank = (lax.axis_index("rows") & 1) == 1
     top = [v.astype(BF16) for v in split(scr, either(odd_rank, core[0], chip[0]))]
     low = [v.astype(BF16) for v in split(scr, either(odd_rank, chip[1], core[1]))]
     weights = conv_weights(w)
@@ -197,10 +197,10 @@
     sum_out[1:2] = second
 
 
-def down_kernel(packed, me_ref, par, x, hid, gain, shift, mix, cot, top_out, *rest):
+def down_kernel(packed, par, x, hid, gain, shift, mix, cot, top_out, *rest):
     mean, rstd = par[0:1], par[1:2]
     chans = x.shape[3]
-    inside = jnp.where(me_ref[0] > 0, 1.0, 0.0)
+    inside = jnp.where(lax.axis_index("rows") > 0, 1.0, 0.0)
     mixed = []
     for c in range(2):
         pre = (hid[0, c] - mean) * rstd * gain[...] + shift[...]
@@ -217,7 +217,7 @@
     last_out[...] = taps[8]
     for t in range(2):
         quarters = [taps[2 * q + t].reshape(-1, outs_chunk, chans) for q in range(4)]
-        halve(me_ref[0] & 1, quarters, keep_out, [send_out], (t,))
+        halve(lax.axis_index("rows") & 1, quarters, keep_out, [send_out], (t,))
 
 
 def halve(core, quarters, keep_out, send_outs, at=()):
@@ -236,7 +236,7 @@
     return jnp.concatenate([hi, full - hi], axis=-2)
 
 
-def back_kernel(width, count, ranks, packed, me_ref, *refs):
+def back_kernel(width, count, ranks, packed, *refs):
     sum_refs = refs[:ranks]
     par, x, hid, gp, gain, _, *refs = refs[ranks:]
     if packed:
@@ -245,7 +245,7 @@
         par_out, g_out, grad_out, small_out = refs
     half = x.shape[2]
     chans = x.shape[3]
-    me = me_ref[0]
+    me = lax.axis_index("rows")
     mean, rstd = par[0:1], par[1:2]
     sums = sum(s[...] for s in sum_refs)
     m2 = grouped(sums[0:1] * gain[...], width) / count
@@ -310,11 +310,11 @@
     done_out[...] = jnp.zeros(done_out.shape, F32)
 
 
-def image_kernel(last, me_ref, par, hid, gm, gain, shift, par2, g, w, gi_out, done_out, scr):
+def image_kernel(last, par, hid, gm, gain, shift, par2, g, w, gi_out, done_out, scr):
     half = g.shape[2]
     chans = g.shape[3]
     mean, rstd = par[0:1], par[1:2]
-    me = me_ref[0]
+    me = lax.axis_index("rows")
     edge = []
     for i, p, there in ((0, 0, me > 0), (1, 3, me < last)):
         keep = jnp.where(there, 1.0, 0.0)
@@ -350,15 +350,15 @@
     return stack(total[:n], last).astype(BF16)
 
 
-def early_kernel(me_ref, keep, got, own, send, done_out):
+def early_kernel(keep, got, own, send, done_out):
     done_out[...] = jnp.zeros(done_out.shape, F32)
-    chip = me_ref[0] >> 1
+    chip = lax.axis_index("rows") >> 1
     own[...] = keep[chip] + got[chip].astype(F32)
     send[...] = (keep[1 - chip] + got[1 - chip].astype(F32)).astype(BF16)
 
 
-def late_kernel(me_ref, owner_ref, keep, got0, got1, e_own, e_got, own, sx, sy, sxy):
-    me, side = me_ref[0], owner_ref[0] & 1
+def late_kernel( keep, got0, got1, e_own, e_got, own, sx, sy, sxy):
+    me, side = lax.axis_index("rows"), lax.axis_index("dp") & 1
     core, chip = me & 1, me >> 1
     mine, other = me == 3, 2 * (1 - chip) + core == 3
     n = e_own.shape[2]
@@ -378,25 +378,25 @@
         sxy[z] = rounded(total(1 - chip, z, 1 - side), other)
 
 
-def pack_kernel(me_ref, owner_ref, own, gx, gy, gxy, after, out, s1, s2, s3, scr):
-    z = owner_ref[0] >> 1
+def pack_kernel( own, gx, gy, gxy, after, out, s1, s2, s3, scr):
+    z = lax.axis_index("dp") >> 1
     n = own.shape[1] - gx.shape[1]
     scr[:, :n, :] = own[:, :n, :] + gy[:, :n, :].astype(F32)
     late = gx[...].astype(F32) + gy[:, n:, :].astype(F32) + gxy[...].astype(F32)
     scr[:, n:, :] = own[:, n:, :] + late
     out[...] = scr[z]
     for k, ref in ((1, s1), (2, s2), (3, s3)):
-        ref[...] = rounded(scr[z ^ k], me_ref[0] == 3)
-
-
-def sum_kernel(me_ref, own, g1, g2, g3, out, send):
+        ref[...] = rounded(scr[(z + k) & 3], lax.axis_index("rows") == 3)
+
+
+def sum_kernel(own, g1, g2, g3, out, send):
     total = own[...] + g1[...].astype(F32) + g2[...].astype(F32) + g3[...].astype(F32)
     out[...] = total
-    send[...] = rounded(total, me_ref[0] == 3)
-
-
-def last_kernel(chunk, me_ref, q0, q1, q2, q3, down, conv, cb, ga, sh, db, scr):
-    me = me_ref[0]
+    send[...] = rounded(total, lax.axis_index("rows") == 3)
+
+
+def last_kernel(chunk, q0, q1, q2, q3, down, conv, cb, ga, sh, db, scr):
+    me = lax.axis_index("rows")
     for k, ref in enumerate((q0, q1, q2, q3)):
         scr[me ^ k] = ref[...].astype(F32)
     wide = 2 * chunk
@@ -424,6 +424,11 @@
     return lax.ppermute(x, axis, [(i, i ^ k) for i in range(lax.axis_size(axis))])
 
 
+def around(x, k):
+    n = lax.axis_size("dp")
+    return lax.ppermute(x, "dp", [(i, (i + 2 * k) % n) for i in range(n)])
+
+
 def swap_both(x, k_rows, k_dp):
     both = ("rows", "dp")
     k = k_rows * lax.axis_size("dp") + k_dp
@@ -439,16 +444,13 @@
     count = float(rows * cols * width * ranks)
     chunk, wide = chans // owners, outs // owners
     packed = ranks == 4 and owners == 8 and chunk == 16 and wide == 32
-    me = lax.axis_index("rows").astype(jnp.int32).reshape(1)
-    owner = lax.axis_index("dp").astype(jnp.int32).reshape(1)
-    smem = pl.BlockSpec(memory_space=pltpu.SMEM)
     vmem = pl.BlockSpec(memory_space=pltpu.VMEM)
     hbm = pl.BlockSpec(memory_space=pltpu.HBM)
 
     def run(kernel, args, outs, scratch=(), specs=None, cost=1 << 27):
         return pl.pallas_call(
             kernel,
-            in_specs=specs or [smem if a is me or a is owner else vmem for a in args],
+            in_specs=specs or [vmem] * len(args),
             out_shape=[jax.ShapeDtypeStruct(s, d) for s, d in outs],
             out_specs=[vmem] * len(outs),
             scratch_shapes=list(scratch),
@@ -463,7 +465,7 @@
     row_scr = pltpu.VMEM((cols, chans), F32)
     block_of = (2, 2, half, chans)
     tile = ((8, chans), F32)
-    (ahead,) = run(first_kernel, (me,), [tile], cost=1 << 34)
+    (ahead,) = run(first_kernel, (), [tile], cost=1 << 34)
     raw = (
         img,
         conv_weight,
@@ -484,14 +486,14 @@
     chip_cot, core_cot = across(cot), swap(cot, "rows", 1)
     x, hid, stat = run(
         functools.partial(hidden_kernel, width),
-        (me, core_img, chip_img, own_x, w, bias),
+        (core_img, chip_img, own_x, w, bias),
         [((4, 2, half, chans), BF16), (block_of, F32), tile],
         [row_scr],
     )
     stats = with_swaps(stat, stat)
     hid_edge, gm = run(
         edge_kernel,
-        (me, core_img, chip_img, x, w, bias, core_cot, chip_cot, dw, own_gm),
+        (core_img, chip_img, x, w, bias, core_cot, chip_cot, dw, own_gm),
         [(block_of, F32), ((4, 2, half, chans), F32)],
         [row_scr],
     )
@@ -507,7 +509,7 @@
 
     mix_top, *down_grad = run(
         functools.partial(down_kernel, packed),
-        (me, par, x, hid_edge, gain, shift, mix, cot),
+        (par, x, hid_edge, gain, shift, mix, cot),
         [((half, 3 * chans), BF16)]
         + (
             [((outs, chans), F32), ((2,) + early_shape, F32), ((2,) + early_shape, BF16)]
@@ -518,13 +520,13 @@
     if packed:
         dlast, keep, send = down_grad
         early_own, early_send, ahead = run(
-            early_kernel, (me, keep, swap(send, "rows", 1)), [(early_shape, F32), (early_shape, BF16), tile]
+            early_kernel, (keep, swap(send, "rows", 1)), [(early_shape, F32), (early_shape, BF16), tile]
         )
         early_got = swap(early_send, "rows", 2)
     block, block_done = run(block_kernel, (ahead, mix_top, mix, dw, dbias), [((half, outs), BF16), tile])
     par2, g, *conv_grad = run(
         functools.partial(back_kernel, width, count, ranks, packed),
-        (me, *all_sums, par, x, hid, gp, gain, block_done) + ((dlast, cbias) if packed else ()),
+        (*all_sums, par, x, hid, gp, gain, block_done) + ((dlast, cbias) if packed else ()),
         [tile, (block_of, BF16)]
         + (
             [((2,) + late_shape, F32)] + [((2, owners // 2, 3 * chunk, chans), BF16)] * 2
@@ -535,7 +537,7 @@
     )
     gi, done = run(
         functools.partial(image_kernel, ranks - 1),
-        (me, par, hid_edge, gm, gain, shift, par2, g, w),
+        (par, hid_edge, gm, gain, shift, par2, g, w),
         [((rows, cols, chans), BF16), tile],
         [row_scr],
     )
@@ -545,31 +547,31 @@
         late_cut, both_cut = (zs, 3 * chunk, chans), (zs, deep, chans)
         own, sx, sy, sxy = run(
             late_kernel,
-            (me, owner, keep, *[swap(send, "rows", 1) for send in sends], early_own, early_got),
+            (keep, *[swap(send, "rows", 1) for send in sends], early_own, early_got),
             [(both_cut, F32), (late_cut, BF16), (both_cut, BF16), (late_cut, BF16)],
         )
         gxy = swap_both(sxy, 2, 1)
         gx, gy = swap(sx, "rows", 2), swap(sy, "dp", 1)
         part, *sends = run(
             pack_kernel,
-            (me, owner, own, gx, gy, gxy, done),
+            (own, gx, gy, gxy, done),
             [((deep, chans), F32)] + [((deep, chans), BF16)] * 3,
             [pltpu.VMEM(both_cut, F32)],
         )
         part, send = run(
             sum_kernel,
-            (me, part, *[swap(sends[k], "dp", 2 * k + 2) for k in (1, 2, 0)]),
+            (part, *[around(sends[k - 1], k) for k in (1, 2, 3)]),
             [((deep, chans), F32), ((deep, chans), BF16)],
         )
         down, conv, cb, ga, sh, db = run(
             functools.partial(last_kernel, chunk),
-            (me, *with_swaps(part, send)),
+            with_swaps(part, send),
             [((9, wide, chans), F32), ((9, chunk, chans), F32)] + [((1, chunk), F32)] * 3 + [((1, wide), F32)],
             [pltpu.VMEM((4, deep, chans), F32)],
         )
     else:
         totals = lax.psum((down_grad[0], conv_grad[0], conv_grad[1], cbias[:1]), ("rows", "dp"))
-        owner = owner[0]
+        owner = lax.axis_index("dp")
         down = totals[0].reshape(outs, 9, chans).transpose(1, 0, 2)
         down = lax.dynamic_slice_in_dim(down, owner * wide, wide, 1)
         conv = totals[1].reshape(3, chans, 3, chans).transpose(2, 0, 1, 3).reshape(9, chans, chans)

time: 46 us -> 45.9 us (level)
  starting transfers between devices: 22.1 us -> 24.1 us
  waiting for transfers between devices: 13.7 us -> 12.2 us
  local copies, waits for them, and re-layouts: 1.19 us -> 0.65 us
    ppermute x0 -> x3, starting transfers between devices: none -> 5.57 us  [around(): return lax.ppermute(x, 'dp', [(i, (i + 2 * k) % n) for i in range(n)])]
    ppermute x20 -> x17, waiting for transfers between devices: 11.8 us -> 7.86 us  [swap(): lax.ppermute(x, axis, [(i, i ^ k) for i in range(lax.axis_size(axis))])]
    ppermute x20 -> x17, starting transfers between devices: 19.8 us -> 16.1 us  [swap(): lax.ppermute(x, axis, [(i, i ^ k) for i in range(lax.axis_size(axis))])]
    ppermute x0 -> x3, waiting for transfers between devices: none -> 2.52 us  [around(): return lax.ppermute(x, 'dp', [(i, (i + 2 * k) % n) for i in range(n)])]
    unnamed x16, local copies, waits for them, and re-layouts: 1.19 us -> 0.65 us
  transfers between devices with their start and end apart: 23 -> 23, of which waited for: 12 -> 13; matrix products, arithmetic and copies ran while one was open for 0% -> 0% of each run, Pallas kernels for 14% -> 14%
where the time goes in v5:
time: 45.9 us; the launch traced here: 45.7 us
  starting transfers between devices  24.1 us (53%)
  waiting for transfers between devices  12.2 us (27%)
  Pallas kernels  7.94 us (17%)
  between operations  0.86 us (2%)
  local copies, waits for them, and re-layouts  0.65 us (1%)
    ppermute x17, starting transfers between devices, swap(): lax.ppermute(x, axis, [(i, i ^ k) for i in range(lax.axis_size(axis))])  16.1 us
    pallas_call x14, Pallas kernels, run(): pl.pallas_call(kernel, in_specs=specs or [vmem] * len(args), out_shape=[j...  7.94 us
    ppermute x17, waiting for transfers between devices, swap(): lax.ppermute(x, axis, [(i, i ^ k) for i in range(lax.axis_size(axis))])  7.86 us
    ppermute x3, starting transfers between devices, around(): return lax.ppermute(x, 'dp', [(i, (i + 2 * k) % n) for i in range(n)])  5.57 us
    ppermute x3, waiting for transfers between devices, around(): return lax.ppermute(x, 'dp', [(i, (i + 2 * k) % n) for i in range(n)])  2.52 us
    ppermute x1, waiting for transfers between devices, swap_both(): lax.ppermute(x, both, [(i, i ^ k) for i in range(lax.axis_size(both))])  1.77 us
    ppermute x2, starting transfers between devices, across(): lax.ppermute(x, 'rows', [p for i in range(1, n - 1, 2) for p in ((i, i +...  1.32 us
    ppermute x1, starting transfers between devices, swap_both(): lax.ppermute(x, both, [(i, i ^ k) for i in range(lax.axis_size(both))])  1.09 us
  transfers between devices with their start and end apart: 23, of which 13 were waited for; matrix products, arithmetic and copies ran while one was open for 0% of the time, Pallas kernels for 14%

profile of v5, /device:TPU:0, one launch (start us, length us, event | category | flops | bytes accessed | tf_op | source)
XLA Modules:
  0.0 45.7 jit_solution(6870309542897328941)
XLA Ops:
  0.7 0.5 %collective-permute-start = (bf16[2,512,128]{2,1,0:T(8,128)(2,1)}, bf16[2,512,128]{2,1,0:T(8,128)(2,1)S(1)}, u32[]{:S(2)}, u32[]{:S(2)}) collective-permute-start(bf16[2,512,128]{2,1,0:T(8,128)(2,1)} %bitcast.18), channel_id=1, source_target_pairs={{0,8},{8,0},{16,24},{24,16},{1,9},{9,1},{17,25},{25,17},{2,10},{10... | collective-permute-start | bytes 786440 | tf_op jit(solution)/shard_map/ppermute | solution.py:424
  1.2 0.7 %collective-permute-start.1 = (bf16[2,512,128]{2,1,0:T(8,128)(2,1)}, bf16[2,512,128]{2,1,0:T(8,128)(2,1)S(1)}, u32[]{:S(2)}, u32[]{:S(2)}) collective-permute-start(bf16[2,512,128]{2,1,0:T(8,128)(2,1)} %bitcast.19), channel_id=1, source_target_pairs={{8,16},{16,8},{9,17},{17,9},{10,18},{18,10},{11,19},{19,11},{12,20... | collective-permute-start | bytes 786440 | tf_op jit(solution)/shard_map/ppermute | solution.py:420
  1.9 0.0 copy-start.4
  1.9 0.0 copy-start.5
  1.9 0.0 copy-done
  1.9 0.0 copy-done.1
  2.0 0.6 %copy-done.6 = f32[128]{0:T(128)S(1)} copy-done((f32[128]{0:T(128)S(1)}, f32[128]{0:T(128)}, u32[]{:S(2)}) %copy-start.6) | copy-done | bytes 536
  2.5 0.0 copy-done.7
  2.5 0.0 copy-done.4
  2.6 0.9 %shard_map.144 = (bf16[3,3,128,128]{3,2,1,0:T(8,128)(2,1)S(1)}, bf16[3,3,128,256]{3,2,1,0:T(8,128)(2,1)S(1)}, bf16[256,256]{1,0:T(8,128)(2,1)S(1)}, f32[1,128]{1...) custom-call(f32[8,128]{1,0:T(8,128)S(1)} %shard_map.143.ahead, ...), custom_call_target="tpu_custom_call" | custom-call | flops 134217728 | bytes 1024 | tf_op jit(solution)/shard_map/pallas_call | solution.py:451
  3.5 4.1 %collective-permute-start.5 = (bf16[256,256]{1,0:T(8,128)(2,1)S(1)}, bf16[256,256]{1,0:T(8,128)(2,1)S(1)}, u32[]{:S(2)}, u32[]{:S(2)}) collective-permute-start(bf16[256,256]{1,0:T(8,128)(2,1)S(1)} %get-tuple-element.65.cot), channel_id=1, source_target_pairs={{0,8},{8,0},{16,24},{24,16},{1,9},{9,1},{17,25},{25,17},{2,10},{10... | collective-permute-start | bytes 393224 | tf_op jit(solution)/shard_map/ppermute | solution.py:424
  7.5 0.7 %collective-permute-start.6 = (bf16[256,256]{1,0:T(8,128)(2,1)S(1)}, bf16[256,256]{1,0:T(8,128)(2,1)S(1)}, u32[]{:S(2)}, u32[]{:S(2)}) collective-permute-start(bf16[256,256]{1,0:T(8,128)(2,1)S(1)} %get-tuple-element.65.cot), channel_id=1, source_target_pairs={{8,16},{16,8},{9,17},{17,9},{10,18},{18,10},{11,19},{19,11},{12,20... | collective-permute-start | bytes 393224 | tf_op jit(solution)/shard_map/ppermute | solution.py:420
  8.2 0.0 collective-permute-done.core
  8.2 0.0 collective-permute-done.1.chip
  8.2 1.1 %shard_map.145 = (bf16[4,2,256,128]{3,2,1,0:T(8,128)(2,1)S(1)}, f32[2,2,256,128]{3,2,1,0:T(8,128)S(1)}, f32[8,128]{1,0:T(8,128)S(1)}) custom-call(bf16[2,512,128]{2,1,0:T(8,128)(2,1)S(1)} %collective-permute-done.core, bf16[2,512,128]{2,1,0:T(8,128)(2,1)S(1)} %collective-permute-done.1.chip, bf16[2,2,256,128]{3,2,1,0:T(8,128)(2,1)S(1)} %get-tuple-element.59.own, ...), custom_call_target="tpu_custom_call" | custom-call | flops 134217728 | bytes 1024 | tf_op jit(solution)/shard_map/pallas_call | solution.py:451
  9.3 1.9 %collective-permute-start.2 = (f32[8,128]{1,0:T(8,128)S(1)}, f32[8,128]{1,0:T(8,128)S(1)}, u32[]{:S(2)}, u32[]{:S(2)}) collective-permute-start(f32[8,128]{1,0:T(8,128)S(1)} %get-tuple-element.62.refs_0_), channel_id=1, source_target_pairs={{0,8},{8,0},{16,24},{24,16},{1,9},{9,1},{17,25},{25,17},{2,10},{10... | collective-permute-start | bytes 12296 | tf_op jit(solution)/shard_map/ppermute | solution.py:424
  11.2 1.6 %collective-permute-start.3 = (f32[8,128]{1,0:T(8,128)S(1)}, f32[8,128]{1,0:T(8,128)S(1)}, u32[]{:S(2)}, u32[]{:S(2)}) collective-permute-start(f32[8,128]{1,0:T(8,128)S(1)} %get-tuple-element.62.refs_0_), channel_id=1, source_target_pairs={{0,16},{8,24},{16,0},{24,8},{1,17},{9,25},{17,1},{25,9},{2,18},{10... | collective-permute-start | bytes 12296 | tf_op jit(solution)/shard_map/ppermute | solution.py:424
  12.9 0.1 collective-permute-start.4
  13.0 0.0 collective-permute-done.5.cot_core
  13.0 0.0 collective-permute-done.6.cot_chip
  13.0 0.8 %shard_map.146 = (f32[2,2,256,128]{3,2,1,0:T(8,128)S(1)}, f32[4,2,256,128]{3,2,1,0:T(8,128)S(1)}) custom-call(bf16[2,512,128]{2,1,0:T(8,128)(2,1)S(1)} %collective-permute-done.core, bf16[2,512,128]{2,1,0:T(8,128)(2,1)S(1)} %collective-permute-done.1.chip, bf16[4,2,256,128]{3,2,1,0:T(8,128)(2,1)S(1)} %get-tuple-element.63.x.refs_4_.refs_5_, ...), custom_call_target="tpu_custom_call" | custom-call | flops 134217728 | bytes 1024 | tf_op jit(solution)/shard_map/pallas_call | solution.py:451
  13.8 0.0 collective-permute-done.2.refs_1_
  13.8 1.0 %collective-permute-done.3.refs_2_ = f32[8,128]{1,0:T(8,128)S(1)} collective-permute-done((f32[8,128]{1,0:T(8,128)S(1)}, f32[8,128]{1,0:T(8,128)S(1)}, u32[]{:S(2)}, u32[]{:S(2)}) %collective-permute-start.3) | collective-permute-done | bytes 4128 | tf_op jit(solution)/shard_map/ppermute | solution.py:424
  14.8 1.1 %collective-permute-done.4.refs_3_ = f32[8,128]{1,0:T(8,128)S(1)} collective-permute-done((f32[8,128]{1,0:T(8,128)S(1)}, f32[8,128]{1,0:T(8,128)S(1)}, u32[]{:S(2)}, u32[]{:S(2)}) %collective-permute-start.4) | collective-permute-done | bytes 4128 | tf_op jit(solution)/shard_map/ppermute | solution.py:424
  15.9 0.4 shard_map.147
  16.3 0.4 shard_map.148
  16.7 0.3 collective-permute-start.7
  17.0 0.5 %collective-permute-start.10 = (f32[8,128]{1,0:T(8,128)S(1)}, f32[8,128]{1,0:T(8,128)S(1)}, u32[]{:S(2)}, u32[]{:S(2)}) collective-permute-start(f32[8,128]{1,0:T(8,128)S(1)} %get-tuple-element.80.refs_0_), channel_id=1, source_target_pairs={{0,24},{8,16},{16,8},{24,0},{1,25},{9,17},{17,9},{25,1},{2,26},{10... | collective-permute-start | bytes 12296 | tf_op jit(solution)/shard_map/ppermute | solution.py:424
  17.5 0.1 collective-permute-start.8
  17.6 1.5 %collective-permute-start.9 = (f32[8,128]{1,0:T(8,128)S(1)}, f32[8,128]{1,0:T(8,128)S(1)}, u32[]{:S(2)}, u32[]{:S(2)}) collective-permute-start(f32[8,128]{1,0:T(8,128)S(1)} %get-tuple-element.80.refs_0_), channel_id=1, source_target_pairs={{0,16},{8,24},{16,0},{24,8},{1,17},{9,25},{17,1},{25,9},{2,18},{10... | collective-permute-start | bytes 12296 | tf_op jit(solution)/shard_map/ppermute | solution.py:424
  19.1 0.0 collective-permute-done.7.got
  19.2 0.6 %collective-permute-start.13 = (bf16[2,8,32,128]{3,2,1,0:T(8,128)(2,1)S(1)}, bf16[2,8,32,128]{3,2,1,0:T(8,128)(2,1)S(1)}, u32[]{:S(2)}, u32[]{:S(2)}) collective-permute-start(bf16[2,8,32,128]{3,2,1,0:T(8,128)(2,1)S(1)} %get-tuple-element.92), channel_id=1, source_target_pairs={{0,16},{8,24},{16,0},{24,8},{1,17},{9,25},{17,1},{25,9},{2,18},{10... | collective-permute-start | bytes 393224 | tf_op jit(solution)/shard_map/ppermute | solution.py:424
  19.8 1.0 %shard_map.150 = (bf16[256,256]{1,0:T(8,128)(2,1)}, f32[8,128]{1,0:T(8,128)S(1)}) custom-call(f32[8,128]{1,0:T(8,128)S(1)} %get-tuple-element.76.ahead, bf16[256,384]{1,0:T(8,128)(2,1)S(1)} %get-tuple-element.77.mix_top, bf16[2,256,384]{2,1,0:T(8,128)(2,1)S(1)} %get-tuple-element.73.mix, bf16[3,3,128,256]{3,2,1,0:T(8,128)(2,1)S(1)} %get-tuple-element.66.dw, ...), custom_call_target="tpu_custom_call" | custom-call | flops 134217728 | bytes 1024 | tf_op jit(solution)/shard_map/pallas_call | solution.py:451
  20.8 0.0 collective-permute-done.10.refs_3_
  20.8 0.0 collective-permute-done.8.refs_1_
  20.8 0.4 collective-permute-done.9.refs_2_
  21.2 0.9 %shard_map.151 = (f32[8,128]{1,0:T(8,128)S(1)}, bf16[2,2,256,128]{3,2,1,0:T(8,128)(2,1)S(1)}, f32[2,8,48,128]{3,2,1,0:T(8,128)S(1)}, bf16[2,4,48,128]{3,2,1,0:T(8,128)(2,1)S(1)}, bf16[2,4,48,128]{3,2,1,0:T(8,128)(2,1)S(1)}) custom-call(f32[8,128]{1,0:T(8,128)S(1)} %get-tuple-element.80.refs_0_, f32[8,128]{1,0:T(8,128)S(1)} %collective-permute-done.8.refs_1_, ...), custom_call_target="tpu_custom_call" | custom-call | flops 4294967296 | bytes 1024 | tf_op jit(solution)/shard_map/pallas_call | solution.py:451
  22.1 0.1 collective-permute-start.11
  22.2 0.5 %collective-permute-start.12 = (bf16[2,4,48,128]{3,2,1,0:T(8,128)(2,1)S(1)}, bf16[2,4,48,128]{3,2,1,0:T(8,128)(2,1)S(1)}, u32[]{:S(2)}, u32[]{:S(2)}) collective-permute-start(bf16[2,4,48,128]{3,2,1,0:T(8,128)(2,1)S(1)} %get-tuple-element.90), channel_id=1, source_target_pairs={{0,8},{8,0},{16,24},{24,16},{1,9},{9,1},{17,25},{25,17},{2,10},{10... | collective-permute-start | bytes 294920 | tf_op jit(solution)/shard_map/ppermute | solution.py:424
  22.7 0.8 %collective-permute-done.11.got0 = bf16[2,4,48,128]{3,2,1,0:T(8,128)(2,1)S(1)} collective-permute-done((bf16[2,4,48,128]{3,2,1,0:T(8,128)(2,1)S(1)}, bf16[2,4,48,128]{3,2,1,0:T(8,128)(2,1)S(1)}, u32[]{:S(2)}, u32[]{:S(2)}) %collective-permute-start.11) | collective-permute-done | bytes 98336 | tf_op jit(solution)/shard_map/ppermute | solution.py:424
  23.4 0.2 collective-permute-done.12.got1
  23.6 1.1 %collective-permute-done.13.e_got = bf16[2,8,32,128]{3,2,1,0:T(8,128)(2,1)S(1)} collective-permute-done((bf16[2,8,32,128]{3,2,1,0:T(8,128)(2,1)S(1)}, bf16[2,8,32,128]{3,2,1,0:T(8,128)(2,1)S(1)}, u32[]{:S(2)}, u32[]{:S(2)}) %collective-permute-start.13) | collective-permute-done | bytes 131104 | tf_op jit(solution)/shard_map/ppermute | solution.py:424
  24.7 0.1 shard_map.153
  24.8 1.6 %collective-permute-start.15 = (bf16[4,112,128]{2,1,0:T(8,128)(2,1)S(1)}, bf16[4,112,128]{2,1,0:T(8,128)(2,1)S(1)}, u32[]{:S(2)}, u32[]{:S(2)}) collective-permute-start(bf16[4,112,128]{2,1,0:T(8,128)(2,1)S(1)} %get-tuple-element.95), channel_id=1, source_target_pairs={{0,1},{1,0},{2,3},{3,2},{4,5},{5,4},{6,7},{7,6},{8,9},{9,8},{10,11... | collective-permute-start | bytes 344072 | tf_op jit(solution)/shard_map/ppermute | solution.py:424
  26.4 0.9 %collective-permute-start.14 = (bf16[4,48,128]{2,1,0:T(8,128)(2,1)S(1)}, bf16[4,48,128]{2,1,0:T(8,128)(2,1)S(1)}, u32[]{:S(2)}, u32[]{:S(2)}) collective-permute-start(bf16[4,48,128]{2,1,0:T(8,128)(2,1)S(1)} %get-tuple-element.94), channel_id=1, source_target_pairs={{0,16},{8,24},{16,0},{24,8},{1,17},{9,25},{17,1},{25,9},{2,18},{10... | collective-permute-start | bytes 147464 | tf_op jit(solution)/shard_map/ppermute | solution.py:424
  27.2 1.1 %collective-permute-start.16 = (bf16[4,48,128]{2,1,0:T(8,128)(2,1)S(1)}, bf16[4,48,128]{2,1,0:T(8,128)(2,1)S(1)}, u32[]{:S(2)}, u32[]{:S(2)}) collective-permute-start(bf16[4,48,128]{2,1,0:T(8,128)(2,1)S(1)} %get-tuple-element.96), channel_id=1, source_target_pairs={{0,17},{1,16},{2,19},{3,18},{4,21},{5,20},{6,23},{7,22},{8,25},{9,... | collective-permute-start | bytes 147464 | tf_op jit(solution)/shard_map/ppermute | solution.py:435
  28.3 1.5 %shard_map.152 = (bf16[2,512,128]{2,1,0:T(8,128)(2,1)}, f32[8,128]{1,0:T(8,128)S(1)}) custom-call(f32[8,128]{1,0:T(8,128)S(1)} %get-tuple-element.71.par.refs_4_, f32[2,2,256,128]{3,2,1,0:T(8,128)S(1)} %get-tuple-element.72.hid, f32[4,2,256,128]{3,2,1,0:T(8,128)S(1)} %get-tuple-element.68.refs_6_.gm, f32[1,128]{1,0:T(1,128)S(1)} %get-tuple-element.69.refs_7_.gain.refs_8_, ...), custom_call_target="tpu_custom_call" | custom-call | flops 134217728 | bytes 1024 | tf_op jit(solution)/shard_map/pallas_call | solution.py:451
  29.8 0.7 %collective-permute-done.14.gx = bf16[4,48,128]{2,1,0:T(8,128)(2,1)S(1)} collective-permute-done((bf16[4,48,128]{2,1,0:T(8,128)(2,1)S(1)}, bf16[4,48,128]{2,1,0:T(8,128)(2,1)S(1)}, u32[]{:S(2)}, u32[]{:S(2)}) %collective-permute-start.14) | collective-permute-done | bytes 49184 | tf_op jit(solution)/shard_map/ppermute | solution.py:424
  30.5 1.8 %collective-permute-done.16.gxy = bf16[4,48,128]{2,1,0:T(8,128)(2,1)S(1)} collective-permute-done((bf16[4,48,128]{2,1,0:T(8,128)(2,1)S(1)}, bf16[4,48,128]{2,1,0:T(8,128)(2,1)S(1)}, u32[]{:S(2)}, u32[]{:S(2)}) %collective-permute-start.16) | collective-permute-done | bytes 49184 | tf_op jit(solution)/shard_map/ppermute | solution.py:435
  32.2 0.0 collective-permute-done.15.gy
  32.2 0.1 shard_map.154
  32.3 1.6 %collective-permute-start.17 = (bf16[112,128]{1,0:T(8,128)(2,1)S(1)}, bf16[112,128]{1,0:T(8,128)(2,1)S(1)}, u32[]{:S(2)}, u32[]{:S(2)}) collective-permute-start(bf16[112,128]{1,0:T(8,128)(2,1)S(1)} %get-tuple-element.99), channel_id=1, source_target_pairs={{0,2},{1,3},{2,4},{3,5},{4,6},{5,7},{6,0},{7,1},{8,10},{9,11},{10,... | collective-permute-start | bytes 86024 | tf_op jit(solution)/shard_map/ppermute | solution.py:429
  33.9 2.6 %collective-permute-start.18 = (bf16[112,128]{1,0:T(8,128)(2,1)S(1)}, bf16[112,128]{1,0:T(8,128)(2,1)S(1)}, u32[]{:S(2)}, u32[]{:S(2)}) collective-permute-start(bf16[112,128]{1,0:T(8,128)(2,1)S(1)} %get-tuple-element.100), channel_id=1, source_target_pairs={{0,4},{1,5},{2,6},{3,7},{4,0},{5,1},{6,2},{7,3},{8,12},{9,13},{10,... | collective-permute-start | bytes 86024 | tf_op jit(solution)/shard_map/ppermute | solution.py:429
  36.5 1.3 %collective-permute-start.19 = (bf16[112,128]{1,0:T(8,128)(2,1)S(1)}, bf16[112,128]{1,0:T(8,128)(2,1)S(1)}, u32[]{:S(2)}, u32[]{:S(2)}) collective-permute-start(bf16[112,128]{1,0:T(8,128)(2,1)S(1)} %get-tuple-element.101), channel_id=1, source_target_pairs={{0,6},{1,7},{2,0},{3,1},{4,2},{5,3},{6,4},{7,5},{8,14},{9,15},{10,... | collective-permute-start | bytes 86024 | tf_op jit(solution)/shard_map/ppermute | solution.py:429
  37.9 0.2 collective-permute-done.17.g1
  38.0 0.7 %collective-permute-done.18.g2 = bf16[112,128]{1,0:T(8,128)(2,1)S(1)} collective-permute-done((bf16[112,128]{1,0:T(8,128)(2,1)S(1)}, bf16[112,128]{1,0:T(8,128)(2,1)S(1)}, u32[]{:S(2)}, u32[]{:S(2)}) %collective-permute-start.18) | collective-permute-done | bytes 28704 | tf_op jit(solution)/shard_map/ppermute | solution.py:429
  38.7 1.7 %collective-permute-done.19.g3 = bf16[112,128]{1,0:T(8,128)(2,1)S(1)} collective-permute-done((bf16[112,128]{1,0:T(8,128)(2,1)S(1)}, bf16[112,128]{1,0:T(8,128)(2,1)S(1)}, u32[]{:S(2)}, u32[]{:S(2)}) %collective-permute-start.19) | collective-permute-done | bytes 28704 | tf_op jit(solution)/shard_map/ppermute | solution.py:429
  40.4 0.1 collective-permute-start.20
  40.5 1.2 %collective-permute-start.21 = (bf16[112,128]{1,0:T(8,128)(2,1)S(1)}, bf16[112,128]{1,0:T(8,128)(2,1)S(1)}, u32[]{:S(2)}, u32[]{:S(2)}) collective-permute-start(bf16[112,128]{1,0:T(8,128)(2,1)S(1)} %get-tuple-element.103), channel_id=1, source_target_pairs={{0,16},{8,24},{16,0},{24,8},{1,17},{9,25},{17,1},{25,9},{2,18},{10... | collective-permute-start | bytes 86024 | tf_op jit(solution)/shard_map/ppermute | solution.py:424
  41.7 0.6 %collective-permute-start.22 = (bf16[112,128]{1,0:T(8,128)(2,1)S(1)}, bf16[112,128]{1,0:T(8,128)(2,1)S(1)}, u32[]{:S(2)}, u32[]{:S(2)}) collective-permute-start(bf16[112,128]{1,0:T(8,128)(2,1)S(1)} %get-tuple-element.103), channel_id=1, source_target_pairs={{0,24},{8,16},{16,8},{24,0},{1,25},{9,17},{17,9},{25,1},{2,26},{10... | collective-permute-start | bytes 86024 | tf_op jit(solution)/shard_map/ppermute | solution.py:424
  42.4 0.0 collective-permute-done.20.q1
  42.4 2.1 %collective-permute-done.21.q2 = bf16[112,128]{1,0:T(8,128)(2,1)S(1)} collective-permute-done((bf16[112,128]{1,0:T(8,128)(2,1)S(1)}, bf16[112,128]{1,0:T(8,128)(2,1)S(1)}, u32[]{:S(2)}, u32[]{:S(2)}) %collective-permute-start.21) | collective-permute-done | bytes 28704 | tf_op jit(solution)/shard_map/ppermute | solution.py:424
  44.4 0.6 %collective-permute-done.22.q3 = bf16[112,128]{1,0:T(8,128)(2,1)S(1)} collective-permute-done((bf16[112,128]{1,0:T(8,128)(2,1)S(1)}, bf16[112,128]{1,0:T(8,128)(2,1)S(1)}, u32[]{:S(2)}, u32[]{:S(2)}) %collective-permute-start.22) | collective-permute-done | bytes 28704 | tf_op jit(solution)/shard_map/ppermute | solution.py:424
  45.0 0.7 %shard_map.156 = (f32[9,32,128]{2,1,0:T(8,128)}, f32[9,16,128]{2,1,0:T(8,128)}, f32[1,16]{1,0:T(1,128)}, f32[1,16]{1,0:T(1,128)}, f32[1,16]{1,0:T(1,128)}, /*index=5*/f32[1,32]{1,0:T(1,128)}) custom-call(f32[112,128]{1,0:T(8,128)S(1)} %get-tuple-element.102.q0, bf16[112,128]{1,0:T(8,128)(2,1)S(1)} %collective-permute-done.20.q1, ...), custom_call_target="tpu_custom_call" | custom-call | flops 134217728 | bytes 1024 | tf_op jit(solution)/shard_map/pallas_call | solution.py:451
  (12 shorter events, 0.1 us)
Async XLA Ops:
  0.6 1.3 %copy-start = (bf16[3,3,128,256]{3,2,1,0:T(8,128)(2,1)S(1)}, bf16[3,3,128,256]{3,2,1,0:T(8,128)(2,1)}, u32[]{:S(2)}) copy-start(bf16[3,3,128,256]{3,2,1,0:T(8,128)(2,1)} %dw.1) | copy-start | bytes 1769476
  0.6 1.3 %copy-start.1 = (bf16[3,3,128,128]{3,2,1,0:T(8,128)(2,1)S(1)}, bf16[3,3,128,128]{3,2,1,0:T(8,128)(2,1)}, u32[]{:S(2)}) copy-start(bf16[3,3,128,128]{3,2,1,0:T(8,128)(2,1)} %w.1) | copy-start | bytes 884740
  0.7 1.3 %copy-start.2 = (bf16[1,2,512,128]{3,2,1,0:T(8,128)(2,1)S(1)}, bf16[1,2,512,128]{3,2,1,0:T(8,128)(2,1)}, u32[]{:S(2)}) copy-start(bf16[1,2,512,128]{3,2,1,0:T(8,128)(2,1)} %param.8) | copy-start | bytes 786436
  0.7 1.3 %copy-start.3 = (bf16[1,1,256,256]{3,2,1,0:T(8,128)(2,1)S(1)}, bf16[1,1,256,256]{3,2,1,0:T(8,128)(2,1)}, u32[]{:S(2)}) copy-start(bf16[1,1,256,256]{3,2,1,0:T(8,128)(2,1)} %param.15) | copy-start | bytes 393220
  0.7 7.5 %collective-permute-start = (bf16[2,512,128]{2,1,0:T(8,128)(2,1)}, bf16[2,512,128]{2,1,0:T(8,128)(2,1)S(1)}, u32[]{:S(2)}, u32[]{:S(2)}) collective-permute-start(bf16[2,512,128]{2,1,0:T(8,128)(2,1)} %bitcast.18), channel_id=1, source_target_pairs={{0,8},{8,0},{16,24},{24,16},{1,9},{9,1},{17,25},{25,17},{2,10},{10... | collective-permute-start | bytes 786440 | tf_op jit(solution)/shard_map/ppermute | solution.py:424
  1.2 7.0 %collective-permute-start.1 = (bf16[2,512,128]{2,1,0:T(8,128)(2,1)}, bf16[2,512,128]{2,1,0:T(8,128)(2,1)S(1)}, u32[]{:S(2)}, u32[]{:S(2)}) collective-permute-start(bf16[2,512,128]{2,1,0:T(8,128)(2,1)} %bitcast.19), channel_id=1, source_target_pairs={{8,16},{16,8},{9,17},{17,9},{10,18},{18,10},{11,19},{19,11},{12,20... | collective-permute-start | bytes 786440 | tf_op jit(solution)/shard_map/ppermute | solution.py:420
  1.9 0.7 %copy-start.6 = (f32[128]{0:T(128)S(1)}, f32[128]{0:T(128)}, u32[]{:S(2)}) copy-start(f32[128]{0:T(128)} %param.11) | copy-start | bytes 1540
  1.9 0.7 %copy-start.7 = (f32[128]{0:T(128)S(1)}, f32[128]{0:T(128)}, u32[]{:S(2)}) copy-start(f32[128]{0:T(128)} %param.12) | copy-start | bytes 1540
  1.9 0.7 %copy-start.4 = (f32[256]{0:T(256)S(1)}, f32[256]{0:T(256)}, u32[]{:S(2)}) copy-start(f32[256]{0:T(256)} %param.14) | copy-start | bytes 3076
  1.9 0.7 %copy-start.5 = (f32[128]{0:T(128)S(1)}, f32[128]{0:T(128)}, u32[]{:S(2)}) copy-start(f32[128]{0:T(128)} %param.10) | copy-start | bytes 1540
  3.5 9.5 %collective-permute-start.5 = (bf16[256,256]{1,0:T(8,128)(2,1)S(1)}, bf16[256,256]{1,0:T(8,128)(2,1)S(1)}, u32[]{:S(2)}, u32[]{:S(2)}) collective-permute-start(bf16[256,256]{1,0:T(8,128)(2,1)S(1)} %get-tuple-element.65.cot), channel_id=1, source_target_pairs={{0,8},{8,0},{16,24},{24,16},{1,9},{9,1},{17,25},{25,17},{2,10},{10... | collective-permute-start | bytes 393224 | tf_op jit(solution)/shard_map/ppermute | solution.py:424
  7.5 5.4 %collective-permute-start.6 = (bf16[256,256]{1,0:T(8,128)(2,1)S(1)}, bf16[256,256]{1,0:T(8,128)(2,1)S(1)}, u32[]{:S(2)}, u32[]{:S(2)}) collective-permute-start(bf16[256,256]{1,0:T(8,128)(2,1)S(1)} %get-tuple-element.65.cot), channel_id=1, source_target_pairs={{8,16},{16,8},{9,17},{17,9},{10,18},{18,10},{11,19},{19,11},{12,20... | collective-permute-start | bytes 393224 | tf_op jit(solution)/shard_map/ppermute | solution.py:420
  9.3 4.5 %collective-permute-start.2 = (f32[8,128]{1,0:T(8,128)S(1)}, f32[8,128]{1,0:T(8,128)S(1)}, u32[]{:S(2)}, u32[]{:S(2)}) collective-permute-start(f32[8,128]{1,0:T(8,128)S(1)} %get-tuple-element.62.refs_0_), channel_id=1, source_target_pairs={{0,8},{8,0},{16,24},{24,16},{1,9},{9,1},{17,25},{25,17},{2,10},{10... | collective-permute-start | bytes 12296 | tf_op jit(solution)/shard_map/ppermute | solution.py:424
  11.2 3.6 %collective-permute-start.3 = (f32[8,128]{1,0:T(8,128)S(1)}, f32[8,128]{1,0:T(8,128)S(1)}, u32[]{:S(2)}, u32[]{:S(2)}) collective-permute-start(f32[8,128]{1,0:T(8,128)S(1)} %get-tuple-element.62.refs_0_), channel_id=1, source_target_pairs={{0,16},{8,24},{16,0},{24,8},{1,17},{9,25},{17,1},{25,9},{2,18},{10... | collective-permute-start | bytes 12296 | tf_op jit(solution)/shard_map/ppermute | solution.py:424
  12.9 3.0 %collective-permute-start.4 = (f32[8,128]{1,0:T(8,128)S(1)}, f32[8,128]{1,0:T(8,128)S(1)}, u32[]{:S(2)}, u32[]{:S(2)}) collective-permute-start(f32[8,128]{1,0:T(8,128)S(1)} %get-tuple-element.62.refs_0_), channel_id=1, source_target_pairs={{0,24},{8,16},{16,8},{24,0},{1,25},{9,17},{17,9},{25,1},{2,26},{10... | collective-permute-start | bytes 12296 | tf_op jit(solution)/shard_map/ppermute | solution.py:424
  16.7 2.4 %collective-permute-start.7 = (bf16[2,2,8,32,128]{4,3,2,1,0:T(8,128)(2,1)S(1)}, bf16[2,2,8,32,128]{4,3,2,1,0:T(8,128)(2,1)S(1)}, u32[]{:S(2)}, u32[]{:S(2)}) collective-permute-start(bf16[2,2,8,32,128]{4,3,2,1,0:T(8,128)(2,1)S(1)} %get-tuple-element.75), channel_id=1, source_target_pairs={{0,8},{8,0},{16,24},{24,16},{1,9},{9,1},{17,25},{25,17},{2,10},{10... | collective-permute-start | bytes 786440 | tf_op jit(solution)/shard_map/ppermute | solution.py:424
  17.0 3.8 %collective-permute-start.10 = (f32[8,128]{1,0:T(8,128)S(1)}, f32[8,128]{1,0:T(8,128)S(1)}, u32[]{:S(2)}, u32[]{:S(2)}) collective-permute-start(f32[8,128]{1,0:T(8,128)S(1)} %get-tuple-element.80.refs_0_), channel_id=1, source_target_pairs={{0,24},{8,16},{16,8},{24,0},{1,25},{9,17},{17,9},{25,1},{2,26},{10... | collective-permute-start | bytes 12296 | tf_op jit(solution)/shard_map/ppermute | solution.py:424
  17.5 3.2 %collective-permute-start.8 = (f32[8,128]{1,0:T(8,128)S(1)}, f32[8,128]{1,0:T(8,128)S(1)}, u32[]{:S(2)}, u32[]{:S(2)}) collective-permute-start(f32[8,128]{1,0:T(8,128)S(1)} %get-tuple-element.80.refs_0_), channel_id=1, source_target_pairs={{0,8},{8,0},{16,24},{24,16},{1,9},{9,1},{17,25},{25,17},{2,10},{10... | collective-permute-start | bytes 12296 | tf_op jit(solution)/shard_map/ppermute | solution.py:424
  17.6 3.6 %collective-permute-start.9 = (f32[8,128]{1,0:T(8,128)S(1)}, f32[8,128]{1,0:T(8,128)S(1)}, u32[]{:S(2)}, u32[]{:S(2)}) collective-permute-start(f32[8,128]{1,0:T(8,128)S(1)} %get-tuple-element.80.refs_0_), channel_id=1, source_target_pairs={{0,16},{8,24},{16,0},{24,8},{1,17},{9,25},{17,1},{25,9},{2,18},{10... | collective-permute-start | bytes 12296 | tf_op jit(solution)/shard_map/ppermute | solution.py:424
  19.2 5.5 %collective-permute-start.13 = (bf16[2,8,32,128]{3,2,1,0:T(8,128)(2,1)S(1)}, bf16[2,8,32,128]{3,2,1,0:T(8,128)(2,1)S(1)}, u32[]{:S(2)}, u32[]{:S(2)}) collective-permute-start(bf16[2,8,32,128]{3,2,1,0:T(8,128)(2,1)S(1)} %get-tuple-element.92), channel_id=1, source_target_pairs={{0,16},{8,24},{16,0},{24,8},{1,17},{9,25},{17,1},{25,9},{2,18},{10... | collective-permute-start | bytes 393224 | tf_op jit(solution)/shard_map/ppermute | solution.py:424
  22.1 1.4 %collective-permute-start.11 = (bf16[2,4,48,128]{3,2,1,0:T(8,128)(2,1)S(1)}, bf16[2,4,48,128]{3,2,1,0:T(8,128)(2,1)S(1)}, u32[]{:S(2)}, u32[]{:S(2)}) collective-permute-start(bf16[2,4,48,128]{3,2,1,0:T(8,128)(2,1)S(1)} %get-tuple-element.89), channel_id=1, source_target_pairs={{0,8},{8,0},{16,24},{24,16},{1,9},{9,1},{17,25},{25,17},{2,10},{10... | collective-permute-start | bytes 294920 | tf_op jit(solution)/shard_map/ppermute | solution.py:424
  22.2 1.4 %collective-permute-start.12 = (bf16[2,4,48,128]{3,2,1,0:T(8,128)(2,1)S(1)}, bf16[2,4,48,128]{3,2,1,0:T(8,128)(2,1)S(1)}, u32[]{:S(2)}, u32[]{:S(2)}) collective-permute-start(bf16[2,4,48,128]{3,2,1,0:T(8,128)(2,1)S(1)} %get-tuple-element.90), channel_id=1, source_target_pairs={{0,8},{8,0},{16,24},{24,16},{1,9},{9,1},{17,25},{25,17},{2,10},{10... | collective-permute-start | bytes 294920 | tf_op jit(solution)/shard_map/ppermute | solution.py:424
  24.8 7.5 %collective-permute-start.15 = (bf16[4,112,128]{2,1,0:T(8,128)(2,1)S(1)}, bf16[4,112,128]{2,1,0:T(8,128)(2,1)S(1)}, u32[]{:S(2)}, u32[]{:S(2)}) collective-permute-start(bf16[4,112,128]{2,1,0:T(8,128)(2,1)S(1)} %get-tuple-element.95), channel_id=1, source_target_pairs={{0,1},{1,0},{2,3},{3,2},{4,5},{5,4},{6,7},{7,6},{8,9},{9,8},{10,11... | collective-permute-start | bytes 344072 | tf_op jit(solution)/shard_map/ppermute | solution.py:424
  26.4 4.1 %collective-permute-start.14 = (bf16[4,48,128]{2,1,0:T(8,128)(2,1)S(1)}, bf16[4,48,128]{2,1,0:T(8,128)(2,1)S(1)}, u32[]{:S(2)}, u32[]{:S(2)}) collective-permute-start(bf16[4,48,128]{2,1,0:T(8,128)(2,1)S(1)} %get-tuple-element.94), channel_id=1, source_target_pairs={{0,16},{8,24},{16,0},{24,8},{1,17},{9,25},{17,1},{25,9},{2,18},{10... | collective-permute-start | bytes 147464 | tf_op jit(solution)/shard_map/ppermute | solution.py:424
  27.2 5.0 %collective-permute-start.16 = (bf16[4,48,128]{2,1,0:T(8,128)(2,1)S(1)}, bf16[4,48,128]{2,1,0:T(8,128)(2,1)S(1)}, u32[]{:S(2)}, u32[]{:S(2)}) collective-permute-start(bf16[4,48,128]{2,1,0:T(8,128)(2,1)S(1)} %get-tuple-element.96), channel_id=1, source_target_pairs={{0,17},{1,16},{2,19},{3,18},{4,21},{5,20},{6,23},{7,22},{8,25},{9,... | collective-permute-start | bytes 147464 | tf_op jit(solution)/shard_map/ppermute | solution.py:435
  32.3 5.7 %collective-permute-start.17 = (bf16[112,128]{1,0:T(8,128)(2,1)S(1)}, bf16[112,128]{1,0:T(8,128)(2,1)S(1)}, u32[]{:S(2)}, u32[]{:S(2)}) collective-permute-start(bf16[112,128]{1,0:T(8,128)(2,1)S(1)} %get-tuple-element.99), channel_id=1, source_target_pairs={{0,2},{1,3},{2,4},{3,5},{4,6},{5,7},{6,0},{7,1},{8,10},{9,11},{10,... | collective-permute-start | bytes 86024 | tf_op jit(solution)/shard_map/ppermute | solution.py:429
  33.9 4.8 %collective-permute-start.18 = (bf16[112,128]{1,0:T(8,128)(2,1)S(1)}, bf16[112,128]{1,0:T(8,128)(2,1)S(1)}, u32[]{:S(2)}, u32[]{:S(2)}) collective-permute-start(bf16[112,128]{1,0:T(8,128)(2,1)S(1)} %get-tuple-element.100), channel_id=1, source_target_pairs={{0,4},{1,5},{2,6},{3,7},{4,0},{5,1},{6,2},{7,3},{8,12},{9,13},{10,... | collective-permute-start | bytes 86024 | tf_op jit(solution)/shard_map/ppermute | solution.py:429
  36.5 3.9 %collective-permute-start.19 = (bf16[112,128]{1,0:T(8,128)(2,1)S(1)}, bf16[112,128]{1,0:T(8,128)(2,1)S(1)}, u32[]{:S(2)}, u32[]{:S(2)}) collective-permute-start(bf16[112,128]{1,0:T(8,128)(2,1)S(1)} %get-tuple-element.101), channel_id=1, source_target_pairs={{0,6},{1,7},{2,0},{3,1},{4,2},{5,3},{6,4},{7,5},{8,14},{9,15},{10,... | collective-permute-start | bytes 86024 | tf_op jit(solution)/shard_map/ppermute | solution.py:429
  40.4 1.9 %collective-permute-start.20 = (bf16[112,128]{1,0:T(8,128)(2,1)S(1)}, bf16[112,128]{1,0:T(8,128)(2,1)S(1)}, u32[]{:S(2)}, u32[]{:S(2)}) collective-permute-start(bf16[112,128]{1,0:T(8,128)(2,1)S(1)} %get-tuple-element.103), channel_id=1, source_target_pairs={{0,8},{8,0},{16,24},{24,16},{1,9},{9,1},{17,25},{25,17},{2,10},{10... | collective-permute-start | bytes 86024 | tf_op jit(solution)/shard_map/ppermute | solution.py:424
  40.5 3.9 %collective-permute-start.21 = (bf16[112,128]{1,0:T(8,128)(2,1)S(1)}, bf16[112,128]{1,0:T(8,128)(2,1)S(1)}, u32[]{:S(2)}, u32[]{:S(2)}) collective-permute-start(bf16[112,128]{1,0:T(8,128)(2,1)S(1)} %get-tuple-element.103), channel_id=1, source_target_pairs={{0,16},{8,24},{16,0},{24,8},{1,17},{9,25},{17,1},{25,9},{2,18},{10... | collective-permute-start | bytes 86024 | tf_op jit(solution)/shard_map/ppermute | solution.py:424
  41.7 3.3 %collective-permute-start.22 = (bf16[112,128]{1,0:T(8,128)(2,1)S(1)}, bf16[112,128]{1,0:T(8,128)(2,1)S(1)}, u32[]{:S(2)}, u32[]{:S(2)}) collective-permute-start(bf16[112,128]{1,0:T(8,128)(2,1)S(1)} %get-tuple-element.103), channel_id=1, source_target_pairs={{0,24},{8,16},{16,8},{24,0},{1,25},{9,17},{17,9},{25,1},{2,26},{10... | collective-permute-start | bytes 86024 | tf_op jit(solution)/shard_map/ppermute | solution.py:424

commit v6 on v5

--- a/solution.py
+++ b/solution.py
@@ -141,11 +141,15 @@
     stat_out[1:2] = grouped(spread, width)
 
 
-def edge_kernel(core, chip, x, w, bias, cot_core, cot_chip, dw, own_gm, hid_out, gm_out, scr):
+def edge_kernel(core, chip, x, w, bias, cot_core, cot_chip, dw, own_gm, cbias, hid_out, gm_out, low_out, cb_out, scr):
     half = x.shape[2]
     odd_rank = (lax.axis_index("rows") & 1) == 1
     top = [v.astype(BF16) for v in split(scr, either(odd_rank, core[0], chip[0]))]
     low = [v.astype(BF16) for v in split(scr, either(odd_rank, chip[1], core[1]))]
+    low_out[0] = low[0]
+    low_out[1] = low[1]
+    both = jnp.sum(cot_core[...].astype(F32), axis=0, keepdims=True) + cbias[0:1]
+    cb_out[...] = jnp.broadcast_to(both, cb_out.shape)
     weights = conv_weights(w)
     even = stack(lanes(top[0], x[0, 0], x[1, 0]), lanes(x[2, 0], x[3, 0], low[0]))
     odd = stack(lanes(top[1], x[0, 1], x[1, 1]), lanes(x[2, 1], x[3, 1], low[1]))
@@ -166,7 +170,7 @@
 
 def norm_kernel(width, count, ranks, *refs):
     stats = refs[:ranks]
-    x, hid, gm, gain, shift, par_out, mix_out, gp_out, sum_out = refs[ranks:]
+    x, hid, gm, gain, shift, par_out, mix_out, gp_out, sum_out, far_out = refs[ranks:]
     half = x.shape[2]
     local = float(4 * half * width)
     mean = sum(s[0:1] for s in stats) / float(len(stats))
@@ -195,9 +199,13 @@
     sum_out[...] = jnp.zeros(sum_out.shape, F32)
     sum_out[0:1] = first
     sum_out[1:2] = second
-
-
-def down_kernel(packed, par, x, hid, gain, shift, mix, cot, top_out, *rest):
+    core = lax.axis_index("rows") & 1
+    far_out[0] = gp_out[core]
+    for c in range(2):
+        far_out[1, c] = hid[core, c] - mean
+
+
+def down_kernel(packed, par, x, hid, gain, shift, mix, cot, cot_core, top_out, *rest):
     mean, rstd = par[0:1], par[1:2]
     chans = x.shape[3]
     inside = jnp.where(lax.axis_index("rows") > 0, 1.0, 0.0)
@@ -214,7 +222,7 @@
     last_out, keep_out, send_out = rest
     outs_chunk = keep_out.shape[3]
     taps = [grad[:, t * chans : (t + 1) * chans] for t in range(9)]
-    last_out[...] = taps[8]
+    last_out[...] = taps[8] + dot_tn(cot_core[...], top[:, 2 * chans :])
     for t in range(2):
         quarters = [taps[2 * q + t].reshape(-1, outs_chunk, chans) for q in range(4)]
         halve(lax.axis_index("rows") & 1, quarters, keep_out, [send_out], (t,))
@@ -236,70 +244,103 @@
     return jnp.concatenate([hi, full - hi], axis=-2)
 
 
-def back_kernel(width, count, ranks, packed, *refs):
-    sum_refs = refs[:ranks]
-    par, x, hid, gp, gain, _, *refs = refs[ranks:]
-    if packed:
-        dlast, cbias, par_out, g_out, keep_out, *send_outs = refs
-    else:
-        par_out, g_out, grad_out, small_out = refs
-    half = x.shape[2]
-    chans = x.shape[3]
-    me = lax.axis_index("rows")
-    mean, rstd = par[0:1], par[1:2]
-    sums = sum(s[...] for s in sum_refs)
-    m2 = grouped(sums[0:1] * gain[...], width) / count
-    m1 = grouped(sums[1:2] * gain[...], width) / count
-    coef = (rstd * gain[...], -(rstd * rstd) * m2, -rstd * m1)
+def gradient(coef, gp, centred):
+    return coef[0] * gp + coef[1] * centred + coef[2]
+
+
+def coefficients(width, count, sums, par, gain, par_out):
+    rstd = par[1:2]
+    m2 = grouped(sums[0:1] * gain, width) / count
+    m1 = grouped(sums[1:2] * gain, width) / count
+    coef = (rstd * gain, -(rstd * rstd) * m2, -rstd * m1)
     par_out[...] = jnp.zeros(par_out.shape, F32)
-    par_out[0:1] = mean
+    par_out[0:1] = par[0:1]
     for i in range(3):
         par_out[1 + i : 2 + i] = coef[i]
+    return coef
+
+
+def shifted(even, odd):
+    even_b, odd_b = even.astype(BF16), odd.astype(BF16)
+    return lanes(odd_b, even_b, later(odd).astype(BF16)), lanes(sooner(even).astype(BF16), odd_b, even_b)
+
+
+def back_kernel(width, count, ranks, *refs):
+    sum_refs = refs[:ranks]
+    par, x, hid, gp, gain, par_out, g_out, grad_out, small_out = refs[ranks:]
+    chans = x.shape[3]
+    coef = coefficients(width, count, sum(s[...] for s in sum_refs), par, gain[...], par_out)
     bias = 0.0
     left, right = [], []
     for p in range(2):
-        ge = coef[0] * gp[p, 0] + coef[1] * (hid[p, 0] - mean) + coef[2]
-        go = coef[0] * gp[p, 1] + coef[1] * (hid[p, 1] - mean) + coef[2]
-        bias = bias + jnp.sum(ge + go, axis=0, keepdims=True)
-        ge_b, go_b = ge.astype(BF16), go.astype(BF16)
-        g_out[p, 0] = ge_b
-        g_out[p, 1] = go_b
-        left += [lanes(go_b, ge_b, later(go).astype(BF16)), lanes(sooner(ge).astype(BF16), go_b, ge_b)]
+        even, odd = [gradient(coef, gp[p, c], hid[p, c] - par[0:1]) for c in range(2)]
+        bias = bias + jnp.sum(even + odd, axis=0, keepdims=True)
+        g_out[p, 0] = even.astype(BF16)
+        g_out[p, 1] = odd.astype(BF16)
+        left += shifted(even, odd)
         right += [lanes(x[p, c], x[p + 1, c], x[p + 2, c]) for c in range(2)]
+    grad_out[...] = dot_tn(stack(*left), stack(*right))
+    small_out[...] = stack(bias, sum_refs[0][0:2], jnp.zeros((5, chans), F32))
+
+
+def chip_kernel(width, count, s0, s1, s2, s3, par, x, low, hid, gp, far, edge, gain, dlast, cbias, early, *refs):
+    par_out, g_out, own, sx, sy, sxy, scr = refs
+    rank = lax.axis_index("rows")
+    core, chip, side = rank & 1, rank >> 1, lax.axis_index("dp") & 1
+    first = core == 0
+    chans = x.shape[3]
+    owners = scr.shape[1]
+    chunk = chans // owners
+    coef = coefficients(width, count, s0[...] + s1[...] + s2[...] + s3[...], par, gain[...], par_out)
+    halo = 1 - core
+    rows = [[gradient(coef, gp[p, c], hid[p, c] - par[0:1]) for c in range(2)] for p in range(2)]
+    rows.append([gradient(coef, edge[halo, 0, c], edge[halo, 1, c]) for c in range(2)])
+    rows.append([gradient(coef, far[0, c], far[1, c]) for c in range(2)])
+    for p in range(2):
+        for c in range(2):
+            g_out[p, c] = rows[p][c].astype(BF16)
+    beside = (2 * core, 1 + 2 * core, 2 - core, 3 - 3 * core)
+    level = (x.at[1], x.at[2], x.at[3], low)
+    bias = 0.0
+    left, right = [], []
+    for (even, odd), at, same in zip(rows, beside, level):
+        bias = bias + jnp.sum(even + odd, axis=0, keepdims=True)
+        left += shifted(even, odd)
+        right += [lanes(x[at, c], same[c]) for c in range(2)]
     grad = dot_tn(stack(*left), stack(*right))
-    full = stack(bias, sum_refs[0][0:2], jnp.zeros((5, chans), F32))
-    if not packed:
-        grad_out[...] = grad
-        small_out[...] = full
-        return
-    owners = keep_out.shape[1]
-    chunk = chans // owners
+    full = stack(bias, s0[0:2] + s1[0:2], jnp.zeros((5, chans), F32))
     wide = [cbias[0:1, i * chans : (i + 1) * chans] for i in range(cbias.shape[1] // chans)]
     row_id = lax.broadcasted_iota(jnp.int32, full.shape, 0)
-    small = []
-    for d in range(owners):
-        at = d * chunk
-        mine = full if at == 0 else pltpu.roll(full, chans - at, 1)
-        at = d * 2 * chunk
-        row = jnp.broadcast_to(wide[at // chans], full.shape)
-        if at % chans:
-            row = pltpu.roll(row, chans - at % chans, 1)
-        small.append(hi_lo(jnp.where(row_id == 3, row, mine))[None])
-    quarters = [
-        jnp.concatenate(
-            [
-                grad[kw * chans : (kw + 1) * chans, kh * chans : (kh + 1) * chans].reshape(owners, chunk, chans)
-                for kw in range(3)
-            ],
-            axis=1,
-        )
-        for kh in range(3)
-    ]
-    quarters.append(jnp.concatenate([dlast[...].reshape(owners, 2 * chunk, chans), stack(*small)], axis=1))
-    halve(me & 1, quarters, keep_out, send_outs)
-
-
-def block_kernel(ahead, mix_top, mix, dw, dbias, block_out, done_out):
+    for kw in range(3):
+        at = slice(kw * chunk, (kw + 1) * chunk)
+        piece = grad[kw * chans : (kw + 1) * chans]
+        scr[0, :, at, :] = piece[:, :chans].reshape(owners, chunk, chans)
+        one = piece[:, chans:].reshape(owners, chunk, chans)
+        if kw < 2:
+            two = dlast[...].reshape(owners, 2 * chunk, chans)[:, at]
+            scr[1, :, at, :] = jnp.where(first, one, two)
+            continue
+        for d in range(owners):
+            start = d * chunk
+            mine = full if start == 0 else pltpu.roll(full, chans - start, 1)
+            start = d * 2 * chunk
+            row = jnp.broadcast_to(wide[start // chans], full.shape)
+            if start % chans:
+                row = pltpu.roll(row, chans - start % chans, 1)
+            scr[1, d, at, :] = jnp.where(first, one[d], hi_lo(jnp.where(row_id == 3, row, mine)))
+    mine, other = rank == 3, 2 * (1 - chip) + core == 3
+    n = early.shape[2]
+    for z in range(own.shape[0]):
+        here, there = 2 * z + side, 2 * z + 1 - side
+        own[z] = scr[chip, here]
+        sx[z] = rounded(scr[1 - chip, here], other)
+        sy[z] = rounded(scr[chip, there], mine)
+        sxy[z, 2 * n :] = rounded(scr[1 - chip, there], other)
+        for t in range(2):
+            sxy[z, t * n : (t + 1) * n] = early[t, z]
+
+
+def block_kernel(mix_top, mix, dw, dbias, block_out, done_out):
     chans, outs = dw.shape[2:]
     flat = [dw[:, k].reshape(3 * chans, outs) for k in range(3)]
     odd_before = lanes(mix_top[:, :chans], mix[0, :, :chans], mix[1, :, :chans])
@@ -310,22 +351,25 @@
     done_out[...] = jnp.zeros(done_out.shape, F32)
 
 
-def image_kernel(last, par, hid, gm, gain, shift, par2, g, w, gi_out, done_out, scr):
+def halo_kernel(ahead, par, hid, gm, gain, shift, out):
+    for i, p in ((0, 0), (1, 3)):
+        for c in range(2):
+            centred = hid[i, c] - par[0:1]
+            pre = centred * par[1:2] * gain[...] + shift[...]
+            sig = jax.nn.sigmoid(pre)
+            out[i, 0, c] = gm[p, c] * (sig * (1.0 + pre * (1.0 - sig)))
+            out[i, 1, c] = centred
+
+
+def image_kernel(last, parts, gm, par2, g, w, gi_out, done_out, scr):
     half = g.shape[2]
     chans = g.shape[3]
-    mean, rstd = par[0:1], par[1:2]
     me = lax.axis_index("rows")
+    coef = [par2[1 + i : 2 + i] for i in range(3)]
     edge = []
-    for i, p, there in ((0, 0, me > 0), (1, 3, me < last)):
+    for i, there in ((0, me > 0), (1, me < last)):
         keep = jnp.where(there, 1.0, 0.0)
-        pair = []
-        for c in range(2):
-            centred = hid[i, c] - mean
-            pre = centred * rstd * gain[...] + shift[...]
-            sig = jax.nn.sigmoid(pre)
-            gp = gm[p, c] * (sig * (1.0 + pre * (1.0 - sig)))
-            pair.append(((par2[1:2] * gp + par2[2:3] * centred + par2[3:4]) * keep).astype(BF16))
-        edge.append(pair)
+        edge.append([(gradient(coef, parts[i, 0, c], parts[i, 1, c]) * keep).astype(BF16) for c in range(2)])
     rows = [edge[0], [g[0, 0], g[0, 1]], [g[1, 0], g[1, 1]], edge[1]]
     tap = [lanes(w[0, k], w[1, k], w[2, k]) for k in range(3)]
     both = stack(lanes(tap[1], tap[0]), lanes(tap[2], tap[1]))
@@ -350,40 +394,34 @@
     return stack(total[:n], last).astype(BF16)
 
 
-def early_kernel(keep, got, own, send, done_out):
+def early_kernel(keep, got, own, sx, sy, sxy, done_out):
     done_out[...] = jnp.zeros(done_out.shape, F32)
-    chip = lax.axis_index("rows") >> 1
-    own[...] = keep[chip] + got[chip].astype(F32)
-    send[...] = (keep[1 - chip] + got[1 - chip].astype(F32)).astype(BF16)
-
-
-def late_kernel( keep, got0, got1, e_own, e_got, own, sx, sy, sxy):
-    me, side = lax.axis_index("rows"), lax.axis_index("dp") & 1
-    core, chip = me & 1, me >> 1
-    mine, other = me == 3, 2 * (1 - chip) + core == 3
-    n = e_own.shape[2]
-
-    def total(x, z, y):
-        got = (got0, got1)[z // 2]
-        return keep[x, 2 * z + y] + got[x, 2 * (z % 2) + y].astype(F32)
-
-    for z in range(own.shape[0]):
-        here, there = 2 * z + side, 2 * z + 1 - side
-        for t in range(2):
-            own[z, t * n : (t + 1) * n] = e_own[t, here] + e_got[t, here].astype(F32)
-            sy[z, t * n : (t + 1) * n] = (e_own[t, there] + e_got[t, there].astype(F32)).astype(BF16)
-        own[z, 2 * n :] = total(chip, z, side)
-        sy[z, 2 * n :] = rounded(total(chip, z, 1 - side), mine)
-        sx[z] = rounded(total(1 - chip, z, side), other)
-        sxy[z] = rounded(total(1 - chip, z, 1 - side), other)
-
-
-def pack_kernel( own, gx, gy, gxy, after, out, s1, s2, s3, scr):
+    chip, side = lax.axis_index("rows") >> 1, lax.axis_index("dp") & 1
+    _, zs, n, _ = own.shape
+    for ref in (sx, sy):
+        ref[2 * zs * n :] = jnp.zeros((ref.shape[0] - 2 * zs * n, ref.shape[1]), BF16)
+    for t in range(2):
+        for z in range(zs):
+
+            def total(x, y):
+                return keep[x, t, 2 * z + y] + got[x, t, 2 * z + y].astype(F32)
+
+            own[t, z] = total(chip, side)
+            sxy[t, z] = total(1 - chip, 1 - side).astype(BF16)
+            at = slice((t * zs + z) * n, (t * zs + z + 1) * n)
+            sx[at] = total(1 - chip, side).astype(BF16)
+            sy[at] = total(chip, 1 - side).astype(BF16)
+
+
+def pack_kernel(own, gx, gy, gxy, early, ex, ey, after, after_too, out, s1, s2, s3, scr):
     z = lax.axis_index("dp") >> 1
-    n = own.shape[1] - gx.shape[1]
-    scr[:, :n, :] = own[:, :n, :] + gy[:, :n, :].astype(F32)
-    late = gx[...].astype(F32) + gy[:, n:, :].astype(F32) + gxy[...].astype(F32)
-    scr[:, n:, :] = own[:, n:, :] + late
+    n = early.shape[2]
+    for t in range(2):
+        at = slice(t * own.shape[0] * n, (t + 1) * own.shape[0] * n)
+        got = (ex[at].astype(F32) + ey[at].astype(F32)).reshape(early.shape[1:])
+        scr[:, t * n : (t + 1) * n, :] = early[t] + got + gxy[:, t * n : (t + 1) * n, :].astype(F32)
+    late = gx[...].astype(F32) + gy[...].astype(F32) + gxy[:, 2 * n :, :].astype(F32)
+    scr[:, 2 * n :, :] = own[...] + late
     out[...] = scr[z]
     for k, ref in ((1, s1), (2, s2), (3, s3)):
         ref[...] = rounded(scr[(z + k) & 3], lax.axis_index("rows") == 3)
@@ -406,7 +444,7 @@
     for kh in range(3):
         for kw in range(3):
             at = 2 * wide + kw * chunk
-            conv[3 * kh + kw] = scr[kh, at : at + chunk, :]
+            conv[3 * kh + kw] = scr[(0, 2, 1)[kh], at : at + chunk, :]
     down[8] = scr[3, 2 * wide : 3 * wide, :]
     rows = scr[3, 3 * wide : 3 * wide + 8, :] + scr[3, 3 * wide + 8 :, :]
     cb[...] = rows[0:1, :chunk]
@@ -433,6 +471,11 @@
     both = ("rows", "dp")
     k = k_rows * lax.axis_size("dp") + k_dp
     return lax.ppermute(x, both, [(i, i ^ k) for i in range(lax.axis_size(both))])
+
+
+def swap_beside(x, y, xy):
+    both = swap_both(xy, 2, 1)
+    return swap(x, "rows", 2), swap(y, "dp", 1), both
 
 
 def shards(images, conv_weight, conv_bias, norm_gain, norm_shift, down_weight, down_bias, cotangent):
@@ -491,16 +534,16 @@
         [row_scr],
     )
     stats = with_swaps(stat, stat)
-    hid_edge, gm = run(
+    hid_edge, gm, low, chip_cbias = run(
         edge_kernel,
-        (core_img, chip_img, x, w, bias, core_cot, chip_cot, dw, own_gm),
-        [(block_of, F32), ((4, 2, half, chans), F32)],
+        (core_img, chip_img, x, w, bias, core_cot, chip_cot, dw, own_gm, cbias),
+        [(block_of, F32), ((4, 2, half, chans), F32), (block_of[1:], BF16), ((8, outs), F32)],
         [row_scr],
     )
-    par, mix, gp, sums = run(
+    par, mix, gp, sums, far = run(
         functools.partial(norm_kernel, width, count, ranks),
         (*stats, x, hid, gm, gain, shift),
-        [tile, ((2, half, 3 * chans), BF16), (block_of, F32), tile],
+        [tile, ((2, half, 3 * chans), BF16), (block_of, F32), tile, (block_of, F32)],
     )
     all_sums = with_swaps(sums, sums)
     early_shape = (2, owners, wide, chans)
@@ -509,7 +552,7 @@
 
     mix_top, *down_grad = run(
         functools.partial(down_kernel, packed),
-        (par, x, hid_edge, gain, shift, mix, cot),
+        (par, x, hid_edge, gain, shift, mix, cot, core_cot),
         [((half, 3 * chans), BF16)]
         + (
             [((outs, chans), F32), ((2,) + early_shape, F32), ((2,) + early_shape, BF16)]
@@ -519,44 +562,44 @@
     )
     if packed:
         dlast, keep, send = down_grad
-        early_own, early_send, ahead = run(
-            early_kernel, (keep, swap(send, "rows", 1)), [(early_shape, F32), (early_shape, BF16), tile]
+        zs = owners // 2
+        late_cut, early_cut = (zs, 3 * chunk, chans), (2, zs, wide, chans)
+        sent = ((2 * zs * wide + zs * deep) // 2 + zs * wide, chans)
+        early_own, sx, sy, early_sxy, ahead = run(
+            early_kernel,
+            (keep, swap(send, "rows", 1)),
+            [(early_cut, F32), (sent, BF16), (sent, BF16), (early_cut, BF16), tile],
         )
-        early_got = swap(early_send, "rows", 2)
-    block, block_done = run(block_kernel, (ahead, mix_top, mix, dw, dbias), [((half, outs), BF16), tile])
-    par2, g, *conv_grad = run(
-        functools.partial(back_kernel, width, count, ranks, packed),
-        (*all_sums, par, x, hid, gp, gain, block_done) + ((dlast, cbias) if packed else ()),
-        [tile, (block_of, BF16)]
-        + (
-            [((2,) + late_shape, F32)] + [((2, owners // 2, 3 * chunk, chans), BF16)] * 2
-            if packed
-            else [((3 * chans, 3 * chans), F32), tile]
-        ),
-        cost=BACK,
-    )
+        early_got = swap(sx, "rows", 2), swap(sy, "dp", 1)
+    block, block_done = run(block_kernel, (mix_top, mix, dw, dbias), [((half, outs), BF16), tile])
+    (edge,) = run(halo_kernel, (ahead, par, hid_edge, gm, gain, shift), [((2,) + block_of, F32)])
+    if packed:
+        far = swap(far, "rows", 1)
+        par2, g, own, sx, sy, sxy = run(
+            functools.partial(chip_kernel, width, count),
+            (*all_sums, par, x, low, hid, gp, far, edge, gain, dlast, chip_cbias, early_sxy),
+            [tile, (block_of, BF16), (late_cut, F32)] + [(late_cut, BF16)] * 2 + [((zs, deep, chans), BF16)],
+            [pltpu.VMEM((2,) + late_shape, F32)],
+            cost=BACK,
+        )
+    else:
+        par2, g, *conv_grad = run(
+            functools.partial(back_kernel, width, count, ranks),
+            (*all_sums, par, x, hid, gp, gain),
+            [tile, (block_of, BF16), ((3 * chans, 3 * chans), F32), tile],
+        )
     gi, done = run(
         functools.partial(image_kernel, ranks - 1),
-        (par, hid_edge, gm, gain, shift, par2, g, w),
+        (edge, gm, par2, g, w),
         [((rows, cols, chans), BF16), tile],
         [row_scr],
     )
     if packed:
-        keep, *sends = conv_grad
-        zs = owners // 2
-        late_cut, both_cut = (zs, 3 * chunk, chans), (zs, deep, chans)
-        own, sx, sy, sxy = run(
-            late_kernel,
-            (keep, *[swap(send, "rows", 1) for send in sends], early_own, early_got),
-            [(both_cut, F32), (late_cut, BF16), (both_cut, BF16), (late_cut, BF16)],
-        )
-        gxy = swap_both(sxy, 2, 1)
-        gx, gy = swap(sx, "rows", 2), swap(sy, "dp", 1)
         part, *sends = run(
             pack_kernel,
-            (own, gx, gy, gxy, done),
+            (own, *swap_beside(sx, sy, sxy), early_own, *early_got, done, block_done),
             [((deep, chans), F32)] + [((deep, chans), BF16)] * 3,
-            [pltpu.VMEM(both_cut, F32)],
+            [pltpu.VMEM((zs, deep, chans), F32)],
         )
         part, send = run(
             sum_kernel,

time: 45.9 us -> 43.8 us (0.954)
  waiting for transfers between devices: 12.2 us -> 8.33 us
  starting transfers between devices: 24.1 us -> 25.6 us
    ppermute x17, waiting for transfers between devices: 7.86 us -> 5.81 us  [swap(): lax.ppermute(x, axis, [(i, i ^ k) for i in range(lax.axis_size(axis))])]
    ppermute x1, waiting for transfers between devices: 1.77 us -> 0.01 us  [swap_both(): lax.ppermute(x, both, [(i, i ^ k) for i in range(lax.axis_size(both))])]
    ppermute x17, starting transfers between devices: 16.1 us -> 17 us  [swap(): lax.ppermute(x, axis, [(i, i ^ k) for i in range(lax.axis_size(axis))])]
    ppermute x1, starting transfers between devices: 1.09 us -> 1.67 us  [swap_both(): lax.ppermute(x, both, [(i, i ^ k) for i in range(lax.axis_size(both))])]
  transfers between devices with their start and end apart: 23 -> 23, of which waited for: 13 -> 9; matrix products, arithmetic and copies ran while one was open for 0% -> 0% of each run, Pallas kernels for 14% -> 16%
where the time goes in v6:
time: 43.8 us; the launch traced here: 43.7 us
  starting transfers between devices  25.6 us (58%)
  waiting for transfers between devices  8.33 us (19%)
  Pallas kernels  8.25 us (19%)
  between operations  0.86 us (2%)
  local copies, waits for them, and re-layouts  0.65 us (1%)
    ppermute x17, starting transfers between devices, swap(): lax.ppermute(x, axis, [(i, i ^ k) for i in range(lax.axis_size(axis))])  17 us
    pallas_call x14, Pallas kernels, run(): pl.pallas_call(kernel, in_specs=specs or [vmem] * len(args), out_shape=[j...  8.25 us
    ppermute x17, waiting for transfers between devices, swap(): lax.ppermute(x, axis, [(i, i ^ k) for i in range(lax.axis_size(axis))])  5.81 us
    ppermute x3, starting transfers between devices, around(): return lax.ppermute(x, 'dp', [(i, (i + 2 * k) % n) for i in range(n)])  5.57 us
    ppermute x3, waiting for transfers between devices, around(): return lax.ppermute(x, 'dp', [(i, (i + 2 * k) % n) for i in range(n)])  2.52 us
    ppermute x1, starting transfers between devices, swap_both(): lax.ppermute(x, both, [(i, i ^ k) for i in range(lax.axis_size(both))])  1.67 us
    ppermute x2, starting transfers between devices, across(): lax.ppermute(x, 'rows', [p for i in range(1, n - 1, 2) for p in ((i, i +...  1.32 us
  transfers between devices with their start and end apart: 23, of which 9 were waited for; matrix products, arithmetic and copies ran while one was open for 0% of the time, Pallas kernels for 16%

profile of v6, /device:TPU:0, one launch (start us, length us, event | category | flops | bytes accessed | tf_op | source)
XLA Modules:
  0.0 43.7 jit_solution(13567319943513768343)
XLA Ops:
  0.6 0.0 copy-start
  0.7 0.5 %collective-permute-start = (bf16[2,512,128]{2,1,0:T(8,128)(2,1)}, bf16[2,512,128]{2,1,0:T(8,128)(2,1)S(1)}, u32[]{:S(2)}, u32[]{:S(2)}) collective-permute-start(bf16[2,512,128]{2,1,0:T(8,128)(2,1)} %bitcast.18), channel_id=1, source_target_pairs={{0,8},{8,0},{16,24},{24,16},{1,9},{9,1},{17,25},{25,17},{2,10},{10... | collective-permute-start | bytes 786440 | tf_op jit(solution)/shard_map/ppermute | solution.py:462
  1.2 0.7 %collective-permute-start.1 = (bf16[2,512,128]{2,1,0:T(8,128)(2,1)}, bf16[2,512,128]{2,1,0:T(8,128)(2,1)S(1)}, u32[]{:S(2)}, u32[]{:S(2)}) collective-permute-start(bf16[2,512,128]{2,1,0:T(8,128)(2,1)} %bitcast.19), channel_id=1, source_target_pairs={{8,16},{16,8},{9,17},{17,9},{10,18},{18,10},{11,19},{19,11},{12,20... | collective-permute-start | bytes 786440 | tf_op jit(solution)/shard_map/ppermute | solution.py:458
  1.9 0.0 copy-start.4
  1.9 0.0 copy-start.5
  2.0 0.6 %copy-done.6 = f32[128]{0:T(128)S(1)} copy-done((f32[128]{0:T(128)S(1)}, f32[128]{0:T(128)}, u32[]{:S(2)}) %copy-start.6) | copy-done | bytes 536
  2.5 0.0 copy-done.7
  2.5 0.0 copy-done.4
  2.6 0.9 %shard_map.144 = (bf16[3,3,128,128]{3,2,1,0:T(8,128)(2,1)S(1)}, bf16[3,3,128,256]{3,2,1,0:T(8,128)(2,1)S(1)}, bf16[256,256]{1,0:T(8,128)(2,1)S(1)}, f32[1,128]{1...) custom-call(f32[8,128]{1,0:T(8,128)S(1)} %shard_map.143.ahead, ...), custom_call_target="tpu_custom_call" | custom-call | flops 134217728 | bytes 1024 | tf_op jit(solution)/shard_map/pallas_call | solution.py:494
  3.5 4.1 %collective-permute-start.5 = (bf16[256,256]{1,0:T(8,128)(2,1)S(1)}, bf16[256,256]{1,0:T(8,128)(2,1)S(1)}, u32[]{:S(2)}, u32[]{:S(2)}) collective-permute-start(bf16[256,256]{1,0:T(8,128)(2,1)S(1)} %get-tuple-element.67.cot), channel_id=1, source_target_pairs={{0,8},{8,0},{16,24},{24,16},{1,9},{9,1},{17,25},{25,17},{2,10},{10... | collective-permute-start | bytes 393224 | tf_op jit(solution)/shard_map/ppermute | solution.py:462
  7.5 0.7 %collective-permute-start.6 = (bf16[256,256]{1,0:T(8,128)(2,1)S(1)}, bf16[256,256]{1,0:T(8,128)(2,1)S(1)}, u32[]{:S(2)}, u32[]{:S(2)}) collective-permute-start(bf16[256,256]{1,0:T(8,128)(2,1)S(1)} %get-tuple-element.67.cot), channel_id=1, source_target_pairs={{8,16},{16,8},{9,17},{17,9},{10,18},{18,10},{11,19},{19,11},{12,20... | collective-permute-start | bytes 393224 | tf_op jit(solution)/shard_map/ppermute | solution.py:458
  8.2 0.0 collective-permute-done.core
  8.2 0.0 collective-permute-done.1.chip
  8.2 1.1 %shard_map.145 = (bf16[4,2,256,128]{3,2,1,0:T(8,128)(2,1)S(1)}, f32[2,2,256,128]{3,2,1,0:T(8,128)S(1)}, f32[8,128]{1,0:T(8,128)S(1)}) custom-call(bf16[2,512,128]{2,1,0:T(8,128)(2,1)S(1)} %collective-permute-done.core, bf16[2,512,128]{2,1,0:T(8,128)(2,1)S(1)} %collective-permute-done.1.chip, bf16[2,2,256,128]{3,2,1,0:T(8,128)(2,1)S(1)} %get-tuple-element.61.own, ...), custom_call_target="tpu_custom_call" | custom-call | flops 134217728 | bytes 1024 | tf_op jit(solution)/shard_map/pallas_call | solution.py:494
  9.3 1.9 %collective-permute-start.2 = (f32[8,128]{1,0:T(8,128)S(1)}, f32[8,128]{1,0:T(8,128)S(1)}, u32[]{:S(2)}, u32[]{:S(2)}) collective-permute-start(f32[8,128]{1,0:T(8,128)S(1)} %get-tuple-element.64.refs_0_), channel_id=1, source_target_pairs={{0,8},{8,0},{16,24},{24,16},{1,9},{9,1},{17,25},{25,17},{2,10},{10... | collective-permute-start | bytes 12296 | tf_op jit(solution)/shard_map/ppermute | solution.py:462
  11.2 1.6 %collective-permute-start.3 = (f32[8,128]{1,0:T(8,128)S(1)}, f32[8,128]{1,0:T(8,128)S(1)}, u32[]{:S(2)}, u32[]{:S(2)}) collective-permute-start(f32[8,128]{1,0:T(8,128)S(1)} %get-tuple-element.64.refs_0_), channel_id=1, source_target_pairs={{0,16},{8,24},{16,0},{24,8},{1,17},{9,25},{17,1},{25,9},{2,18},{10... | collective-permute-start | bytes 12296 | tf_op jit(solution)/shard_map/ppermute | solution.py:462
  12.9 0.1 collective-permute-start.4
  13.0 0.0 collective-permute-done.5.cot_core
  13.0 0.0 collective-permute-done.6.cot_chip
  13.0 0.8 %shard_map.146 = (f32[2,2,256,128]{3,2,1,0:T(8,128)S(1)}, f32[4,2,256,128]{3,2,1,0:T(8,128)S(1)}, bf16[2,256,128]{2,1,0:T(8,128)(2,1)S(1)}, f32[8,256]{1,0:T(8,128)S(1)}) custom-call(bf16[2,512,128]{2,1,0:T(8,128)(2,1)S(1)} %collective-permute-done.core, bf16[2,512,128]{2,1,0:T(8,128)(2,1)S(1)} %collective-permute-done.1.chip, ...), custom_call_target="tpu_custom_call" | custom-call | flops 134217728 | bytes 1024 | tf_op jit(solution)/shard_map/pallas_call | solution.py:494
  13.9 0.0 collective-permute-done.2.refs_1_
  13.9 1.0 %collective-permute-done.3.refs_2_ = f32[8,128]{1,0:T(8,128)S(1)} collective-permute-done((f32[8,128]{1,0:T(8,128)S(1)}, f32[8,128]{1,0:T(8,128)S(1)}, u32[]{:S(2)}, u32[]{:S(2)}) %collective-permute-start.3) | collective-permute-done | bytes 4128 | tf_op jit(solution)/shard_map/ppermute | solution.py:462
  14.8 1.1 %collective-permute-done.4.refs_3_ = f32[8,128]{1,0:T(8,128)S(1)} collective-permute-done((f32[8,128]{1,0:T(8,128)S(1)}, f32[8,128]{1,0:T(8,128)S(1)}, u32[]{:S(2)}, u32[]{:S(2)}) %collective-permute-start.4) | collective-permute-done | bytes 4128 | tf_op jit(solution)/shard_map/ppermute | solution.py:462
  15.9 0.5 %shard_map.147 = (f32[8,128]{1,0:T(8,128)S(1)}, bf16[2,256,384]{2,1,0:T(8,128)(2,1)S(1)}, f32[2,2,256,128]{3,2,1,0:T(8,128)S(1)}, f32[8,128]{1,0:T(8,128)S(1)}, f32[2,2,256,128]{3,2,1,0:T(8,128)S(1)}) custom-call(f32[8,128]{1,0:T(8,128)S(1)} %get-tuple-element.64.refs_0_, f32[8,128]{1,0:T(8,128)S(1)} %collective-permute-done.2.refs_1_, ...), custom_call_target="tpu_custom_call" | custom-call | flops 134217728 | bytes 1024 | tf_op jit(solution)/shard_map/pallas_call | solution.py:494
  16.4 0.3 collective-permute-start.11
  16.7 0.5 %shard_map.148 = (bf16[256,384]{1,0:T(8,128)(2,1)S(1)}, f32[256,128]{1,0:T(8,128)S(1)}, f32[2,2,8,32,128]{4,3,2,1,0:T(8,128)S(1)}, bf16[2,2,8,32,128]{4,3,2,1,0:T(8,128)(2,1)S(1)}) custom-call(f32[8,128]{1,0:T(8,128)S(1)} %get-tuple-element.74.par, bf16[4,2,256,128]{3,2,1,0:T(8,128)(2,1)S(1)} %get-tuple-element.65.x.refs_4_, ...), custom_call_target="tpu_custom_call" | custom-call | flops 134217728 | bytes 1024 | tf_op jit(solution)/shard_map/pallas_call | solution.py:494
  17.2 0.4 collective-permute-start.7
  17.5 0.2 collective-permute-start.8
  17.7 0.5 %collective-permute-start.9 = (f32[8,128]{1,0:T(8,128)S(1)}, f32[8,128]{1,0:T(8,128)S(1)}, u32[]{:S(2)}, u32[]{:S(2)}) collective-permute-start(f32[8,128]{1,0:T(8,128)S(1)} %get-tuple-element.83.s0), channel_id=1, source_target_pairs={{0,16},{8,24},{16,0},{24,8},{1,17},{9,25},{17,1},{25,9},{2,18},{10... | collective-permute-start | bytes 12296 | tf_op jit(solution)/shard_map/ppermute | solution.py:462
  18.2 1.2 %collective-permute-start.10 = (f32[8,128]{1,0:T(8,128)S(1)}, f32[8,128]{1,0:T(8,128)S(1)}, u32[]{:S(2)}, u32[]{:S(2)}) collective-permute-start(f32[8,128]{1,0:T(8,128)S(1)} %get-tuple-element.83.s0), channel_id=1, source_target_pairs={{0,24},{8,16},{16,8},{24,0},{1,25},{9,17},{17,9},{25,1},{2,26},{10... | collective-permute-start | bytes 12296 | tf_op jit(solution)/shard_map/ppermute | solution.py:462
  19.4 0.0 collective-permute-done.7.got
  19.4 0.1 shard_map.150
  19.5 0.2 shard_map.151.edge.parts
  19.7 0.7 %collective-permute-start.15 = (bf16[480,128]{1,0:T(8,128)(2,1)S(1)}, bf16[480,128]{1,0:T(8,128)(2,1)S(1)}, u32[]{:S(2)}, u32[]{:S(2)}) collective-permute-start(bf16[480,128]{1,0:T(8,128)(2,1)S(1)} %get-tuple-element.98), channel_id=1, source_target_pairs={{0,16},{8,24},{16,0},{24,8},{1,17},{9,25},{17,1},{25,9},{2,18},{10... | collective-permute-start | bytes 368648 | tf_op jit(solution)/shard_map/ppermute | solution.py:462
  20.4 0.0 collective-permute-done.8.s1
  20.4 1.8 %collective-permute-start.16 = (bf16[480,128]{1,0:T(8,128)(2,1)S(1)}, bf16[480,128]{1,0:T(8,128)(2,1)S(1)}, u32[]{:S(2)}, u32[]{:S(2)}) collective-permute-start(bf16[480,128]{1,0:T(8,128)(2,1)S(1)} %get-tuple-element.99), channel_id=1, source_target_pairs={{0,1},{1,0},{2,3},{3,2},{4,5},{5,4},{6,7},{7,6},{8,9},{9,8},{10,11... | collective-permute-start | bytes 368648 | tf_op jit(solution)/shard_map/ppermute | solution.py:462
  22.1 0.0 collective-permute-done.9.s2
  22.2 0.0 collective-permute-done.10.s3
  22.2 0.0 collective-permute-done.11.far
  22.2 1.0 %shard_map.152 = (f32[8,128]{1,0:T(8,128)S(1)}, bf16[2,2,256,128]{3,2,1,0:T(8,128)(2,1)S(1)}, f32[4,48,128]{2,1,0:T(8,128)S(1)}, bf16[4,48,128]{2,1,0:T(8,128)(2...) custom-call(f32[8,128]{1,0:T(8,128)S(1)} %get-tuple-element.83.s0, ...), custom_call_target="tpu_custom_call" | custom-call | flops 4294967296 | bytes 1024 | tf_op jit(solution)/shard_map/pallas_call | solution.py:494
  23.1 1.7 %collective-permute-start.14 = (bf16[4,112,128]{2,1,0:T(8,128)(2,1)S(1)}, bf16[4,112,128]{2,1,0:T(8,128)(2,1)S(1)}, u32[]{:S(2)}, u32[]{:S(2)}) collective-permute-start(bf16[4,112,128]{2,1,0:T(8,128)(2,1)S(1)} %get-tuple-element.96), channel_id=1, source_target_pairs={{0,17},{1,16},{2,19},{3,18},{4,21},{5,20},{6,23},{7,22},{8,25},{9,... | collective-permute-start | bytes 344072 | tf_op jit(solution)/shard_map/ppermute | solution.py:473
  24.8 0.7 %collective-permute-start.12 = (bf16[4,48,128]{2,1,0:T(8,128)(2,1)S(1)}, bf16[4,48,128]{2,1,0:T(8,128)(2,1)S(1)}, u32[]{:S(2)}, u32[]{:S(2)}) collective-permute-start(bf16[4,48,128]{2,1,0:T(8,128)(2,1)S(1)} %get-tuple-element.94), channel_id=1, source_target_pairs={{0,16},{8,24},{16,0},{24,8},{1,17},{9,25},{17,1},{25,9},{2,18},{10... | collective-permute-start | bytes 147464 | tf_op jit(solution)/shard_map/ppermute | solution.py:462
  25.5 1.1 %collective-permute-start.13 = (bf16[4,48,128]{2,1,0:T(8,128)(2,1)S(1)}, bf16[4,48,128]{2,1,0:T(8,128)(2,1)S(1)}, u32[]{:S(2)}, u32[]{:S(2)}) collective-permute-start(bf16[4,48,128]{2,1,0:T(8,128)(2,1)S(1)} %get-tuple-element.95), channel_id=1, source_target_pairs={{0,1},{1,0},{2,3},{3,2},{4,5},{5,4},{6,7},{7,6},{8,9},{9,8},{10,11... | collective-permute-start | bytes 147464 | tf_op jit(solution)/shard_map/ppermute | solution.py:462
  26.7 1.0 %shard_map.149 = (bf16[256,256]{1,0:T(8,128)(2,1)}, f32[8,128]{1,0:T(8,128)S(1)}) custom-call(bf16[256,384]{1,0:T(8,128)(2,1)S(1)} %get-tuple-element.77.mix_top, bf16[2,256,384]{2,1,0:T(8,128)(2,1)S(1)} %get-tuple-element.76.mix, bf16[3,3,128,256]{3,2,1,0:T(8,128)(2,1)S(1)} %get-tuple-element.68.dw, f32[1,256]{1,0:T(1,128)S(1)} %get-tuple-element.78.dbias), custom_call_target="tpu_custom_call" | custom-call | flops 134217728 | bytes 1024 | tf_op jit(solution)/shard_map/pallas_call | solution.py:494
  27.7 1.4 %shard_map.153 = (bf16[2,512,128]{2,1,0:T(8,128)(2,1)}, f32[8,128]{1,0:T(8,128)S(1)}) custom-call(f32[2,2,2,256,128]{4,3,2,1,0:T(8,128)S(1)} %shard_map.151.edge.parts, f32[4,2,256,128]{3,2,1,0:T(8,128)S(1)} %get-tuple-element.71.refs_6_.gm, f32[8,128]{1,0:T(8,128)S(1)} %get-tuple-element.90.par2, bf16[2,2,256,128]{3,2,1,0:T(8,128)(2,1)S(1)} %get-tuple-element.91.g, ...), custom_call_target="tpu_custom_call" | custom-call | flops 134217728 | bytes 1024 | tf_op jit(solution)/shard_map/pallas_call | solution.py:494
  29.0 0.0 collective-permute-done.15.ex
  29.0 0.0 collective-permute-done.16.ey
  29.0 0.7 %collective-permute-done.12.gx = bf16[4,48,128]{2,1,0:T(8,128)(2,1)S(1)} collective-permute-done((bf16[4,48,128]{2,1,0:T(8,128)(2,1)S(1)}, bf16[4,48,128]{2,1,0:T(8,128)(2,1)S(1)}, u32[]{:S(2)}, u32[]{:S(2)}) %collective-permute-start.12) | collective-permute-done | bytes 49184 | tf_op jit(solution)/shard_map/ppermute | solution.py:462
  29.8 0.2 collective-permute-done.13.gy
  30.0 0.0 collective-permute-done.14.gxy
  30.0 0.1 shard_map.154
  30.1 1.6 %collective-permute-start.17 = (bf16[112,128]{1,0:T(8,128)(2,1)S(1)}, bf16[112,128]{1,0:T(8,128)(2,1)S(1)}, u32[]{:S(2)}, u32[]{:S(2)}) collective-permute-start(bf16[112,128]{1,0:T(8,128)(2,1)S(1)} %get-tuple-element.103), channel_id=1, source_target_pairs={{0,2},{1,3},{2,4},{3,5},{4,6},{5,7},{6,0},{7,1},{8,10},{9,11},{10,... | collective-permute-start | bytes 86024 | tf_op jit(solution)/shard_map/ppermute | solution.py:467
  31.7 2.6 %collective-permute-start.18 = (bf16[112,128]{1,0:T(8,128)(2,1)S(1)}, bf16[112,128]{1,0:T(8,128)(2,1)S(1)}, u32[]{:S(2)}, u32[]{:S(2)}) collective-permute-start(bf16[112,128]{1,0:T(8,128)(2,1)S(1)} %get-tuple-element.104), channel_id=1, source_target_pairs={{0,4},{1,5},{2,6},{3,7},{4,0},{5,1},{6,2},{7,3},{8,12},{9,13},{10,... | collective-permute-start | bytes 86024 | tf_op jit(solution)/shard_map/ppermute | solution.py:467
  34.3 1.4 %collective-permute-start.19 = (bf16[112,128]{1,0:T(8,128)(2,1)S(1)}, bf16[112,128]{1,0:T(8,128)(2,1)S(1)}, u32[]{:S(2)}, u32[]{:S(2)}) collective-permute-start(bf16[112,128]{1,0:T(8,128)(2,1)S(1)} %get-tuple-element.105), channel_id=1, source_target_pairs={{0,6},{1,7},{2,0},{3,1},{4,2},{5,3},{6,4},{7,5},{8,14},{9,15},{10,... | collective-permute-start | bytes 86024 | tf_op jit(solution)/shard_map/ppermute | solution.py:467
  35.7 0.3 collective-permute-done.17.g1
  36.0 0.5 %collective-permute-done.18.g2 = bf16[112,128]{1,0:T(8,128)(2,1)S(1)} collective-permute-done((bf16[112,128]{1,0:T(8,128)(2,1)S(1)}, bf16[112,128]{1,0:T(8,128)(2,1)S(1)}, u32[]{:S(2)}, u32[]{:S(2)}) %collective-permute-start.18) | collective-permute-done | bytes 28704 | tf_op jit(solution)/shard_map/ppermute | solution.py:467
  36.5 1.7 %collective-permute-done.19.g3 = bf16[112,128]{1,0:T(8,128)(2,1)S(1)} collective-permute-done((bf16[112,128]{1,0:T(8,128)(2,1)S(1)}, bf16[112,128]{1,0:T(8,128)(2,1)S(1)}, u32[]{:S(2)}, u32[]{:S(2)}) %collective-permute-start.19) | collective-permute-done | bytes 28704 | tf_op jit(solution)/shard_map/ppermute | solution.py:467
  38.2 0.1 collective-permute-start.20
  38.3 1.4 %collective-permute-start.21 = (bf16[112,128]{1,0:T(8,128)(2,1)S(1)}, bf16[112,128]{1,0:T(8,128)(2,1)S(1)}, u32[]{:S(2)}, u32[]{:S(2)}) collective-permute-start(bf16[112,128]{1,0:T(8,128)(2,1)S(1)} %get-tuple-element.107), channel_id=1, source_target_pairs={{0,16},{8,24},{16,0},{24,8},{1,17},{9,25},{17,1},{25,9},{2,18},{10... | collective-permute-start | bytes 86024 | tf_op jit(solution)/shard_map/ppermute | solution.py:462
  39.6 0.5 %collective-permute-start.22 = (bf16[112,128]{1,0:T(8,128)(2,1)S(1)}, bf16[112,128]{1,0:T(8,128)(2,1)S(1)}, u32[]{:S(2)}, u32[]{:S(2)}) collective-permute-start(bf16[112,128]{1,0:T(8,128)(2,1)S(1)} %get-tuple-element.107), channel_id=1, source_target_pairs={{0,24},{8,16},{16,8},{24,0},{1,25},{9,17},{17,9},{25,1},{2,26},{10... | collective-permute-start | bytes 86024 | tf_op jit(solution)/shard_map/ppermute | solution.py:462
  40.1 0.0 collective-permute-done.20.q1
  40.1 2.1 %collective-permute-done.21.q2 = bf16[112,128]{1,0:T(8,128)(2,1)S(1)} collective-permute-done((bf16[112,128]{1,0:T(8,128)(2,1)S(1)}, bf16[112,128]{1,0:T(8,128)(2,1)S(1)}, u32[]{:S(2)}, u32[]{:S(2)}) %collective-permute-start.21) | collective-permute-done | bytes 28704 | tf_op jit(solution)/shard_map/ppermute | solution.py:462
  42.2 0.7 %collective-permute-done.22.q3 = bf16[112,128]{1,0:T(8,128)(2,1)S(1)} collective-permute-done((bf16[112,128]{1,0:T(8,128)(2,1)S(1)}, bf16[112,128]{1,0:T(8,128)(2,1)S(1)}, u32[]{:S(2)}, u32[]{:S(2)}) %collective-permute-start.22) | collective-permute-done | bytes 28704 | tf_op jit(solution)/shard_map/ppermute | solution.py:462
  42.9 0.7 %shard_map.156 = (f32[9,32,128]{2,1,0:T(8,128)}, f32[9,16,128]{2,1,0:T(8,128)}, f32[1,16]{1,0:T(1,128)}, f32[1,16]{1,0:T(1,128)}, f32[1,16]{1,0:T(1,128)}, /*index=5*/f32[1,32]{1,0:T(1,128)}) custom-call(f32[112,128]{1,0:T(8,128)S(1)} %get-tuple-element.106.q0, bf16[112,128]{1,0:T(8,128)(2,1)S(1)} %collective-permute-done.20.q1, ...), custom_call_target="tpu_custom_call" | custom-call | flops 134217728 | bytes 1024 | tf_op jit(solution)/shard_map/pallas_call | solution.py:494
  (12 shorter events, 0.0 us)
Async XLA Ops:
  0.6 1.3 %copy-start = (bf16[3,3,128,256]{3,2,1,0:T(8,128)(2,1)S(1)}, bf16[3,3,128,256]{3,2,1,0:T(8,128)(2,1)}, u32[]{:S(2)}) copy-start(bf16[3,3,128,256]{3,2,1,0:T(8,128)(2,1)} %dw.1) | copy-start | bytes 1769476
  0.6 1.3 %copy-start.1 = (bf16[3,3,128,128]{3,2,1,0:T(8,128)(2,1)S(1)}, bf16[3,3,128,128]{3,2,1,0:T(8,128)(2,1)}, u32[]{:S(2)}) copy-start(bf16[3,3,128,128]{3,2,1,0:T(8,128)(2,1)} %w.1) | copy-start | bytes 884740
  0.7 1.3 %copy-start.2 = (bf16[1,2,512,128]{3,2,1,0:T(8,128)(2,1)S(1)}, bf16[1,2,512,128]{3,2,1,0:T(8,128)(2,1)}, u32[]{:S(2)}) copy-start(bf16[1,2,512,128]{3,2,1,0:T(8,128)(2,1)} %param.8) | copy-start | bytes 786436
  0.7 1.3 %copy-start.3 = (bf16[1,1,256,256]{3,2,1,0:T(8,128)(2,1)S(1)}, bf16[1,1,256,256]{3,2,1,0:T(8,128)(2,1)}, u32[]{:S(2)}) copy-start(bf16[1,1,256,256]{3,2,1,0:T(8,128)(2,1)} %param.15) | copy-start | bytes 393220
  0.7 7.5 %collective-permute-start = (bf16[2,512,128]{2,1,0:T(8,128)(2,1)}, bf16[2,512,128]{2,1,0:T(8,128)(2,1)S(1)}, u32[]{:S(2)}, u32[]{:S(2)}) collective-permute-start(bf16[2,512,128]{2,1,0:T(8,128)(2,1)} %bitcast.18), channel_id=1, source_target_pairs={{0,8},{8,0},{16,24},{24,16},{1,9},{9,1},{17,25},{25,17},{2,10},{10... | collective-permute-start | bytes 786440 | tf_op jit(solution)/shard_map/ppermute | solution.py:462
  1.2 7.0 %collective-permute-start.1 = (bf16[2,512,128]{2,1,0:T(8,128)(2,1)}, bf16[2,512,128]{2,1,0:T(8,128)(2,1)S(1)}, u32[]{:S(2)}, u32[]{:S(2)}) collective-permute-start(bf16[2,512,128]{2,1,0:T(8,128)(2,1)} %bitcast.19), channel_id=1, source_target_pairs={{8,16},{16,8},{9,17},{17,9},{10,18},{18,10},{11,19},{19,11},{12,20... | collective-permute-start | bytes 786440 | tf_op jit(solution)/shard_map/ppermute | solution.py:458
  1.9 0.7 %copy-start.6 = (f32[128]{0:T(128)S(1)}, f32[128]{0:T(128)}, u32[]{:S(2)}) copy-start(f32[128]{0:T(128)} %param.11) | copy-start | bytes 1540
  1.9 0.7 %copy-start.7 = (f32[128]{0:T(128)S(1)}, f32[128]{0:T(128)}, u32[]{:S(2)}) copy-start(f32[128]{0:T(128)} %param.12) | copy-start | bytes 1540
  1.9 0.7 %copy-start.4 = (f32[256]{0:T(256)S(1)}, f32[256]{0:T(256)}, u32[]{:S(2)}) copy-start(f32[256]{0:T(256)} %param.14) | copy-start | bytes 3076
  1.9 0.7 %copy-start.5 = (f32[128]{0:T(128)S(1)}, f32[128]{0:T(128)}, u32[]{:S(2)}) copy-start(f32[128]{0:T(128)} %param.10) | copy-start | bytes 1540
  3.5 9.5 %collective-permute-start.5 = (bf16[256,256]{1,0:T(8,128)(2,1)S(1)}, bf16[256,256]{1,0:T(8,128)(2,1)S(1)}, u32[]{:S(2)}, u32[]{:S(2)}) collective-permute-start(bf16[256,256]{1,0:T(8,128)(2,1)S(1)} %get-tuple-element.67.cot), channel_id=1, source_target_pairs={{0,8},{8,0},{16,24},{24,16},{1,9},{9,1},{17,25},{25,17},{2,10},{10... | collective-permute-start | bytes 393224 | tf_op jit(solution)/shard_map/ppermute | solution.py:462
  7.5 5.5 %collective-permute-start.6 = (bf16[256,256]{1,0:T(8,128)(2,1)S(1)}, bf16[256,256]{1,0:T(8,128)(2,1)S(1)}, u32[]{:S(2)}, u32[]{:S(2)}) collective-permute-start(bf16[256,256]{1,0:T(8,128)(2,1)S(1)} %get-tuple-element.67.cot), channel_id=1, source_target_pairs={{8,16},{16,8},{9,17},{17,9},{10,18},{18,10},{11,19},{19,11},{12,20... | collective-permute-start | bytes 393224 | tf_op jit(solution)/shard_map/ppermute | solution.py:458
  9.3 4.5 %collective-permute-start.2 = (f32[8,128]{1,0:T(8,128)S(1)}, f32[8,128]{1,0:T(8,128)S(1)}, u32[]{:S(2)}, u32[]{:S(2)}) collective-permute-start(f32[8,128]{1,0:T(8,128)S(1)} %get-tuple-element.64.refs_0_), channel_id=1, source_target_pairs={{0,8},{8,0},{16,24},{24,16},{1,9},{9,1},{17,25},{25,17},{2,10},{10... | collective-permute-start | bytes 12296 | tf_op jit(solution)/shard_map/ppermute | solution.py:462
  11.2 3.6 %collective-permute-start.3 = (f32[8,128]{1,0:T(8,128)S(1)}, f32[8,128]{1,0:T(8,128)S(1)}, u32[]{:S(2)}, u32[]{:S(2)}) collective-permute-start(f32[8,128]{1,0:T(8,128)S(1)} %get-tuple-element.64.refs_0_), channel_id=1, source_target_pairs={{0,16},{8,24},{16,0},{24,8},{1,17},{9,25},{17,1},{25,9},{2,18},{10... | collective-permute-start | bytes 12296 | tf_op jit(solution)/shard_map/ppermute | solution.py:462
  12.9 3.0 %collective-permute-start.4 = (f32[8,128]{1,0:T(8,128)S(1)}, f32[8,128]{1,0:T(8,128)S(1)}, u32[]{:S(2)}, u32[]{:S(2)}) collective-permute-start(f32[8,128]{1,0:T(8,128)S(1)} %get-tuple-element.64.refs_0_), channel_id=1, source_target_pairs={{0,24},{8,16},{16,8},{24,0},{1,25},{9,17},{17,9},{25,1},{2,26},{10... | collective-permute-start | bytes 12296 | tf_op jit(solution)/shard_map/ppermute | solution.py:462
  16.4 5.7 %collective-permute-start.11 = (f32[2,2,256,128]{3,2,1,0:T(8,128)S(1)}, f32[2,2,256,128]{3,2,1,0:T(8,128)S(1)}, u32[]{:S(2)}, u32[]{:S(2)}) collective-permute-start(f32[2,2,256,128]{3,2,1,0:T(8,128)S(1)} %get-tuple-element.86), channel_id=1, source_target_pairs={{0,8},{8,0},{16,24},{24,16},{1,9},{9,1},{17,25},{25,17},{2,10},{10... | collective-permute-start | bytes 1572872 | tf_op jit(solution)/shard_map/ppermute | solution.py:462
  17.2 2.2 %collective-permute-start.7 = (bf16[2,2,8,32,128]{4,3,2,1,0:T(8,128)(2,1)S(1)}, bf16[2,2,8,32,128]{4,3,2,1,0:T(8,128)(2,1)S(1)}, u32[]{:S(2)}, u32[]{:S(2)}) collective-permute-start(bf16[2,2,8,32,128]{4,3,2,1,0:T(8,128)(2,1)S(1)} %get-tuple-element.81), channel_id=1, source_target_pairs={{0,8},{8,0},{16,24},{24,16},{1,9},{9,1},{17,25},{25,17},{2,10},{10... | collective-permute-start | bytes 786440 | tf_op jit(solution)/shard_map/ppermute | solution.py:462
  17.5 2.8 %collective-permute-start.8 = (f32[8,128]{1,0:T(8,128)S(1)}, f32[8,128]{1,0:T(8,128)S(1)}, u32[]{:S(2)}, u32[]{:S(2)}) collective-permute-start(f32[8,128]{1,0:T(8,128)S(1)} %get-tuple-element.83.s0), channel_id=1, source_target_pairs={{0,8},{8,0},{16,24},{24,16},{1,9},{9,1},{17,25},{25,17},{2,10},{10... | collective-permute-start | bytes 12296 | tf_op jit(solution)/shard_map/ppermute | solution.py:462
  17.7 4.4 %collective-permute-start.9 = (f32[8,128]{1,0:T(8,128)S(1)}, f32[8,128]{1,0:T(8,128)S(1)}, u32[]{:S(2)}, u32[]{:S(2)}) collective-permute-start(f32[8,128]{1,0:T(8,128)S(1)} %get-tuple-element.83.s0), channel_id=1, source_target_pairs={{0,16},{8,24},{16,0},{24,8},{1,17},{9,25},{17,1},{25,9},{2,18},{10... | collective-permute-start | bytes 12296 | tf_op jit(solution)/shard_map/ppermute | solution.py:462
  18.2 3.9 %collective-permute-start.10 = (f32[8,128]{1,0:T(8,128)S(1)}, f32[8,128]{1,0:T(8,128)S(1)}, u32[]{:S(2)}, u32[]{:S(2)}) collective-permute-start(f32[8,128]{1,0:T(8,128)S(1)} %get-tuple-element.83.s0), channel_id=1, source_target_pairs={{0,24},{8,16},{16,8},{24,0},{1,25},{9,17},{17,9},{25,1},{2,26},{10... | collective-permute-start | bytes 12296 | tf_op jit(solution)/shard_map/ppermute | solution.py:462
  19.7 9.4 %collective-permute-start.15 = (bf16[480,128]{1,0:T(8,128)(2,1)S(1)}, bf16[480,128]{1,0:T(8,128)(2,1)S(1)}, u32[]{:S(2)}, u32[]{:S(2)}) collective-permute-start(bf16[480,128]{1,0:T(8,128)(2,1)S(1)} %get-tuple-element.98), channel_id=1, source_target_pairs={{0,16},{8,24},{16,0},{24,8},{1,17},{9,25},{17,1},{25,9},{2,18},{10... | collective-permute-start | bytes 368648 | tf_op jit(solution)/shard_map/ppermute | solution.py:462
  20.4 8.7 %collective-permute-start.16 = (bf16[480,128]{1,0:T(8,128)(2,1)S(1)}, bf16[480,128]{1,0:T(8,128)(2,1)S(1)}, u32[]{:S(2)}, u32[]{:S(2)}) collective-permute-start(bf16[480,128]{1,0:T(8,128)(2,1)S(1)} %get-tuple-element.99), channel_id=1, source_target_pairs={{0,1},{1,0},{2,3},{3,2},{4,5},{5,4},{6,7},{7,6},{8,9},{9,8},{10,11... | collective-permute-start | bytes 368648 | tf_op jit(solution)/shard_map/ppermute | solution.py:462
  23.1 6.9 %collective-permute-start.14 = (bf16[4,112,128]{2,1,0:T(8,128)(2,1)S(1)}, bf16[4,112,128]{2,1,0:T(8,128)(2,1)S(1)}, u32[]{:S(2)}, u32[]{:S(2)}) collective-permute-start(bf16[4,112,128]{2,1,0:T(8,128)(2,1)S(1)} %get-tuple-element.96), channel_id=1, source_target_pairs={{0,17},{1,16},{2,19},{3,18},{4,21},{5,20},{6,23},{7,22},{8,25},{9,... | collective-permute-start | bytes 344072 | tf_op jit(solution)/shard_map/ppermute | solution.py:473
  24.8 5.0 %collective-permute-start.12 = (bf16[4,48,128]{2,1,0:T(8,128)(2,1)S(1)}, bf16[4,48,128]{2,1,0:T(8,128)(2,1)S(1)}, u32[]{:S(2)}, u32[]{:S(2)}) collective-permute-start(bf16[4,48,128]{2,1,0:T(8,128)(2,1)S(1)} %get-tuple-element.94), channel_id=1, source_target_pairs={{0,16},{8,24},{16,0},{24,8},{1,17},{9,25},{17,1},{25,9},{2,18},{10... | collective-permute-start | bytes 147464 | tf_op jit(solution)/shard_map/ppermute | solution.py:462
  25.5 4.5 %collective-permute-start.13 = (bf16[4,48,128]{2,1,0:T(8,128)(2,1)S(1)}, bf16[4,48,128]{2,1,0:T(8,128)(2,1)S(1)}, u32[]{:S(2)}, u32[]{:S(2)}) collective-permute-start(bf16[4,48,128]{2,1,0:T(8,128)(2,1)S(1)} %get-tuple-element.95), channel_id=1, source_target_pairs={{0,1},{1,0},{2,3},{3,2},{4,5},{5,4},{6,7},{7,6},{8,9},{9,8},{10,11... | collective-permute-start | bytes 147464 | tf_op jit(solution)/shard_map/ppermute | solution.py:462
  30.1 5.9 %collective-permute-start.17 = (bf16[112,128]{1,0:T(8,128)(2,1)S(1)}, bf16[112,128]{1,0:T(8,128)(2,1)S(1)}, u32[]{:S(2)}, u32[]{:S(2)}) collective-permute-start(bf16[112,128]{1,0:T(8,128)(2,1)S(1)} %get-tuple-element.103), channel_id=1, source_target_pairs={{0,2},{1,3},{2,4},{3,5},{4,6},{5,7},{6,0},{7,1},{8,10},{9,11},{10,... | collective-permute-start | bytes 86024 | tf_op jit(solution)/shard_map/ppermute | solution.py:467
  31.7 4.8 %collective-permute-start.18 = (bf16[112,128]{1,0:T(8,128)(2,1)S(1)}, bf16[112,128]{1,0:T(8,128)(2,1)S(1)}, u32[]{:S(2)}, u32[]{:S(2)}) collective-permute-start(bf16[112,128]{1,0:T(8,128)(2,1)S(1)} %get-tuple-element.104), channel_id=1, source_target_pairs={{0,4},{1,5},{2,6},{3,7},{4,0},{5,1},{6,2},{7,3},{8,12},{9,13},{10,... | collective-permute-start | bytes 86024 | tf_op jit(solution)/shard_map/ppermute | solution.py:467
  34.3 3.9 %collective-permute-start.19 = (bf16[112,128]{1,0:T(8,128)(2,1)S(1)}, bf16[112,128]{1,0:T(8,128)(2,1)S(1)}, u32[]{:S(2)}, u32[]{:S(2)}) collective-permute-start(bf16[112,128]{1,0:T(8,128)(2,1)S(1)} %get-tuple-element.105), channel_id=1, source_target_pairs={{0,6},{1,7},{2,0},{3,1},{4,2},{5,3},{6,4},{7,5},{8,14},{9,15},{10,... | collective-permute-start | bytes 86024 | tf_op jit(solution)/shard_map/ppermute | solution.py:467
  38.2 1.9 %collective-permute-start.20 = (bf16[112,128]{1,0:T(8,128)(2,1)S(1)}, bf16[112,128]{1,0:T(8,128)(2,1)S(1)}, u32[]{:S(2)}, u32[]{:S(2)}) collective-permute-start(bf16[112,128]{1,0:T(8,128)(2,1)S(1)} %get-tuple-element.107), channel_id=1, source_target_pairs={{0,8},{8,0},{16,24},{24,16},{1,9},{9,1},{17,25},{25,17},{2,10},{10... | collective-permute-start | bytes 86024 | tf_op jit(solution)/shard_map/ppermute | solution.py:462
  38.3 3.9 %collective-permute-start.21 = (bf16[112,128]{1,0:T(8,128)(2,1)S(1)}, bf16[112,128]{1,0:T(8,128)(2,1)S(1)}, u32[]{:S(2)}, u32[]{:S(2)}) collective-permute-start(bf16[112,128]{1,0:T(8,128)(2,1)S(1)} %get-tuple-element.107), channel_id=1, source_target_pairs={{0,16},{8,24},{16,0},{24,8},{1,17},{9,25},{17,1},{25,9},{2,18},{10... | collective-permute-start | bytes 86024 | tf_op jit(solution)/shard_map/ppermute | solution.py:462
  39.6 3.3 %collective-permute-start.22 = (bf16[112,128]{1,0:T(8,128)(2,1)S(1)}, bf16[112,128]{1,0:T(8,128)(2,1)S(1)}, u32[]{:S(2)}, u32[]{:S(2)}) collective-permute-start(bf16[112,128]{1,0:T(8,128)(2,1)S(1)} %get-tuple-element.107), channel_id=1, source_target_pairs={{0,24},{8,16},{16,8},{24,0},{1,25},{9,17},{17,9},{25,1},{2,26},{10... | collective-permute-start | bytes 86024 | tf_op jit(solution)/shard_map/ppermute | solution.py:462

commit v7 on v6

--- a/solution.py
+++ b/solution.py
@@ -13,6 +13,7 @@
 BF16 = jnp.bfloat16
 MIB = 1 << 20
 BACK = 1 << 32
+JOIN = 1 << 29
 
 
 def dot(a, b):
@@ -340,7 +341,7 @@
             sxy[z, t * n : (t + 1) * n] = early[t, z]
 
 
-def block_kernel(mix_top, mix, dw, dbias, block_out, done_out):
+def block_kernel(ahead, mix_top, mix, dw, dbias, block_out, done_out):
     chans, outs = dw.shape[2:]
     flat = [dw[:, k].reshape(3 * chans, outs) for k in range(3)]
     odd_before = lanes(mix_top[:, :chans], mix[0, :, :chans], mix[1, :, :chans])
@@ -398,8 +399,6 @@
     done_out[...] = jnp.zeros(done_out.shape, F32)
     chip, side = lax.axis_index("rows") >> 1, lax.axis_index("dp") & 1
     _, zs, n, _ = own.shape
-    for ref in (sx, sy):
-        ref[2 * zs * n :] = jnp.zeros((ref.shape[0] - 2 * zs * n, ref.shape[1]), BF16)
     for t in range(2):
         for z in range(zs):
 
@@ -408,18 +407,19 @@
 
             own[t, z] = total(chip, side)
             sxy[t, z] = total(1 - chip, 1 - side).astype(BF16)
-            at = slice((t * zs + z) * n, (t * zs + z + 1) * n)
-            sx[at] = total(1 - chip, side).astype(BF16)
-            sy[at] = total(chip, 1 - side).astype(BF16)
-
-
-def pack_kernel(own, gx, gy, gxy, early, ex, ey, after, after_too, out, s1, s2, s3, scr):
+            sx[t, z] = total(1 - chip, side).astype(BF16)
+            sy[t, z] = total(chip, 1 - side).astype(BF16)
+
+
+def join_kernel(early, ex, ey, out):
+    out[...] = early[...] + ex[...].astype(F32) + ey[...].astype(F32)
+
+
+def pack_kernel(own, gx, gy, gxy, early, after, after_too, out, s1, s2, s3, scr):
     z = lax.axis_index("dp") >> 1
     n = early.shape[2]
     for t in range(2):
-        at = slice(t * own.shape[0] * n, (t + 1) * own.shape[0] * n)
-        got = (ex[at].astype(F32) + ey[at].astype(F32)).reshape(early.shape[1:])
-        scr[:, t * n : (t + 1) * n, :] = early[t] + got + gxy[:, t * n : (t + 1) * n, :].astype(F32)
+        scr[:, t * n : (t + 1) * n, :] = early[t] + gxy[:, t * n : (t + 1) * n, :].astype(F32)
     late = gx[...].astype(F32) + gy[...].astype(F32) + gxy[:, 2 * n :, :].astype(F32)
     scr[:, 2 * n :, :] = own[...] + late
     out[...] = scr[z]
@@ -564,14 +564,14 @@
         dlast, keep, send = down_grad
         zs = owners // 2
         late_cut, early_cut = (zs, 3 * chunk, chans), (2, zs, wide, chans)
-        sent = ((2 * zs * wide + zs * deep) // 2 + zs * wide, chans)
         early_own, sx, sy, early_sxy, ahead = run(
             early_kernel,
             (keep, swap(send, "rows", 1)),
-            [(early_cut, F32), (sent, BF16), (sent, BF16), (early_cut, BF16), tile],
+            [(early_cut, F32)] + [(early_cut, BF16)] * 3 + [tile],
         )
-        early_got = swap(sx, "rows", 2), swap(sy, "dp", 1)
-    block, block_done = run(block_kernel, (mix_top, mix, dw, dbias), [((half, outs), BF16), tile])
+        (early,) = run(
+            join_kernel, (early_own, swap(sx, "rows", 2), swap(sy, "dp", 1)), [(early_cut, F32)], cost=JOIN
+        )
     (edge,) = run(halo_kernel, (ahead, par, hid_edge, gm, gain, shift), [((2,) + block_of, F32)])
     if packed:
         far = swap(far, "rows", 1)
@@ -588,6 +588,7 @@
             (*all_sums, par, x, hid, gp, gain),
             [tile, (block_of, BF16), ((3 * chans, 3 * chans), F32), tile],
         )
+    block, block_done = run(block_kernel, (par2, mix_top, mix, dw, dbias), [((half, outs), BF16), tile])
     gi, done = run(
         functools.partial(image_kernel, ranks - 1),
         (edge, gm, par2, g, w),
@@ -597,7 +598,7 @@
     if packed:
         part, *sends = run(
             pack_kernel,
-            (own, *swap_beside(sx, sy, sxy), early_own, *early_got, done, block_done),
+            (own, *swap_beside(sx, sy, sxy), early, done, block_done),
             [((deep, chans), F32)] + [((deep, chans), BF16)] * 3,
             [pltpu.VMEM((zs, deep, chans), F32)],
         )

time: 43.8 us -> 43.2 us (0.986)
  starting transfers between devices: 25.6 us -> 25.1 us
    ppermute x17, starting transfers between devices: 17 us -> 16.2 us  [swap(): lax.ppermute(x, axis, [(i, i ^ k) for i in range(lax.axis_size(axis))])]
    pallas_call x14 -> x15, Pallas kernels: 8.25 us -> 8.25 us  [run(): pl.pallas_call(kernel, in_specs=specs or [vmem] * len(args), out_shape=[j...]
  transfers between devices with their start and end apart: 23 -> 23, of which waited for: 9 -> 8; matrix products, arithmetic and copies ran while one was open for 0% -> 0% of each run, Pallas kernels for 16% -> 16%
where the time goes in v7:
time: 43.2 us; the launch traced here: 43 us
  starting transfers between devices  25.1 us (58%)
  Pallas kernels  8.25 us (19%)
  waiting for transfers between devices  8.16 us (19%)
  between operations  0.83 us (2%)
  local copies, waits for them, and re-layouts  0.67 us (2%)
    ppermute x17, starting transfers between devices, swap(): lax.ppermute(x, axis, [(i, i ^ k) for i in range(lax.axis_size(axis))])  16.2 us
    pallas_call x15, Pallas kernels, run(): pl.pallas_call(kernel, in_specs=specs or [vmem] * len(args), out_shape=[j...  8.25 us
    ppermute x17, waiting for transfers between devices, swap(): lax.ppermute(x, axis, [(i, i ^ k) for i in range(lax.axis_size(axis))])  5.63 us
    ppermute x3, starting transfers between devices, around(): return lax.ppermute(x, 'dp', [(i, (i + 2 * k) % n) for i in range(n)])  5.56 us
    ppermute x3, waiting for transfers between devices, around(): return lax.ppermute(x, 'dp', [(i, (i + 2 * k) % n) for i in range(n)])  2.53 us
    ppermute x1, starting transfers between devices, swap_both(): lax.ppermute(x, both, [(i, i ^ k) for i in range(lax.axis_size(both))])  1.79 us
    ppermute x2, starting transfers between devices, across(): lax.ppermute(x, 'rows', [p for i in range(1, n - 1, 2) for p in ((i, i +...  1.48 us
  transfers between devices with their start and end apart: 23, of which 8 were waited for; matrix products, arithmetic and copies ran while one was open for 0% of the time, Pallas kernels for 16%

profile of v7, /device:TPU:0, one launch (start us, length us, event | category | flops | bytes accessed | tf_op | source)
XLA Modules:
  0.0 43.0 jit_solution(6368349257071080133)
XLA Ops:
  0.6 0.0 copy-start
  0.6 0.0 copy-start.1
  0.7 0.8 %collective-permute-start.1 = (bf16[2,512,128]{2,1,0:T(8,128)(2,1)}, bf16[2,512,128]{2,1,0:T(8,128)(2,1)S(1)}, u32[]{:S(2)}, u32[]{:S(2)}) collective-permute-start(bf16[2,512,128]{2,1,0:T(8,128)(2,1)} %bitcast.18), channel_id=1, source_target_pairs={{8,16},{16,8},{9,17},{17,9},{10,18},{18,10},{11,19},{19,11},{12,20... | collective-permute-start | bytes 786440 | tf_op jit(solution)/shard_map/ppermute | solution.py:458
  1.5 4.3 %collective-permute-start = (bf16[2,512,128]{2,1,0:T(8,128)(2,1)}, bf16[2,512,128]{2,1,0:T(8,128)(2,1)S(1)}, u32[]{:S(2)}, u32[]{:S(2)}) collective-permute-start(bf16[2,512,128]{2,1,0:T(8,128)(2,1)} %bitcast.19), channel_id=1, source_target_pairs={{0,8},{8,0},{16,24},{24,16},{1,9},{9,1},{17,25},{25,17},{2,10},{10... | collective-permute-start | bytes 786440 | tf_op jit(solution)/shard_map/ppermute | solution.py:462
  5.9 0.0 copy-start.5
  5.9 0.6 %copy-done.6 = f32[128]{0:T(128)S(1)} copy-done((f32[128]{0:T(128)S(1)}, f32[128]{0:T(128)}, u32[]{:S(2)}) %copy-start.6) | copy-done | bytes 536
  6.5 0.0 copy-done.7
  6.5 0.0 copy-done.4
  6.6 0.9 %shard_map.144 = (bf16[3,3,128,128]{3,2,1,0:T(8,128)(2,1)S(1)}, bf16[3,3,128,256]{3,2,1,0:T(8,128)(2,1)S(1)}, bf16[256,256]{1,0:T(8,128)(2,1)S(1)}, f32[1,128]{1...) custom-call(f32[8,128]{1,0:T(8,128)S(1)} %shard_map.143.ahead, ...), custom_call_target="tpu_custom_call" | custom-call | flops 134217728 | bytes 1024 | tf_op jit(solution)/shard_map/pallas_call | solution.py:494
  7.5 0.7 %collective-permute-start.6 = (bf16[256,256]{1,0:T(8,128)(2,1)S(1)}, bf16[256,256]{1,0:T(8,128)(2,1)S(1)}, u32[]{:S(2)}, u32[]{:S(2)}) collective-permute-start(bf16[256,256]{1,0:T(8,128)(2,1)S(1)} %get-tuple-element.67.cot), channel_id=1, source_target_pairs={{8,16},{16,8},{9,17},{17,9},{10,18},{18,10},{11,19},{19,11},{12,20... | collective-permute-start | bytes 393224 | tf_op jit(solution)/shard_map/ppermute | solution.py:458
  8.1 1.3 %collective-permute-start.5 = (bf16[256,256]{1,0:T(8,128)(2,1)S(1)}, bf16[256,256]{1,0:T(8,128)(2,1)S(1)}, u32[]{:S(2)}, u32[]{:S(2)}) collective-permute-start(bf16[256,256]{1,0:T(8,128)(2,1)S(1)} %get-tuple-element.67.cot), channel_id=1, source_target_pairs={{0,8},{8,0},{16,24},{24,16},{1,9},{9,1},{17,25},{25,17},{2,10},{10... | collective-permute-start | bytes 393224 | tf_op jit(solution)/shard_map/ppermute | solution.py:462
  9.5 0.0 collective-permute-done.1.chip
  9.5 0.0 collective-permute-done.core
  9.5 1.1 %shard_map.145 = (bf16[4,2,256,128]{3,2,1,0:T(8,128)(2,1)S(1)}, f32[2,2,256,128]{3,2,1,0:T(8,128)S(1)}, f32[8,128]{1,0:T(8,128)S(1)}) custom-call(bf16[2,512,128]{2,1,0:T(8,128)(2,1)S(1)} %collective-permute-done.core, bf16[2,512,128]{2,1,0:T(8,128)(2,1)S(1)} %collective-permute-done.1.chip, bf16[2,2,256,128]{3,2,1,0:T(8,128)(2,1)S(1)} %get-tuple-element.61.own, ...), custom_call_target="tpu_custom_call" | custom-call | flops 134217728 | bytes 1024 | tf_op jit(solution)/shard_map/pallas_call | solution.py:494
  10.6 1.7 %collective-permute-start.4 = (f32[8,128]{1,0:T(8,128)S(1)}, f32[8,128]{1,0:T(8,128)S(1)}, u32[]{:S(2)}, u32[]{:S(2)}) collective-permute-start(f32[8,128]{1,0:T(8,128)S(1)} %get-tuple-element.64.refs_0_), channel_id=1, source_target_pairs={{0,24},{8,16},{16,8},{24,0},{1,25},{9,17},{17,9},{25,1},{2,26},{10... | collective-permute-start | bytes 12296 | tf_op jit(solution)/shard_map/ppermute | solution.py:462
  12.3 0.5 %collective-permute-start.3 = (f32[8,128]{1,0:T(8,128)S(1)}, f32[8,128]{1,0:T(8,128)S(1)}, u32[]{:S(2)}, u32[]{:S(2)}) collective-permute-start(f32[8,128]{1,0:T(8,128)S(1)} %get-tuple-element.64.refs_0_), channel_id=1, source_target_pairs={{0,16},{8,24},{16,0},{24,8},{1,17},{9,25},{17,1},{25,9},{2,18},{10... | collective-permute-start | bytes 12296 | tf_op jit(solution)/shard_map/ppermute | solution.py:462
  12.8 0.1 collective-permute-start.2
  12.9 0.0 collective-permute-done.6.cot_chip
  12.9 0.0 collective-permute-done.5.cot_core
  12.9 0.8 %shard_map.146 = (f32[2,2,256,128]{3,2,1,0:T(8,128)S(1)}, f32[4,2,256,128]{3,2,1,0:T(8,128)S(1)}, bf16[2,256,128]{2,1,0:T(8,128)(2,1)S(1)}, f32[8,256]{1,0:T(8,128)S(1)}) custom-call(bf16[2,512,128]{2,1,0:T(8,128)(2,1)S(1)} %collective-permute-done.core, bf16[2,512,128]{2,1,0:T(8,128)(2,1)S(1)} %collective-permute-done.1.chip, ...), custom_call_target="tpu_custom_call" | custom-call | flops 134217728 | bytes 1024 | tf_op jit(solution)/shard_map/pallas_call | solution.py:494
  13.7 0.0 collective-permute-done.4.refs_3_
  13.8 2.2 %collective-permute-done.3.refs_2_ = f32[8,128]{1,0:T(8,128)S(1)} collective-permute-done((f32[8,128]{1,0:T(8,128)S(1)}, f32[8,128]{1,0:T(8,128)S(1)}, u32[]{:S(2)}, u32[]{:S(2)}) %collective-permute-start.3) | collective-permute-done | bytes 4128 | tf_op jit(solution)/shard_map/ppermute | solution.py:462
  15.9 0.0 collective-permute-done.2.refs_1_
  15.9 0.5 %shard_map.147 = (f32[8,128]{1,0:T(8,128)S(1)}, bf16[2,256,384]{2,1,0:T(8,128)(2,1)S(1)}, f32[2,2,256,128]{3,2,1,0:T(8,128)S(1)}, f32[8,128]{1,0:T(8,128)S(1)}, f32[2,2,256,128]{3,2,1,0:T(8,128)S(1)}) custom-call(f32[8,128]{1,0:T(8,128)S(1)} %get-tuple-element.64.refs_0_, f32[8,128]{1,0:T(8,128)S(1)} %collective-permute-done.2.refs_1_, ...), custom_call_target="tpu_custom_call" | custom-call | flops 134217728 | bytes 1024 | tf_op jit(solution)/shard_map/pallas_call | solution.py:494
  16.5 0.1 collective-permute-start.10
  16.6 0.5 %shard_map.148 = (bf16[256,384]{1,0:T(8,128)(2,1)S(1)}, f32[256,128]{1,0:T(8,128)S(1)}, f32[2,2,8,32,128]{4,3,2,1,0:T(8,128)S(1)}, bf16[2,2,8,32,128]{4,3,2,1,0:T(8,128)(2,1)S(1)}) custom-call(f32[8,128]{1,0:T(8,128)S(1)} %get-tuple-element.75.par, bf16[4,2,256,128]{3,2,1,0:T(8,128)(2,1)S(1)} %get-tuple-element.65.x.refs_4_, ...), custom_call_target="tpu_custom_call" | custom-call | flops 134217728 | bytes 1024 | tf_op jit(solution)/shard_map/pallas_call | solution.py:494
  17.0 0.6 %collective-permute-start.11 = (bf16[2,2,8,32,128]{4,3,2,1,0:T(8,128)(2,1)S(1)}, bf16[2,2,8,32,128]{4,3,2,1,0:T(8,128)(2,1)S(1)}, u32[]{:S(2)}, u32[]{:S(2)}) collective-permute-start(bf16[2,2,8,32,128]{4,3,2,1,0:T(8,128)(2,1)S(1)} %get-tuple-element.82), channel_id=1, source_target_pairs={{0,8},{8,0},{16,24},{24,16},{1,9},{9,1},{17,25},{25,17},{2,10},{10... | collective-permute-start | bytes 786440 | tf_op jit(solution)/shard_map/ppermute | solution.py:462
  17.6 0.2 collective-permute-start.9
  17.7 1.5 %collective-permute-start.8 = (f32[8,128]{1,0:T(8,128)S(1)}, f32[8,128]{1,0:T(8,128)S(1)}, u32[]{:S(2)}, u32[]{:S(2)}) collective-permute-start(f32[8,128]{1,0:T(8,128)S(1)} %get-tuple-element.74.s0), channel_id=1, source_target_pairs={{0,16},{8,24},{16,0},{24,8},{1,17},{9,25},{17,1},{25,9},{2,18},{10... | collective-permute-start | bytes 12296 | tf_op jit(solution)/shard_map/ppermute | solution.py:462
  19.3 0.2 collective-permute-start.7
  19.5 0.0 collective-permute-done.11.got
  19.5 0.1 shard_map.149
  19.5 0.5 %collective-permute-start.15 = (bf16[2,4,32,128]{3,2,1,0:T(8,128)(2,1)S(1)}, bf16[2,4,32,128]{3,2,1,0:T(8,128)(2,1)S(1)}, u32[]{:S(2)}, u32[]{:S(2)}) collective-permute-start(bf16[2,4,32,128]{3,2,1,0:T(8,128)(2,1)S(1)} %get-tuple-element.98), channel_id=1, source_target_pairs={{0,16},{8,24},{16,0},{24,8},{1,17},{9,25},{17,1},{25,9},{2,18},{10... | collective-permute-start | bytes 196616 | tf_op jit(solution)/shard_map/ppermute | solution.py:462
  20.1 0.2 shard_map.150.edge.parts
  20.3 0.4 collective-permute-done.9.s3
  20.6 1.5 %collective-permute-start.16 = (bf16[2,4,32,128]{3,2,1,0:T(8,128)(2,1)S(1)}, bf16[2,4,32,128]{3,2,1,0:T(8,128)(2,1)S(1)}, u32[]{:S(2)}, u32[]{:S(2)}) collective-permute-start(bf16[2,4,32,128]{3,2,1,0:T(8,128)(2,1)S(1)} %get-tuple-element.99), channel_id=1, source_target_pairs={{0,1},{1,0},{2,3},{3,2},{4,5},{5,4},{6,7},{7,6},{8,9},{9,8},{10,11... | collective-permute-start | bytes 196616 | tf_op jit(solution)/shard_map/ppermute | solution.py:462
  22.1 0.0 collective-permute-done.8.s2
  22.1 0.0 collective-permute-done.7.s1
  22.1 0.0 collective-permute-done.10.far
  22.1 1.0 %shard_map.151 = (f32[8,128]{1,0:T(8,128)S(1)}, bf16[2,2,256,128]{3,2,1,0:T(8,128)(2,1)S(1)}, f32[4,48,128]{2,1,0:T(8,128)S(1)}, bf16[4,48,128]{2,1,0:T(8,128)(2...) custom-call(f32[8,128]{1,0:T(8,128)S(1)} %get-tuple-element.74.s0, ...), custom_call_target="tpu_custom_call" | custom-call | flops 4294967296 | bytes 1024 | tf_op jit(solution)/shard_map/pallas_call | solution.py:494
  23.1 1.8 %collective-permute-start.14 = (bf16[4,112,128]{2,1,0:T(8,128)(2,1)S(1)}, bf16[4,112,128]{2,1,0:T(8,128)(2,1)S(1)}, u32[]{:S(2)}, u32[]{:S(2)}) collective-permute-start(bf16[4,112,128]{2,1,0:T(8,128)(2,1)S(1)} %get-tuple-element.96), channel_id=1, source_target_pairs={{0,17},{1,16},{2,19},{3,18},{4,21},{5,20},{6,23},{7,22},{8,25},{9,... | collective-permute-start | bytes 344072 | tf_op jit(solution)/shard_map/ppermute | solution.py:473
  24.9 0.5 %collective-permute-start.12 = (bf16[4,48,128]{2,1,0:T(8,128)(2,1)S(1)}, bf16[4,48,128]{2,1,0:T(8,128)(2,1)S(1)}, u32[]{:S(2)}, u32[]{:S(2)}) collective-permute-start(bf16[4,48,128]{2,1,0:T(8,128)(2,1)S(1)} %get-tuple-element.94), channel_id=1, source_target_pairs={{0,16},{8,24},{16,0},{24,8},{1,17},{9,25},{17,1},{25,9},{2,18},{10... | collective-permute-start | bytes 147464 | tf_op jit(solution)/shard_map/ppermute | solution.py:462
  25.4 1.3 %collective-permute-start.13 = (bf16[4,48,128]{2,1,0:T(8,128)(2,1)S(1)}, bf16[4,48,128]{2,1,0:T(8,128)(2,1)S(1)}, u32[]{:S(2)}, u32[]{:S(2)}) collective-permute-start(bf16[4,48,128]{2,1,0:T(8,128)(2,1)S(1)} %get-tuple-element.95), channel_id=1, source_target_pairs={{0,1},{1,0},{2,3},{3,2},{4,5},{5,4},{6,7},{7,6},{8,9},{9,8},{10,11... | collective-permute-start | bytes 147464 | tf_op jit(solution)/shard_map/ppermute | solution.py:462
  26.7 0.0 collective-permute-done.15.ex
  26.7 0.0 collective-permute-done.16.ey
  26.7 1.4 %shard_map.153 = (bf16[2,512,128]{2,1,0:T(8,128)(2,1)}, f32[8,128]{1,0:T(8,128)S(1)}) custom-call(f32[2,2,2,256,128]{4,3,2,1,0:T(8,128)S(1)} %shard_map.150.edge.parts, f32[4,2,256,128]{3,2,1,0:T(8,128)S(1)} %get-tuple-element.71.refs_6_.gm, f32[8,128]{1,0:T(8,128)S(1)} %get-tuple-element.87.ahead.par2, bf16[2,2,256,128]{3,2,1,0:T(8,128)(2,1)S(1)} %get-tuple-element.91.g, ...), custom_call_target="tpu_custom_call" | custom-call | flops 134217728 | bytes 1024 | tf_op jit(solution)/shard_map/pallas_call | solution.py:494
  28.1 1.0 %shard_map.152 = (bf16[256,256]{1,0:T(8,128)(2,1)}, f32[8,128]{1,0:T(8,128)S(1)}) custom-call(f32[8,128]{1,0:T(8,128)S(1)} %get-tuple-element.87.ahead.par2, bf16[256,384]{1,0:T(8,128)(2,1)S(1)} %get-tuple-element.88.mix_top, bf16[2,256,384]{2,1,0:T(8,128)(2,1)S(1)} %get-tuple-element.80.mix, bf16[3,3,128,256]{3,2,1,0:T(8,128)(2,1)S(1)} %get-tuple-element.68.dw, ...), custom_call_target="tpu_custom_call" | custom-call | flops 134217728 | bytes 1024 | tf_op jit(solution)/shard_map/pallas_call | solution.py:494
  29.1 0.0 collective-permute-done.12.gx
  29.1 0.9 %collective-permute-done.13.gy = bf16[4,48,128]{2,1,0:T(8,128)(2,1)S(1)} collective-permute-done((bf16[4,48,128]{2,1,0:T(8,128)(2,1)S(1)}, bf16[4,48,128]{2,1,0:T(8,128)(2,1)S(1)}, u32[]{:S(2)}, u32[]{:S(2)}) %collective-permute-start.13) | collective-permute-done | bytes 49184 | tf_op jit(solution)/shard_map/ppermute | solution.py:462
  30.0 0.0 collective-permute-done.14.gxy
  30.0 0.1 shard_map.155
  30.1 1.6 %collective-permute-start.17 = (bf16[112,128]{1,0:T(8,128)(2,1)S(1)}, bf16[112,128]{1,0:T(8,128)(2,1)S(1)}, u32[]{:S(2)}, u32[]{:S(2)}) collective-permute-start(bf16[112,128]{1,0:T(8,128)(2,1)S(1)} %get-tuple-element.103), channel_id=1, source_target_pairs={{0,2},{1,3},{2,4},{3,5},{4,6},{5,7},{6,0},{7,1},{8,10},{9,11},{10,... | collective-permute-start | bytes 86024 | tf_op jit(solution)/shard_map/ppermute | solution.py:467
  31.7 2.6 %collective-permute-start.18 = (bf16[112,128]{1,0:T(8,128)(2,1)S(1)}, bf16[112,128]{1,0:T(8,128)(2,1)S(1)}, u32[]{:S(2)}, u32[]{:S(2)}) collective-permute-start(bf16[112,128]{1,0:T(8,128)(2,1)S(1)} %get-tuple-element.104), channel_id=1, source_target_pairs={{0,4},{1,5},{2,6},{3,7},{4,0},{5,1},{6,2},{7,3},{8,12},{9,13},{10,... | collective-permute-start | bytes 86024 | tf_op jit(solution)/shard_map/ppermute | solution.py:467
  34.3 1.3 %collective-permute-start.19 = (bf16[112,128]{1,0:T(8,128)(2,1)S(1)}, bf16[112,128]{1,0:T(8,128)(2,1)S(1)}, u32[]{:S(2)}, u32[]{:S(2)}) collective-permute-start(bf16[112,128]{1,0:T(8,128)(2,1)S(1)} %get-tuple-element.105), channel_id=1, source_target_pairs={{0,6},{1,7},{2,0},{3,1},{4,2},{5,3},{6,4},{7,5},{8,14},{9,15},{10,... | collective-permute-start | bytes 86024 | tf_op jit(solution)/shard_map/ppermute | solution.py:467
  35.7 0.3 collective-permute-done.17.g1
  35.9 0.6 %collective-permute-done.18.g2 = bf16[112,128]{1,0:T(8,128)(2,1)S(1)} collective-permute-done((bf16[112,128]{1,0:T(8,128)(2,1)S(1)}, bf16[112,128]{1,0:T(8,128)(2,1)S(1)}, u32[]{:S(2)}, u32[]{:S(2)}) %collective-permute-start.18) | collective-permute-done | bytes 28704 | tf_op jit(solution)/shard_map/ppermute | solution.py:467
  36.5 1.7 %collective-permute-done.19.g3 = bf16[112,128]{1,0:T(8,128)(2,1)S(1)} collective-permute-done((bf16[112,128]{1,0:T(8,128)(2,1)S(1)}, bf16[112,128]{1,0:T(8,128)(2,1)S(1)}, u32[]{:S(2)}, u32[]{:S(2)}) %collective-permute-start.19) | collective-permute-done | bytes 28704 | tf_op jit(solution)/shard_map/ppermute | solution.py:467
  38.2 0.1 collective-permute-start.22
  38.3 1.3 %collective-permute-start.21 = (bf16[112,128]{1,0:T(8,128)(2,1)S(1)}, bf16[112,128]{1,0:T(8,128)(2,1)S(1)}, u32[]{:S(2)}, u32[]{:S(2)}) collective-permute-start(bf16[112,128]{1,0:T(8,128)(2,1)S(1)} %get-tuple-element.107), channel_id=1, source_target_pairs={{0,16},{8,24},{16,0},{24,8},{1,17},{9,25},{17,1},{25,9},{2,18},{10... | collective-permute-start | bytes 86024 | tf_op jit(solution)/shard_map/ppermute | solution.py:462
  39.6 0.6 %collective-permute-start.20 = (bf16[112,128]{1,0:T(8,128)(2,1)S(1)}, bf16[112,128]{1,0:T(8,128)(2,1)S(1)}, u32[]{:S(2)}, u32[]{:S(2)}) collective-permute-start(bf16[112,128]{1,0:T(8,128)(2,1)S(1)} %get-tuple-element.107), channel_id=1, source_target_pairs={{0,8},{8,0},{16,24},{24,16},{1,9},{9,1},{17,25},{25,17},{2,10},{10... | collective-permute-start | bytes 86024 | tf_op jit(solution)/shard_map/ppermute | solution.py:462
  40.1 1.5 %collective-permute-done.22.q3 = bf16[112,128]{1,0:T(8,128)(2,1)S(1)} collective-permute-done((bf16[112,128]{1,0:T(8,128)(2,1)S(1)}, bf16[112,128]{1,0:T(8,128)(2,1)S(1)}, u32[]{:S(2)}, u32[]{:S(2)}) %collective-permute-start.22) | collective-permute-done | bytes 28704 | tf_op jit(solution)/shard_map/ppermute | solution.py:462
  41.6 0.6 %collective-permute-done.21.q2 = bf16[112,128]{1,0:T(8,128)(2,1)S(1)} collective-permute-done((bf16[112,128]{1,0:T(8,128)(2,1)S(1)}, bf16[112,128]{1,0:T(8,128)(2,1)S(1)}, u32[]{:S(2)}, u32[]{:S(2)}) %collective-permute-start.21) | collective-permute-done | bytes 28704 | tf_op jit(solution)/shard_map/ppermute | solution.py:462
  42.2 0.0 collective-permute-done.20.q1
  42.2 0.7 %shard_map.157 = (f32[9,32,128]{2,1,0:T(8,128)}, f32[9,16,128]{2,1,0:T(8,128)}, f32[1,16]{1,0:T(1,128)}, f32[1,16]{1,0:T(1,128)}, f32[1,16]{1,0:T(1,128)}, /*index=5*/f32[1,32]{1,0:T(1,128)}) custom-call(f32[112,128]{1,0:T(8,128)S(1)} %get-tuple-element.106.q0, bf16[112,128]{1,0:T(8,128)(2,1)S(1)} %collective-permute-done.20.q1, ...), custom_call_target="tpu_custom_call" | custom-call | flops 134217728 | bytes 1024 | tf_op jit(solution)/shard_map/pallas_call | solution.py:494
  (13 shorter events, 0.1 us)
Async XLA Ops:
  0.6 5.2 %copy-start = (bf16[3,3,128,256]{3,2,1,0:T(8,128)(2,1)S(1)}, bf16[3,3,128,256]{3,2,1,0:T(8,128)(2,1)}, u32[]{:S(2)}) copy-start(bf16[3,3,128,256]{3,2,1,0:T(8,128)(2,1)} %dw.1) | copy-start | bytes 1769476
  0.6 5.2 %copy-start.1 = (bf16[3,3,128,128]{3,2,1,0:T(8,128)(2,1)S(1)}, bf16[3,3,128,128]{3,2,1,0:T(8,128)(2,1)}, u32[]{:S(2)}) copy-start(bf16[3,3,128,128]{3,2,1,0:T(8,128)(2,1)} %w.1) | copy-start | bytes 884740
  0.7 5.2 %copy-start.2 = (bf16[1,2,512,128]{3,2,1,0:T(8,128)(2,1)S(1)}, bf16[1,2,512,128]{3,2,1,0:T(8,128)(2,1)}, u32[]{:S(2)}) copy-start(bf16[1,2,512,128]{3,2,1,0:T(8,128)(2,1)} %param.8) | copy-start | bytes 786436
  0.7 5.2 %copy-start.3 = (bf16[1,1,256,256]{3,2,1,0:T(8,128)(2,1)S(1)}, bf16[1,1,256,256]{3,2,1,0:T(8,128)(2,1)}, u32[]{:S(2)}) copy-start(bf16[1,1,256,256]{3,2,1,0:T(8,128)(2,1)} %param.15) | copy-start | bytes 393220
  0.7 8.8 %collective-permute-start.1 = (bf16[2,512,128]{2,1,0:T(8,128)(2,1)}, bf16[2,512,128]{2,1,0:T(8,128)(2,1)S(1)}, u32[]{:S(2)}, u32[]{:S(2)}) collective-permute-start(bf16[2,512,128]{2,1,0:T(8,128)(2,1)} %bitcast.18), channel_id=1, source_target_pairs={{8,16},{16,8},{9,17},{17,9},{10,18},{18,10},{11,19},{19,11},{12,20... | collective-permute-start | bytes 786440 | tf_op jit(solution)/shard_map/ppermute | solution.py:458
  1.5 8.0 %collective-permute-start = (bf16[2,512,128]{2,1,0:T(8,128)(2,1)}, bf16[2,512,128]{2,1,0:T(8,128)(2,1)S(1)}, u32[]{:S(2)}, u32[]{:S(2)}) collective-permute-start(bf16[2,512,128]{2,1,0:T(8,128)(2,1)} %bitcast.19), channel_id=1, source_target_pairs={{0,8},{8,0},{16,24},{24,16},{1,9},{9,1},{17,25},{25,17},{2,10},{10... | collective-permute-start | bytes 786440 | tf_op jit(solution)/shard_map/ppermute | solution.py:462
  5.8 0.7 %copy-start.6 = (f32[128]{0:T(128)S(1)}, f32[128]{0:T(128)}, u32[]{:S(2)}) copy-start(f32[128]{0:T(128)} %param.11) | copy-start | bytes 1540
  5.8 0.7 %copy-start.7 = (f32[128]{0:T(128)S(1)}, f32[128]{0:T(128)}, u32[]{:S(2)}) copy-start(f32[128]{0:T(128)} %param.12) | copy-start | bytes 1540
  5.8 0.7 %copy-start.4 = (f32[256]{0:T(256)S(1)}, f32[256]{0:T(256)}, u32[]{:S(2)}) copy-start(f32[256]{0:T(256)} %param.14) | copy-start | bytes 3076
  5.9 0.7 %copy-start.5 = (f32[128]{0:T(128)S(1)}, f32[128]{0:T(128)}, u32[]{:S(2)}) copy-start(f32[128]{0:T(128)} %param.10) | copy-start | bytes 1540
  7.5 5.4 %collective-permute-start.6 = (bf16[256,256]{1,0:T(8,128)(2,1)S(1)}, bf16[256,256]{1,0:T(8,128)(2,1)S(1)}, u32[]{:S(2)}, u32[]{:S(2)}) collective-permute-start(bf16[256,256]{1,0:T(8,128)(2,1)S(1)} %get-tuple-element.67.cot), channel_id=1, source_target_pairs={{8,16},{16,8},{9,17},{17,9},{10,18},{18,10},{11,19},{19,11},{12,20... | collective-permute-start | bytes 393224 | tf_op jit(solution)/shard_map/ppermute | solution.py:458
  8.1 4.8 %collective-permute-start.5 = (bf16[256,256]{1,0:T(8,128)(2,1)S(1)}, bf16[256,256]{1,0:T(8,128)(2,1)S(1)}, u32[]{:S(2)}, u32[]{:S(2)}) collective-permute-start(bf16[256,256]{1,0:T(8,128)(2,1)S(1)} %get-tuple-element.67.cot), channel_id=1, source_target_pairs={{0,8},{8,0},{16,24},{24,16},{1,9},{9,1},{17,25},{25,17},{2,10},{10... | collective-permute-start | bytes 393224 | tf_op jit(solution)/shard_map/ppermute | solution.py:462
  10.6 3.2 %collective-permute-start.4 = (f32[8,128]{1,0:T(8,128)S(1)}, f32[8,128]{1,0:T(8,128)S(1)}, u32[]{:S(2)}, u32[]{:S(2)}) collective-permute-start(f32[8,128]{1,0:T(8,128)S(1)} %get-tuple-element.64.refs_0_), channel_id=1, source_target_pairs={{0,24},{8,16},{16,8},{24,0},{1,25},{9,17},{17,9},{25,1},{2,26},{10... | collective-permute-start | bytes 12296 | tf_op jit(solution)/shard_map/ppermute | solution.py:462
  12.3 3.6 %collective-permute-start.3 = (f32[8,128]{1,0:T(8,128)S(1)}, f32[8,128]{1,0:T(8,128)S(1)}, u32[]{:S(2)}, u32[]{:S(2)}) collective-permute-start(f32[8,128]{1,0:T(8,128)S(1)} %get-tuple-element.64.refs_0_), channel_id=1, source_target_pairs={{0,16},{8,24},{16,0},{24,8},{1,17},{9,25},{17,1},{25,9},{2,18},{10... | collective-permute-start | bytes 12296 | tf_op jit(solution)/shard_map/ppermute | solution.py:462
  12.8 3.1 %collective-permute-start.2 = (f32[8,128]{1,0:T(8,128)S(1)}, f32[8,128]{1,0:T(8,128)S(1)}, u32[]{:S(2)}, u32[]{:S(2)}) collective-permute-start(f32[8,128]{1,0:T(8,128)S(1)} %get-tuple-element.64.refs_0_), channel_id=1, source_target_pairs={{0,8},{8,0},{16,24},{24,16},{1,9},{9,1},{17,25},{25,17},{2,10},{10... | collective-permute-start | bytes 12296 | tf_op jit(solution)/shard_map/ppermute | solution.py:462
  16.5 5.7 %collective-permute-start.10 = (f32[2,2,256,128]{3,2,1,0:T(8,128)S(1)}, f32[2,2,256,128]{3,2,1,0:T(8,128)S(1)}, u32[]{:S(2)}, u32[]{:S(2)}) collective-permute-start(f32[2,2,256,128]{3,2,1,0:T(8,128)S(1)} %get-tuple-element.78), channel_id=1, source_target_pairs={{0,8},{8,0},{16,24},{24,16},{1,9},{9,1},{17,25},{25,17},{2,10},{10... | collective-permute-start | bytes 1572872 | tf_op jit(solution)/shard_map/ppermute | solution.py:462
  17.0 2.4 %collective-permute-start.11 = (bf16[2,2,8,32,128]{4,3,2,1,0:T(8,128)(2,1)S(1)}, bf16[2,2,8,32,128]{4,3,2,1,0:T(8,128)(2,1)S(1)}, u32[]{:S(2)}, u32[]{:S(2)}) collective-permute-start(bf16[2,2,8,32,128]{4,3,2,1,0:T(8,128)(2,1)S(1)} %get-tuple-element.82), channel_id=1, source_target_pairs={{0,8},{8,0},{16,24},{24,16},{1,9},{9,1},{17,25},{25,17},{2,10},{10... | collective-permute-start | bytes 786440 | tf_op jit(solution)/shard_map/ppermute | solution.py:462
  17.6 3.0 %collective-permute-start.9 = (f32[8,128]{1,0:T(8,128)S(1)}, f32[8,128]{1,0:T(8,128)S(1)}, u32[]{:S(2)}, u32[]{:S(2)}) collective-permute-start(f32[8,128]{1,0:T(8,128)S(1)} %get-tuple-element.74.s0), channel_id=1, source_target_pairs={{0,24},{8,16},{16,8},{24,0},{1,25},{9,17},{17,9},{25,1},{2,26},{10... | collective-permute-start | bytes 12296 | tf_op jit(solution)/shard_map/ppermute | solution.py:462
  17.7 4.4 %collective-permute-start.8 = (f32[8,128]{1,0:T(8,128)S(1)}, f32[8,128]{1,0:T(8,128)S(1)}, u32[]{:S(2)}, u32[]{:S(2)}) collective-permute-start(f32[8,128]{1,0:T(8,128)S(1)} %get-tuple-element.74.s0), channel_id=1, source_target_pairs={{0,16},{8,24},{16,0},{24,8},{1,17},{9,25},{17,1},{25,9},{2,18},{10... | collective-permute-start | bytes 12296 | tf_op jit(solution)/shard_map/ppermute | solution.py:462
  19.3 2.8 %collective-permute-start.7 = (f32[8,128]{1,0:T(8,128)S(1)}, f32[8,128]{1,0:T(8,128)S(1)}, u32[]{:S(2)}, u32[]{:S(2)}) collective-permute-start(f32[8,128]{1,0:T(8,128)S(1)} %get-tuple-element.74.s0), channel_id=1, source_target_pairs={{0,8},{8,0},{16,24},{24,16},{1,9},{9,1},{17,25},{25,17},{2,10},{10... | collective-permute-start | bytes 12296 | tf_op jit(solution)/shard_map/ppermute | solution.py:462
  19.5 7.2 %collective-permute-start.15 = (bf16[2,4,32,128]{3,2,1,0:T(8,128)(2,1)S(1)}, bf16[2,4,32,128]{3,2,1,0:T(8,128)(2,1)S(1)}, u32[]{:S(2)}, u32[]{:S(2)}) collective-permute-start(bf16[2,4,32,128]{3,2,1,0:T(8,128)(2,1)S(1)} %get-tuple-element.98), channel_id=1, source_target_pairs={{0,16},{8,24},{16,0},{24,8},{1,17},{9,25},{17,1},{25,9},{2,18},{10... | collective-permute-start | bytes 196616 | tf_op jit(solution)/shard_map/ppermute | solution.py:462
  20.6 6.1 %collective-permute-start.16 = (bf16[2,4,32,128]{3,2,1,0:T(8,128)(2,1)S(1)}, bf16[2,4,32,128]{3,2,1,0:T(8,128)(2,1)S(1)}, u32[]{:S(2)}, u32[]{:S(2)}) collective-permute-start(bf16[2,4,32,128]{3,2,1,0:T(8,128)(2,1)S(1)} %get-tuple-element.99), channel_id=1, source_target_pairs={{0,1},{1,0},{2,3},{3,2},{4,5},{5,4},{6,7},{7,6},{8,9},{9,8},{10,11... | collective-permute-start | bytes 196616 | tf_op jit(solution)/shard_map/ppermute | solution.py:462
  23.1 6.9 %collective-permute-start.14 = (bf16[4,112,128]{2,1,0:T(8,128)(2,1)S(1)}, bf16[4,112,128]{2,1,0:T(8,128)(2,1)S(1)}, u32[]{:S(2)}, u32[]{:S(2)}) collective-permute-start(bf16[4,112,128]{2,1,0:T(8,128)(2,1)S(1)} %get-tuple-element.96), channel_id=1, source_target_pairs={{0,17},{1,16},{2,19},{3,18},{4,21},{5,20},{6,23},{7,22},{8,25},{9,... | collective-permute-start | bytes 344072 | tf_op jit(solution)/shard_map/ppermute | solution.py:473
  24.9 4.2 %collective-permute-start.12 = (bf16[4,48,128]{2,1,0:T(8,128)(2,1)S(1)}, bf16[4,48,128]{2,1,0:T(8,128)(2,1)S(1)}, u32[]{:S(2)}, u32[]{:S(2)}) collective-permute-start(bf16[4,48,128]{2,1,0:T(8,128)(2,1)S(1)} %get-tuple-element.94), channel_id=1, source_target_pairs={{0,16},{8,24},{16,0},{24,8},{1,17},{9,25},{17,1},{25,9},{2,18},{10... | collective-permute-start | bytes 147464 | tf_op jit(solution)/shard_map/ppermute | solution.py:462
  25.4 4.6 %collective-permute-start.13 = (bf16[4,48,128]{2,1,0:T(8,128)(2,1)S(1)}, bf16[4,48,128]{2,1,0:T(8,128)(2,1)S(1)}, u32[]{:S(2)}, u32[]{:S(2)}) collective-permute-start(bf16[4,48,128]{2,1,0:T(8,128)(2,1)S(1)} %get-tuple-element.95), channel_id=1, source_target_pairs={{0,1},{1,0},{2,3},{3,2},{4,5},{5,4},{6,7},{7,6},{8,9},{9,8},{10,11... | collective-permute-start | bytes 147464 | tf_op jit(solution)/shard_map/ppermute | solution.py:462
  30.1 5.8 %collective-permute-start.17 = (bf16[112,128]{1,0:T(8,128)(2,1)S(1)}, bf16[112,128]{1,0:T(8,128)(2,1)S(1)}, u32[]{:S(2)}, u32[]{:S(2)}) collective-permute-start(bf16[112,128]{1,0:T(8,128)(2,1)S(1)} %get-tuple-element.103), channel_id=1, source_target_pairs={{0,2},{1,3},{2,4},{3,5},{4,6},{5,7},{6,0},{7,1},{8,10},{9,11},{10,... | collective-permute-start | bytes 86024 | tf_op jit(solution)/shard_map/ppermute | solution.py:467
  31.7 4.8 %collective-permute-start.18 = (bf16[112,128]{1,0:T(8,128)(2,1)S(1)}, bf16[112,128]{1,0:T(8,128)(2,1)S(1)}, u32[]{:S(2)}, u32[]{:S(2)}) collective-permute-start(bf16[112,128]{1,0:T(8,128)(2,1)S(1)} %get-tuple-element.104), channel_id=1, source_target_pairs={{0,4},{1,5},{2,6},{3,7},{4,0},{5,1},{6,2},{7,3},{8,12},{9,13},{10,... | collective-permute-start | bytes 86024 | tf_op jit(solution)/shard_map/ppermute | solution.py:467
  34.3 3.9 %collective-permute-start.19 = (bf16[112,128]{1,0:T(8,128)(2,1)S(1)}, bf16[112,128]{1,0:T(8,128)(2,1)S(1)}, u32[]{:S(2)}, u32[]{:S(2)}) collective-permute-start(bf16[112,128]{1,0:T(8,128)(2,1)S(1)} %get-tuple-element.105), channel_id=1, source_target_pairs={{0,6},{1,7},{2,0},{3,1},{4,2},{5,3},{6,4},{7,5},{8,14},{9,15},{10,... | collective-permute-start | bytes 86024 | tf_op jit(solution)/shard_map/ppermute | solution.py:467
  38.2 3.4 %collective-permute-start.22 = (bf16[112,128]{1,0:T(8,128)(2,1)S(1)}, bf16[112,128]{1,0:T(8,128)(2,1)S(1)}, u32[]{:S(2)}, u32[]{:S(2)}) collective-permute-start(bf16[112,128]{1,0:T(8,128)(2,1)S(1)} %get-tuple-element.107), channel_id=1, source_target_pairs={{0,24},{8,16},{16,8},{24,0},{1,25},{9,17},{17,9},{25,1},{2,26},{10... | collective-permute-start | bytes 86024 | tf_op jit(solution)/shard_map/ppermute | solution.py:462
  38.3 4.0 %collective-permute-start.21 = (bf16[112,128]{1,0:T(8,128)(2,1)S(1)}, bf16[112,128]{1,0:T(8,128)(2,1)S(1)}, u32[]{:S(2)}, u32[]{:S(2)}) collective-permute-start(bf16[112,128]{1,0:T(8,128)(2,1)S(1)} %get-tuple-element.107), channel_id=1, source_target_pairs={{0,16},{8,24},{16,0},{24,8},{1,17},{9,25},{17,1},{25,9},{2,18},{10... | collective-permute-start | bytes 86024 | tf_op jit(solution)/shard_map/ppermute | solution.py:462
  39.6 2.7 %collective-permute-start.20 = (bf16[112,128]{1,0:T(8,128)(2,1)S(1)}, bf16[112,128]{1,0:T(8,128)(2,1)S(1)}, u32[]{:S(2)}, u32[]{:S(2)}) collective-permute-start(bf16[112,128]{1,0:T(8,128)(2,1)S(1)} %get-tuple-element.107), channel_id=1, source_target_pairs={{0,8},{8,0},{16,24},{24,16},{1,9},{9,1},{17,25},{25,17},{2,10},{10... | collective-permute-start | bytes 86024 | tf_op jit(solution)/shard_map/ppermute | solution.py:462

commit v8 on v7

--- a/solution.py
+++ b/solution.py
@@ -75,12 +75,20 @@
     return base[:, :chans] + bias, base[:, chans:] + bias, from_odd, from_even
 
 
+def conv_sum(rows, w):
+    even, odd = lanes(*[r[0] for r in rows]), lanes(*[r[1] for r in rows])
+    taps = [stack(*[w[r[2], k] for r in rows]) for k in range(3)]
+    base = dot(lanes(even, odd), stack(lanes(taps[1], taps[0]), lanes(taps[2], taps[1])))
+    chans = base.shape[1] // 2
+    return base[:, :chans] + later(dot(odd, taps[0])), base[:, chans:] + sooner(dot(even, taps[2]))
+
+
 def first_kernel(out):
     out[...] = jnp.zeros(out.shape, F32)
 
 
 def prep_kernel(ahead, img, w, dw, cot, bias, gain, shift, dbias, *refs):
-    outs, (x_out, gm_out, cb_out, img_v, scr, sems) = refs[:7], refs[7:]
+    outs, (x_out, part_out, gm_out, cb_out, img_v, scr, sems) = refs[:7], refs[7:]
     pairs = list(zip((img, w, dw, cot, bias, gain, shift, dbias), (img_v,) + outs))
     copies = [pltpu.make_async_copy(src, dst, sems.at[i]) for i, (src, dst) in enumerate(pairs)]
     for copy in copies:
@@ -92,7 +100,12 @@
         x_out[p, 1] = odd.astype(BF16)
     for copy in copies[1:]:
         copy.wait()
-    dw_v, cot_v = outs[1], outs[2]
+    w_v, dw_v, cot_v, bias_v = outs[:4]
+    own = [(x_out[p, 0], x_out[p, 1]) for p in range(2)]
+    for p in range(2):
+        he, ho = conv_sum([(*own[0], 1 - p), (*own[1], 2 - p)], w_v)
+        part_out[p, 0] = he + bias_v[...]
+        part_out[p, 1] = ho + bias_v[...]
     for p, kh in enumerate(range(3)):
         even, odd, late = back_taps(cot_v[...], dw_v, kh)
         gm_out[p, 0] = even
@@ -110,7 +123,7 @@
     return jnp.where(flag, a.astype(F32), b.astype(F32))
 
 
-def hidden_kernel(width, core, chip, own, w, bias, x_out, hid_out, stat_out, scr):
+def hidden_kernel(width, core, chip, own, part, w, x_out, hid_out, stat_out, scr):
     half = x_out.shape[2]
     odd_rank = (lax.axis_index("rows") & 1) == 1
     for p, row in ((0, either(odd_rank, core[1], chip[1])), (3, either(odd_rank, chip[0], core[0]))):
@@ -119,15 +132,10 @@
         x_out[p, 1] = odd.astype(BF16)
     for p in range(2):
         x_out[p + 1] = own[p]
-    weights = conv_weights(w)
-    even = stack(*[lanes(x_out[p, 0], x_out[p + 1, 0], x_out[p + 2, 0]) for p in range(2)])
-    odd = stack(*[lanes(x_out[p, 1], x_out[p + 1, 1], x_out[p + 2, 1]) for p in range(2)])
-    base_e, base_o, from_odd, from_even = conv_rows(even, odd, weights, bias[...])
     total = 0.0
     for p in range(2):
-        sl = slice(p * half, (p + 1) * half)
-        he = base_e[sl] + later(from_odd[sl])
-        ho = base_o[sl] + sooner(from_even[sl])
+        he, ho = conv_sum([(x_out[3 * p, 0], x_out[3 * p, 1], 2 * p)], w)
+        he, ho = part[p, 0] + he, part[p, 1] + ho
         hid_out[p, 0] = he
         hid_out[p, 1] = ho
         total = total + jnp.sum(he + ho, axis=0, keepdims=True)
@@ -519,17 +527,17 @@
         norm_shift.reshape(1, chans),
         down_bias.reshape(1, outs),
     )
-    w, dw, cot, bias, gain, shift, dbias, own_x, own_gm, cbias = run(
+    w, dw, cot, bias, gain, shift, dbias, own_x, part, own_gm, cbias = run(
         prep_kernel,
         (ahead, *raw),
-        [(v.shape, v.dtype) for v in raw[1:]] + [(block_of, BF16), ((3, 2, half, chans), F32), ((8, outs), F32)],
+        [(v.shape, v.dtype) for v in raw[1:]] + [(block_of, BF16), (block_of, F32), ((3, 2, half, chans), F32), ((8, outs), F32)],
         [pltpu.VMEM(img.shape, BF16), row_scr, pltpu.SemaphoreType.DMA((len(raw),))],
         [vmem] + [hbm] * len(raw),
     )
     chip_cot, core_cot = across(cot), swap(cot, "rows", 1)
     x, hid, stat = run(
         functools.partial(hidden_kernel, width),
-        (core_img, chip_img, own_x, w, bias),
+        (core_img, chip_img, own_x, part, w),
         [((4, 2, half, chans), BF16), (block_of, F32), tile],
         [row_scr],
     )

time: 43.2 us -> 43.2 us (level)
  starting transfers between devices: 25.1 us -> 24.6 us
  waiting for transfers between devices: 8.16 us -> 8.65 us
    ppermute x17, starting transfers between devices: 16.2 us -> 15.7 us  [swap(): lax.ppermute(x, axis, [(i, i ^ k) for i in range(lax.axis_size(axis))])]
    ppermute x17, waiting for transfers between devices: 5.63 us -> 6.12 us  [swap(): lax.ppermute(x, axis, [(i, i ^ k) for i in range(lax.axis_size(axis))])]
  transfers between devices with their start and end apart: 23 -> 23, of which waited for: 8 -> 9; matrix products, arithmetic and copies ran while one was open for 0% -> 0% of each run, Pallas kernels for 16% -> 16%
where the time goes in v8:
time: 43.2 us; the launch traced here: 43 us
  starting transfers between devices  24.6 us (57%)
  waiting for transfers between devices  8.65 us (20%)
  Pallas kernels  8.24 us (19%)
  between operations  0.82 us (2%)
  local copies, waits for them, and re-layouts  0.67 us (2%)
    ppermute x17, starting transfers between devices, swap(): lax.ppermute(x, axis, [(i, i ^ k) for i in range(lax.axis_size(axis))])  15.7 us
    pallas_call x15, Pallas kernels, run(): pl.pallas_call(kernel, in_specs=specs or [vmem] * len(args), out_shape=[j...  8.24 us
    ppermute x17, waiting for transfers between devices, swap(): lax.ppermute(x, axis, [(i, i ^ k) for i in range(lax.axis_size(axis))])  6.12 us
    ppermute x3, starting transfers between devices, around(): return lax.ppermute(x, 'dp', [(i, (i + 2 * k) % n) for i in range(n)])  5.57 us
    ppermute x3, waiting for transfers between devices, around(): return lax.ppermute(x, 'dp', [(i, (i + 2 * k) % n) for i in range(n)])  2.52 us
    ppermute x1, starting transfers between devices, swap_both(): lax.ppermute(x, both, [(i, i ^ k) for i in range(lax.axis_size(both))])  1.8 us
    ppermute x2, starting transfers between devices, across(): lax.ppermute(x, 'rows', [p for i in range(1, n - 1, 2) for p in ((i, i +...  1.48 us
  transfers between devices with their start and end apart: 23, of which 9 were waited for; matrix products, arithmetic and copies ran while one was open for 0% of the time, Pallas kernels for 16%

profile of v8, /device:TPU:0, one launch (start us, length us, event | category | flops | bytes accessed | tf_op | source)
XLA Modules:
  0.0 43.0 jit_solution(3957134806964657831)
XLA Ops:
  0.6 0.0 copy-start
  0.6 0.0 copy-start.1
  0.7 0.8 %collective-permute-start.1 = (bf16[2,512,128]{2,1,0:T(8,128)(2,1)}, bf16[2,512,128]{2,1,0:T(8,128)(2,1)S(1)}, u32[]{:S(2)}, u32[]{:S(2)}) collective-permute-start(bf16[2,512,128]{2,1,0:T(8,128)(2,1)} %bitcast.18), channel_id=1, source_target_pairs={{8,16},{16,8},{9,17},{17,9},{10,18},{18,10},{11,19},{19,11},{12,20... | collective-permute-start | bytes 786440 | tf_op jit(solution)/shard_map/ppermute | solution.py:466
  1.5 4.3 %collective-permute-start = (bf16[2,512,128]{2,1,0:T(8,128)(2,1)}, bf16[2,512,128]{2,1,0:T(8,128)(2,1)S(1)}, u32[]{:S(2)}, u32[]{:S(2)}) collective-permute-start(bf16[2,512,128]{2,1,0:T(8,128)(2,1)} %bitcast.19), channel_id=1, source_target_pairs={{0,8},{8,0},{16,24},{24,16},{1,9},{9,1},{17,25},{25,17},{2,10},{10... | collective-permute-start | bytes 786440 | tf_op jit(solution)/shard_map/ppermute | solution.py:470
  5.9 0.0 copy-start.5
  5.9 0.6 %copy-done.6 = f32[128]{0:T(128)S(1)} copy-done((f32[128]{0:T(128)S(1)}, f32[128]{0:T(128)}, u32[]{:S(2)}) %copy-start.6) | copy-done | bytes 536
  6.5 0.0 copy-done.7
  6.5 0.0 copy-done.4
  6.6 1.2 %shard_map.144 = (bf16[3,3,128,128]{3,2,1,0:T(8,128)(2,1)S(1)}, bf16[3,3,128,256]{3,2,1,0:T(8,128)(2,1)S(1)}, bf16[256,256]{1,0:T(8,128)(2,1)S(1)}, f32[1,128]{1...) custom-call(f32[8,128]{1,0:T(8,128)S(1)} %shard_map.143.ahead, ...), custom_call_target="tpu_custom_call" | custom-call | flops 134217728 | bytes 1024 | tf_op jit(solution)/shard_map/pallas_call | solution.py:502
  7.7 0.7 %collective-permute-start.6 = (bf16[256,256]{1,0:T(8,128)(2,1)S(1)}, bf16[256,256]{1,0:T(8,128)(2,1)S(1)}, u32[]{:S(2)}, u32[]{:S(2)}) collective-permute-start(bf16[256,256]{1,0:T(8,128)(2,1)S(1)} %get-tuple-element.69.cot), channel_id=1, source_target_pairs={{8,16},{16,8},{9,17},{17,9},{10,18},{18,10},{11,19},{19,11},{12,20... | collective-permute-start | bytes 393224 | tf_op jit(solution)/shard_map/ppermute | solution.py:466
  8.4 1.3 %collective-permute-start.5 = (bf16[256,256]{1,0:T(8,128)(2,1)S(1)}, bf16[256,256]{1,0:T(8,128)(2,1)S(1)}, u32[]{:S(2)}, u32[]{:S(2)}) collective-permute-start(bf16[256,256]{1,0:T(8,128)(2,1)S(1)} %get-tuple-element.69.cot), channel_id=1, source_target_pairs={{0,8},{8,0},{16,24},{24,16},{1,9},{9,1},{17,25},{25,17},{2,10},{10... | collective-permute-start | bytes 393224 | tf_op jit(solution)/shard_map/ppermute | solution.py:470
  9.8 0.0 collective-permute-done.1.chip
  9.8 0.0 collective-permute-done.core
  9.8 0.8 %shard_map.145 = (bf16[4,2,256,128]{3,2,1,0:T(8,128)(2,1)S(1)}, f32[2,2,256,128]{3,2,1,0:T(8,128)S(1)}, f32[8,128]{1,0:T(8,128)S(1)}) custom-call(bf16[2,512,128]{2,1,0:T(8,128)(2,1)S(1)} %collective-permute-done.core, bf16[2,512,128]{2,1,0:T(8,128)(2,1)S(1)} %collective-permute-done.1.chip, bf16[2,2,256,128]{3,2,1,0:T(8,128)(2,1)S(1)} %get-tuple-element.62.own, ...), custom_call_target="tpu_custom_call" | custom-call | flops 134217728 | bytes 1024 | tf_op jit(solution)/shard_map/pallas_call | solution.py:502
  10.6 1.7 %collective-permute-start.4 = (f32[8,128]{1,0:T(8,128)S(1)}, f32[8,128]{1,0:T(8,128)S(1)}, u32[]{:S(2)}, u32[]{:S(2)}) collective-permute-start(f32[8,128]{1,0:T(8,128)S(1)} %get-tuple-element.65.refs_0_), channel_id=1, source_target_pairs={{0,24},{8,16},{16,8},{24,0},{1,25},{9,17},{17,9},{25,1},{2,26},{10... | collective-permute-start | bytes 12296 | tf_op jit(solution)/shard_map/ppermute | solution.py:470
  12.3 0.2 collective-permute-start.3
  12.5 0.1 collective-permute-start.2
  12.6 0.0 collective-permute-done.6.cot_chip
  12.6 0.0 collective-permute-done.5.cot_core
  12.6 0.8 %shard_map.146 = (f32[2,2,256,128]{3,2,1,0:T(8,128)S(1)}, f32[4,2,256,128]{3,2,1,0:T(8,128)S(1)}, bf16[2,256,128]{2,1,0:T(8,128)(2,1)S(1)}, f32[8,256]{1,0:T(8,128)S(1)}) custom-call(bf16[2,512,128]{2,1,0:T(8,128)(2,1)S(1)} %collective-permute-done.core, bf16[2,512,128]{2,1,0:T(8,128)(2,1)S(1)} %collective-permute-done.1.chip, ...), custom_call_target="tpu_custom_call" | custom-call | flops 134217728 | bytes 1024 | tf_op jit(solution)/shard_map/pallas_call | solution.py:502
  13.5 0.2 collective-permute-done.4.refs_3_
  13.7 2.3 %collective-permute-done.3.refs_2_ = f32[8,128]{1,0:T(8,128)S(1)} collective-permute-done((f32[8,128]{1,0:T(8,128)S(1)}, f32[8,128]{1,0:T(8,128)S(1)}, u32[]{:S(2)}, u32[]{:S(2)}) %collective-permute-start.3) | collective-permute-done | bytes 4128 | tf_op jit(solution)/shard_map/ppermute | solution.py:470
  15.9 0.0 collective-permute-done.2.refs_1_
  15.9 0.5 %shard_map.147 = (f32[8,128]{1,0:T(8,128)S(1)}, bf16[2,256,384]{2,1,0:T(8,128)(2,1)S(1)}, f32[2,2,256,128]{3,2,1,0:T(8,128)S(1)}, f32[8,128]{1,0:T(8,128)S(1)}, f32[2,2,256,128]{3,2,1,0:T(8,128)S(1)}) custom-call(f32[8,128]{1,0:T(8,128)S(1)} %get-tuple-element.65.refs_0_, f32[8,128]{1,0:T(8,128)S(1)} %collective-permute-done.2.refs_1_, ...), custom_call_target="tpu_custom_call" | custom-call | flops 134217728 | bytes 1024 | tf_op jit(solution)/shard_map/pallas_call | solution.py:502
  16.5 0.1 collective-permute-start.10
  16.5 0.5 %shard_map.148 = (bf16[256,384]{1,0:T(8,128)(2,1)S(1)}, f32[256,128]{1,0:T(8,128)S(1)}, f32[2,2,8,32,128]{4,3,2,1,0:T(8,128)S(1)}, bf16[2,2,8,32,128]{4,3,2,1,0:T(8,128)(2,1)S(1)}) custom-call(f32[8,128]{1,0:T(8,128)S(1)} %get-tuple-element.77.par, bf16[4,2,256,128]{3,2,1,0:T(8,128)(2,1)S(1)} %get-tuple-element.66.x.refs_4_, ...), custom_call_target="tpu_custom_call" | custom-call | flops 134217728 | bytes 1024 | tf_op jit(solution)/shard_map/pallas_call | solution.py:502
  17.0 0.6 %collective-permute-start.11 = (bf16[2,2,8,32,128]{4,3,2,1,0:T(8,128)(2,1)S(1)}, bf16[2,2,8,32,128]{4,3,2,1,0:T(8,128)(2,1)S(1)}, u32[]{:S(2)}, u32[]{:S(2)}) collective-permute-start(bf16[2,2,8,32,128]{4,3,2,1,0:T(8,128)(2,1)S(1)} %get-tuple-element.84), channel_id=1, source_target_pairs={{0,8},{8,0},{16,24},{24,16},{1,9},{9,1},{17,25},{25,17},{2,10},{10... | collective-permute-start | bytes 786440 | tf_op jit(solution)/shard_map/ppermute | solution.py:470
  17.6 0.0 collective-permute-start.9
  17.6 1.7 %collective-permute-start.8 = (f32[8,128]{1,0:T(8,128)S(1)}, f32[8,128]{1,0:T(8,128)S(1)}, u32[]{:S(2)}, u32[]{:S(2)}) collective-permute-start(f32[8,128]{1,0:T(8,128)S(1)} %get-tuple-element.76.s0), channel_id=1, source_target_pairs={{0,16},{8,24},{16,0},{24,8},{1,17},{9,25},{17,1},{25,9},{2,18},{10... | collective-permute-start | bytes 12296 | tf_op jit(solution)/shard_map/ppermute | solution.py:470
  19.3 0.2 collective-permute-start.7
  19.4 0.0 collective-permute-done.11.got
  19.5 0.1 shard_map.149
  19.5 0.3 collective-permute-start.15
  19.8 0.2 shard_map.150.edge.parts
  20.0 0.6 %collective-permute-done.9.s3 = f32[8,128]{1,0:T(8,128)S(1)} collective-permute-done((f32[8,128]{1,0:T(8,128)S(1)}, f32[8,128]{1,0:T(8,128)S(1)}, u32[]{:S(2)}, u32[]{:S(2)}) %collective-permute-start.9) | collective-permute-done | bytes 4128 | tf_op jit(solution)/shard_map/ppermute | solution.py:470
  20.6 1.5 %collective-permute-start.16 = (bf16[2,4,32,128]{3,2,1,0:T(8,128)(2,1)S(1)}, bf16[2,4,32,128]{3,2,1,0:T(8,128)(2,1)S(1)}, u32[]{:S(2)}, u32[]{:S(2)}) collective-permute-start(bf16[2,4,32,128]{3,2,1,0:T(8,128)(2,1)S(1)} %get-tuple-element.101), channel_id=1, source_target_pairs={{0,1},{1,0},{2,3},{3,2},{4,5},{5,4},{6,7},{7,6},{8,9},{9,8},{10,11... | collective-permute-start | bytes 196616 | tf_op jit(solution)/shard_map/ppermute | solution.py:470
  22.1 0.0 collective-permute-done.8.s2
  22.1 0.0 collective-permute-done.7.s1
  22.1 0.0 collective-permute-done.10.far
  22.1 1.0 %shard_map.151 = (f32[8,128]{1,0:T(8,128)S(1)}, bf16[2,2,256,128]{3,2,1,0:T(8,128)(2,1)S(1)}, f32[4,48,128]{2,1,0:T(8,128)S(1)}, bf16[4,48,128]{2,1,0:T(8,128)(2...) custom-call(f32[8,128]{1,0:T(8,128)S(1)} %get-tuple-element.76.s0, ...), custom_call_target="tpu_custom_call" | custom-call | flops 4294967296 | bytes 1024 | tf_op jit(solution)/shard_map/pallas_call | solution.py:502
  23.1 1.8 %collective-permute-start.14 = (bf16[4,112,128]{2,1,0:T(8,128)(2,1)S(1)}, bf16[4,112,128]{2,1,0:T(8,128)(2,1)S(1)}, u32[]{:S(2)}, u32[]{:S(2)}) collective-permute-start(bf16[4,112,128]{2,1,0:T(8,128)(2,1)S(1)} %get-tuple-element.98), channel_id=1, source_target_pairs={{0,17},{1,16},{2,19},{3,18},{4,21},{5,20},{6,23},{7,22},{8,25},{9,... | collective-permute-start | bytes 344072 | tf_op jit(solution)/shard_map/ppermute | solution.py:481
  24.9 0.3 collective-permute-start.12
  25.2 1.4 %collective-permute-start.13 = (bf16[4,48,128]{2,1,0:T(8,128)(2,1)S(1)}, bf16[4,48,128]{2,1,0:T(8,128)(2,1)S(1)}, u32[]{:S(2)}, u32[]{:S(2)}) collective-permute-start(bf16[4,48,128]{2,1,0:T(8,128)(2,1)S(1)} %get-tuple-element.97), channel_id=1, source_target_pairs={{0,1},{1,0},{2,3},{3,2},{4,5},{5,4},{6,7},{7,6},{8,9},{9,8},{10,11... | collective-permute-start | bytes 147464 | tf_op jit(solution)/shard_map/ppermute | solution.py:470
  26.7 0.0 collective-permute-done.15.ex
  26.7 0.0 collective-permute-done.16.ey
  26.7 1.4 %shard_map.153 = (bf16[2,512,128]{2,1,0:T(8,128)(2,1)}, f32[8,128]{1,0:T(8,128)S(1)}) custom-call(f32[2,2,2,256,128]{4,3,2,1,0:T(8,128)S(1)} %shard_map.150.edge.parts, f32[4,2,256,128]{3,2,1,0:T(8,128)S(1)} %get-tuple-element.73.refs_6_.gm, f32[8,128]{1,0:T(8,128)S(1)} %get-tuple-element.89.ahead.par2, bf16[2,2,256,128]{3,2,1,0:T(8,128)(2,1)S(1)} %get-tuple-element.93.g, ...), custom_call_target="tpu_custom_call" | custom-call | flops 134217728 | bytes 1024 | tf_op jit(solution)/shard_map/pallas_call | solution.py:502
  28.1 1.0 %shard_map.152 = (bf16[256,256]{1,0:T(8,128)(2,1)}, f32[8,128]{1,0:T(8,128)S(1)}) custom-call(f32[8,128]{1,0:T(8,128)S(1)} %get-tuple-element.89.ahead.par2, bf16[256,384]{1,0:T(8,128)(2,1)S(1)} %get-tuple-element.90.mix_top, bf16[2,256,384]{2,1,0:T(8,128)(2,1)S(1)} %get-tuple-element.82.mix, bf16[3,3,128,256]{3,2,1,0:T(8,128)(2,1)S(1)} %get-tuple-element.70.dw, ...), custom_call_target="tpu_custom_call" | custom-call | flops 134217728 | bytes 1024 | tf_op jit(solution)/shard_map/pallas_call | solution.py:502
  29.1 0.0 collective-permute-done.12.gx
  29.1 0.9 %collective-permute-done.13.gy = bf16[4,48,128]{2,1,0:T(8,128)(2,1)S(1)} collective-permute-done((bf16[4,48,128]{2,1,0:T(8,128)(2,1)S(1)}, bf16[4,48,128]{2,1,0:T(8,128)(2,1)S(1)}, u32[]{:S(2)}, u32[]{:S(2)}) %collective-permute-start.13) | collective-permute-done | bytes 49184 | tf_op jit(solution)/shard_map/ppermute | solution.py:470
  30.0 0.0 collective-permute-done.14.gxy
  30.0 0.1 shard_map.155
  30.1 1.6 %collective-permute-start.17 = (bf16[112,128]{1,0:T(8,128)(2,1)S(1)}, bf16[112,128]{1,0:T(8,128)(2,1)S(1)}, u32[]{:S(2)}, u32[]{:S(2)}) collective-permute-start(bf16[112,128]{1,0:T(8,128)(2,1)S(1)} %get-tuple-element.105), channel_id=1, source_target_pairs={{0,2},{1,3},{2,4},{3,5},{4,6},{5,7},{6,0},{7,1},{8,10},{9,11},{10,... | collective-permute-start | bytes 86024 | tf_op jit(solution)/shard_map/ppermute | solution.py:475
  31.7 2.6 %collective-permute-start.18 = (bf16[112,128]{1,0:T(8,128)(2,1)S(1)}, bf16[112,128]{1,0:T(8,128)(2,1)S(1)}, u32[]{:S(2)}, u32[]{:S(2)}) collective-permute-start(bf16[112,128]{1,0:T(8,128)(2,1)S(1)} %get-tuple-element.106), channel_id=1, source_target_pairs={{0,4},{1,5},{2,6},{3,7},{4,0},{5,1},{6,2},{7,3},{8,12},{9,13},{10,... | collective-permute-start | bytes 86024 | tf_op jit(solution)/shard_map/ppermute | solution.py:475
  34.3 1.3 %collective-permute-start.19 = (bf16[112,128]{1,0:T(8,128)(2,1)S(1)}, bf16[112,128]{1,0:T(8,128)(2,1)S(1)}, u32[]{:S(2)}, u32[]{:S(2)}) collective-permute-start(bf16[112,128]{1,0:T(8,128)(2,1)S(1)} %get-tuple-element.107), channel_id=1, source_target_pairs={{0,6},{1,7},{2,0},{3,1},{4,2},{5,3},{6,4},{7,5},{8,14},{9,15},{10,... | collective-permute-start | bytes 86024 | tf_op jit(solution)/shard_map/ppermute | solution.py:475
  35.6 0.3 collective-permute-done.17.g1
  35.9 0.6 %collective-permute-done.18.g2 = bf16[112,128]{1,0:T(8,128)(2,1)S(1)} collective-permute-done((bf16[112,128]{1,0:T(8,128)(2,1)S(1)}, bf16[112,128]{1,0:T(8,128)(2,1)S(1)}, u32[]{:S(2)}, u32[]{:S(2)}) %collective-permute-start.18) | collective-permute-done | bytes 28704 | tf_op jit(solution)/shard_map/ppermute | solution.py:475
  36.5 1.7 %collective-permute-done.19.g3 = bf16[112,128]{1,0:T(8,128)(2,1)S(1)} collective-permute-done((bf16[112,128]{1,0:T(8,128)(2,1)S(1)}, bf16[112,128]{1,0:T(8,128)(2,1)S(1)}, u32[]{:S(2)}, u32[]{:S(2)}) %collective-permute-start.19) | collective-permute-done | bytes 28704 | tf_op jit(solution)/shard_map/ppermute | solution.py:475
  38.2 0.1 collective-permute-start.22
  38.3 1.3 %collective-permute-start.21 = (bf16[112,128]{1,0:T(8,128)(2,1)S(1)}, bf16[112,128]{1,0:T(8,128)(2,1)S(1)}, u32[]{:S(2)}, u32[]{:S(2)}) collective-permute-start(bf16[112,128]{1,0:T(8,128)(2,1)S(1)} %get-tuple-element.109), channel_id=1, source_target_pairs={{0,16},{8,24},{16,0},{24,8},{1,17},{9,25},{17,1},{25,9},{2,18},{10... | collective-permute-start | bytes 86024 | tf_op jit(solution)/shard_map/ppermute | solution.py:470
  39.6 0.6 %collective-permute-start.20 = (bf16[112,128]{1,0:T(8,128)(2,1)S(1)}, bf16[112,128]{1,0:T(8,128)(2,1)S(1)}, u32[]{:S(2)}, u32[]{:S(2)}) collective-permute-start(bf16[112,128]{1,0:T(8,128)(2,1)S(1)} %get-tuple-element.109), channel_id=1, source_target_pairs={{0,8},{8,0},{16,24},{24,16},{1,9},{9,1},{17,25},{25,17},{2,10},{10... | collective-permute-start | bytes 86024 | tf_op jit(solution)/shard_map/ppermute | solution.py:470
  40.1 1.5 %collective-permute-done.22.q3 = bf16[112,128]{1,0:T(8,128)(2,1)S(1)} collective-permute-done((bf16[112,128]{1,0:T(8,128)(2,1)S(1)}, bf16[112,128]{1,0:T(8,128)(2,1)S(1)}, u32[]{:S(2)}, u32[]{:S(2)}) %collective-permute-start.22) | collective-permute-done | bytes 28704 | tf_op jit(solution)/shard_map/ppermute | solution.py:470
  41.6 0.6 %collective-permute-done.21.q2 = bf16[112,128]{1,0:T(8,128)(2,1)S(1)} collective-permute-done((bf16[112,128]{1,0:T(8,128)(2,1)S(1)}, bf16[112,128]{1,0:T(8,128)(2,1)S(1)}, u32[]{:S(2)}, u32[]{:S(2)}) %collective-permute-start.21) | collective-permute-done | bytes 28704 | tf_op jit(solution)/shard_map/ppermute | solution.py:470
  42.2 0.0 collective-permute-done.20.q1
  42.2 0.7 %shard_map.157 = (f32[9,32,128]{2,1,0:T(8,128)}, f32[9,16,128]{2,1,0:T(8,128)}, f32[1,16]{1,0:T(1,128)}, f32[1,16]{1,0:T(1,128)}, f32[1,16]{1,0:T(1,128)}, /*index=5*/f32[1,32]{1,0:T(1,128)}) custom-call(f32[112,128]{1,0:T(8,128)S(1)} %get-tuple-element.108.q0, bf16[112,128]{1,0:T(8,128)(2,1)S(1)} %collective-permute-done.20.q1, ...), custom_call_target="tpu_custom_call" | custom-call | flops 134217728 | bytes 1024 | tf_op jit(solution)/shard_map/pallas_call | solution.py:502
  (13 shorter events, 0.1 us)
Async XLA Ops:
  0.6 5.2 %copy-start = (bf16[3,3,128,256]{3,2,1,0:T(8,128)(2,1)S(1)}, bf16[3,3,128,256]{3,2,1,0:T(8,128)(2,1)}, u32[]{:S(2)}) copy-start(bf16[3,3,128,256]{3,2,1,0:T(8,128)(2,1)} %dw.1) | copy-start | bytes 1769476
  0.6 5.2 %copy-start.1 = (bf16[3,3,128,128]{3,2,1,0:T(8,128)(2,1)S(1)}, bf16[3,3,128,128]{3,2,1,0:T(8,128)(2,1)}, u32[]{:S(2)}) copy-start(bf16[3,3,128,128]{3,2,1,0:T(8,128)(2,1)} %w.1) | copy-start | bytes 884740
  0.7 5.2 %copy-start.2 = (bf16[1,2,512,128]{3,2,1,0:T(8,128)(2,1)S(1)}, bf16[1,2,512,128]{3,2,1,0:T(8,128)(2,1)}, u32[]{:S(2)}) copy-start(bf16[1,2,512,128]{3,2,1,0:T(8,128)(2,1)} %param.8) | copy-start | bytes 786436
  0.7 5.2 %copy-start.3 = (bf16[1,1,256,256]{3,2,1,0:T(8,128)(2,1)S(1)}, bf16[1,1,256,256]{3,2,1,0:T(8,128)(2,1)}, u32[]{:S(2)}) copy-start(bf16[1,1,256,256]{3,2,1,0:T(8,128)(2,1)} %param.15) | copy-start | bytes 393220
  0.7 9.1 %collective-permute-start.1 = (bf16[2,512,128]{2,1,0:T(8,128)(2,1)}, bf16[2,512,128]{2,1,0:T(8,128)(2,1)S(1)}, u32[]{:S(2)}, u32[]{:S(2)}) collective-permute-start(bf16[2,512,128]{2,1,0:T(8,128)(2,1)} %bitcast.18), channel_id=1, source_target_pairs={{8,16},{16,8},{9,17},{17,9},{10,18},{18,10},{11,19},{19,11},{12,20... | collective-permute-start | bytes 786440 | tf_op jit(solution)/shard_map/ppermute | solution.py:466
  1.5 8.3 %collective-permute-start = (bf16[2,512,128]{2,1,0:T(8,128)(2,1)}, bf16[2,512,128]{2,1,0:T(8,128)(2,1)S(1)}, u32[]{:S(2)}, u32[]{:S(2)}) collective-permute-start(bf16[2,512,128]{2,1,0:T(8,128)(2,1)} %bitcast.19), channel_id=1, source_target_pairs={{0,8},{8,0},{16,24},{24,16},{1,9},{9,1},{17,25},{25,17},{2,10},{10... | collective-permute-start | bytes 786440 | tf_op jit(solution)/shard_map/ppermute | solution.py:470
  5.8 0.7 %copy-start.6 = (f32[128]{0:T(128)S(1)}, f32[128]{0:T(128)}, u32[]{:S(2)}) copy-start(f32[128]{0:T(128)} %param.11) | copy-start | bytes 1540
  5.8 0.7 %copy-start.7 = (f32[128]{0:T(128)S(1)}, f32[128]{0:T(128)}, u32[]{:S(2)}) copy-start(f32[128]{0:T(128)} %param.12) | copy-start | bytes 1540
  5.8 0.7 %copy-start.4 = (f32[256]{0:T(256)S(1)}, f32[256]{0:T(256)}, u32[]{:S(2)}) copy-start(f32[256]{0:T(256)} %param.14) | copy-start | bytes 3076
  5.9 0.7 %copy-start.5 = (f32[128]{0:T(128)S(1)}, f32[128]{0:T(128)}, u32[]{:S(2)}) copy-start(f32[128]{0:T(128)} %param.10) | copy-start | bytes 1540
  7.7 4.9 %collective-permute-start.6 = (bf16[256,256]{1,0:T(8,128)(2,1)S(1)}, bf16[256,256]{1,0:T(8,128)(2,1)S(1)}, u32[]{:S(2)}, u32[]{:S(2)}) collective-permute-start(bf16[256,256]{1,0:T(8,128)(2,1)S(1)} %get-tuple-element.69.cot), channel_id=1, source_target_pairs={{8,16},{16,8},{9,17},{17,9},{10,18},{18,10},{11,19},{19,11},{12,20... | collective-permute-start | bytes 393224 | tf_op jit(solution)/shard_map/ppermute | solution.py:466
  8.4 4.2 %collective-permute-start.5 = (bf16[256,256]{1,0:T(8,128)(2,1)S(1)}, bf16[256,256]{1,0:T(8,128)(2,1)S(1)}, u32[]{:S(2)}, u32[]{:S(2)}) collective-permute-start(bf16[256,256]{1,0:T(8,128)(2,1)S(1)} %get-tuple-element.69.cot), channel_id=1, source_target_pairs={{0,8},{8,0},{16,24},{24,16},{1,9},{9,1},{17,25},{25,17},{2,10},{10... | collective-permute-start | bytes 393224 | tf_op jit(solution)/shard_map/ppermute | solution.py:470
  10.6 3.1 %collective-permute-start.4 = (f32[8,128]{1,0:T(8,128)S(1)}, f32[8,128]{1,0:T(8,128)S(1)}, u32[]{:S(2)}, u32[]{:S(2)}) collective-permute-start(f32[8,128]{1,0:T(8,128)S(1)} %get-tuple-element.65.refs_0_), channel_id=1, source_target_pairs={{0,24},{8,16},{16,8},{24,0},{1,25},{9,17},{17,9},{25,1},{2,26},{10... | collective-permute-start | bytes 12296 | tf_op jit(solution)/shard_map/ppermute | solution.py:470
  12.3 3.6 %collective-permute-start.3 = (f32[8,128]{1,0:T(8,128)S(1)}, f32[8,128]{1,0:T(8,128)S(1)}, u32[]{:S(2)}, u32[]{:S(2)}) collective-permute-start(f32[8,128]{1,0:T(8,128)S(1)} %get-tuple-element.65.refs_0_), channel_id=1, source_target_pairs={{0,16},{8,24},{16,0},{24,8},{1,17},{9,25},{17,1},{25,9},{2,18},{10... | collective-permute-start | bytes 12296 | tf_op jit(solution)/shard_map/ppermute | solution.py:470
  12.5 3.4 %collective-permute-start.2 = (f32[8,128]{1,0:T(8,128)S(1)}, f32[8,128]{1,0:T(8,128)S(1)}, u32[]{:S(2)}, u32[]{:S(2)}) collective-permute-start(f32[8,128]{1,0:T(8,128)S(1)} %get-tuple-element.65.refs_0_), channel_id=1, source_target_pairs={{0,8},{8,0},{16,24},{24,16},{1,9},{9,1},{17,25},{25,17},{2,10},{10... | collective-permute-start | bytes 12296 | tf_op jit(solution)/shard_map/ppermute | solution.py:470
  16.5 5.7 %collective-permute-start.10 = (f32[2,2,256,128]{3,2,1,0:T(8,128)S(1)}, f32[2,2,256,128]{3,2,1,0:T(8,128)S(1)}, u32[]{:S(2)}, u32[]{:S(2)}) collective-permute-start(f32[2,2,256,128]{3,2,1,0:T(8,128)S(1)} %get-tuple-element.80), channel_id=1, source_target_pairs={{0,8},{8,0},{16,24},{24,16},{1,9},{9,1},{17,25},{25,17},{2,10},{10... | collective-permute-start | bytes 1572872 | tf_op jit(solution)/shard_map/ppermute | solution.py:470
  17.0 2.4 %collective-permute-start.11 = (bf16[2,2,8,32,128]{4,3,2,1,0:T(8,128)(2,1)S(1)}, bf16[2,2,8,32,128]{4,3,2,1,0:T(8,128)(2,1)S(1)}, u32[]{:S(2)}, u32[]{:S(2)}) collective-permute-start(bf16[2,2,8,32,128]{4,3,2,1,0:T(8,128)(2,1)S(1)} %get-tuple-element.84), channel_id=1, source_target_pairs={{0,8},{8,0},{16,24},{24,16},{1,9},{9,1},{17,25},{25,17},{2,10},{10... | collective-permute-start | bytes 786440 | tf_op jit(solution)/shard_map/ppermute | solution.py:470
  17.6 3.0 %collective-permute-start.9 = (f32[8,128]{1,0:T(8,128)S(1)}, f32[8,128]{1,0:T(8,128)S(1)}, u32[]{:S(2)}, u32[]{:S(2)}) collective-permute-start(f32[8,128]{1,0:T(8,128)S(1)} %get-tuple-element.76.s0), channel_id=1, source_target_pairs={{0,24},{8,16},{16,8},{24,0},{1,25},{9,17},{17,9},{25,1},{2,26},{10... | collective-permute-start | bytes 12296 | tf_op jit(solution)/shard_map/ppermute | solution.py:470
  17.6 4.6 %collective-permute-start.8 = (f32[8,128]{1,0:T(8,128)S(1)}, f32[8,128]{1,0:T(8,128)S(1)}, u32[]{:S(2)}, u32[]{:S(2)}) collective-permute-start(f32[8,128]{1,0:T(8,128)S(1)} %get-tuple-element.76.s0), channel_id=1, source_target_pairs={{0,16},{8,24},{16,0},{24,8},{1,17},{9,25},{17,1},{25,9},{2,18},{10... | collective-permute-start | bytes 12296 | tf_op jit(solution)/shard_map/ppermute | solution.py:470
  19.3 2.8 %collective-permute-start.7 = (f32[8,128]{1,0:T(8,128)S(1)}, f32[8,128]{1,0:T(8,128)S(1)}, u32[]{:S(2)}, u32[]{:S(2)}) collective-permute-start(f32[8,128]{1,0:T(8,128)S(1)} %get-tuple-element.76.s0), channel_id=1, source_target_pairs={{0,8},{8,0},{16,24},{24,16},{1,9},{9,1},{17,25},{25,17},{2,10},{10... | collective-permute-start | bytes 12296 | tf_op jit(solution)/shard_map/ppermute | solution.py:470
  19.5 7.2 %collective-permute-start.15 = (bf16[2,4,32,128]{3,2,1,0:T(8,128)(2,1)S(1)}, bf16[2,4,32,128]{3,2,1,0:T(8,128)(2,1)S(1)}, u32[]{:S(2)}, u32[]{:S(2)}) collective-permute-start(bf16[2,4,32,128]{3,2,1,0:T(8,128)(2,1)S(1)} %get-tuple-element.100), channel_id=1, source_target_pairs={{0,16},{8,24},{16,0},{24,8},{1,17},{9,25},{17,1},{25,9},{2,18},{10... | collective-permute-start | bytes 196616 | tf_op jit(solution)/shard_map/ppermute | solution.py:470
  20.6 6.1 %collective-permute-start.16 = (bf16[2,4,32,128]{3,2,1,0:T(8,128)(2,1)S(1)}, bf16[2,4,32,128]{3,2,1,0:T(8,128)(2,1)S(1)}, u32[]{:S(2)}, u32[]{:S(2)}) collective-permute-start(bf16[2,4,32,128]{3,2,1,0:T(8,128)(2,1)S(1)} %get-tuple-element.101), channel_id=1, source_target_pairs={{0,1},{1,0},{2,3},{3,2},{4,5},{5,4},{6,7},{7,6},{8,9},{9,8},{10,11... | collective-permute-start | bytes 196616 | tf_op jit(solution)/shard_map/ppermute | solution.py:470
  23.1 6.9 %collective-permute-start.14 = (bf16[4,112,128]{2,1,0:T(8,128)(2,1)S(1)}, bf16[4,112,128]{2,1,0:T(8,128)(2,1)S(1)}, u32[]{:S(2)}, u32[]{:S(2)}) collective-permute-start(bf16[4,112,128]{2,1,0:T(8,128)(2,1)S(1)} %get-tuple-element.98), channel_id=1, source_target_pairs={{0,17},{1,16},{2,19},{3,18},{4,21},{5,20},{6,23},{7,22},{8,25},{9,... | collective-permute-start | bytes 344072 | tf_op jit(solution)/shard_map/ppermute | solution.py:481
  24.9 4.2 %collective-permute-start.12 = (bf16[4,48,128]{2,1,0:T(8,128)(2,1)S(1)}, bf16[4,48,128]{2,1,0:T(8,128)(2,1)S(1)}, u32[]{:S(2)}, u32[]{:S(2)}) collective-permute-start(bf16[4,48,128]{2,1,0:T(8,128)(2,1)S(1)} %get-tuple-element.96), channel_id=1, source_target_pairs={{0,16},{8,24},{16,0},{24,8},{1,17},{9,25},{17,1},{25,9},{2,18},{10... | collective-permute-start | bytes 147464 | tf_op jit(solution)/shard_map/ppermute | solution.py:470
  25.2 4.8 %collective-permute-start.13 = (bf16[4,48,128]{2,1,0:T(8,128)(2,1)S(1)}, bf16[4,48,128]{2,1,0:T(8,128)(2,1)S(1)}, u32[]{:S(2)}, u32[]{:S(2)}) collective-permute-start(bf16[4,48,128]{2,1,0:T(8,128)(2,1)S(1)} %get-tuple-element.97), channel_id=1, source_target_pairs={{0,1},{1,0},{2,3},{3,2},{4,5},{5,4},{6,7},{7,6},{8,9},{9,8},{10,11... | collective-permute-start | bytes 147464 | tf_op jit(solution)/shard_map/ppermute | solution.py:470
  30.1 5.8 %collective-permute-start.17 = (bf16[112,128]{1,0:T(8,128)(2,1)S(1)}, bf16[112,128]{1,0:T(8,128)(2,1)S(1)}, u32[]{:S(2)}, u32[]{:S(2)}) collective-permute-start(bf16[112,128]{1,0:T(8,128)(2,1)S(1)} %get-tuple-element.105), channel_id=1, source_target_pairs={{0,2},{1,3},{2,4},{3,5},{4,6},{5,7},{6,0},{7,1},{8,10},{9,11},{10,... | collective-permute-start | bytes 86024 | tf_op jit(solution)/shard_map/ppermute | solution.py:475
  31.7 4.8 %collective-permute-start.18 = (bf16[112,128]{1,0:T(8,128)(2,1)S(1)}, bf16[112,128]{1,0:T(8,128)(2,1)S(1)}, u32[]{:S(2)}, u32[]{:S(2)}) collective-permute-start(bf16[112,128]{1,0:T(8,128)(2,1)S(1)} %get-tuple-element.106), channel_id=1, source_target_pairs={{0,4},{1,5},{2,6},{3,7},{4,0},{5,1},{6,2},{7,3},{8,12},{9,13},{10,... | collective-permute-start | bytes 86024 | tf_op jit(solution)/shard_map/ppermute | solution.py:475
  34.3 3.9 %collective-permute-start.19 = (bf16[112,128]{1,0:T(8,128)(2,1)S(1)}, bf16[112,128]{1,0:T(8,128)(2,1)S(1)}, u32[]{:S(2)}, u32[]{:S(2)}) collective-permute-start(bf16[112,128]{1,0:T(8,128)(2,1)S(1)} %get-tuple-element.107), channel_id=1, source_target_pairs={{0,6},{1,7},{2,0},{3,1},{4,2},{5,3},{6,4},{7,5},{8,14},{9,15},{10,... | collective-permute-start | bytes 86024 | tf_op jit(solution)/shard_map/ppermute | solution.py:475
  38.2 3.4 %collective-permute-start.22 = (bf16[112,128]{1,0:T(8,128)(2,1)S(1)}, bf16[112,128]{1,0:T(8,128)(2,1)S(1)}, u32[]{:S(2)}, u32[]{:S(2)}) collective-permute-start(bf16[112,128]{1,0:T(8,128)(2,1)S(1)} %get-tuple-element.109), channel_id=1, source_target_pairs={{0,24},{8,16},{16,8},{24,0},{1,25},{9,17},{17,9},{25,1},{2,26},{10... | collective-permute-start | bytes 86024 | tf_op jit(solution)/shard_map/ppermute | solution.py:470
  38.3 4.0 %collective-permute-start.21 = (bf16[112,128]{1,0:T(8,128)(2,1)S(1)}, bf16[112,128]{1,0:T(8,128)(2,1)S(1)}, u32[]{:S(2)}, u32[]{:S(2)}) collective-permute-start(bf16[112,128]{1,0:T(8,128)(2,1)S(1)} %get-tuple-element.109), channel_id=1, source_target_pairs={{0,16},{8,24},{16,0},{24,8},{1,17},{9,25},{17,1},{25,9},{2,18},{10... | collective-permute-start | bytes 86024 | tf_op jit(solution)/shard_map/ppermute | solution.py:470
  39.6 2.7 %collective-permute-start.20 = (bf16[112,128]{1,0:T(8,128)(2,1)S(1)}, bf16[112,128]{1,0:T(8,128)(2,1)S(1)}, u32[]{:S(2)}, u32[]{:S(2)}) collective-permute-start(bf16[112,128]{1,0:T(8,128)(2,1)S(1)} %get-tuple-element.109), channel_id=1, source_target_pairs={{0,8},{8,0},{16,24},{24,16},{1,9},{9,1},{17,25},{25,17},{2,10},{10... | collective-permute-start | bytes 86024 | tf_op jit(solution)/shard_map/ppermute | solution.py:470
